TPU v7x, 32 devices: a whole 2x2x4 slice. The times are simulated.
32 devices in a mesh: dp: 2 (over x), tm: 4 (over y, core), mp: 4 (over z).
Axes of the slice: x: 2, y: 2, z: 4, core: 2. Of those that a mesh axis runs over, the one named last changes fastest.
Arguments:
- activations: bfloat16 [2, 8, 5, 40, 1280], P('dp', 'tm', None, None, 'mp'), may hold values from -1200 to 1200
- norm_gain: float32 [1280], P('mp'), may hold values from 0.25 to 1.75
- norm_bias: float32 [1280], P('mp'), may hold values from -3 to 3
- spatial_weight: bfloat16 [9, 1280, 1280], P(None, 'mp', 'tm'), may hold values from -0.0546875 to 0.0546875
- temporal_weight: bfloat16 [3, 1280, 1280], P(None, 'tm', 'mp'), may hold values from -0.09375 to 0.09375
- cotangent: bfloat16 [2, 8, 5, 40, 1280], P('dp', 'tm', None, None, 'mp'), may hold values from -6 to 6
Outputs:
- block_output: bfloat16 [2, 8, 5, 40, 1280], P('dp', 'tm', None, None, 'mp')
- temporal_grad: float32 [3, 1280, 1280], P(None, 'tm', 'mp')
All inputs are finite; a program needn't handle non-finite values.
Results may differ from a plain program's by a relative error of at most 0.0058.
Values may be sent and summed in bfloat16 or wider, within the bound.
No kernel may reach another device: no remote copies, remote signals or barrier semaphores. Data moves between devices by JAX's collectives and lax.ppermute only.
A program may use at most 64 MiB of HBM per device.

v0:
```python
import jax
import jax.numpy as jnp
from jax import lax
from jax.sharding import PartitionSpec as P

CHANNELS = 1280
GROUPS = 32


epsilon = 1e-05


def clip_gather(block):
    return lax.all_gather(block, "tm", axis=1, tiled=True)


def group_mean(channel_sums, total_count, group_width):
    grouped = channel_sums.reshape(-1, group_width).sum(axis=1) / total_count
    return jnp.repeat(grouped, group_width)


def body(activations, norm_gain, norm_bias, spatial_weight, temporal_weight, cotangent):
    frames_dev = activations.shape[1]
    rows_band = activations.shape[2]
    columns = activations.shape[3]
    width_mp = activations.shape[4]
    width_tm = spatial_weight.shape[2]
    tm_count = lax.axis_size("tm")
    mp_count = lax.axis_size("mp")
    frames_all = frames_dev * tm_count
    group_width = CHANNELS // GROUPS
    total_count = float(frames_all * rows_band * columns * group_width)
    values = clip_gather(activations).astype(jnp.float32)
    mean_full = group_mean(values.sum(axis=(0, 1, 2, 3)), total_count, group_width)
    centered = values - mean_full
    var_full = group_mean((centered * centered).sum(axis=(0, 1, 2, 3)), total_count, group_width)
    normed = centered * lax.rsqrt(var_full + epsilon) * norm_gain + norm_bias
    hidden = jax.nn.silu(normed).astype(jnp.bfloat16)
    padded = jnp.pad(hidden[0], ((0, 0), (1, 1), (1, 1), (0, 0)))
    portion = padded
    summed = jnp.zeros(
        (lax.axis_size("mp") * (frames_all // mp_count) * rows_band * columns, width_tm),
        jnp.float32,
    )
    for spatial_tap_index in range(9):
        row_shift = spatial_tap_index // 3
        col_shift = spatial_tap_index % 3
        spatial_window = portion[
            :, row_shift : row_shift + rows_band, col_shift : col_shift + columns, :
        ].reshape(-1, width_mp)
        summed = summed + jnp.dot(
            spatial_window, spatial_weight[spatial_tap_index], preferred_element_type=jnp.float32
        )
    spatial_out = lax.psum_scatter(
        summed.reshape(
            lax.axis_size("mp") * (frames_all // mp_count), rows_band, columns, width_tm
        ),
        "mp",
        scatter_dimension=0,
        tiled=True,
    ).astype(jnp.bfloat16)
    spatial_all = lax.all_gather(spatial_out, "mp", axis=0, tiled=True)
    spatial_pad = jnp.pad(spatial_all, ((1, 1), (0, 0), (0, 0), (0, 0)))
    portion = spatial_pad
    summed = jnp.zeros(
        (lax.axis_size("tm") * frames_dev * rows_band * columns, width_mp), jnp.float32
    )
    for temporal_tap_index in range(3):
        temporal_window = portion[
            temporal_tap_index : temporal_tap_index + lax.axis_size("tm") * frames_dev
        ].reshape(-1, width_tm)
        summed = summed + jnp.dot(
            temporal_window, temporal_weight[temporal_tap_index], preferred_element_type=jnp.float32
        )
    block_output = lax.psum_scatter(
        summed.reshape(lax.axis_size("tm") * frames_dev, rows_band, columns, width_mp),
        "tm",
        scatter_dimension=0,
        tiled=True,
    ).astype(jnp.bfloat16)[None]
    grad_all = clip_gather(cotangent)[0].reshape(-1, width_mp)
    tap_grads = []
    for tap_index in range(3):
        window = spatial_pad[tap_index : tap_index + frames_all].reshape(-1, width_tm)
        tap_grads.append(
            lax.dot_general(
                window, grad_all, (((0,), (0,)), ((), ())), preferred_element_type=jnp.float32
            )
        )
    clip_count = lax.axis_size("dp")
    temporal_grad = lax.psum(jnp.stack(tap_grads), "dp") / clip_count
    return (block_output, temporal_grad)


def solution(mesh):
    in_specs = (
        P("dp", "tm", None, None, "mp"),
        P("mp"),
        P("mp"),
        P(None, "mp", "tm"),
        P(None, "tm", "mp"),
        P("dp", "tm", None, None, "mp"),
    )
    out_specs = (P("dp", "tm", None, None, "mp"), P(None, "tm", "mp"))
    return jax.shard_map(body, mesh=mesh, in_specs=in_specs, out_specs=out_specs, check_vma=False)
```

profile of v0, /device:TPU:0, one launch (start us, length us, event | category | flops | bytes accessed | tf_op | source)
XLA Modules:
  0.0 209.4 jit_solution(15808437181234581535)
XLA Ops:
  7.2 12.7 %all_gather.9 = bf16[1,8,5,40,320]{4,3,2,0,1:T(8,128)(2,1)S(1)} all-gather(bf16[1,2,5,40,320]{4,3,2,0,1:T(8,128)(2,1)} %bitcast.101), channel_id=1, replica_groups=mesh['dp'=2,'tm'=4,'mp'=4] {'tm'}, dimensions={1}, use_global_device_ids=true | all-gather | bytes 1280000 | tf_op jit(solution)/shard_map/all_gather | solution.py:14
  21.4 0.9 fusion.55
  22.2 0.9 fusion.10
  23.1 2.9 %pad_slice_fusion = (bf16[8,5,40,320]{3,2,1,0:T(8,128)(2,1)S(1)}, bf16[8,5,40,320]{3,2,1,0:T(8,128)(2,1)S(1)}, bf16[8,5,40,320]{3,2,1,0:T(8,128)(2,1)S(1)}, bf16...) fusion(bf16[8,5,40,320]{3,2,1,0:T(8,128)(2,1)S(1)} %fusion.55), kind=kLoop, calls=%fused_computation | loop fusion | bytes 9216000 | tf_op jit(solution)/shard_map/slice | solution.py:48
  26.0 0.8 fusion.23
  26.8 0.8 convolution_add_fusion.9
  27.6 0.8 convolution_add_fusion.8
  28.4 0.8 convolution_add_fusion.7
  29.3 0.8 convolution_add_fusion.6
  30.1 0.8 convolution_add_fusion.5
  30.9 0.8 convolution_add_fusion.4
  31.7 0.8 convolution_add_fusion.3
  32.5 0.8 convolution_add_fusion.2
  33.3 2.1 %copy.16 = f32[1600,320]{1,0:T(8,128)} copy(f32[1600,320]{0,1:T(8,128)S(1)} %convolution_add_fusion.2) | data formatting | bytes 4096000 | tf_op jit(solution)/shard_map/add | solution.py:51
  35.5 0.9 copy-done.6
  36.4 11.1 %all_gather.11 = bf16[1,8,5,40,320]{4,3,2,0,1:T(8,128)(2,1)S(1)} all-gather(bf16[1,2,5,40,320]{4,3,2,0,1:T(8,128)(2,1)S(1)} %bitcast.102), channel_id=1, replica_groups=mesh['dp'=2,'tm'=4,'mp'=4] {'tm'}, dimensions={1}, use_global_device_ids=true | all-gather | bytes 1280000 | tf_op jit(solution)/shard_map/all_gather | solution.py:14
  47.5 38.5 %reduce-scatter.3.cloned.1.call-done = f32[2,5,40,320]{3,2,1,0:T(8,128)} async-done(((f32[8,5,40,320]{3,2,1,0:T(8,128)}), f32[2,5,40,320]{3,2,1,0:T(8,128)}) %reduce-scatter.3.cloned.1.call-update) | async-done | bytes 512016 | tf_op jit(solution)/shard_map/reduce_scatter | solution.py:54
  86.0 1.1 convert_element_type.18
  87.1 24.2 %all_gather.10 = bf16[8,5,40,320]{3,2,1,0:T(8,128)(2,1)S(1)} all-gather(bf16[2,5,40,320]{3,2,1,0:T(8,128)(2,1)S(1)} %convert_element_type.18), channel_id=1, replica_groups=mesh['dp'=2,'tm'=4,'mp'=4] {'mp'}, dimensions={0}, use_global_device_ids=true | all-gather | bytes 1280000 | tf_op jit(solution)/shard_map/all_gather | solution.py:62
  111.6 0.8 convolution_bitcast_fusion
  112.4 0.8 convolution_bitcast_fusion.2
  113.2 0.8 convolution_bitcast_fusion.1
  114.0 1.2 pad_maximum_fusion
  115.2 0.5 copy-done.1
  116.0 0.8 fusion.13
  116.8 0.8 convolution_add_fusion.1
  118.1 0.8 convolution_add_fusion
  118.9 2.1 %copy.17 = f32[1600,320]{1,0:T(8,128)} copy(f32[1600,320]{0,1:T(8,128)S(1)} %convolution_add_fusion) | data formatting | bytes 4096000 | tf_op jit(solution)/shard_map/add | solution.py:72
  121.0 43.8 %all-reduce.4.cloned.1.call-done = f32[3,320,320]{2,1,0:T(8,128)} async-done(((f32[3,320,320]{2,1,0:T(8,128)}), f32[3,320,320]{2,1,0:T(8,128)}) %all-reduce.4.cloned.1.call-update) | async-done | bytes 1228816 | tf_op jit(solution)/shard_map/psum | solution.py:91
  164.8 2.6 %broadcast_multiply_fusion = f32[3,320,320]{2,1,0:T(8,128)} fusion(f32[3,320,320]{2,1,0:T(8,128)} %all-reduce.4.cloned.1.call-done), kind=kLoop, calls=%fused_computation.37 | loop fusion | flops 307200 | bytes 2457600 | tf_op jit(solution)/shard_map/div | solution.py:91
  167.4 33.7 %reduce-scatter.5.cloned.1.call-done = f32[2,5,40,320]{3,2,1,0:T(8,128)} async-done(((f32[8,5,40,320]{3,2,1,0:T(8,128)}), f32[2,5,40,320]{3,2,1,0:T(8,128)}) %reduce-scatter.5.cloned.1.call-update) | async-done | bytes 512016 | tf_op jit(solution)/shard_map/reduce_scatter | solution.py:75
  201.0 1.8 convert_bitcast_fusion
  (35 shorter events, 2.5 us)
Async XLA Ops:
  7.2 14.2 %copy-start.8 = (f32[320]{0:T(512)S(1)}, f32[320]{0:T(512)}, u32[]{:S(2)}) copy-start(f32[320]{0:T(512)} %param.7) | copy-start | bytes 3844
  7.2 14.2 %copy-start.7 = (f32[320]{0:T(512)S(1)}, f32[320]{0:T(512)}, u32[]{:S(2)}) copy-start(f32[320]{0:T(512)} %param.8) | copy-start | bytes 3844
  7.2 78.8 %reduce-scatter.3.cloned.1.call-start = ((), (), s32[]{:S(2)}) async-start(), calls=%async_computation.2 | async-start | bytes 3072000 | tf_op jit(solution)/shard_map/reduce_scatter | solution.py:54
  23.1 2.9 %copy-start.4 = (bf16[9,320,320]{2,1,0:T(8,128)(2,1)S(1)}, bf16[9,320,320]{2,1,0:T(8,128)(2,1)}, u32[]{:S(2)}) copy-start(bf16[9,320,320]{2,1,0:T(8,128)(2,1)} %param.9) | copy-start | bytes 5529604
  35.4 1.0 copy-start.6
  35.4 129.3 %all-reduce.4.cloned.1.call-start = ((), (), s32[]{:S(2)}) async-start(), calls=%async_computation.4 | async-start | bytes 2949120 | tf_op jit(solution)/shard_map/psum | solution.py:91
  111.6 1.6 copy-start
  111.6 1.6 copy-start.2
  113.9 1.8 copy-start.1
  114.0 2.0 copy-start.5
  115.2 85.9 %reduce-scatter.5.cloned.1.call-start = ((), (), s32[]{:S(2)}) async-start(), calls=%async_computation.3 | async-start | bytes 3072000 | tf_op jit(solution)/shard_map/reduce_scatter | solution.py:75
  116.8 1.3 copy-start.3
Sparse Core Ops, SparseCore 0:
  35.5 50.4 reduce-scatter.2
  115.3 49.4 all-reduce.3
  167.3 33.6 reduce-scatter.4
where the time goes:
time: 210 us; the launch traced here: 209 us
  waiting for transfers between devices  116 us (55%)
  blocking collectives  48 us (23%)
  between operations  14 us (7%)
  matrix products  12 us (6%)
  local copies, waits for them, and re-layouts  9.87 us (5%)
  other arithmetic  9.39 us (4%)
    psum x1, waiting for transfers between devices, body(): temporal_grad = lax.psum(jnp.stack(tap_grads), 'dp') / clip_count  43.8 us
    reduce_scatter x1, waiting for transfers between devices, body(): lax.psum_scatter(summed.reshape(lax.axis_size('mp') * (frames_all // mp_c...  38.5 us
    reduce_scatter x1, waiting for transfers between devices, body(): lax.psum_scatter(summed.reshape(lax.axis_size('tm') * frames_dev, rows_ba...  33.7 us
    all_gather x1, blocking collectives, body(): spatial_all = lax.all_gather(spatial_out, 'mp', axis=0, tiled=True)  24.2 us
    all_gather x2, blocking collectives, clip_gather(): return lax.all_gather(block, 'tm', axis=1, tiled=True)  23.8 us
    dot_general x9, matrix products, body(): jnp.dot(spatial_window, spatial_weight[spatial_tap_index], preferred_elem...  7.22 us
  transfers between devices with their start and end apart: 3, of which 3 were waited for; matrix products, arithmetic and copies ran while one was open for 3% of the time, Pallas kernels for 0%

commit v1 on v0

v1 whole, which is shorter than its diff:
```python
import functools

import jax
import jax.numpy as jnp
from jax import lax
from jax.experimental import pallas as pl
from jax.experimental.pallas import tpu as pltpu
from jax.sharding import PartitionSpec as P

CHANNELS = 1280
GROUPS = 32
GROUP_WIDTH = CHANNELS // GROUPS
EPSILON = 1e-05

f32 = jnp.float32
bf16 = jnp.bfloat16


def group_sum(rows):
    width = rows.shape[1]
    first = lax.broadcasted_iota(jnp.int32, (width, width), 0) // GROUP_WIDTH
    second = lax.broadcasted_iota(jnp.int32, (width, width), 1) // GROUP_WIDTH
    same = jnp.where(first == second, 1.0, 0.0).astype(f32)
    return jnp.dot(rows, same, precision=lax.Precision.HIGHEST, preferred_element_type=f32)


def stats_kernel(x_ref, out_ref):
    frames, rows, cols, width = x_ref.shape
    count = frames * rows * cols
    values = x_ref[...].astype(f32).reshape(count // 8, 8, width)
    mean = group_sum(values.sum(axis=0)).sum(axis=0, keepdims=True) / (count * GROUP_WIDTH)
    centered = values - mean[None]
    square = group_sum((centered * centered).sum(axis=0)).sum(axis=0, keepdims=True)
    out_ref[0:8, :] = jnp.broadcast_to(mean, (8, width))
    out_ref[8:16, :] = jnp.broadcast_to(square, (8, width))


def piece_stats(piece):
    return pl.pallas_call(
        stats_kernel,
        out_shape=jax.ShapeDtypeStruct((16, piece.shape[-1]), f32),
        in_specs=[pl.BlockSpec(memory_space=pltpu.VMEM)],
        out_specs=pl.BlockSpec(memory_space=pltpu.VMEM),
        name="piece_stats",
    )(piece)


def conv_kernel(x_ref, s0_ref, s1_ref, s2_ref, s3_ref, gain_ref, bias_ref, w_ref, out_ref, cols_ref):
    frames, rows, cols, width = x_ref.shape
    band = frames * cols
    stats = [s0_ref, s1_ref, s2_ref, s3_ref]
    means = [s[0:8, :] for s in stats]
    mean = (means[0] + means[1] + means[2] + means[3]) / 4.0
    count = frames * rows * cols * GROUP_WIDTH
    square = sum(s[8:16, :] for s in stats)
    square = square + count * sum((m - mean) * (m - mean) for m in means)
    scale = lax.rsqrt(square / (4.0 * count) + EPSILON)[0:1]
    mean = mean[0:1]
    gain = gain_ref[...]
    bias = bias_ref[...]
    cols_ref[0:band, :] = jnp.zeros((band, 3 * width), bf16)
    cols_ref[(rows + 1) * band :, :] = jnp.zeros((band, 3 * width), bf16)
    column = lax.broadcasted_iota(jnp.int32, (band, width), 0) % cols
    for row in range(rows):
        values = jnp.concatenate([x_ref[f, row].astype(f32) for f in range(frames)], axis=0)
        normed = (values - mean) * scale * gain + bias
        hidden = normed / (1.0 + jnp.exp(-normed))
        left = jnp.where(column == 0, 0.0, pltpu.roll(hidden, 1, 0))
        right = jnp.where(column == cols - 1, 0.0, pltpu.roll(hidden, band - 1, 0))
        line = jnp.concatenate([left.astype(bf16), hidden.astype(bf16), right.astype(bf16)], axis=1)
        cols_ref[(row + 1) * band : (row + 2) * band, :] = line
    total = jnp.dot(cols_ref[0 : rows * band, :], w_ref[0], preferred_element_type=f32)
    for tap in (1, 2):
        total = total + jnp.dot(
            cols_ref[tap * band : (tap + rows) * band, :], w_ref[tap], preferred_element_type=f32
        )
    out_ref[...] = total.astype(bf16)


def piece_conv(piece, stats, gain, bias, weight):
    frames, rows, cols, width = piece.shape
    width_out = weight.shape[-1]
    count = frames * rows * cols
    return pl.pallas_call(
        conv_kernel,
        out_shape=jax.ShapeDtypeStruct((count, width_out), bf16),
        in_specs=[pl.BlockSpec(memory_space=pltpu.VMEM)] * 8,
        out_specs=pl.BlockSpec(memory_space=pltpu.VMEM),
        scratch_shapes=[pltpu.VMEM(((rows + 2) * frames * cols, 3 * width), bf16)],
        compiler_params=pltpu.CompilerParams(vmem_limit_bytes=32 * 1024 * 1024),
        cost_estimate=pl.CostEstimate(
            flops=2 * count * 9 * width * width_out,
            bytes_accessed=2 * 9 * width * width_out + 4 * count * width,
            transcendentals=count * width,
        ),
        name="piece_conv",
    )(piece, *stats, gain, bias, weight)


def xor(axis_size, bit):
    return [(i, i ^ bit) for i in range(axis_size)]


def add16(a, b):
    return (a.astype(f32) + b.astype(f32)).astype(bf16)


def tie(x, *others):
    return lax.optimization_barrier((x,) + others)[0]


def line_all_reduce(parts):
    position = lax.axis_index("mp")
    at_end = (position == 0) | (position == 3)
    n = len(parts)
    arrived = [lax.ppermute(p, "mp", [(0, 1), (3, 2)]) for p in parts]
    half, other, full, back, out = ([None] * n for _ in range(5))
    last = parts[0]
    for k in range(n + 2):
        if k < n:
            half[k] = add16(tie(parts[k], last), arrived[k])
            other[k] = lax.ppermute(half[k], "mp", [(1, 2), (2, 1)])
            last = half[k]
        if 0 <= k - 1 < n:
            full[k - 1] = add16(tie(half[k - 1], last), other[k - 1])
            back[k - 1] = lax.ppermute(full[k - 1], "mp", [(1, 0), (2, 3)])
            last = full[k - 1]
        if 0 <= k - 2 < n:
            out[k - 2] = jnp.where(at_end, back[k - 2], tie(full[k - 2], last))
            last = out[k - 2]
    return out


def in_order(pieces):
    index = lax.axis_index("tm")
    odd = (index & 1) == 1
    high = (index & 2) == 2
    a, b, c, d = pieces
    a, b = jnp.where(odd, b, a), jnp.where(odd, a, b)
    c, d = jnp.where(odd, d, c), jnp.where(odd, c, d)
    a, c = jnp.where(high, c, a), jnp.where(high, a, c)
    b, d = jnp.where(high, d, b), jnp.where(high, b, d)
    return jnp.concatenate([a, b, c, d], axis=0)


def body(activations, norm_gain, norm_bias, spatial_weight, temporal_weight, cotangent):
    own = activations[0]
    frames, rows, cols, width = own.shape
    width_out = spatial_weight.shape[2]
    core, chip = xor(4, 1), xor(4, 2)
    count = rows * cols

    st_own = piece_stats(own)
    st_chip = lax.ppermute(st_own, "tm", chip)
    st_core = lax.ppermute(st_own, "tm", core)
    st_both = lax.ppermute(st_own, "tm", xor(4, 3))
    raw_core = lax.ppermute(own, "tm", core)
    raw_chip = lax.ppermute(own, "tm", chip)
    raw_both = lax.ppermute(raw_chip, "tm", core)
    stats = (st_own, st_core, st_chip, st_both)

    gain = norm_gain.reshape(1, width)
    bias = norm_bias.reshape(1, width)
    taps = spatial_weight.reshape(3, 3 * width, width_out)
    parts = []
    for piece in (own, raw_core, raw_chip, raw_both):
        parts.append(piece_conv(piece, stats, gain, bias, taps))
    reduced = line_all_reduce(parts)

    cot_own = cotangent[0]
    cot_core = lax.ppermute(cot_own, "tm", core)
    cot_chip = lax.ppermute(cot_own, "tm", chip)
    cot_both = lax.ppermute(cot_chip, "tm", core)
    cot = in_order([cot_own, cot_core, cot_chip, cot_both]).reshape(-1, cot_own.shape[-1])

    spatial = in_order(
        [r.reshape(rows, frames, cols, width_out).transpose(1, 0, 2, 3) for r in reduced]
    )
    frames_all = 4 * frames
    padded = jnp.pad(spatial, ((1, 1), (0, 0), (0, 0), (0, 0)))
    windows = [padded[k : k + frames_all].reshape(-1, width_out) for k in range(3)]

    clips = lax.axis_size("dp")
    grads = []
    for k in range(3):
        grads.append(
            lax.dot_general(
                windows[k], cot, (((0,), (0,)), ((), ())), preferred_element_type=f32
            )
        )
    grad = jnp.stack(grads)
    if clips == 2:
        sent = grad.astype(bf16)
        other = lax.ppermute(sent, "dp", [(0, 1), (1, 0)])
        temporal_grad = (sent.astype(f32) + other.astype(f32)) / clips
    else:
        temporal_grad = lax.psum(grad, "dp") / clips

    summed = sum(
        jnp.dot(windows[k], temporal_weight[k], preferred_element_type=f32) for k in range(3)
    ).reshape(4, frames, rows, cols, -1)
    index = lax.axis_index("tm")
    part = [lax.dynamic_index_in_dim(summed, index ^ i, 0, keepdims=False) for i in range(4)]
    far = lax.ppermute(part[3].astype(bf16), "tm", core)
    near = lax.ppermute(part[1].astype(bf16), "tm", core)
    to_chip = (part[2] + far.astype(f32)).astype(bf16)
    from_chip = lax.ppermute(to_chip, "tm", chip)
    block = (part[0] + near.astype(f32) + from_chip.astype(f32)).astype(bf16)[None]
    return block, temporal_grad


def solution(mesh):
    in_specs = (
        P("dp", "tm", None, None, "mp"),
        P("mp"),
        P("mp"),
        P(None, "mp", "tm"),
        P(None, "tm", "mp"),
        P("dp", "tm", None, None, "mp"),
    )
    out_specs = (P("dp", "tm", None, None, "mp"), P(None, "tm", "mp"))
    return jax.shard_map(body, mesh=mesh, in_specs=in_specs, out_specs=out_specs, check_vma=False)
```

time: 210 us -> 117 us (0.56)
  waiting for transfers between devices: 116 us -> 44 us
  blocking collectives: 48 us -> 0 us
  starting transfers between devices: 0.12 us -> 35.6 us
  between operations: 14 us -> 1.15 us
  Pallas kernels: 0 us -> 9.46 us
  matrix products: 12 us -> 7.38 us
    reduce_scatter x2 -> x0, waiting for transfers between devices: 72.2 us -> none  [the longest x1 38.5 us: body(): lax.psum_scatter(summed.reshape(lax.axis_size('mp') * (frames_all // mp_c...]
    all_gather x3 -> x0, blocking collectives: 48 us -> none  [the longest x1 24.2 us: body(): spatial_all = lax.all_gather(spatial_out, 'mp', axis=0, tiled=True)]
    ppermute x0 -> x25, waiting for transfers between devices: none -> 44 us  [the longest x4 21.8 us: line_all_reduce(): back[k - 1] = lax.ppermute(full[k - 1], 'mp', [(1, 0), (2, 3)])]
    psum x1 -> x0, waiting for transfers between devices: 43.8 us -> none  [body(): temporal_grad = lax.psum(jnp.stack(tap_grads), 'dp') / clip_count]
    ppermute x0 -> x25, starting transfers between devices: none -> 35.6 us  [the longest x4 19.4 us: line_all_reduce(): arrived = [lax.ppermute(p, 'mp', [(0, 1), (3, 2)]) for p in parts]]
    pallas_call x0 -> x5, Pallas kernels: none -> 9.46 us  [the longest x4 7 us: piece_conv(): pl.pallas_call(conv_kernel, out_shape=jax.ShapeDtypeStruct((count, width_...]
    dot_general x15 -> x6, matrix products: 12 us -> 7.38 us  [the longest x3 4.96 us: body(): lax.dot_general(windows[k], cot, (((0,), (0,)), ((), ())), preferred_elem...]
    slice x2 -> x1, local copies, waits for them, and re-layouts: 3.09 us -> 0.21 us  [body(): padded[k:k + frames_all].reshape(-1, width_out)]
  transfers between devices with their start and end apart: 3 -> 25, of which waited for: 3 -> 9; matrix products, arithmetic and copies ran while one was open for 3% -> 8% of each run, Pallas kernels for 0% -> 8%
where the time goes in v1:
time: 117 us
  waiting for transfers between devices  44 us (38%)
  starting transfers between devices  35.6 us (30%)
  local copies, waits for them, and re-layouts  10.3 us (9%)
  Pallas kernels  9.46 us (8%)
  other arithmetic  8.69 us (7%)
  matrix products  7.38 us (6%)
    ppermute x4, waiting for transfers between devices, line_all_reduce(): back[k - 1] = lax.ppermute(full[k - 1], 'mp', [(1, 0), (2, 3)])  21.8 us
    ppermute x4, starting transfers between devices, line_all_reduce(): arrived = [lax.ppermute(p, 'mp', [(0, 1), (3, 2)]) for p in parts]  19.4 us
    ppermute x1, waiting for transfers between devices, body(): from_chip = lax.ppermute(to_chip, 'tm', chip)  9.23 us
    ppermute x4, waiting for transfers between devices, line_all_reduce(): arrived = [lax.ppermute(p, 'mp', [(0, 1), (3, 2)]) for p in parts]  7.28 us
    pallas_call x4, Pallas kernels, piece_conv(): pl.pallas_call(conv_kernel, out_shape=jax.ShapeDtypeStruct((count, width_...  7 us
    ppermute x1, waiting for transfers between devices, body(): other = lax.ppermute(sent, 'dp', [(0, 1), (1, 0)])  5.49 us
    ppermute x4, starting transfers between devices, line_all_reduce(): back[k - 1] = lax.ppermute(full[k - 1], 'mp', [(1, 0), (2, 3)])  5.34 us
    dot_general x3, matrix products, body(): lax.dot_general(windows[k], cot, (((0,), (0,)), ((), ())), preferred_elem...  4.96 us
  transfers between devices with their start and end apart: 25, of which 9 were waited for; matrix products, arithmetic and copies ran while one was open for 8% of the time, Pallas kernels for 8%

profile of v1, /device:TPU:0, one launch (start us, length us, event | category | flops | bytes accessed | tf_op | source)
XLA Modules:
  0.0 116.5 jit_solution(9956820787288795860)
XLA Ops:
  1.1 2.5 %piece_stats.1.s0_ref = f32[16,320]{1,0:T(8,128)} custom-call(bf16[2,5,40,320]{3,2,1,0:T(8,128)(2,1)} %bitcast.88), custom_call_target="tpu_custom_call" | custom-call | tf_op jit(solution)/shard_map/piece_stats/pallas_call | solution.py:39
  3.7 3.0 %collective-permute-start.3 = (f32[16,320]{1,0:T(8,128)}, f32[16,320]{1,0:T(8,128)S(1)}, u32[]{:S(2)}, u32[]{:S(2)}) collective-permute-start(f32[16,320]{1,0:T(8,128)} %piece_stats.1.s0_ref), channel_id=1, source_target_pairs={{0,8},{4,12},{8,0},{12,4},{1,9},{5,13},{9,1},{13,5},{2,10},{6,14},... | collective-permute-start | bytes 61448 | tf_op jit(solution)/shard_map/ppermute | solution.py:154
  6.6 1.4 %collective-permute-start = (bf16[2,5,40,320]{3,2,1,0:T(8,128)(2,1)}, bf16[2,5,40,320]{3,2,1,0:T(8,128)(2,1)S(1)}, u32[]{:S(2)}, u32[]{:S(2)}) collective-permute-start(bf16[2,5,40,320]{3,2,1,0:T(8,128)(2,1)} %bitcast.89), channel_id=1, source_target_pairs={{0,8},{4,12},{8,0},{12,4},{1,9},{5,13},{9,1},{13,5},{2,10},{6,14},... | collective-permute-start | bytes 768008 | tf_op jit(solution)/shard_map/ppermute | solution.py:158
  10.3 1.6 %copy-done = bf16[9,320,320]{2,1,0:T(8,128)(2,1)S(1)} copy-done((bf16[9,320,320]{2,1,0:T(8,128)(2,1)S(1)}, bf16[9,320,320]{2,1,0:T(8,128)(2,1)}, u32[]{:S(2)}) %copy-start) | copy-done | bytes 1843224
  13.6 1.7 %piece_conv.5 = bf16[400,320]{1,0:T(8,128)(2,1)S(1)} custom-call(bf16[2,5,40,320]{3,2,1,0:T(8,128)(2,1)S(1)} %bitcast.90, f32[16,320]{1,0:T(8,128)S(1)} %copy-done.3, f32[16,320]{1,0:T(8,128)S(1)} %collective-permute-done.2.s1_ref, f32[16,320]{1,0:T(8,128)S(1)} %collective-permute-done.3.s2_ref, f32[16,320]{1,0:T(8,128)S(1)} %collective-permute-done.4.s3_ref, ...), custom_call_target="tpu_custom_call" | custom-call | flops 737280000 | bytes 2355200 | tf_op jit(solution)/shard_map/piece_conv/pallas_call | solution.py:84
  15.3 3.5 %collective-permute-start.5 = (bf16[400,320]{1,0:T(8,128)(2,1)S(1)}, bf16[400,320]{1,0:T(8,128)(2,1)S(1)}, u32[]{:S(2)}, u32[]{:S(2)}) collective-permute-start(bf16[400,320]{1,0:T(8,128)(2,1)S(1)} %piece_conv.5), channel_id=1, source_target_pairs={{0,1},{3,2},{4,5},{7,6},{8,9},{11,10},{12,13},{15,14},{16,17},{19,... | collective-permute-start | bytes 768008 | tf_op jit(solution)/shard_map/ppermute | solution.py:116
  19.0 1.8 %piece_conv.6 = bf16[400,320]{1,0:T(8,128)(2,1)S(1)} custom-call(bf16[2,5,40,320]{3,2,1,0:T(8,128)(2,1)S(1)} %collective-permute-done.6.x_ref, f32[16,320]{1,0:T(8,128)S(1)} %copy-done.4, f32[16,320]{1,0:T(8,128)S(1)} %collective-permute-done.2.s1_ref, f32[16,320]{1,0:T(8,128)S(1)} %collective-permute-done.3.s2_ref, ...), custom_call_target="tpu_custom_call" | custom-call | flops 737280000 | bytes 2355200 | tf_op jit(solution)/shard_map/piece_conv/pallas_call | solution.py:84
  20.8 1.3 %collective-permute-start.7 = (bf16[400,320]{1,0:T(8,128)(2,1)S(1)}, bf16[400,320]{1,0:T(8,128)(2,1)S(1)}, u32[]{:S(2)}, u32[]{:S(2)}) collective-permute-start(bf16[400,320]{1,0:T(8,128)(2,1)S(1)} %piece_conv.6), channel_id=1, source_target_pairs={{0,1},{3,2},{4,5},{7,6},{8,9},{11,10},{12,13},{15,14},{16,17},{19,... | collective-permute-start | bytes 768008 | tf_op jit(solution)/shard_map/ppermute | solution.py:116
  22.1 1.8 %piece_conv.7 = bf16[400,320]{1,0:T(8,128)(2,1)S(1)} custom-call(bf16[2,5,40,320]{3,2,1,0:T(8,128)(2,1)S(1)} %collective-permute-done.x_ref, f32[16,320]{1,0:T(8,128)S(1)} %copy-done.4, f32[16,320]{1,0:T(8,128)S(1)} %collective-permute-done.2.s1_ref, f32[16,320]{1,0:T(8,128)S(1)} %collective-permute-done.3.s2_ref, ...), custom_call_target="tpu_custom_call" | custom-call | flops 737280000 | bytes 2355200 | tf_op jit(solution)/shard_map/piece_conv/pallas_call | solution.py:84
  23.9 1.3 %collective-permute-start.10 = (bf16[400,320]{1,0:T(8,128)(2,1)S(1)}, bf16[400,320]{1,0:T(8,128)(2,1)S(1)}, u32[]{:S(2)}, u32[]{:S(2)}) collective-permute-start(bf16[400,320]{1,0:T(8,128)(2,1)S(1)} %piece_conv.7), channel_id=1, source_target_pairs={{0,1},{3,2},{4,5},{7,6},{8,9},{11,10},{12,13},{15,14},{16,17},{19,... | collective-permute-start | bytes 768008 | tf_op jit(solution)/shard_map/ppermute | solution.py:116
  26.6 6.5 %collective-permute-done.7 = bf16[400,320]{1,0:T(8,128)(2,1)S(1)} collective-permute-done((bf16[400,320]{1,0:T(8,128)(2,1)S(1)}, bf16[400,320]{1,0:T(8,128)(2,1)S(1)}, u32[]{:S(2)}, u32[]{:S(2)}) %collective-permute-start.7) | collective-permute-done | bytes 256032 | tf_op jit(solution)/shard_map/ppermute | solution.py:116
  34.5 1.8 %piece_conv.4 = bf16[400,320]{1,0:T(8,128)(2,1)S(1)} custom-call(bf16[2,5,40,320]{3,2,1,0:T(8,128)(2,1)S(1)} %collective-permute-done.1.x_ref, f32[16,320]{1,0:T(8,128)S(1)} %copy-done.4, f32[16,320]{1,0:T(8,128)S(1)} %collective-permute-done.2.s1_ref, f32[16,320]{1,0:T(8,128)S(1)} %collective-permute-done.3.s2_ref, ...), custom_call_target="tpu_custom_call" | custom-call | flops 737280000 | bytes 2355200 | tf_op jit(solution)/shard_map/piece_conv/pallas_call | solution.py:84
  36.3 13.2 %collective-permute-start.12 = (bf16[400,320]{1,0:T(8,128)(2,1)S(1)}, bf16[400,320]{1,0:T(8,128)(2,1)S(1)}, u32[]{:S(2)}, u32[]{:S(2)}) collective-permute-start(bf16[400,320]{1,0:T(8,128)(2,1)S(1)} %piece_conv.4), channel_id=1, source_target_pairs={{0,1},{3,2},{4,5},{7,6},{8,9},{11,10},{12,13},{15,14},{16,17},{19,... | collective-permute-start | bytes 768008 | tf_op jit(solution)/shard_map/ppermute | solution.py:116
  49.6 1.3 %collective-permute-start.9 = (bf16[400,320]{1,0:T(8,128)(2,1)S(1)}, bf16[400,320]{1,0:T(8,128)(2,1)S(1)}, u32[]{:S(2)}, u32[]{:S(2)}) collective-permute-start(bf16[400,320]{1,0:T(8,128)(2,1)S(1)} %add_convert_fusion.5), channel_id=1, source_target_pairs={{1,0},{2,3},{5,4},{6,7},{9,8},{10,11},{13,12},{14,15},{17,16},{18,... | collective-permute-start | bytes 768008 | tf_op jit(solution)/shard_map/ppermute | solution.py:126
  51.8 9.0 %collective-permute-done.9 = bf16[400,320]{1,0:T(8,128)(2,1)S(1)} collective-permute-done((bf16[400,320]{1,0:T(8,128)(2,1)S(1)}, bf16[400,320]{1,0:T(8,128)(2,1)S(1)}, u32[]{:S(2)}, u32[]{:S(2)}) %collective-permute-start.9) | collective-permute-done | bytes 256032 | tf_op jit(solution)/shard_map/ppermute | solution.py:126
  60.8 1.3 %collective-permute-start.13 = (bf16[400,320]{1,0:T(8,128)(2,1)S(1)}, bf16[400,320]{1,0:T(8,128)(2,1)S(1)}, u32[]{:S(2)}, u32[]{:S(2)}) collective-permute-start(bf16[400,320]{1,0:T(8,128)(2,1)S(1)} %add_convert_fusion.3), channel_id=1, source_target_pairs={{1,0},{2,3},{5,4},{6,7},{9,8},{10,11},{13,12},{14,15},{17,16},{18,... | collective-permute-start | bytes 768008 | tf_op jit(solution)/shard_map/ppermute | solution.py:126
  63.0 1.3 %collective-permute-start.17 = (bf16[400,320]{1,0:T(8,128)(2,1)S(1)}, bf16[400,320]{1,0:T(8,128)(2,1)S(1)}, u32[]{:S(2)}, u32[]{:S(2)}) collective-permute-start(bf16[400,320]{1,0:T(8,128)(2,1)S(1)} %add_convert_fusion.1), channel_id=1, source_target_pairs={{1,0},{2,3},{5,4},{6,7},{9,8},{10,11},{13,12},{14,15},{17,16},{18,... | collective-permute-start | bytes 768008 | tf_op jit(solution)/shard_map/ppermute | solution.py:126
  64.3 6.9 %collective-permute-done.13 = bf16[400,320]{1,0:T(8,128)(2,1)S(1)} collective-permute-done((bf16[400,320]{1,0:T(8,128)(2,1)S(1)}, bf16[400,320]{1,0:T(8,128)(2,1)S(1)}, u32[]{:S(2)}, u32[]{:S(2)}) %collective-permute-start.13) | collective-permute-done | bytes 256032 | tf_op jit(solution)/shard_map/ppermute | solution.py:126
  71.4 1.5 %collective-permute-start.16 = (bf16[400,320]{1,0:T(8,128)(2,1)S(1)}, bf16[400,320]{1,0:T(8,128)(2,1)S(1)}, u32[]{:S(2)}, u32[]{:S(2)}) collective-permute-start(bf16[400,320]{1,0:T(8,128)(2,1)S(1)} %add_convert_fusion), channel_id=1, source_target_pairs={{1,0},{2,3},{5,4},{6,7},{9,8},{10,11},{13,12},{14,15},{17,16},{18,... | collective-permute-start | bytes 768008 | tf_op jit(solution)/shard_map/ppermute | solution.py:126
  72.9 1.3 %broadcast_select_fusion.7 = (bf16[2,5,40,320]{3,2,1,0:T(8,128)(2,1)S(1)}, bf16[2,5,40,320]{3,2,1,0:T(8,128)(2,1)S(1)}, bf16[2,5,40,320]{3,2,1,0:T(8,128)(2,1)S(1)}, bf16[2,5,40,320]{3,2,1,0:T(8,128)(2,1)S(1)}) fusion(pred[]{:T(512)S(6)} %eq.14, bf16[2,5,40,320]{3,2,1,0:T(8,128)(2,1)S(1)} %collective-permute-done.22, ...), kind=kLoop, calls=%fused_computation.46 | loop fusion | flops 1024000 | bytes 2048002 | tf_op jit(solution)/shard_map/jit(_where)/select_n | solution.py:141
  74.3 1.8 %collective-permute-done.17 = bf16[400,320]{1,0:T(8,128)(2,1)S(1)} collective-permute-done((bf16[400,320]{1,0:T(8,128)(2,1)S(1)}, bf16[400,320]{1,0:T(8,128)(2,1)S(1)}, u32[]{:S(2)}, u32[]{:S(2)}) %collective-permute-start.17) | collective-permute-done | bytes 256032 | tf_op jit(solution)/shard_map/ppermute | solution.py:126
  76.2 4.0 %collective-permute-done.16 = bf16[400,320]{1,0:T(8,128)(2,1)S(1)} collective-permute-done((bf16[400,320]{1,0:T(8,128)(2,1)S(1)}, bf16[400,320]{1,0:T(8,128)(2,1)S(1)}, u32[]{:S(2)}, u32[]{:S(2)}) %collective-permute-start.16) | collective-permute-done | bytes 256032 | tf_op jit(solution)/shard_map/ppermute | solution.py:126
  80.9 1.5 %fusion.3 = bf16[1,320,320]{2,1,0:T(8,128)(2,1)} fusion(bf16[2,5,40,320]{3,2,1,0:T(8,128)(2,1)S(1)} %get-tuple-element.33, bf16[2,5,40,320]{3,2,1,0:T(8,128)(2,1)S(1)} %get-tuple-element.32, bf16[2,5,40,320]{3,2,1,0:T(8,128)(2,1)S(1)} %get-tuple-element.31, bf16[2,5,40,320]{3,2,1,0:T(8,128)(2,1)S(1)} %get-tuple-element.30, ...), kind=kOutput, calls=%fused_computation.13 | convolution fusion | flops 295014400 | bytes 2252800 | tf_op jit(solution)/shard_map/dot_general | solution.py:187
  82.4 1.5 %fusion.4 = bf16[1,320,320]{2,1,0:T(8,128)(2,1)} fusion(bf16[2,5,40,320]{3,2,1,0:T(8,128)(2,1)S(1)} %get-tuple-element.33, bf16[2,5,40,320]{3,2,1,0:T(8,128)(2,1)S(1)} %get-tuple-element.32, bf16[2,5,40,320]{3,2,1,0:T(8,128)(2,1)S(1)} %get-tuple-element.31, bf16[2,5,40,320]{3,2,1,0:T(8,128)(2,1)S(1)} %get-tuple-element.30, ...), kind=kOutput, calls=%fused_computation.14 | convolution fusion | flops 295014400 | bytes 2252800 | tf_op jit(solution)/shard_map/dot_general | solution.py:187
  87.5 2.1 %copy.20 = f32[1600,320]{1,0:T(8,128)} copy(f32[1600,320]{0,1:T(8,128)S(1)} %convolution_add_fusion) | data formatting | bytes 4096000 | tf_op jit(solution)/shard_map/add | solution.py:199
  89.6 2.1 %fusion.9 = (bf16[2,5,40,320]{3,2,1,0:T(8,128)(2,1)}, bf16[2,5,40,320]{3,2,1,0:T(8,128)(2,1)S(1)}) fusion(f32[4,2,5,40,320]{4,3,2,1,0:T(8,128)} %bitcast.92, s32[]{:T(128)S(6)} %select_n.163, s32[]{:T(128)S(6)} %select_n.165), kind=kLoop, calls=%fused_computation.32 | loop fusion | bytes 1024008 | tf_op jit(solution)/shard_map/convert_element_type | solution.py:205
  91.8 2.0 %fusion.5 = bf16[1,320,320]{2,1,0:T(8,128)(2,1)S(1)} fusion(bf16[2,5,40,320]{3,2,1,0:T(8,128)(2,1)} %copy-done.21, bf16[2,5,40,320]{3,2,1,0:T(8,128)(2,1)S(1)} %copy-done.20, bf16[2,5,40,320]{3,2,1,0:T(8,128)(2,1)S(1)} %copy-done.18, bf16[2,5,40,320]{3,2,1,0:T(8,128)(2,1)S(1)} %copy-done.16, bf16[2,5,40,320]{3,2,1,0:T(8,128)(2,1)S(1)} %get-tuple-element.39, ...), kind=kOutput, calls=%fused_computation.15 | convolution fusion | flops 330854400 | bytes 2252800 | tf_op jit(solution)/shard_map/dot_general | solution.py:187
  95.3 1.4 %collective-permute-start.24 = (bf16[3,320,320]{2,1,0:T(8,128)(2,1)}, bf16[3,320,320]{2,1,0:T(8,128)(2,1)}, u32[]{:S(2)}, u32[]{:S(2)}) collective-permute-start(bf16[3,320,320]{2,1,0:T(8,128)(2,1)} %pad_maximum_fusion.2), channel_id=1, source_target_pairs={{0,16},{16,0},{1,17},{17,1},{2,18},{18,2},{3,19},{19,3},{4,20},{20... | collective-permute-start | bytes 1843208 | tf_op jit(solution)/shard_map/ppermute | solution.py:194
  97.6 9.2 %collective-permute-done.20 = bf16[2,5,40,320]{3,2,1,0:T(8,128)(2,1)} collective-permute-done((bf16[2,5,40,320]{3,2,1,0:T(8,128)(2,1)}, bf16[2,5,40,320]{3,2,1,0:T(8,128)(2,1)}, u32[]{:S(2)}, u32[]{:S(2)}) %collective-permute-start.20) | collective-permute-done | bytes 256032 | tf_op jit(solution)/shard_map/ppermute | solution.py:207
  106.8 1.8 %fusion.11 = bf16[1,2,5,40,320]{4,3,2,1,0:T(8,128)(2,1)} fusion(bf16[2,5,40,320]{3,2,1,0:T(8,128)(2,1)} %collective-permute-done.20, bf16[2,5,40,320]{3,2,1,0:T(8,128)(2,1)S(1)} %collective-permute-done.18, f32[4,2,5,40,320]{4,3,2,1,0:T(8,128)S(1)} %bitcast.94, s32[]{:T(128)S(6)} %select_n.162), kind=kLoop, calls=%fused_computation.34 | loop fusion | flops 640000 | bytes 1280004 | tf_op jit(solution)/shard_map/broadcast_in_dim | solution.py:208
  108.6 5.5 %collective-permute-done.24 = bf16[3,320,320]{2,1,0:T(8,128)(2,1)} collective-permute-done((bf16[3,320,320]{2,1,0:T(8,128)(2,1)}, bf16[3,320,320]{2,1,0:T(8,128)(2,1)}, u32[]{:S(2)}, u32[]{:S(2)}) %collective-permute-start.24) | collective-permute-done | bytes 614432 | tf_op jit(solution)/shard_map/ppermute | solution.py:194
  114.1 2.4 %add_multiply_fusion = f32[3,320,320]{2,1,0:T(8,128)} fusion(bf16[3,320,320]{2,1,0:T(8,128)(2,1)} %collective-permute-done.24, bf16[1,320,320]{2,1,0:T(8,128)(2,1)S(1)} %copy-done.9, bf16[1,320,320]{2,1,0:T(8,128)(2,1)S(1)} %copy-done.13, bf16[1,320,320]{2,1,0:T(8,128)(2,1)S(1)} %copy-done.11), kind=kLoop, calls=%fused_computation.4 | loop fusion | flops 1843200 | bytes 2457600 | tf_op jit(solution)/shard_map/div | solution.py:195
  (99 shorter events, 16.1 us)
Async XLA Ops:
  0.6 18.3 %collective-permute-start.6 = (bf16[2,5,40,320]{3,2,1,0:T(8,128)(2,1)}, bf16[2,5,40,320]{3,2,1,0:T(8,128)(2,1)S(1)}, u32[]{:S(2)}, u32[]{:S(2)}) collective-permute-start(bf16[2,5,40,320]{3,2,1,0:T(8,128)(2,1)} %bitcast.87), channel_id=1, source_target_pairs={{0,4},{4,0},{8,12},{12,8},{1,5},{5,1},{9,13},{13,9},{2,6},{6,2},{1... | collective-permute-start | bytes 768008 | tf_op jit(solution)/shard_map/ppermute | solution.py:157
  3.6 5.8 %collective-permute-start.2 = (f32[16,320]{1,0:T(8,128)}, f32[16,320]{1,0:T(8,128)S(1)}, u32[]{:S(2)}, u32[]{:S(2)}) collective-permute-start(f32[16,320]{1,0:T(8,128)} %piece_stats.1.s0_ref), channel_id=1, source_target_pairs={{0,4},{4,0},{8,12},{12,8},{1,5},{5,1},{9,13},{13,9},{2,6},{6,2},{1... | collective-permute-start | bytes 61448 | tf_op jit(solution)/shard_map/ppermute | solution.py:155
  3.7 6.4 %collective-permute-start.3 = (f32[16,320]{1,0:T(8,128)}, f32[16,320]{1,0:T(8,128)S(1)}, u32[]{:S(2)}, u32[]{:S(2)}) collective-permute-start(f32[16,320]{1,0:T(8,128)} %piece_stats.1.s0_ref), channel_id=1, source_target_pairs={{0,8},{4,12},{8,0},{12,4},{1,9},{5,13},{9,1},{13,5},{2,10},{6,14},... | collective-permute-start | bytes 61448 | tf_op jit(solution)/shard_map/ppermute | solution.py:154
  6.6 3.6 %collective-permute-start.4 = (f32[16,320]{1,0:T(8,128)}, f32[16,320]{1,0:T(8,128)S(1)}, u32[]{:S(2)}, u32[]{:S(2)}) collective-permute-start(f32[16,320]{1,0:T(8,128)} %piece_stats.1.s0_ref), channel_id=1, source_target_pairs={{0,12},{4,8},{8,4},{12,0},{1,13},{5,9},{9,5},{13,1},{2,14},{6,10},... | collective-permute-start | bytes 61448 | tf_op jit(solution)/shard_map/ppermute | solution.py:156
  6.6 15.4 %collective-permute-start = (bf16[2,5,40,320]{3,2,1,0:T(8,128)(2,1)}, bf16[2,5,40,320]{3,2,1,0:T(8,128)(2,1)S(1)}, u32[]{:S(2)}, u32[]{:S(2)}) collective-permute-start(bf16[2,5,40,320]{3,2,1,0:T(8,128)(2,1)} %bitcast.89), channel_id=1, source_target_pairs={{0,8},{4,12},{8,0},{12,4},{1,9},{5,13},{9,1},{13,5},{2,10},{6,14},... | collective-permute-start | bytes 768008 | tf_op jit(solution)/shard_map/ppermute | solution.py:158
  9.4 15.8 %collective-permute-start.21 = (bf16[2,5,40,320]{3,2,1,0:T(8,128)(2,1)}, bf16[2,5,40,320]{3,2,1,0:T(8,128)(2,1)}, u32[]{:S(2)}, u32[]{:S(2)}) collective-permute-start(bf16[2,5,40,320]{3,2,1,0:T(8,128)(2,1)} %bitcast.22), channel_id=1, source_target_pairs={{0,8},{4,12},{8,0},{12,4},{1,9},{5,13},{9,1},{13,5},{2,10},{6,14},... | collective-permute-start | bytes 768008 | tf_op jit(solution)/shard_map/ppermute | solution.py:172
  15.3 11.1 %collective-permute-start.5 = (bf16[400,320]{1,0:T(8,128)(2,1)S(1)}, bf16[400,320]{1,0:T(8,128)(2,1)S(1)}, u32[]{:S(2)}, u32[]{:S(2)}) collective-permute-start(bf16[400,320]{1,0:T(8,128)(2,1)S(1)} %piece_conv.5), channel_id=1, source_target_pairs={{0,1},{3,2},{4,5},{7,6},{8,9},{11,10},{12,13},{15,14},{16,17},{19,... | collective-permute-start | bytes 768008 | tf_op jit(solution)/shard_map/ppermute | solution.py:116
  18.9 54.1 %collective-permute-start.23 = (bf16[2,5,40,320]{3,2,1,0:T(8,128)(2,1)}, bf16[2,5,40,320]{3,2,1,0:T(8,128)(2,1)}, u32[]{:S(2)}, u32[]{:S(2)}) collective-permute-start(bf16[2,5,40,320]{3,2,1,0:T(8,128)(2,1)} %bitcast.22), channel_id=1, source_target_pairs={{0,4},{4,0},{8,12},{12,8},{1,5},{5,1},{9,13},{13,9},{2,6},{6,2},{1... | collective-permute-start | bytes 768008 | tf_op jit(solution)/shard_map/ppermute | solution.py:171
  20.8 12.3 %collective-permute-start.7 = (bf16[400,320]{1,0:T(8,128)(2,1)S(1)}, bf16[400,320]{1,0:T(8,128)(2,1)S(1)}, u32[]{:S(2)}, u32[]{:S(2)}) collective-permute-start(bf16[400,320]{1,0:T(8,128)(2,1)S(1)} %piece_conv.6), channel_id=1, source_target_pairs={{0,1},{3,2},{4,5},{7,6},{8,9},{11,10},{12,13},{15,14},{16,17},{19,... | collective-permute-start | bytes 768008 | tf_op jit(solution)/shard_map/ppermute | solution.py:116
  23.9 25.8 %collective-permute-start.10 = (bf16[400,320]{1,0:T(8,128)(2,1)S(1)}, bf16[400,320]{1,0:T(8,128)(2,1)S(1)}, u32[]{:S(2)}, u32[]{:S(2)}) collective-permute-start(bf16[400,320]{1,0:T(8,128)(2,1)S(1)} %piece_conv.7), channel_id=1, source_target_pairs={{0,1},{3,2},{4,5},{7,6},{8,9},{11,10},{12,13},{15,14},{16,17},{19,... | collective-permute-start | bytes 768008 | tf_op jit(solution)/shard_map/ppermute | solution.py:116
  25.2 8.6 %collective-permute-start.1 = (bf16[2,5,40,320]{3,2,1,0:T(8,128)(2,1)S(1)}, bf16[2,5,40,320]{3,2,1,0:T(8,128)(2,1)S(1)}, u32[]{:S(2)}, u32[]{:S(2)}) collective-permute-start(bf16[2,5,40,320]{3,2,1,0:T(8,128)(2,1)S(1)} %collective-permute-done.x_ref), channel_id=1, source_target_pairs={{0,4},{4,0},{8,12},{12,8},{1,5},{5,1},{9,13},{13,9},{2,6},{6,2},{1... | collective-permute-start | bytes 768008 | tf_op jit(solution)/shard_map/ppermute | solution.py:159
  26.5 46.5 %collective-permute-start.22 = (bf16[2,5,40,320]{3,2,1,0:T(8,128)(2,1)}, bf16[2,5,40,320]{3,2,1,0:T(8,128)(2,1)S(1)}, u32[]{:S(2)}, u32[]{:S(2)}) collective-permute-start(bf16[2,5,40,320]{3,2,1,0:T(8,128)(2,1)} %collective-permute-done.21), channel_id=1, source_target_pairs={{0,4},{4,0},{8,12},{12,8},{1,5},{5,1},{9,13},{13,9},{2,6},{6,2},{1... | collective-permute-start | bytes 768008 | tf_op jit(solution)/shard_map/ppermute | solution.py:173
  33.1 3.2 %collective-permute-start.8 = (bf16[400,320]{1,0:T(8,128)(2,1)S(1)}, bf16[400,320]{1,0:T(8,128)(2,1)S(1)}, u32[]{:S(2)}, u32[]{:S(2)}) collective-permute-start(bf16[400,320]{1,0:T(8,128)(2,1)S(1)} %add_convert_fusion.7), channel_id=1, source_target_pairs={{1,2},{2,1},{5,6},{6,5},{9,10},{10,9},{13,14},{14,13},{17,18},{18,... | collective-permute-start | bytes 768008 | tf_op jit(solution)/shard_map/ppermute | solution.py:122
  33.8 17.2 %collective-permute-start.11 = (bf16[400,320]{1,0:T(8,128)(2,1)S(1)}, bf16[400,320]{1,0:T(8,128)(2,1)S(1)}, u32[]{:S(2)}, u32[]{:S(2)}) collective-permute-start(bf16[400,320]{1,0:T(8,128)(2,1)S(1)} %add_convert_fusion.6), channel_id=1, source_target_pairs={{1,2},{2,1},{5,6},{6,5},{9,10},{10,9},{13,14},{14,13},{17,18},{18,... | collective-permute-start | bytes 768008 | tf_op jit(solution)/shard_map/ppermute | solution.py:122
  36.3 25.9 %collective-permute-start.12 = (bf16[400,320]{1,0:T(8,128)(2,1)S(1)}, bf16[400,320]{1,0:T(8,128)(2,1)S(1)}, u32[]{:S(2)}, u32[]{:S(2)}) collective-permute-start(bf16[400,320]{1,0:T(8,128)(2,1)S(1)} %piece_conv.4), channel_id=1, source_target_pairs={{0,1},{3,2},{4,5},{7,6},{8,9},{11,10},{12,13},{15,14},{16,17},{19,... | collective-permute-start | bytes 768008 | tf_op jit(solution)/shard_map/ppermute | solution.py:116
  49.6 11.2 %collective-permute-start.9 = (bf16[400,320]{1,0:T(8,128)(2,1)S(1)}, bf16[400,320]{1,0:T(8,128)(2,1)S(1)}, u32[]{:S(2)}, u32[]{:S(2)}) collective-permute-start(bf16[400,320]{1,0:T(8,128)(2,1)S(1)} %add_convert_fusion.5), channel_id=1, source_target_pairs={{1,0},{2,3},{5,4},{6,7},{9,8},{10,11},{13,12},{14,15},{17,16},{18,... | collective-permute-start | bytes 768008 | tf_op jit(solution)/shard_map/ppermute | solution.py:126
  51.0 11.9 %collective-permute-start.14 = (bf16[400,320]{1,0:T(8,128)(2,1)S(1)}, bf16[400,320]{1,0:T(8,128)(2,1)S(1)}, u32[]{:S(2)}, u32[]{:S(2)}) collective-permute-start(bf16[400,320]{1,0:T(8,128)(2,1)S(1)} %add_convert_fusion.4), channel_id=1, source_target_pairs={{1,2},{2,1},{5,6},{6,5},{9,10},{10,9},{13,14},{14,13},{17,18},{18,... | collective-permute-start | bytes 768008 | tf_op jit(solution)/shard_map/ppermute | solution.py:122
  60.8 10.5 %collective-permute-start.13 = (bf16[400,320]{1,0:T(8,128)(2,1)S(1)}, bf16[400,320]{1,0:T(8,128)(2,1)S(1)}, u32[]{:S(2)}, u32[]{:S(2)}) collective-permute-start(bf16[400,320]{1,0:T(8,128)(2,1)S(1)} %add_convert_fusion.3), channel_id=1, source_target_pairs={{1,0},{2,3},{5,4},{6,7},{9,8},{10,11},{13,12},{14,15},{17,16},{18,... | collective-permute-start | bytes 768008 | tf_op jit(solution)/shard_map/ppermute | solution.py:126
  62.3 9.1 %collective-permute-start.15 = (bf16[400,320]{1,0:T(8,128)(2,1)S(1)}, bf16[400,320]{1,0:T(8,128)(2,1)S(1)}, u32[]{:S(2)}, u32[]{:S(2)}) collective-permute-start(bf16[400,320]{1,0:T(8,128)(2,1)S(1)} %add_convert_fusion.2), channel_id=1, source_target_pairs={{1,2},{2,1},{5,6},{6,5},{9,10},{10,9},{13,14},{14,13},{17,18},{18,... | collective-permute-start | bytes 768008 | tf_op jit(solution)/shard_map/ppermute | solution.py:122
  63.0 13.1 %collective-permute-start.17 = (bf16[400,320]{1,0:T(8,128)(2,1)S(1)}, bf16[400,320]{1,0:T(8,128)(2,1)S(1)}, u32[]{:S(2)}, u32[]{:S(2)}) collective-permute-start(bf16[400,320]{1,0:T(8,128)(2,1)S(1)} %add_convert_fusion.1), channel_id=1, source_target_pairs={{1,0},{2,3},{5,4},{6,7},{9,8},{10,11},{13,12},{14,15},{17,16},{18,... | collective-permute-start | bytes 768008 | tf_op jit(solution)/shard_map/ppermute | solution.py:126
  71.4 8.7 %collective-permute-start.16 = (bf16[400,320]{1,0:T(8,128)(2,1)S(1)}, bf16[400,320]{1,0:T(8,128)(2,1)S(1)}, u32[]{:S(2)}, u32[]{:S(2)}) collective-permute-start(bf16[400,320]{1,0:T(8,128)(2,1)S(1)} %add_convert_fusion), channel_id=1, source_target_pairs={{1,0},{2,3},{5,4},{6,7},{9,8},{10,11},{13,12},{14,15},{17,16},{18,... | collective-permute-start | bytes 768008 | tf_op jit(solution)/shard_map/ppermute | solution.py:126
  74.3 8.1 %copy-start.15 = (bf16[2,5,40,320]{3,2,1,0:T(8,128)(2,1)}, bf16[2,5,40,320]{3,2,1,0:T(8,128)(2,1)S(1)}, u32[]{:S(2)}) copy-start(bf16[2,5,40,320]{3,2,1,0:T(8,128)(2,1)S(1)} %get-tuple-element.30) | copy-start | bytes 768004
  74.3 8.1 %copy-start.17 = (bf16[2,5,40,320]{3,2,1,0:T(8,128)(2,1)}, bf16[2,5,40,320]{3,2,1,0:T(8,128)(2,1)S(1)}, u32[]{:S(2)}) copy-start(bf16[2,5,40,320]{3,2,1,0:T(8,128)(2,1)S(1)} %get-tuple-element.31) | copy-start | bytes 768004
  74.3 8.1 %copy-start.19 = (bf16[2,5,40,320]{3,2,1,0:T(8,128)(2,1)}, bf16[2,5,40,320]{3,2,1,0:T(8,128)(2,1)S(1)}, u32[]{:S(2)}) copy-start(bf16[2,5,40,320]{3,2,1,0:T(8,128)(2,1)S(1)} %get-tuple-element.32) | copy-start | bytes 768004
  74.3 8.1 %copy-start.21 = (bf16[2,5,40,320]{3,2,1,0:T(8,128)(2,1)}, bf16[2,5,40,320]{3,2,1,0:T(8,128)(2,1)S(1)}, u32[]{:S(2)}) copy-start(bf16[2,5,40,320]{3,2,1,0:T(8,128)(2,1)S(1)} %get-tuple-element.33) | copy-start | bytes 768004
  91.7 5.1 %collective-permute-start.19 = (bf16[2,5,40,320]{3,2,1,0:T(8,128)(2,1)S(1)}, bf16[2,5,40,320]{3,2,1,0:T(8,128)(2,1)S(1)}, u32[]{:S(2)}, u32[]{:S(2)}) collective-permute-start(bf16[2,5,40,320]{3,2,1,0:T(8,128)(2,1)S(1)} %get-tuple-element.29), channel_id=1, source_target_pairs={{0,4},{4,0},{8,12},{12,8},{1,5},{5,1},{9,13},{13,9},{2,6},{6,2},{1... | collective-permute-start | bytes 768008 | tf_op jit(solution)/shard_map/ppermute | solution.py:204
  93.8 3.8 %collective-permute-start.18 = (bf16[2,5,40,320]{3,2,1,0:T(8,128)(2,1)}, bf16[2,5,40,320]{3,2,1,0:T(8,128)(2,1)S(1)}, u32[]{:S(2)}, u32[]{:S(2)}) collective-permute-start(bf16[2,5,40,320]{3,2,1,0:T(8,128)(2,1)} %get-tuple-element.28), channel_id=1, source_target_pairs={{0,4},{4,0},{8,12},{12,8},{1,5},{5,1},{9,13},{13,9},{2,6},{6,2},{1... | collective-permute-start | bytes 768008 | tf_op jit(solution)/shard_map/ppermute | solution.py:205
  95.3 18.7 %copy-start.9 = (bf16[1,320,320]{2,1,0:T(8,128)(2,1)S(1)}, bf16[1,320,320]{2,1,0:T(8,128)(2,1)}, u32[]{:S(2)}) copy-start(bf16[1,320,320]{2,1,0:T(8,128)(2,1)} %fusion.3) | copy-start | bytes 614404
  95.3 18.7 %copy-start.11 = (bf16[1,320,320]{2,1,0:T(8,128)(2,1)S(1)}, bf16[1,320,320]{2,1,0:T(8,128)(2,1)}, u32[]{:S(2)}) copy-start(bf16[1,320,320]{2,1,0:T(8,128)(2,1)} %fusion.4) | copy-start | bytes 614404
  95.3 18.7 %collective-permute-start.24 = (bf16[3,320,320]{2,1,0:T(8,128)(2,1)}, bf16[3,320,320]{2,1,0:T(8,128)(2,1)}, u32[]{:S(2)}, u32[]{:S(2)}) collective-permute-start(bf16[3,320,320]{2,1,0:T(8,128)(2,1)} %pad_maximum_fusion.2), channel_id=1, source_target_pairs={{0,16},{16,0},{1,17},{17,1},{2,18},{18,2},{3,19},{19,3},{4,20},{20... | collective-permute-start | bytes 1843208 | tf_op jit(solution)/shard_map/ppermute | solution.py:194
  97.6 9.2 %collective-permute-start.20 = (bf16[2,5,40,320]{3,2,1,0:T(8,128)(2,1)}, bf16[2,5,40,320]{3,2,1,0:T(8,128)(2,1)}, u32[]{:S(2)}, u32[]{:S(2)}) collective-permute-start(bf16[2,5,40,320]{3,2,1,0:T(8,128)(2,1)} %fusion.6), channel_id=1, source_target_pairs={{0,8},{4,12},{8,0},{12,4},{1,9},{5,13},{9,1},{13,5},{2,10},{6,14},... | collective-permute-start | bytes 768008 | tf_op jit(solution)/shard_map/ppermute | solution.py:207
  97.6 16.5 %copy-start.13 = (bf16[1,320,320]{2,1,0:T(8,128)(2,1)S(1)}, bf16[1,320,320]{2,1,0:T(8,128)(2,1)}, u32[]{:S(2)}) copy-start(bf16[1,320,320]{2,1,0:T(8,128)(2,1)} %copy-done.12) | copy-start | bytes 614404
  (15 other events, 39.7 us)

commit v2 on v1

v2 whole, which is shorter than its diff:
```python
import functools

import jax
import jax.numpy as jnp
from jax import lax
from jax.experimental import pallas as pl
from jax.experimental.pallas import tpu as pltpu
from jax.sharding import PartitionSpec as P

CHANNELS = 1280
GROUPS = 32
GROUP_WIDTH = CHANNELS // GROUPS
EPSILON = 1e-05

f32 = jnp.float32
bf16 = jnp.bfloat16


def group_sum(rows):
    width = rows.shape[1]
    first = lax.broadcasted_iota(jnp.int32, (width, width), 0) // GROUP_WIDTH
    second = lax.broadcasted_iota(jnp.int32, (width, width), 1) // GROUP_WIDTH
    same = jnp.where(first == second, 1.0, 0.0).astype(f32)
    return jnp.dot(rows, same, precision=lax.Precision.HIGHEST, preferred_element_type=f32)


def stats_kernel(x_ref, out_ref):
    frames, rows, cols, width = x_ref.shape
    count = frames * rows * cols
    values = x_ref[...].astype(f32).reshape(count // 8, 8, width)
    mean = group_sum(values.sum(axis=0)).sum(axis=0, keepdims=True) / (count * GROUP_WIDTH)
    centered = values - mean[None]
    square = group_sum((centered * centered).sum(axis=0)).sum(axis=0, keepdims=True)
    out_ref[0:8, :] = jnp.broadcast_to(mean, (8, width))
    out_ref[8:16, :] = jnp.broadcast_to(square, (8, width))


def vmem_spec():
    return pl.BlockSpec(memory_space=pltpu.VMEM)


def params(mebibytes):
    return pltpu.CompilerParams(vmem_limit_bytes=mebibytes * 1024 * 1024)


def piece_stats(piece):
    return pl.pallas_call(
        stats_kernel,
        out_shape=jax.ShapeDtypeStruct((16, piece.shape[-1]), f32),
        in_specs=[vmem_spec()],
        out_specs=vmem_spec(),
        compiler_params=params(6),
        name="piece_stats",
    )(piece)


def conv_kernel(x_ref, s0_ref, s1_ref, s2_ref, s3_ref, gain_ref, bias_ref, w_ref, keep_ref, send_ref, cols_ref):
    frames, rows, cols, width = x_ref.shape
    band = frames * cols
    stats = [s0_ref, s1_ref, s2_ref, s3_ref]
    means = [s[0:8, :] for s in stats]
    mean = (means[0] + means[1] + means[2] + means[3]) / 4.0
    count = frames * rows * cols * GROUP_WIDTH
    square = sum(s[8:16, :] for s in stats)
    square = square + count * sum((m - mean) * (m - mean) for m in means)
    scale = lax.rsqrt(square / (4.0 * count) + EPSILON)[0:1]
    mean = mean[0:1]
    gain = gain_ref[...].reshape(1, width)
    bias = bias_ref[...].reshape(1, width)
    cols_ref[0:band, :] = jnp.zeros((band, 3 * width), bf16)
    cols_ref[(rows + 1) * band :, :] = jnp.zeros((band, 3 * width), bf16)
    column = lax.broadcasted_iota(jnp.int32, (band, width), 0) % cols
    for row in range(rows):
        values = jnp.concatenate([x_ref[f, row].astype(f32) for f in range(frames)], axis=0)
        normed = (values - mean) * scale * gain + bias
        hidden = normed / (1.0 + jnp.exp(-normed))
        left = jnp.where(column == 0, 0.0, pltpu.roll(hidden, 1, 0))
        right = jnp.where(column == cols - 1, 0.0, pltpu.roll(hidden, band - 1, 0))
        line = jnp.concatenate([left.astype(bf16), hidden.astype(bf16), right.astype(bf16)], axis=1)
        cols_ref[(row + 1) * band : (row + 2) * band, :] = line
    total = jnp.dot(cols_ref[0 : rows * band, :], w_ref[0], preferred_element_type=f32)
    for tap in (1, 2):
        total = total + jnp.dot(
            cols_ref[tap * band : (tap + rows) * band, :], w_ref[tap], preferred_element_type=f32
        )
    total = total.reshape(rows, frames, cols, total.shape[-1])
    half = frames // 2
    low = total[:, :half].reshape(rows, half * cols, -1)
    high = total[:, half:].reshape(rows, half * cols, -1)
    odd = lax.axis_index("mp") % 2

    @pl.when(odd == 0)
    def _():
        keep_ref[...] = low.reshape(keep_ref.shape)
        send_ref[...] = high.reshape(keep_ref.shape).astype(bf16)

    @pl.when(odd == 1)
    def _():
        keep_ref[...] = high.reshape(keep_ref.shape)
        send_ref[...] = low.reshape(keep_ref.shape).astype(bf16)


def piece_conv(piece, stats, gain, bias, weight):
    frames, rows, cols, width = piece.shape
    width_out = weight.shape[-1]
    count = frames * rows * cols
    return pl.pallas_call(
        conv_kernel,
        out_shape=(
            jax.ShapeDtypeStruct((count // 2, width_out), f32),
            jax.ShapeDtypeStruct((count // 2, width_out), bf16),
        ),
        in_specs=[vmem_spec()] * 8,
        out_specs=(vmem_spec(), vmem_spec()),
        scratch_shapes=[pltpu.VMEM(((rows + 2) * frames * cols, 3 * width), bf16)],
        compiler_params=params(14),
        cost_estimate=pl.CostEstimate(
            flops=2 * count * 9 * width * width_out,
            bytes_accessed=2 * 9 * width * width_out + 4 * count * width,
            transcendentals=count * width,
        ),
        name="piece_conv",
    )(piece, *stats, gain, bias, weight)


PAD = 8


def fill_frames(scratch, mine, other):
    tm = lax.axis_index("tm")
    odd = lax.axis_index("mp") % 2
    frames, rows, width = scratch.shape
    scratch[0] = jnp.zeros((rows, width), bf16)
    scratch[frames - 1] = jnp.zeros((rows, width), bf16)
    for i in range(4):
        block = 1 + 2 * jnp.bitwise_xor(tm, i)
        scratch[block + odd, 0 : rows - PAD] = mine[i][...]
        scratch[block + 1 - odd, 0 : rows - PAD] = other[i][...]
    for f in range(1, frames - 1):
        scratch[f, rows - PAD :] = jnp.zeros((PAD, width), bf16)


def grad_kernel(m0, m1, m2, m3, o0, o1, o2, o3, c0, c1, c2, c3, out_ref, s_ref, c_ref):
    fill_frames(s_ref, [m0, m1, m2, m3], [o0, o1, o2, o3])
    tm = lax.axis_index("tm")
    frames, rows, width = c_ref.shape
    for i, c in enumerate((c0, c1, c2, c3)):
        block = 2 * jnp.bitwise_xor(tm, i)
        for f in range(2):
            c_ref[block + f, 0 : rows - PAD] = c[f]
    for f in range(frames):
        c_ref[f, rows - PAD :] = jnp.zeros((PAD, width), bf16)
    cot = c_ref[...].reshape(frames * rows, width)
    for k in range(3):
        window = s_ref[k : k + frames].reshape(frames * rows, s_ref.shape[-1])
        out_ref[k] = lax.dot_general(
            window, cot, (((0,), (0,)), ((), ())), preferred_element_type=f32
        ).astype(out_ref.dtype)


def temporal_grads(mine, other, cot, dtype):
    count, width = mine[0].shape
    width_out = cot[0].shape[-1]
    return pl.pallas_call(
        grad_kernel,
        out_shape=jax.ShapeDtypeStruct((3, width, width_out), dtype),
        in_specs=[vmem_spec()] * 12,
        out_specs=vmem_spec(),
        scratch_shapes=[
            pltpu.VMEM((10, count + PAD, width), bf16),
            pltpu.VMEM((8, count + PAD, width_out), bf16),
        ],
        compiler_params=params(20),
        cost_estimate=pl.CostEstimate(
            flops=2 * 3 * 8 * count * width * width_out,
            bytes_accessed=4 * 8 * count * width,
            transcendentals=0,
        ),
        name="temporal_grads",
    )(*mine, *other, *cot)


def temporal_kernel(blocks, m0, m1, m2, m3, o0, o1, o2, o3, w_ref, send_ref, keep_ref, s_ref):
    fill_frames(s_ref, [m0, m1, m2, m3], [o0, o1, o2, o3])
    tm = lax.axis_index("tm")
    frames, rows, width = s_ref.shape
    for i, out in zip(blocks, (send_ref, keep_ref), strict=True):
        first = 2 * jnp.bitwise_xor(tm, i)
        total = None
        for k in range(3):
            window = s_ref[pl.ds(first + k, 2)].reshape(2 * rows, width)
            term = jnp.dot(window, w_ref[k], preferred_element_type=f32)
            total = term if total is None else total + term
        total = total.reshape(2, rows, -1)[:, : rows - PAD]
        out[...] = total.astype(out.dtype)


def temporal_conv(blocks, mine, other, weight):
    count, width = mine[0].shape
    width_out = weight.shape[-1]
    return pl.pallas_call(
        functools.partial(temporal_kernel, blocks),
        out_shape=(
            jax.ShapeDtypeStruct((2, count, width_out), bf16),
            jax.ShapeDtypeStruct((2, count, width_out), f32),
        ),
        in_specs=[vmem_spec()] * 9,
        out_specs=(vmem_spec(), vmem_spec()),
        scratch_shapes=[pltpu.VMEM((10, count + PAD, width), bf16)],
        compiler_params=params(16),
        cost_estimate=pl.CostEstimate(
            flops=2 * 3 * 4 * count * width * width_out,
            bytes_accessed=4 * 8 * count * width,
            transcendentals=0,
        ),
        name="temporal_conv",
    )(*mine, *other, weight)


def xor(axis_size, bit):
    return [(i, i ^ bit) for i in range(axis_size)]


def add16(a, b):
    return (a.astype(f32) + b.astype(f32)).astype(bf16)


def tie(x, *others):
    return lax.optimization_barrier((x,) + others)[0]


def body(activations, norm_gain, norm_bias, spatial_weight, temporal_weight, cotangent):
    own = activations[0]
    frames, rows, cols, width = own.shape
    width_out = spatial_weight.shape[2]
    core, chip = xor(4, 1), xor(4, 2)
    near, far = xor(4, 1), xor(4, 2)
    count = rows * cols

    raw_core = lax.ppermute(own, "tm", core)
    raw_chip = lax.ppermute(own, "tm", chip)
    st_own = piece_stats(own)
    st_chip = lax.ppermute(st_own, "tm", chip)
    st_core = lax.ppermute(st_own, "tm", core)
    st_both = lax.ppermute(st_own, "tm", xor(4, 3))
    raw_both = lax.ppermute(raw_chip, "tm", core)
    stats = (st_own, st_core, st_chip, st_both)
    taps = spatial_weight.reshape(3, 3 * width, width_out)

    pieces = (own, raw_core, raw_chip, raw_both)
    keep, got, part, across, mine, other = ([None] * 4 for _ in range(6))
    last = None
    for step, i in ("c0", "c1", "c2", "s0", "c3", "s1", "f0", "s2", "f1", "s3", "f2", "f3"):
        i = int(i)
        if step == "c":
            piece = pieces[i] if last is None else tie(pieces[i], last)
            keep[i], send = piece_conv(piece, stats, norm_gain, norm_bias, taps)
            got[i] = lax.ppermute(send, "mp", near)
            last = keep[i]
        elif step == "s":
            part[i] = add16(tie(keep[i], last), got[i])
            across[i] = lax.ppermute(part[i], "mp", far)
            last = part[i]
        else:
            mine[i] = add16(tie(part[i], last), across[i])
            other[i] = lax.ppermute(mine[i], "mp", near)
            last = mine[i]

    cot_own = tie(cotangent[0].reshape(frames, count, width), part[1])
    cot_core = lax.ppermute(cot_own, "tm", core)
    cot_chip = lax.ppermute(cot_own, "tm", chip)
    cot_both = lax.ppermute(cot_chip, "tm", core)
    cot = (cot_own, cot_core, cot_chip, cot_both)

    clips = lax.axis_size("dp")
    if clips == 2:
        sent = temporal_grads(mine, other, cot, bf16)
        theirs = lax.ppermute(sent, "dp", [(0, 1), (1, 0)])
        temporal_grad = (sent.astype(f32) + theirs.astype(f32)) / clips
    else:
        sent = temporal_grads(mine, other, cot, f32)
        temporal_grad = lax.psum(sent, "dp") / clips

    send, keep_chip = temporal_conv((3, 2), [tie(mine[0], sent)] + mine[1:], other, temporal_weight)
    far_part = lax.ppermute(send, "tm", core)
    send, keep_own = temporal_conv((1, 0), [tie(mine[0], send)] + mine[1:], other, temporal_weight)
    near_part = lax.ppermute(send, "tm", core)
    from_chip = lax.ppermute(add16(keep_chip, far_part), "tm", chip)
    block = (keep_own + near_part.astype(f32) + from_chip.astype(f32)).astype(bf16)
    return block.reshape(activations.shape), temporal_grad


def solution(mesh):
    in_specs = (
        P("dp", "tm", None, None, "mp"),
        P("mp"),
        P("mp"),
        P(None, "mp", "tm"),
        P(None, "tm", "mp"),
        P("dp", "tm", None, None, "mp"),
    )
    out_specs = (P("dp", "tm", None, None, "mp"), P(None, "tm", "mp"))
    return jax.shard_map(body, mesh=mesh, in_specs=in_specs, out_specs=out_specs, check_vma=False)
```

time: 117 us -> 94.2 us (0.81)
  starting transfers between devices: 35.6 us -> 25 us
  matrix products: 7.38 us -> 0 us
  other arithmetic: 8.69 us -> 2.55 us
  local copies, waits for them, and re-layouts: 10.3 us -> 4.98 us
  Pallas kernels: 9.46 us -> 13.2 us
  waiting for transfers between devices: 44 us -> 47.3 us
    ppermute x16, starting transfers between devices: 29.4 us -> 18.2 us  [the longest x4 6.02 us: body(): across[i] = lax.ppermute(part[i], 'mp', far)]
    dot_general x6 -> x0, matrix products: 7.38 us -> none  [the longest x3 4.96 us: body(): lax.dot_general(windows[k], cot, (((0,), (0,)), ((), ())), preferred_elem...]
    pallas_call x4 -> x7, Pallas kernels: 7 us -> 12.4 us  [the longest x4 7.34 us: piece_conv(): pl.pallas_call(conv_kernel, out_shape=(jax.ShapeDtypeStruct((count // 2,...]
    ppermute x1, waiting for transfers between devices: 0.01 us -> 5.11 us  [body(): st_chip = lax.ppermute(st_own, 'tm', chip)]
    ppermute x1, starting transfers between devices: 2.97 us -> 0.27 us  [body(): st_chip = lax.ppermute(st_own, 'tm', chip)]
    convert_element_type x1 -> x0, local copies, waits for them, and re-layouts: 2.15 us -> none  [body(): near = lax.ppermute(part[1].astype(bf16), 'tm', core)]
    add x1 -> x0, local copies, waits for them, and re-layouts: 2.1 us -> none  [body(): sum((jnp.dot(windows[k], temporal_weight[k], preferred_element_type=f32)...]
    broadcast_in_dim x1 -> x0, other arithmetic: 1.78 us -> none  [body(): (part[0] + near.astype(f32) + from_chip.astype(f32)).astype(bf16)[None]]
  transfers between devices with their start and end apart: 25 -> 25, of which waited for: 9 -> 11; matrix products, arithmetic and copies ran while one was open for 8% -> 1% of each run, Pallas kernels for 8% -> 10%
where the time goes in v2:
time: 94.2 us; the launch traced here: 93.9 us
  waiting for transfers between devices  47.3 us (50%)
  starting transfers between devices  25 us (27%)
  Pallas kernels  13.2 us (14%)
  local copies, waits for them, and re-layouts  4.98 us (5%)
  other arithmetic  2.55 us (3%)
    ppermute x4, waiting for transfers between devices, body(): across[i] = lax.ppermute(part[i], 'mp', far)  11.4 us
    ppermute x4, waiting for transfers between devices, body(): got[i] = lax.ppermute(send, 'mp', near)  11.3 us
    ppermute x1, waiting for transfers between devices, body(): from_chip = lax.ppermute(add16(keep_chip, far_part), 'tm', chip)  8.04 us
    pallas_call x4, Pallas kernels, piece_conv(): pl.pallas_call(conv_kernel, out_shape=(jax.ShapeDtypeStruct((count // 2,...  7.34 us
    ppermute x4, waiting for transfers between devices, body(): other[i] = lax.ppermute(mine[i], 'mp', near)  6.3 us
    ppermute x4, starting transfers between devices, body(): across[i] = lax.ppermute(part[i], 'mp', far)  6.02 us
    ppermute x1, waiting for transfers between devices, body(): theirs = lax.ppermute(sent, 'dp', [(0, 1), (1, 0)])  5.14 us
    ppermute x1, waiting for transfers between devices, body(): st_chip = lax.ppermute(st_own, 'tm', chip)  5.11 us
  transfers between devices with their start and end apart: 25, of which 11 were waited for; matrix products, arithmetic and copies ran while one was open for 1% of the time, Pallas kernels for 10%

profile of v2, /device:TPU:0, one launch (start us, length us, event | category | flops | bytes accessed | tf_op | source)
XLA Modules:
  0.0 93.9 jit_solution(11951386476414007885)
XLA Ops:
  1.1 2.6 %collective-permute-start.3 = (bf16[2,5,40,320]{3,2,1,0:T(8,128)(2,1)}, bf16[2,5,40,320]{3,2,1,0:T(8,128)(2,1)S(1)}, u32[]{:S(2)}, u32[]{:S(2)}) collective-permute-start(bf16[2,5,40,320]{3,2,1,0:T(8,128)(2,1)} %bitcast.5), channel_id=1, source_target_pairs={{0,8},{4,12},{8,0},{12,4},{1,9},{5,13},{9,1},{13,5},{2,10},{6,14},... | collective-permute-start | bytes 768008 | tf_op jit(solution)/shard_map/ppermute | solution.py:241
  3.7 1.0 %copy-done.1 = bf16[1,2,5,40,320]{4,3,2,1,0:T(8,128)(2,1)S(1)} copy-done((bf16[1,2,5,40,320]{4,3,2,1,0:T(8,128)(2,1)S(1)}, bf16[1,2,5,40,320]{4,3,2,1,0:T(8,128)(2,1)}, u32[]{:S(2)}) %copy-start.1) | copy-done | bytes 256024
  6.1 1.4 %collective-permute-start.2 = (f32[16,320]{1,0:T(8,128)S(1)}, f32[16,320]{1,0:T(8,128)S(1)}, u32[]{:S(2)}, u32[]{:S(2)}) collective-permute-start(f32[16,320]{1,0:T(8,128)S(1)} %piece_stats.1.s0_ref), channel_id=1, source_target_pairs={{0,12},{4,8},{8,4},{12,0},{1,13},{5,9},{9,5},{13,1},{2,14},{6,10},... | collective-permute-start | bytes 61448 | tf_op jit(solution)/shard_map/ppermute | solution.py:245
  7.5 5.1 %collective-permute-done.1.s2_ref = f32[16,320]{1,0:T(8,128)S(1)} collective-permute-done((f32[16,320]{1,0:T(8,128)S(1)}, f32[16,320]{1,0:T(8,128)S(1)}, u32[]{:S(2)}, u32[]{:S(2)}) %collective-permute-start.1) | collective-permute-done | bytes 20512 | tf_op jit(solution)/shard_map/ppermute | solution.py:243
  12.6 1.0 %copy-done.2 = bf16[1,2,5,40,320]{4,3,2,1,0:T(8,128)(2,1)S(1)} copy-done((bf16[1,2,5,40,320]{4,3,2,1,0:T(8,128)(2,1)S(1)}, bf16[1,2,5,40,320]{4,3,2,1,0:T(8,128)(2,1)}, u32[]{:S(2)}) %copy-start.2) | copy-done | bytes 256024
  13.6 1.6 %copy-done.3 = bf16[9,320,320]{2,1,0:T(8,128)(2,1)S(1)} copy-done((bf16[9,320,320]{2,1,0:T(8,128)(2,1)S(1)}, bf16[9,320,320]{2,1,0:T(8,128)(2,1)}, u32[]{:S(2)}) %copy-start.3) | copy-done | bytes 1843224
  16.6 1.8 %piece_conv.4 = (f32[200,320]{1,0:T(8,128)S(1)}, bf16[200,320]{1,0:T(8,128)(2,1)S(1)}) custom-call(bf16[2,5,40,320]{3,2,1,0:T(8,128)(2,1)S(1)} %bitcast.7, f32[16,320]{1,0:T(8,128)S(1)} %piece_stats.1.s0_ref, f32[16,320]{1,0:T(8,128)S(1)} %collective-permute-done.s1_ref, f32[16,320]{1,0:T(8,128)S(1)} %collective-permute-done.1.s2_ref, ...), custom_call_target="tpu_custom_call" | custom-call | flops 737280000 | bytes 2355200 | tf_op jit(solution)/shard_map/piece_conv/pallas_call | solution.py:107
  18.4 1.9 %collective-permute-start.5 = (bf16[200,320]{1,0:T(8,128)(2,1)S(1)}, bf16[200,320]{1,0:T(8,128)(2,1)S(1)}, u32[]{:S(2)}, u32[]{:S(2)}) collective-permute-start(bf16[200,320]{1,0:T(8,128)(2,1)S(1)} %get-tuple-element.34), channel_id=1, source_target_pairs={{0,1},{1,0},{2,3},{3,2},{4,5},{5,4},{6,7},{7,6},{8,9},{9,8},{10,11... | collective-permute-start | bytes 384008 | tf_op jit(solution)/shard_map/ppermute | solution.py:258
  20.3 1.8 %piece_conv.5 = (f32[200,320]{1,0:T(8,128)S(1)}, bf16[200,320]{1,0:T(8,128)(2,1)S(1)}) custom-call(bf16[2,5,40,320]{3,2,1,0:T(8,128)(2,1)S(1)} %collective-permute-done.4.x_ref, f32[16,320]{1,0:T(8,128)S(1)} %piece_stats.1.s0_ref, f32[16,320]{1,0:T(8,128)S(1)} %collective-permute-done.s1_ref, f32[16,320]{1,0:T(8,128)S(1)} %collective-permute-done.1.s2_ref, ...), custom_call_target="tpu_custom_call" | custom-call | flops 737280000 | bytes 2355200 | tf_op jit(solution)/shard_map/piece_conv/pallas_call | solution.py:107
  22.2 1.8 %piece_conv.6 = (f32[200,320]{1,0:T(8,128)S(1)}, bf16[200,320]{1,0:T(8,128)(2,1)S(1)}) custom-call(bf16[2,5,40,320]{3,2,1,0:T(8,128)(2,1)S(1)} %collective-permute-done.3.x_ref, f32[16,320]{1,0:T(8,128)S(1)} %piece_stats.1.s0_ref, f32[16,320]{1,0:T(8,128)S(1)} %collective-permute-done.s1_ref, f32[16,320]{1,0:T(8,128)S(1)} %collective-permute-done.1.s2_ref, ...), custom_call_target="tpu_custom_call" | custom-call | flops 737280000 | bytes 2355200 | tf_op jit(solution)/shard_map/piece_conv/pallas_call | solution.py:107
  24.6 2.8 %collective-permute-start.8 = (bf16[200,320]{1,0:T(8,128)(2,1)S(1)}, bf16[200,320]{1,0:T(8,128)(2,1)S(1)}, u32[]{:S(2)}, u32[]{:S(2)}) collective-permute-start(bf16[200,320]{1,0:T(8,128)(2,1)S(1)} %add_convert_fusion.9), channel_id=1, source_target_pairs={{0,2},{1,3},{2,0},{3,1},{4,6},{5,7},{6,4},{7,5},{8,10},{9,11},{10,... | collective-permute-start | bytes 384008 | tf_op jit(solution)/shard_map/ppermute | solution.py:262
  27.4 1.6 %collective-permute-start.9 = (bf16[200,320]{1,0:T(8,128)(2,1)S(1)}, bf16[200,320]{1,0:T(8,128)(2,1)S(1)}, u32[]{:S(2)}, u32[]{:S(2)}) collective-permute-start(bf16[200,320]{1,0:T(8,128)(2,1)S(1)} %get-tuple-element.41), channel_id=1, source_target_pairs={{0,1},{1,0},{2,3},{3,2},{4,5},{5,4},{6,7},{7,6},{8,9},{9,8},{10,11... | collective-permute-start | bytes 384008 | tf_op jit(solution)/shard_map/ppermute | solution.py:258
  29.0 2.0 %piece_conv.7 = (f32[200,320]{1,0:T(8,128)S(1)}, bf16[200,320]{1,0:T(8,128)(2,1)S(1)}) custom-call(bf16[2,5,40,320]{3,2,1,0:T(8,128)(2,1)S(1)} %collective-permute-done.6.x_ref, f32[16,320]{1,0:T(8,128)S(1)} %piece_stats.1.s0_ref, f32[16,320]{1,0:T(8,128)S(1)} %collective-permute-done.s1_ref, f32[16,320]{1,0:T(8,128)S(1)} %collective-permute-done.1.s2_ref, ...), custom_call_target="tpu_custom_call" | custom-call | flops 737280000 | bytes 2355200 | tf_op jit(solution)/shard_map/piece_conv/pallas_call | solution.py:107
  31.0 3.2 %collective-permute-done.7 = bf16[200,320]{1,0:T(8,128)(2,1)S(1)} collective-permute-done((bf16[200,320]{1,0:T(8,128)(2,1)S(1)}, bf16[200,320]{1,0:T(8,128)(2,1)S(1)}, u32[]{:S(2)}, u32[]{:S(2)}) %collective-permute-start.7) | collective-permute-done | bytes 128032 | tf_op jit(solution)/shard_map/ppermute | solution.py:258
  34.3 2.7 %collective-permute-done.9 = bf16[200,320]{1,0:T(8,128)(2,1)S(1)} collective-permute-done((bf16[200,320]{1,0:T(8,128)(2,1)S(1)}, bf16[200,320]{1,0:T(8,128)(2,1)S(1)}, u32[]{:S(2)}, u32[]{:S(2)}) %collective-permute-start.9) | collective-permute-done | bytes 128032 | tf_op jit(solution)/shard_map/ppermute | solution.py:258
  37.0 3.1 %collective-permute-start.12 = (bf16[200,320]{1,0:T(8,128)(2,1)S(1)}, bf16[200,320]{1,0:T(8,128)(2,1)S(1)}, u32[]{:S(2)}, u32[]{:S(2)}) collective-permute-start(bf16[200,320]{1,0:T(8,128)(2,1)S(1)} %add_convert_fusion.6), channel_id=1, source_target_pairs={{0,2},{1,3},{2,0},{3,1},{4,6},{5,7},{6,4},{7,5},{8,10},{9,11},{10,... | collective-permute-start | bytes 384008 | tf_op jit(solution)/shard_map/ppermute | solution.py:262
  40.9 1.7 %collective-permute-start.19 = (bf16[2,200,320]{2,1,0:T(8,128)(2,1)S(1)}, bf16[2,200,320]{2,1,0:T(8,128)(2,1)S(1)}, u32[]{:S(2)}, u32[]{:S(2)}) collective-permute-start(bf16[2,200,320]{2,1,0:T(8,128)(2,1)S(1)} %bitcast.13), channel_id=1, source_target_pairs={{0,8},{4,12},{8,0},{12,4},{1,9},{5,13},{9,1},{13,5},{2,10},{6,14},... | collective-permute-start | bytes 768008 | tf_op jit(solution)/shard_map/ppermute | solution.py:271
  42.5 5.5 %collective-permute-done.10 = bf16[200,320]{1,0:T(8,128)(2,1)S(1)} collective-permute-done((bf16[200,320]{1,0:T(8,128)(2,1)S(1)}, bf16[200,320]{1,0:T(8,128)(2,1)S(1)}, u32[]{:S(2)}, u32[]{:S(2)}) %collective-permute-start.10) | collective-permute-done | bytes 128032 | tf_op jit(solution)/shard_map/ppermute | solution.py:262
  48.1 5.2 %collective-permute-done.11 = bf16[200,320]{1,0:T(8,128)(2,1)S(1)} collective-permute-done((bf16[200,320]{1,0:T(8,128)(2,1)S(1)}, bf16[200,320]{1,0:T(8,128)(2,1)S(1)}, u32[]{:S(2)}, u32[]{:S(2)}) %collective-permute-start.11) | collective-permute-done | bytes 128032 | tf_op jit(solution)/shard_map/ppermute | solution.py:258
  53.4 2.2 %collective-permute-start.15 = (bf16[200,320]{1,0:T(8,128)(2,1)S(1)}, bf16[200,320]{1,0:T(8,128)(2,1)S(1)}, u32[]{:S(2)}, u32[]{:S(2)}) collective-permute-start(bf16[200,320]{1,0:T(8,128)(2,1)S(1)} %add_convert_fusion.5.m1), channel_id=1, source_target_pairs={{0,1},{1,0},{2,3},{3,2},{4,5},{5,4},{6,7},{7,6},{8,9},{9,8},{10,11... | collective-permute-start | bytes 384008 | tf_op jit(solution)/shard_map/ppermute | solution.py:266
  55.7 5.9 %collective-permute-done.13 = bf16[200,320]{1,0:T(8,128)(2,1)S(1)} collective-permute-done((bf16[200,320]{1,0:T(8,128)(2,1)S(1)}, bf16[200,320]{1,0:T(8,128)(2,1)S(1)}, u32[]{:S(2)}, u32[]{:S(2)}) %collective-permute-start.13) | collective-permute-done | bytes 128032 | tf_op jit(solution)/shard_map/ppermute | solution.py:262
  61.7 2.1 %collective-permute-start.17 = (bf16[200,320]{1,0:T(8,128)(2,1)S(1)}, bf16[200,320]{1,0:T(8,128)(2,1)S(1)}, u32[]{:S(2)}, u32[]{:S(2)}) collective-permute-start(bf16[200,320]{1,0:T(8,128)(2,1)S(1)} %add_convert_fusion.2.m3), channel_id=1, source_target_pairs={{0,1},{1,0},{2,3},{3,2},{4,5},{5,4},{6,7},{7,6},{8,9},{9,8},{10,11... | collective-permute-start | bytes 384008 | tf_op jit(solution)/shard_map/ppermute | solution.py:266
  63.7 4.6 %collective-permute-done.16.o2 = bf16[200,320]{1,0:T(8,128)(2,1)S(1)} collective-permute-done((bf16[200,320]{1,0:T(8,128)(2,1)S(1)}, bf16[200,320]{1,0:T(8,128)(2,1)S(1)}, u32[]{:S(2)}, u32[]{:S(2)}) %collective-permute-start.16) | collective-permute-done | bytes 128032 | tf_op jit(solution)/shard_map/ppermute | solution.py:266
  68.4 1.6 %collective-permute-done.17.o3 = bf16[200,320]{1,0:T(8,128)(2,1)S(1)} collective-permute-done((bf16[200,320]{1,0:T(8,128)(2,1)S(1)}, bf16[200,320]{1,0:T(8,128)(2,1)S(1)}, u32[]{:S(2)}, u32[]{:S(2)}) %collective-permute-start.17) | collective-permute-done | bytes 128032 | tf_op jit(solution)/shard_map/ppermute | solution.py:266
  70.0 2.1 %temporal_grads.1 = bf16[3,320,320]{2,1,0:T(8,128)(2,1)S(1)} custom-call(bf16[200,320]{1,0:T(8,128)(2,1)S(1)} %add_convert_fusion.7.m0, bf16[200,320]{1,0:T(8,128)(2,1)S(1)} %add_convert_fusion.5.m1, bf16[200,320]{1,0:T(8,128)(2,1)S(1)} %add_convert_fusion.3.m2, bf16[200,320]{1,0:T(8,128)(2,1)S(1)} %add_convert_fusion.2.m3, ...), custom_call_target="tpu_custom_call" | custom-call | flops 983040000 | bytes 2048000 | tf_op jit(solution)/shard_map/temporal_grads/pallas_call | solution.py:164
  72.2 1.4 %temporal_conv.2 = (bf16[2,200,320]{2,1,0:T(8,128)(2,1)S(1)}, f32[2,200,320]{2,1,0:T(8,128)S(1)}) custom-call(bf16[200,320]{1,0:T(8,128)(2,1)S(1)} %add_convert_fusion.7.m0, bf16[200,320]{1,0:T(8,128)(2,1)S(1)} %add_convert_fusion.5.m1, bf16[200,320]{1,0:T(8,128)(2,1)S(1)} %add_convert_fusion.3.m2, bf16[200,320]{1,0:T(8,128)(2,1)S(1)} %add_convert_fusion.2.m3, ...), custom_call_target="tpu_custom_call" | custom-call | flops 491520000 | bytes 2048000 | tf_op jit(solution)/shard_map/temporal_conv/pallas_call | solution.py:201
  73.7 1.6 %collective-permute-start.24 = (bf16[3,320,320]{2,1,0:T(8,128)(2,1)S(1)}, bf16[3,320,320]{2,1,0:T(8,128)(2,1)S(1)}, u32[]{:S(2)}, u32[]{:S(2)}) collective-permute-start(bf16[3,320,320]{2,1,0:T(8,128)(2,1)S(1)} %temporal_grads.1), channel_id=1, source_target_pairs={{0,16},{16,0},{1,17},{17,1},{2,18},{18,2},{3,19},{19,3},{4,20},{20... | collective-permute-start | bytes 1843208 | tf_op jit(solution)/shard_map/ppermute | solution.py:278
  75.3 1.4 %temporal_conv.3 = (bf16[2,200,320]{2,1,0:T(8,128)(2,1)S(1)}, f32[2,200,320]{2,1,0:T(8,128)S(1)}) custom-call(bf16[200,320]{1,0:T(8,128)(2,1)S(1)} %add_convert_fusion.7.m0, bf16[200,320]{1,0:T(8,128)(2,1)S(1)} %add_convert_fusion.5.m1, bf16[200,320]{1,0:T(8,128)(2,1)S(1)} %add_convert_fusion.3.m2, bf16[200,320]{1,0:T(8,128)(2,1)S(1)} %add_convert_fusion.2.m3, ...), custom_call_target="tpu_custom_call" | custom-call | flops 491520000 | bytes 2048000 | tf_op jit(solution)/shard_map/temporal_conv/pallas_call | solution.py:201
  77.0 1.6 %collective-permute-start.23 = (bf16[2,200,320]{2,1,0:T(8,128)(2,1)S(1)}, bf16[2,200,320]{2,1,0:T(8,128)(2,1)S(1)}, u32[]{:S(2)}, u32[]{:S(2)}) collective-permute-start(bf16[2,200,320]{2,1,0:T(8,128)(2,1)S(1)} %add_convert_fusion.1), channel_id=1, source_target_pairs={{0,8},{4,12},{8,0},{12,4},{1,9},{5,13},{9,1},{13,5},{2,10},{6,14},... | collective-permute-start | bytes 768008 | tf_op jit(solution)/shard_map/ppermute | solution.py:288
  78.6 8.0 %collective-permute-done.23 = bf16[2,200,320]{2,1,0:T(8,128)(2,1)S(1)} collective-permute-done((bf16[2,200,320]{2,1,0:T(8,128)(2,1)S(1)}, bf16[2,200,320]{2,1,0:T(8,128)(2,1)S(1)}, u32[]{:S(2)}, u32[]{:S(2)}) %collective-permute-start.23) | collective-permute-done | bytes 256032 | tf_op jit(solution)/shard_map/ppermute | solution.py:288
  87.5 5.1 %collective-permute-done.24 = bf16[3,320,320]{2,1,0:T(8,128)(2,1)S(1)} collective-permute-done((bf16[3,320,320]{2,1,0:T(8,128)(2,1)S(1)}, bf16[3,320,320]{2,1,0:T(8,128)(2,1)S(1)}, u32[]{:S(2)}, u32[]{:S(2)}) %collective-permute-start.24) | collective-permute-done | bytes 614432 | tf_op jit(solution)/shard_map/ppermute | solution.py:278
  92.6 1.3 %add_multiply_fusion = f32[3,320,320]{2,1,0:T(8,128)} fusion(bf16[3,320,320]{2,1,0:T(8,128)(2,1)S(1)} %collective-permute-done.24, bf16[3,320,320]{2,1,0:T(8,128)(2,1)S(1)} %temporal_grads.1), kind=kLoop, calls=%fused_computation | loop fusion | flops 1228800 | bytes 2457600 | tf_op jit(solution)/shard_map/div | solution.py:279
  (57 shorter events, 6.3 us)
Async XLA Ops:
  0.6 19.6 %collective-permute-start.4 = (bf16[2,5,40,320]{3,2,1,0:T(8,128)(2,1)}, bf16[2,5,40,320]{3,2,1,0:T(8,128)(2,1)S(1)}, u32[]{:S(2)}, u32[]{:S(2)}) collective-permute-start(bf16[2,5,40,320]{3,2,1,0:T(8,128)(2,1)} %bitcast.4), channel_id=1, source_target_pairs={{0,4},{4,0},{8,12},{12,8},{1,5},{5,1},{9,13},{13,9},{2,6},{6,2},{1... | collective-permute-start | bytes 768008 | tf_op jit(solution)/shard_map/ppermute | solution.py:240
  1.1 20.9 %collective-permute-start.3 = (bf16[2,5,40,320]{3,2,1,0:T(8,128)(2,1)}, bf16[2,5,40,320]{3,2,1,0:T(8,128)(2,1)S(1)}, u32[]{:S(2)}, u32[]{:S(2)}) collective-permute-start(bf16[2,5,40,320]{3,2,1,0:T(8,128)(2,1)} %bitcast.5), channel_id=1, source_target_pairs={{0,8},{4,12},{8,0},{12,4},{1,9},{5,13},{9,1},{13,5},{2,10},{6,14},... | collective-permute-start | bytes 768008 | tf_op jit(solution)/shard_map/ppermute | solution.py:241
  3.7 1.0 %copy-start.1 = (bf16[1,2,5,40,320]{4,3,2,1,0:T(8,128)(2,1)S(1)}, bf16[1,2,5,40,320]{4,3,2,1,0:T(8,128)(2,1)}, u32[]{:S(2)}) copy-start(bf16[1,2,5,40,320]{4,3,2,1,0:T(8,128)(2,1)} %param.6) | copy-start | bytes 768004
  5.6 1.9 %collective-permute-start = (f32[16,320]{1,0:T(8,128)S(1)}, f32[16,320]{1,0:T(8,128)S(1)}, u32[]{:S(2)}, u32[]{:S(2)}) collective-permute-start(f32[16,320]{1,0:T(8,128)S(1)} %piece_stats.1.s0_ref), channel_id=1, source_target_pairs={{0,4},{4,0},{8,12},{12,8},{1,5},{5,1},{9,13},{13,9},{2,6},{6,2},{1... | collective-permute-start | bytes 61448 | tf_op jit(solution)/shard_map/ppermute | solution.py:244
  5.8 6.8 %collective-permute-start.1 = (f32[16,320]{1,0:T(8,128)S(1)}, f32[16,320]{1,0:T(8,128)S(1)}, u32[]{:S(2)}, u32[]{:S(2)}) collective-permute-start(f32[16,320]{1,0:T(8,128)S(1)} %piece_stats.1.s0_ref), channel_id=1, source_target_pairs={{0,8},{4,12},{8,0},{12,4},{1,9},{5,13},{9,1},{13,5},{2,10},{6,14},... | collective-permute-start | bytes 61448 | tf_op jit(solution)/shard_map/ppermute | solution.py:243
  6.1 6.5 %collective-permute-start.2 = (f32[16,320]{1,0:T(8,128)S(1)}, f32[16,320]{1,0:T(8,128)S(1)}, u32[]{:S(2)}, u32[]{:S(2)}) collective-permute-start(f32[16,320]{1,0:T(8,128)S(1)} %piece_stats.1.s0_ref), channel_id=1, source_target_pairs={{0,12},{4,8},{8,4},{12,0},{1,13},{5,9},{9,5},{13,1},{2,14},{6,10},... | collective-permute-start | bytes 61448 | tf_op jit(solution)/shard_map/ppermute | solution.py:245
  13.6 1.6 %copy-start.3 = (bf16[9,320,320]{2,1,0:T(8,128)(2,1)S(1)}, bf16[9,320,320]{2,1,0:T(8,128)(2,1)}, u32[]{:S(2)}) copy-start(bf16[9,320,320]{2,1,0:T(8,128)(2,1)} %param.9) | copy-start | bytes 5529604
  16.6 3.7 %copy-start.4 = (bf16[9,320,320]{2,1,0:T(8,128)(2,1)S(1)}, bf16[9,320,320]{2,1,0:T(8,128)(2,1)}, u32[]{:S(2)}) copy-start(bf16[9,320,320]{2,1,0:T(8,128)(2,1)} %param.9) | copy-start | bytes 5529604
  18.4 3.8 %copy-start.7 = (f32[320]{0:T(512)S(1)}, f32[320]{0:T(512)}, u32[]{:S(2)}) copy-start(f32[320]{0:T(512)} %gain_ref.7) | copy-start | bytes 3844
  18.4 3.8 %copy-start.9 = (f32[320]{0:T(512)S(1)}, f32[320]{0:T(512)}, u32[]{:S(2)}) copy-start(f32[320]{0:T(512)} %bias_ref.7) | copy-start | bytes 3844
  18.4 6.1 %collective-permute-start.5 = (bf16[200,320]{1,0:T(8,128)(2,1)S(1)}, bf16[200,320]{1,0:T(8,128)(2,1)S(1)}, u32[]{:S(2)}, u32[]{:S(2)}) collective-permute-start(bf16[200,320]{1,0:T(8,128)(2,1)S(1)} %get-tuple-element.34), channel_id=1, source_target_pairs={{0,1},{1,0},{2,3},{3,2},{4,5},{5,4},{6,7},{7,6},{8,9},{9,8},{10,11... | collective-permute-start | bytes 384008 | tf_op jit(solution)/shard_map/ppermute | solution.py:258
  22.1 6.9 %collective-permute-start.6 = (bf16[2,5,40,320]{3,2,1,0:T(8,128)(2,1)S(1)}, bf16[2,5,40,320]{3,2,1,0:T(8,128)(2,1)S(1)}, u32[]{:S(2)}, u32[]{:S(2)}) collective-permute-start(bf16[2,5,40,320]{3,2,1,0:T(8,128)(2,1)S(1)} %collective-permute-done.3.x_ref), channel_id=1, source_target_pairs={{0,4},{4,0},{8,12},{12,8},{1,5},{5,1},{9,13},{13,9},{2,6},{6,2},{1... | collective-permute-start | bytes 768008 | tf_op jit(solution)/shard_map/ppermute | solution.py:246
  24.0 10.1 %collective-permute-start.7 = (bf16[200,320]{1,0:T(8,128)(2,1)S(1)}, bf16[200,320]{1,0:T(8,128)(2,1)S(1)}, u32[]{:S(2)}, u32[]{:S(2)}) collective-permute-start(bf16[200,320]{1,0:T(8,128)(2,1)S(1)} %get-tuple-element.38), channel_id=1, source_target_pairs={{0,1},{1,0},{2,3},{3,2},{4,5},{5,4},{6,7},{7,6},{8,9},{9,8},{10,11... | collective-permute-start | bytes 384008 | tf_op jit(solution)/shard_map/ppermute | solution.py:258
  24.6 9.7 %collective-permute-start.8 = (bf16[200,320]{1,0:T(8,128)(2,1)S(1)}, bf16[200,320]{1,0:T(8,128)(2,1)S(1)}, u32[]{:S(2)}, u32[]{:S(2)}) collective-permute-start(bf16[200,320]{1,0:T(8,128)(2,1)S(1)} %add_convert_fusion.9), channel_id=1, source_target_pairs={{0,2},{1,3},{2,0},{3,1},{4,6},{5,7},{6,4},{7,5},{8,10},{9,11},{10,... | collective-permute-start | bytes 384008 | tf_op jit(solution)/shard_map/ppermute | solution.py:262
  27.4 9.6 %collective-permute-start.9 = (bf16[200,320]{1,0:T(8,128)(2,1)S(1)}, bf16[200,320]{1,0:T(8,128)(2,1)S(1)}, u32[]{:S(2)}, u32[]{:S(2)}) collective-permute-start(bf16[200,320]{1,0:T(8,128)(2,1)S(1)} %get-tuple-element.41), channel_id=1, source_target_pairs={{0,1},{1,0},{2,3},{3,2},{4,5},{5,4},{6,7},{7,6},{8,9},{9,8},{10,11... | collective-permute-start | bytes 384008 | tf_op jit(solution)/shard_map/ppermute | solution.py:258
  30.9 9.9 %copy-start.5 = (bf16[1,2,5,40,320]{4,3,2,1,0:T(8,128)(2,1)S(1)}, bf16[1,2,5,40,320]{4,3,2,1,0:T(8,128)(2,1)}, u32[]{:S(2)}) copy-start(bf16[1,2,5,40,320]{4,3,2,1,0:T(8,128)(2,1)} %param.11) | copy-start | bytes 768004
  34.2 13.9 %collective-permute-start.10 = (bf16[200,320]{1,0:T(8,128)(2,1)S(1)}, bf16[200,320]{1,0:T(8,128)(2,1)S(1)}, u32[]{:S(2)}, u32[]{:S(2)}) collective-permute-start(bf16[200,320]{1,0:T(8,128)(2,1)S(1)} %add_convert_fusion.8), channel_id=1, source_target_pairs={{0,2},{1,3},{2,0},{3,1},{4,6},{5,7},{6,4},{7,5},{8,10},{9,11},{10,... | collective-permute-start | bytes 384008 | tf_op jit(solution)/shard_map/ppermute | solution.py:262
  37.0 16.4 %collective-permute-start.12 = (bf16[200,320]{1,0:T(8,128)(2,1)S(1)}, bf16[200,320]{1,0:T(8,128)(2,1)S(1)}, u32[]{:S(2)}, u32[]{:S(2)}) collective-permute-start(bf16[200,320]{1,0:T(8,128)(2,1)S(1)} %add_convert_fusion.6), channel_id=1, source_target_pairs={{0,2},{1,3},{2,0},{3,1},{4,6},{5,7},{6,4},{7,5},{8,10},{9,11},{10,... | collective-permute-start | bytes 384008 | tf_op jit(solution)/shard_map/ppermute | solution.py:262
  40.1 21.5 %collective-permute-start.14 = (bf16[200,320]{1,0:T(8,128)(2,1)S(1)}, bf16[200,320]{1,0:T(8,128)(2,1)S(1)}, u32[]{:S(2)}, u32[]{:S(2)}) collective-permute-start(bf16[200,320]{1,0:T(8,128)(2,1)S(1)} %add_convert_fusion.7.m0), channel_id=1, source_target_pairs={{0,1},{1,0},{2,3},{3,2},{4,5},{5,4},{6,7},{7,6},{8,9},{9,8},{10,11... | collective-permute-start | bytes 384008 | tf_op jit(solution)/shard_map/ppermute | solution.py:266
  40.9 27.5 %collective-permute-start.18 = (bf16[2,200,320]{2,1,0:T(8,128)(2,1)S(1)}, bf16[2,200,320]{2,1,0:T(8,128)(2,1)S(1)}, u32[]{:S(2)}, u32[]{:S(2)}) collective-permute-start(bf16[2,200,320]{2,1,0:T(8,128)(2,1)S(1)} %bitcast.12), channel_id=1, source_target_pairs={{0,4},{4,0},{8,12},{12,8},{1,5},{5,1},{9,13},{13,9},{2,6},{6,2},{1... | collective-permute-start | bytes 768008 | tf_op jit(solution)/shard_map/ppermute | solution.py:270
  40.9 20.7 %collective-permute-start.19 = (bf16[2,200,320]{2,1,0:T(8,128)(2,1)S(1)}, bf16[2,200,320]{2,1,0:T(8,128)(2,1)S(1)}, u32[]{:S(2)}, u32[]{:S(2)}) collective-permute-start(bf16[2,200,320]{2,1,0:T(8,128)(2,1)S(1)} %bitcast.13), channel_id=1, source_target_pairs={{0,8},{4,12},{8,0},{12,4},{1,9},{5,13},{9,1},{13,5},{2,10},{6,14},... | collective-permute-start | bytes 768008 | tf_op jit(solution)/shard_map/ppermute | solution.py:271
  48.1 5.2 %collective-permute-start.11 = (bf16[200,320]{1,0:T(8,128)(2,1)S(1)}, bf16[200,320]{1,0:T(8,128)(2,1)S(1)}, u32[]{:S(2)}, u32[]{:S(2)}) collective-permute-start(bf16[200,320]{1,0:T(8,128)(2,1)S(1)} %get-tuple-element.44), channel_id=1, source_target_pairs={{0,1},{1,0},{2,3},{3,2},{4,5},{5,4},{6,7},{7,6},{8,9},{9,8},{10,11... | collective-permute-start | bytes 384008 | tf_op jit(solution)/shard_map/ppermute | solution.py:258
  53.3 8.2 %collective-permute-start.13 = (bf16[200,320]{1,0:T(8,128)(2,1)S(1)}, bf16[200,320]{1,0:T(8,128)(2,1)S(1)}, u32[]{:S(2)}, u32[]{:S(2)}) collective-permute-start(bf16[200,320]{1,0:T(8,128)(2,1)S(1)} %add_convert_fusion.4), channel_id=1, source_target_pairs={{0,2},{1,3},{2,0},{3,1},{4,6},{5,7},{6,4},{7,5},{8,10},{9,11},{10,... | collective-permute-start | bytes 384008 | tf_op jit(solution)/shard_map/ppermute | solution.py:262
  53.4 10.3 %collective-permute-start.15 = (bf16[200,320]{1,0:T(8,128)(2,1)S(1)}, bf16[200,320]{1,0:T(8,128)(2,1)S(1)}, u32[]{:S(2)}, u32[]{:S(2)}) collective-permute-start(bf16[200,320]{1,0:T(8,128)(2,1)S(1)} %add_convert_fusion.5.m1), channel_id=1, source_target_pairs={{0,1},{1,0},{2,3},{3,2},{4,5},{5,4},{6,7},{7,6},{8,9},{9,8},{10,11... | collective-permute-start | bytes 384008 | tf_op jit(solution)/shard_map/ppermute | solution.py:266
  61.6 6.8 %collective-permute-start.16 = (bf16[200,320]{1,0:T(8,128)(2,1)S(1)}, bf16[200,320]{1,0:T(8,128)(2,1)S(1)}, u32[]{:S(2)}, u32[]{:S(2)}) collective-permute-start(bf16[200,320]{1,0:T(8,128)(2,1)S(1)} %add_convert_fusion.3.m2), channel_id=1, source_target_pairs={{0,1},{1,0},{2,3},{3,2},{4,5},{5,4},{6,7},{7,6},{8,9},{9,8},{10,11... | collective-permute-start | bytes 384008 | tf_op jit(solution)/shard_map/ppermute | solution.py:266
  61.6 8.5 %collective-permute-start.20 = (bf16[2,200,320]{2,1,0:T(8,128)(2,1)S(1)}, bf16[2,200,320]{2,1,0:T(8,128)(2,1)S(1)}, u32[]{:S(2)}, u32[]{:S(2)}) collective-permute-start(bf16[2,200,320]{2,1,0:T(8,128)(2,1)S(1)} %collective-permute-done.19.c2), channel_id=1, source_target_pairs={{0,4},{4,0},{8,12},{12,8},{1,5},{5,1},{9,13},{13,9},{2,6},{6,2},{1... | collective-permute-start | bytes 768008 | tf_op jit(solution)/shard_map/ppermute | solution.py:272
  61.6 10.5 %copy-start = (bf16[3,320,320]{2,1,0:T(8,128)(2,1)S(1)}, bf16[3,320,320]{2,1,0:T(8,128)(2,1)}, u32[]{:S(2)}) copy-start(bf16[3,320,320]{2,1,0:T(8,128)(2,1)} %w_ref.3) | copy-start | bytes 1843204
  61.7 8.4 %collective-permute-start.17 = (bf16[200,320]{1,0:T(8,128)(2,1)S(1)}, bf16[200,320]{1,0:T(8,128)(2,1)S(1)}, u32[]{:S(2)}, u32[]{:S(2)}) collective-permute-start(bf16[200,320]{1,0:T(8,128)(2,1)S(1)} %add_convert_fusion.2.m3), channel_id=1, source_target_pairs={{0,1},{1,0},{2,3},{3,2},{4,5},{5,4},{6,7},{7,6},{8,9},{9,8},{10,11... | collective-permute-start | bytes 384008 | tf_op jit(solution)/shard_map/ppermute | solution.py:266
  73.7 3.3 %collective-permute-start.22 = (bf16[2,200,320]{2,1,0:T(8,128)(2,1)S(1)}, bf16[2,200,320]{2,1,0:T(8,128)(2,1)S(1)}, u32[]{:S(2)}, u32[]{:S(2)}) collective-permute-start(bf16[2,200,320]{2,1,0:T(8,128)(2,1)S(1)} %get-tuple-element.49), channel_id=1, source_target_pairs={{0,4},{4,0},{8,12},{12,8},{1,5},{5,1},{9,13},{13,9},{2,6},{6,2},{1... | collective-permute-start | bytes 768008 | tf_op jit(solution)/shard_map/ppermute | solution.py:285
  73.7 18.9 %collective-permute-start.24 = (bf16[3,320,320]{2,1,0:T(8,128)(2,1)S(1)}, bf16[3,320,320]{2,1,0:T(8,128)(2,1)S(1)}, u32[]{:S(2)}, u32[]{:S(2)}) collective-permute-start(bf16[3,320,320]{2,1,0:T(8,128)(2,1)S(1)} %temporal_grads.1), channel_id=1, source_target_pairs={{0,16},{16,0},{1,17},{17,1},{2,18},{18,2},{3,19},{19,3},{4,20},{20... | collective-permute-start | bytes 1843208 | tf_op jit(solution)/shard_map/ppermute | solution.py:278
  76.7 1.9 %collective-permute-start.21 = (bf16[2,200,320]{2,1,0:T(8,128)(2,1)S(1)}, bf16[2,200,320]{2,1,0:T(8,128)(2,1)S(1)}, u32[]{:S(2)}, u32[]{:S(2)}) collective-permute-start(bf16[2,200,320]{2,1,0:T(8,128)(2,1)S(1)} %get-tuple-element.52), channel_id=1, source_target_pairs={{0,4},{4,0},{8,12},{12,8},{1,5},{5,1},{9,13},{13,9},{2,6},{6,2},{1... | collective-permute-start | bytes 768008 | tf_op jit(solution)/shard_map/ppermute | solution.py:287
  77.0 9.6 %collective-permute-start.23 = (bf16[2,200,320]{2,1,0:T(8,128)(2,1)S(1)}, bf16[2,200,320]{2,1,0:T(8,128)(2,1)S(1)}, u32[]{:S(2)}, u32[]{:S(2)}) collective-permute-start(bf16[2,200,320]{2,1,0:T(8,128)(2,1)S(1)} %add_convert_fusion.1), channel_id=1, source_target_pairs={{0,8},{4,12},{8,0},{12,4},{1,9},{5,13},{9,1},{13,5},{2,10},{6,14},... | collective-permute-start | bytes 768008 | tf_op jit(solution)/shard_map/ppermute | solution.py:288
  (3 other events, 2.3 us)

commit v3 on v0

v3 whole, which is shorter than its diff:
```python
import functools

import jax
import jax.numpy as jnp
from jax import lax
from jax.experimental import pallas as pl
from jax.experimental.pallas import tpu as pltpu
from jax.sharding import PartitionSpec as P

CHANNELS = 1280
GROUPS = 32
GROUP_WIDTH = CHANNELS // GROUPS
EPSILON = 1e-05


def cost(microseconds):
    return pl.CostEstimate(flops=int(microseconds * 1.15e9), bytes_accessed=1, transcendentals=0)


f32 = jnp.float32
bf16 = jnp.bfloat16


def group_sum(rows):
    width = rows.shape[1]
    first = lax.broadcasted_iota(jnp.int32, (width, width), 0) // GROUP_WIDTH
    second = lax.broadcasted_iota(jnp.int32, (width, width), 1) // GROUP_WIDTH
    same = jnp.where(first == second, 1.0, 0.0).astype(f32)
    return jnp.dot(rows, same, precision=lax.Precision.HIGHEST, preferred_element_type=f32)


def vmem_spec():
    return pl.BlockSpec(memory_space=pltpu.VMEM)


def any_spec():
    return pl.BlockSpec(memory_space=pltpu.HBM)


def params(mebibytes):
    return pltpu.CompilerParams(vmem_limit_bytes=mebibytes * 1024 * 1024)


def stats_kernel(own_ref, core_ref, stats_ref, frames_ref):
    core = lax.axis_index("tm") % 2
    frames_ref[core] = own_ref[...]
    frames_ref[1 - core] = core_ref[...]
    width = frames_ref.shape[-1]
    values = [ref[...].astype(f32).reshape(-1, 8, width) for ref in (own_ref, core_ref)]
    mean, square = moments(jnp.concatenate(values, axis=0))
    stats_ref[0:8, :] = jnp.broadcast_to(mean, (8, width))
    stats_ref[8:16, :] = jnp.broadcast_to(square, (8, width))


def chip_stats(own, sibling):
    width = own.shape[-1]
    return pl.pallas_call(
        stats_kernel,
        out_shape=(
            jax.ShapeDtypeStruct((16, width), f32),
            jax.ShapeDtypeStruct((2,) + own.shape, bf16),
        ),
        in_specs=[vmem_spec()] * 2,
        out_specs=(vmem_spec(),) * 2,
        compiler_params=params(10),
        cost_estimate=cost(1.5),
        name="chip_stats",
    )(own, sibling)


def hold_kernel(w_ref, gain_ref, bias_ref, taps_ref, affine_ref, sem):
    copy = pltpu.make_async_copy(w_ref, taps_ref, sem)
    copy.start()
    width = gain_ref.shape[0]
    affine_ref[0:8, :] = jnp.broadcast_to(gain_ref[...].reshape(1, width), (8, width))
    affine_ref[8:16, :] = jnp.broadcast_to(bias_ref[...].reshape(1, width), (8, width))
    copy.wait()


def hold(taps, gain, bias):
    width = gain.shape[0]
    return pl.pallas_call(
        hold_kernel,
        out_shape=(
            jax.ShapeDtypeStruct(taps.shape, bf16),
            jax.ShapeDtypeStruct((16, width), f32),
        ),
        in_specs=[any_spec(), vmem_spec(), vmem_spec()],
        out_specs=(vmem_spec(),) * 2,
        scratch_shapes=[pltpu.SemaphoreType.DMA],
        compiler_params=params(4),
        cost_estimate=cost(1.0),
        name="hold_weights",
    )(taps, gain, bias)


def moments(values):
    count = values.shape[0] * 8 * GROUP_WIDTH
    mean = group_sum(values.sum(axis=0)).sum(axis=0, keepdims=True) / count
    centered = values - mean[None]
    square = group_sum((centered * centered).sum(axis=0)).sum(axis=0, keepdims=True)
    return mean, square


def held_half():
    z = lax.axis_index("mp")
    return (z + z // 2) % 2


def conv_kernel(x_ref, norm_ref, w_ref, keep_ref, send_ref, cols_ref):
    n, frames, rows, cols, width = x_ref.shape
    band = frames * cols
    odd = held_half()
    mean, scale = norm_ref[0:1, :], norm_ref[8:9, :]
    gain, bias = norm_ref[16:17, :], norm_ref[24:25, :]
    column = lax.broadcasted_iota(jnp.int32, (band, width), 0) % cols
    size = keep_ref.shape[0] // n
    for j in range(n):
        cols_ref[j, 0:band, :] = jnp.zeros((band, 3 * width), bf16)
        cols_ref[j, (rows + 1) * band :, :] = jnp.zeros((band, 3 * width), bf16)
        for row in range(rows):
            values = jnp.concatenate([x_ref[j, f, row].astype(f32) for f in range(frames)], axis=0)
            normed = (values - mean) * scale * gain + bias
            hidden = normed / (1.0 + jnp.exp(-normed))
            left = jnp.where(column == 0, 0.0, pltpu.roll(hidden, 1, 0))
            right = jnp.where(column == cols - 1, 0.0, pltpu.roll(hidden, band - 1, 0))
            line = [left.astype(bf16), hidden.astype(bf16), right.astype(bf16)]
            cols_ref[j, (row + 1) * band : (row + 2) * band, :] = jnp.concatenate(line, axis=1)
        total = None
        for tap in range(3):
            window = cols_ref[j, tap * band : (tap + rows) * band, :]
            term = jnp.dot(window, w_ref[tap], preferred_element_type=f32)
            total = term if total is None else total + term
        total = total.reshape(rows, frames, cols, total.shape[-1])
        half = frames // 2
        low = total[:, :half].reshape(size, -1)
        high = total[:, half:].reshape(size, -1)
        here = slice(j * size, (j + 1) * size)

        @pl.when(odd == 0)
        def _():
            keep_ref[here] = low
            send_ref[here] = high.astype(bf16)

        @pl.when(odd == 1)
        def _():
            keep_ref[here] = high
            send_ref[here] = low.astype(bf16)


def pair_conv(pairs, norm, taps, weight):
    n, frames, rows, cols, width = pairs.shape
    width_out = taps.shape[-1]
    count = n * frames * rows * cols // 2
    return pl.pallas_call(
        conv_kernel,
        out_shape=(
            jax.ShapeDtypeStruct((count, width_out), f32),
            jax.ShapeDtypeStruct((count, width_out), bf16),
        ),
        in_specs=[vmem_spec()] * 3,
        out_specs=(vmem_spec(),) * 2,
        scratch_shapes=[pltpu.VMEM((n, (rows + 2) * frames * cols, 3 * width), bf16)],
        compiler_params=params(20),
        cost_estimate=cost(weight),
        name="pair_conv",
    )(pairs, norm, taps)


PAD = 8

CLAIM = {
    "merge": 50.0,
    "conv0": 50.0,
    "collect": 0.01,
    "part": 0.01,
    "part0": 80.0,
    "conv1": 1.0,
    "mine": 50.0,
    "t1": 0.01,
    "g1": 0.01,
    "t2": 0.01,
    "g2": 50.0,
}


def pair_of(step):
    t = lax.axis_index("tm")
    return (t - t % 2, t - t % 2 + 1, jnp.bitwise_xor(t, 2), jnp.bitwise_xor(t, 3))[step]


def zero_frames(ref, lead, count, rows, width):
    ref[lead + (0,)] = jnp.zeros((rows, width), bf16)
    ref[lead + (count - 1,)] = jnp.zeros((rows, width), bf16)
    for f in range(1, count - 1):
        ref[lead + (f, slice(rows - PAD, rows))] = jnp.zeros((PAD, width), bf16)


def put_pairs(ref, lead, steps, pieces):
    odd = held_half()
    count = ref.shape[-2] - PAD
    steps = list(steps)
    for mine, other in zip(pieces[::2], pieces[1::2], strict=True):
        for j in range(mine.shape[0] // count):
            at = 1 + 2 * pair_of(steps.pop(0))
            ref[lead + (at + odd, slice(0, count))] = mine[j * count : (j + 1) * count]
            ref[lead + (at + 1 - odd, slice(0, count))] = other[j * count : (j + 1) * count]


def grad_kernel(steps, held, *refs):
    clips = refs[0].shape[0]
    cots, refs = refs[:4], refs[4:]
    *start, out_ref, s_ref, c_ref = refs[held * clips :]
    pieces = refs[: held * clips]
    t = lax.axis_index("tm")
    own = lax.axis_index("dp") if clips > 1 else 0
    frames, rows, width = s_ref.shape[1:]
    for clip in range(clips):
        at = own if clip == 0 else 1 - own
        zero_frames(s_ref, (at,), frames, rows, width)
        zero_frames(c_ref, (at,), frames, rows, c_ref.shape[-1])
        put_pairs(s_ref, (at,), steps, pieces[clip * held : (clip + 1) * held])
        for block, cot in enumerate(cots):
            first = 1 + 2 * jnp.bitwise_xor(t, block)
            for f in range(2):
                c_ref[at, first + f, 0 : rows - PAD] = cot[clip, f]
    chip = t // 2 if steps[0] == 0 else 1 - t // 2
    first, length = 1 + 4 * chip, 4
    turned = [
        s_ref[clip, pl.ds(first, length)].reshape(length * rows, width).T for clip in range(clips)
    ]
    for k in range(3):
        total = start[0][k] if start else None
        for clip in range(clips):
            cot = c_ref[clip, pl.ds(first + 1 - k, length)].reshape(length * rows, -1)
            term = jnp.dot(turned[clip], cot, preferred_element_type=f32)
            total = term if total is None else total + term
        out_ref[k] = total.astype(out_ref.dtype)


def temporal_grads(steps, cots, pieces, start, dtype, weight):
    clips, _, count, width_out = cots[0].shape
    width = pieces[0][0].shape[-1]
    held = len(pieces[0])
    operands = (*cots, *(p for clip in pieces for p in clip), *start)
    return pl.pallas_call(
        functools.partial(grad_kernel, steps, held),
        out_shape=jax.ShapeDtypeStruct((3, width, width_out), dtype),
        in_specs=[vmem_spec()] * len(operands),
        out_specs=vmem_spec(),
        scratch_shapes=[
            pltpu.VMEM((clips, 10, count + PAD, width), bf16),
            pltpu.VMEM((clips, 10, count + PAD, width_out), bf16),
        ],
        compiler_params=params(20),
        cost_estimate=cost(weight),
        name="temporal_grads",
    )(*operands)


def temporal_kernel(steps, blocks, *refs):
    *pieces, w_ref, send_ref, keep_ref, s_ref = refs
    frames, rows, width = s_ref.shape
    zero_frames(s_ref, (), frames, rows, width)
    put_pairs(s_ref, (), steps, pieces)
    for i, out in zip(blocks, (send_ref, keep_ref), strict=True):
        first = 2 * jnp.bitwise_xor(lax.axis_index("tm"), i)
        total = None
        for k in range(3):
            window = s_ref[pl.ds(first + k, 2)].reshape(2 * rows, width)
            term = jnp.dot(window, w_ref[k], preferred_element_type=f32)
            total = term if total is None else total + term
        total = total.reshape(2, rows, -1)[:, : rows - PAD]
        out[...] = total.astype(out.dtype)


def temporal_conv(steps, blocks, count, pieces, taps, weight):
    width, width_out = taps.shape[1:]
    return pl.pallas_call(
        functools.partial(temporal_kernel, steps, blocks),
        out_shape=(
            jax.ShapeDtypeStruct((2, count, width_out), bf16),
            jax.ShapeDtypeStruct((2, count, width_out), f32),
        ),
        in_specs=[vmem_spec()] * (len(pieces) + 1),
        out_specs=(vmem_spec(), vmem_spec()),
        scratch_shapes=[pltpu.VMEM((10, count + PAD, width), bf16)],
        compiler_params=params(16),
        cost_estimate=cost(weight),
        name="temporal_conv",
    )(*pieces, taps)


def xor(axis_size, bit):
    return [(i, i ^ bit) for i in range(axis_size)]


def add_kernel(a_ref, b_ref, out_ref):
    out_ref[...] = (a_ref[...].astype(f32) + b_ref[...].astype(f32)).astype(bf16)


def add16(a, b, weight):
    return pl.pallas_call(
        add_kernel,
        out_shape=jax.ShapeDtypeStruct(a.shape, bf16),
        in_specs=[vmem_spec()] * 2,
        out_specs=vmem_spec(),
        compiler_params=params(4),
        cost_estimate=cost(weight),
        name="add_parts",
    )(a, b)


def merge_kernel(s0_ref, s1_ref, affine_ref, out_ref, *, count):
    first, second = s0_ref[0:8, :], s1_ref[0:8, :]
    mean = (first + second) * 0.5
    square = s0_ref[8:16, :] + s1_ref[8:16, :]
    square = square + count * ((first - mean) * (first - mean) + (second - mean) * (second - mean))
    out_ref[0:8, :] = mean
    out_ref[8:16, :] = lax.rsqrt(square / (2.0 * count) + EPSILON)
    out_ref[16:32, :] = affine_ref[...]


def merge_stats(st_own, st_chip, affine, count, weight):
    return pl.pallas_call(
        functools.partial(merge_kernel, count=count),
        out_shape=jax.ShapeDtypeStruct((32, st_own.shape[1]), f32),
        in_specs=[vmem_spec()] * 3,
        out_specs=vmem_spec(),
        compiler_params=params(4),
        cost_estimate=cost(weight),
        name="merge_stats",
    )(st_own, st_chip, affine)


def collect_kernel(a_ref, b_ref, out_ref):
    out_ref[0] = a_ref[...]
    out_ref[1] = b_ref[...]


def collect(a, b, weight):
    return pl.pallas_call(
        collect_kernel,
        out_shape=jax.ShapeDtypeStruct((2,) + a.shape, a.dtype),
        in_specs=[vmem_spec()] * 2,
        out_specs=vmem_spec(),
        compiler_params=params(6),
        cost_estimate=cost(weight),
        name="collect_pairs",
    )(a, b)


def tie(x, *others):
    return lax.optimization_barrier((x,) + others)[0]


def body(activations, norm_gain, norm_bias, spatial_weight, temporal_weight, cotangent):
    own = activations[0]
    frames, rows, cols, width = own.shape
    width_out = spatial_weight.shape[2]
    core, chip = xor(4, 1), xor(4, 2)
    near, across = xor(4, 1), xor(4, 3)
    count = rows * cols
    clips = lax.axis_size("dp")
    sibling = lax.ppermute(own, "tm", core)
    st_own, pairs = chip_stats(own, sibling)
    st_chip = lax.ppermute(st_own, "tm", chip)
    taps, affine = hold(spatial_weight.reshape(3, 3 * width, width_out), norm_gain, norm_bias)
    raw_chip = lax.ppermute(tie(own, affine), "tm", chip)
    norm = merge_stats(st_own, st_chip, affine, 2 * frames * count * GROUP_WIDTH, CLAIM["merge"])

    keep0, send0 = pair_conv(pairs, norm, taps, CLAIM["conv0"])
    got0 = lax.ppermute(send0, "mp", near)
    raw_chip = tie(raw_chip, keep0)
    raw_both = lax.ppermute(raw_chip, "tm", core)
    far_pairs = collect(raw_chip, raw_both, CLAIM["collect"])
    part0 = add16(keep0, got0, CLAIM["part0"])
    came0 = lax.ppermute(part0, "mp", across)
    keep1, send1 = pair_conv(tie(far_pairs, part0), norm, taps, CLAIM["conv1"])
    got1 = lax.ppermute(send1, "mp", near)
    mine0 = add16(tie(part0, keep1), came0, CLAIM["mine"])
    part1 = add16(tie(keep1, mine0), got1, CLAIM["part"])
    came1 = lax.ppermute(part1, "mp", across)
    other0 = lax.ppermute(mine0, "mp", near)
    cot = cotangent.reshape(1, frames, count, width)
    cot_core = lax.ppermute(tie(cot, mine0), "tm", core)
    cot_chip = lax.ppermute(tie(cot, mine0), "tm", chip)
    mine1 = add16(tie(part1, mine0), came1, CLAIM["mine"])
    other1 = lax.ppermute(mine1, "mp", near)
    cot_both = lax.ppermute(tie(cot_chip, mine1), "tm", core)
    cots = (cot, cot_core, cot_chip, cot_both)

    steps = (0, 1, 2, 3)
    held = [tie(mine0, mine1), other0]
    grad = temporal_grads((0, 1), cots, [held], (), f32, CLAIM["g1"])
    sent = temporal_grads((2, 3), cots, [[mine1, other1]], (grad,), bf16 if clips == 2 else f32, CLAIM["g2"])
    pieces = [tie(mine0, sent), other0, mine1, other1]
    send, keep_chip = temporal_conv(steps, (3, 2), count, pieces, temporal_weight, CLAIM["t1"])
    far_part = lax.ppermute(send, "tm", core)
    later = [tie(mine0, keep_chip)] + pieces[1:]
    send, keep_own = temporal_conv(steps, (1, 0), count, later, temporal_weight, CLAIM["t2"])
    near_part = lax.ppermute(send, "tm", core)
    to_chip = add16(tie(keep_chip, keep_own), far_part, CLAIM["part"])
    from_chip = lax.ppermute(to_chip, "tm", chip)
    block = (keep_own + near_part.astype(f32) + from_chip.astype(f32)).astype(bf16)
    if clips == 2:
        theirs = lax.ppermute(sent, "dp", [(0, 1), (1, 0)])
        temporal_grad = (sent.astype(f32) + theirs.astype(f32)) / clips
    else:
        temporal_grad = lax.psum(sent, "dp") / clips
    return block.reshape(activations.shape), temporal_grad


def solution(mesh):
    in_specs = (
        P("dp", "tm", None, None, "mp"),
        P("mp"),
        P("mp"),
        P(None, "mp", "tm"),
        P(None, "tm", "mp"),
        P("dp", "tm", None, None, "mp"),
    )
    out_specs = (P("dp", "tm", None, None, "mp"), P(None, "tm", "mp"))
    return jax.shard_map(body, mesh=mesh, in_specs=in_specs, out_specs=out_specs, check_vma=False)
```

time: 210 us -> 84.8 us (0.40)
  waiting for transfers between devices: 116 us -> 46.5 us
  blocking collectives: 48 us -> 0 us
  starting transfers between devices: 0.12 us -> 19.6 us
  Pallas kernels: 0 us -> 15.6 us
  between operations: 14 us -> 0.79 us
  matrix products: 12 us -> 0 us
  local copies, waits for them, and re-layouts: 9.87 us -> 0.03 us
  other arithmetic: 9.39 us -> 2.13 us
    reduce_scatter x2 -> x0, waiting for transfers between devices: 72.2 us -> none  [the longest x1 38.5 us: body(): lax.psum_scatter(summed.reshape(lax.axis_size('mp') * (frames_all // mp_c...]
    all_gather x3 -> x0, blocking collectives: 48 us -> none  [the longest x1 24.2 us: body(): spatial_all = lax.all_gather(spatial_out, 'mp', axis=0, tiled=True)]
    ppermute x0 -> x17, waiting for transfers between devices: none -> 46.5 us  [the longest x1 8.24 us: body(): from_chip = lax.ppermute(to_chip, 'tm', chip)]
    psum x1 -> x0, waiting for transfers between devices: 43.8 us -> none  [body(): temporal_grad = lax.psum(jnp.stack(tap_grads), 'dp') / clip_count]
    ppermute x0 -> x17, starting transfers between devices: none -> 19.6 us  [the longest x1 3.8 us: body(): came0 = lax.ppermute(part0, 'mp', across)]
    pallas_call x0 -> x15, Pallas kernels: none -> 15.6 us  [the longest x2 7.18 us: pair_conv(): pl.pallas_call(conv_kernel, out_shape=(jax.ShapeDtypeStruct((count, width...]
    dot_general x15 -> x0, matrix products: 12 us -> none  [the longest x9 7.22 us: body(): jnp.dot(spatial_window, spatial_weight[spatial_tap_index], preferred_elem...]
    add x2 -> x0, local copies, waits for them, and re-layouts: 4.2 us -> none  [the longest x1 2.1 us: body(): summed + jnp.dot(spatial_window, spatial_weight[spatial_tap_index], prefe...]
  transfers between devices with their start and end apart: 3 -> 17, of which waited for: 3 -> 13; matrix products, arithmetic and copies ran while one was open for 3% -> 1% of each run, Pallas kernels for 0% -> 13%
where the time goes in v3:
time: 84.8 us; the launch traced here: 84.7 us
  waiting for transfers between devices  46.5 us (55%)
  starting transfers between devices  19.6 us (23%)
  Pallas kernels  15.6 us (18%)
  other arithmetic  2.13 us (3%)
    ppermute x1, waiting for transfers between devices, body(): from_chip = lax.ppermute(to_chip, 'tm', chip)  8.24 us
    ppermute x1, waiting for transfers between devices, body(): came1 = lax.ppermute(part1, 'mp', across)  7.73 us
    pallas_call x2, Pallas kernels, pair_conv(): pl.pallas_call(conv_kernel, out_shape=(jax.ShapeDtypeStruct((count, width...  7.18 us
    ppermute x1, waiting for transfers between devices, body(): other1 = lax.ppermute(mine1, 'mp', near)  5.25 us
    ppermute x1, waiting for transfers between devices, body(): theirs = lax.ppermute(sent, 'dp', [(0, 1), (1, 0)])  5.24 us
    ppermute x1, waiting for transfers between devices, body(): got1 = lax.ppermute(send1, 'mp', near)  4.57 us
    ppermute x1, waiting for transfers between devices, body(): got0 = lax.ppermute(send0, 'mp', near)  4.3 us
    ppermute x1, waiting for transfers between devices, body(): came0 = lax.ppermute(part0, 'mp', across)  4.22 us
  transfers between devices with their start and end apart: 17, of which 13 were waited for; matrix products, arithmetic and copies ran while one was open for 1% of the time, Pallas kernels for 13%

profile of v3, /device:TPU:0, one launch (start us, length us, event | category | flops | bytes accessed | tf_op | source)
XLA Modules:
  0.0 84.7 jit_solution(7378653358816568600)
XLA Ops:
  0.7 0.5 collective-permute-start
  1.2 1.4 %collective-permute-done.core_ref = bf16[2,5,40,320]{3,2,1,0:T(8,128)(2,1)S(1)} collective-permute-done((bf16[2,5,40,320]{3,2,1,0:T(8,128)(2,1)}, bf16[2,5,40,320]{3,2,1,0:T(8,128)(2,1)S(1)}, u32[]{:S(2)}, u32[]{:S(2)}) %collective-permute-start) | collective-permute-done | bytes 256032 | tf_op jit(solution)/shard_map/ppermute | solution.py:365
  2.6 2.1 %chip_stats.1 = (f32[16,320]{1,0:T(8,128)S(1)}, bf16[2,2,5,40,320]{4,3,2,1,0:T(8,128)(2,1)S(1)}) custom-call(bf16[2,5,40,320]{3,2,1,0:T(8,128)(2,1)} %bitcast.own_ref, bf16[2,5,40,320]{3,2,1,0:T(8,128)(2,1)S(1)} %collective-permute-done.core_ref), custom_call_target="tpu_custom_call" | custom-call | flops 1724999936 | bytes 1 | tf_op jit(solution)/shard_map/chip_stats/pallas_call | solution.py:57
  4.7 2.9 %collective-permute-start.1 = (f32[16,320]{1,0:T(8,128)S(1)}, f32[16,320]{1,0:T(8,128)S(1)}, u32[]{:S(2)}, u32[]{:S(2)}) collective-permute-start(f32[16,320]{1,0:T(8,128)S(1)} %get-tuple-element.27.s0_ref), channel_id=1, source_target_pairs={{0,8},{4,12},{8,0},{12,4},{1,9},{5,13},{9,1},{13,5},{2,10},{6,14},... | collective-permute-start | bytes 61448 | tf_op jit(solution)/shard_map/ppermute | solution.py:367
  7.6 0.3 hold_weights.1
  8.0 1.4 %collective-permute-done.1.s1_ref = f32[16,320]{1,0:T(8,128)S(1)} collective-permute-done((f32[16,320]{1,0:T(8,128)S(1)}, f32[16,320]{1,0:T(8,128)S(1)}, u32[]{:S(2)}, u32[]{:S(2)}) %collective-permute-start.1) | collective-permute-done | bytes 20512 | tf_op jit(solution)/shard_map/ppermute | solution.py:367
  9.4 3.5 %pair_conv.2 = (f32[400,320]{1,0:T(8,128)S(1)}, bf16[400,320]{1,0:T(8,128)(2,1)S(1)}) custom-call(bf16[2,2,5,40,320]{4,3,2,1,0:T(8,128)(2,1)S(1)} %get-tuple-element.26.x_ref, f32[32,320]{1,0:T(8,128)S(1)} %merge_stats.1.norm_ref, bf16[3,960,320]{2,1,0:T(8,128)(2,1)S(1)} %get-tuple-element.29.w_ref), custom_call_target="tpu_custom_call" | custom-call | flops 57500000256 | bytes 1 | tf_op jit(solution)/shard_map/pair_conv/pallas_call | solution.py:155
  12.9 2.2 %collective-permute-start.2 = (bf16[400,320]{1,0:T(8,128)(2,1)S(1)}, bf16[400,320]{1,0:T(8,128)(2,1)S(1)}, u32[]{:S(2)}, u32[]{:S(2)}) collective-permute-start(bf16[400,320]{1,0:T(8,128)(2,1)S(1)} %get-tuple-element.31), channel_id=1, source_target_pairs={{0,1},{1,0},{2,3},{3,2},{4,5},{5,4},{6,7},{7,6},{8,9},{9,8},{10,11... | collective-permute-start | bytes 768008 | tf_op jit(solution)/shard_map/ppermute | solution.py:373
  15.1 2.1 %collective-permute-done.3.a_ref = bf16[2,5,40,320]{3,2,1,0:T(8,128)(2,1)S(1)} collective-permute-done((bf16[2,5,40,320]{3,2,1,0:T(8,128)(2,1)}, bf16[2,5,40,320]{3,2,1,0:T(8,128)(2,1)S(1)}, u32[]{:S(2)}, u32[]{:S(2)}) %collective-permute-start.3) | collective-permute-done | bytes 256032 | tf_op jit(solution)/shard_map/ppermute | solution.py:369
  17.2 4.3 %collective-permute-done.2.b_ref = bf16[400,320]{1,0:T(8,128)(2,1)S(1)} collective-permute-done((bf16[400,320]{1,0:T(8,128)(2,1)S(1)}, bf16[400,320]{1,0:T(8,128)(2,1)S(1)}, u32[]{:S(2)}, u32[]{:S(2)}) %collective-permute-start.2) | collective-permute-done | bytes 256032 | tf_op jit(solution)/shard_map/ppermute | solution.py:373
  21.6 3.8 %collective-permute-start.5 = (bf16[400,320]{1,0:T(8,128)(2,1)S(1)}, bf16[400,320]{1,0:T(8,128)(2,1)S(1)}, u32[]{:S(2)}, u32[]{:S(2)}) collective-permute-start(bf16[400,320]{1,0:T(8,128)(2,1)S(1)} %add_parts.5.a_ref), channel_id=1, source_target_pairs={{0,3},{1,2},{2,1},{3,0},{4,7},{5,6},{6,5},{7,4},{8,11},{9,10},{10,... | collective-permute-start | bytes 768008 | tf_op jit(solution)/shard_map/ppermute | solution.py:378
  25.5 3.7 %pair_conv.3 = (f32[400,320]{1,0:T(8,128)S(1)}, bf16[400,320]{1,0:T(8,128)(2,1)S(1)}) custom-call(bf16[2,2,5,40,320]{4,3,2,1,0:T(8,128)(2,1)S(1)} %collect_pairs.1.x_ref, f32[32,320]{1,0:T(8,128)S(1)} %merge_stats.1.norm_ref, bf16[3,960,320]{2,1,0:T(8,128)(2,1)S(1)} %get-tuple-element.29.w_ref), custom_call_target="tpu_custom_call" | custom-call | flops 1150000000 | bytes 1 | tf_op jit(solution)/shard_map/pair_conv/pallas_call | solution.py:155
  29.3 4.2 %collective-permute-done.5.b_ref = bf16[400,320]{1,0:T(8,128)(2,1)S(1)} collective-permute-done((bf16[400,320]{1,0:T(8,128)(2,1)S(1)}, bf16[400,320]{1,0:T(8,128)(2,1)S(1)}, u32[]{:S(2)}, u32[]{:S(2)}) %collective-permute-start.5) | collective-permute-done | bytes 256032 | tf_op jit(solution)/shard_map/ppermute | solution.py:378
  33.6 4.6 %collective-permute-done.8.b_ref = bf16[400,320]{1,0:T(8,128)(2,1)S(1)} collective-permute-done((bf16[400,320]{1,0:T(8,128)(2,1)S(1)}, bf16[400,320]{1,0:T(8,128)(2,1)S(1)}, u32[]{:S(2)}, u32[]{:S(2)}) %collective-permute-start.8) | collective-permute-done | bytes 256032 | tf_op jit(solution)/shard_map/ppermute | solution.py:380
  38.2 3.1 %collective-permute-start.9 = (bf16[400,320]{1,0:T(8,128)(2,1)S(1)}, bf16[400,320]{1,0:T(8,128)(2,1)S(1)}, u32[]{:S(2)}, u32[]{:S(2)}) collective-permute-start(bf16[400,320]{1,0:T(8,128)(2,1)S(1)} %add_parts.7.a_ref), channel_id=1, source_target_pairs={{0,3},{1,2},{2,1},{3,0},{4,7},{5,6},{6,5},{7,4},{8,11},{9,10},{10,... | collective-permute-start | bytes 768008 | tf_op jit(solution)/shard_map/ppermute | solution.py:383
  41.3 1.3 %collective-permute-start.7 = (bf16[1,2,200,320]{3,2,1,0:T(8,128)(2,1)S(1)}, bf16[1,2,200,320]{3,2,1,0:T(8,128)(2,1)S(1)}, u32[]{:S(2)}, u32[]{:S(2)}) collective-permute-start(bf16[1,2,200,320]{3,2,1,0:T(8,128)(2,1)S(1)} %bitcast.5), channel_id=1, source_target_pairs={{0,8},{4,12},{8,0},{12,4},{1,9},{5,13},{9,1},{13,5},{2,10},{6,14},... | collective-permute-start | bytes 768008 | tf_op jit(solution)/shard_map/ppermute | solution.py:387
  42.5 7.7 %collective-permute-done.9.b_ref = bf16[400,320]{1,0:T(8,128)(2,1)S(1)} collective-permute-done((bf16[400,320]{1,0:T(8,128)(2,1)S(1)}, bf16[400,320]{1,0:T(8,128)(2,1)S(1)}, u32[]{:S(2)}, u32[]{:S(2)}) %collective-permute-start.9) | collective-permute-done | bytes 256032 | tf_op jit(solution)/shard_map/ppermute | solution.py:383
  50.4 0.6 collective-permute-done.7.refs_2_
  51.0 2.7 %collective-permute-start.11 = (bf16[400,320]{1,0:T(8,128)(2,1)S(1)}, bf16[400,320]{1,0:T(8,128)(2,1)S(1)}, u32[]{:S(2)}, u32[]{:S(2)}) collective-permute-start(bf16[400,320]{1,0:T(8,128)(2,1)S(1)} %add_parts.8.refs_4_.refs_2_), channel_id=1, source_target_pairs={{0,1},{1,0},{2,3},{3,2},{4,5},{5,4},{6,7},{7,6},{8,9},{9,8},{10,11... | collective-permute-start | bytes 768008 | tf_op jit(solution)/shard_map/ppermute | solution.py:389
  53.7 1.2 %collective-permute-done.12.refs_5_.refs_1_ = bf16[400,320]{1,0:T(8,128)(2,1)S(1)} collective-permute-done((bf16[400,320]{1,0:T(8,128)(2,1)S(1)}, bf16[400,320]{1,0:T(8,128)(2,1)S(1)}, u32[]{:S(2)}, u32[]{:S(2)}) %collective-permute-start.12) | collective-permute-done | bytes 256032 | tf_op jit(solution)/shard_map/ppermute | solution.py:384
  54.9 1.4 %temporal_grads.2.refs_6_ = f32[3,320,320]{2,1,0:T(8,128)S(1)} custom-call(bf16[1,2,200,320]{3,2,1,0:T(8,128)(2,1)S(1)} %bitcast.6, bf16[1,2,200,320]{3,2,1,0:T(8,128)(2,1)S(1)} %collective-permute-done.6.refs_1_, bf16[1,2,200,320]{3,2,1,0:T(8,128)(2,1)S(1)} %collective-permute-done.7.refs_2_, bf16[1,2,200,320]{3,2,1,0:T(8,128)(2,1)S(1)} %collective-permute-done.10.refs_3_, ...), custom_call_target="tpu_custom_call" | custom-call | flops 11500000 | bytes 1 | tf_op jit(solution)/shard_map/temporal_grads/pallas_call | solution.py:246
  56.3 5.3 %collective-permute-done.11.refs_5_.refs_3_ = bf16[400,320]{1,0:T(8,128)(2,1)S(1)} collective-permute-done((bf16[400,320]{1,0:T(8,128)(2,1)S(1)}, bf16[400,320]{1,0:T(8,128)(2,1)S(1)}, u32[]{:S(2)}, u32[]{:S(2)}) %collective-permute-start.11) | collective-permute-done | bytes 256032 | tf_op jit(solution)/shard_map/ppermute | solution.py:389
  61.6 1.4 %temporal_grads.3 = bf16[3,320,320]{2,1,0:T(8,128)(2,1)S(1)} custom-call(bf16[1,2,200,320]{3,2,1,0:T(8,128)(2,1)S(1)} %bitcast.7, bf16[1,2,200,320]{3,2,1,0:T(8,128)(2,1)S(1)} %collective-permute-done.6.refs_1_, bf16[1,2,200,320]{3,2,1,0:T(8,128)(2,1)S(1)} %collective-permute-done.7.refs_2_, bf16[1,2,200,320]{3,2,1,0:T(8,128)(2,1)S(1)} %collective-permute-done.10.refs_3_, ...), custom_call_target="tpu_custom_call" | custom-call | flops 57500000256 | bytes 1 | tf_op jit(solution)/shard_map/temporal_grads/pallas_call | solution.py:246
  63.0 1.4 %temporal_conv.2 = (bf16[2,200,320]{2,1,0:T(8,128)(2,1)S(1)}, f32[2,200,320]{2,1,0:T(8,128)S(1)}) custom-call(bf16[400,320]{1,0:T(8,128)(2,1)S(1)} %add_parts.6.refs_4_.refs_0_, bf16[400,320]{1,0:T(8,128)(2,1)S(1)} %collective-permute-done.12.refs_5_.refs_1_, bf16[400,320]{1,0:T(8,128)(2,1)S(1)} %add_parts.8.refs_4_.refs_2_, ...), custom_call_target="tpu_custom_call" | custom-call | flops 11500000 | bytes 1 | tf_op jit(solution)/shard_map/temporal_conv/pallas_call | solution.py:279
  64.5 1.5 %collective-permute-start.16 = (bf16[3,320,320]{2,1,0:T(8,128)(2,1)S(1)}, bf16[3,320,320]{2,1,0:T(8,128)(2,1)S(1)}, u32[]{:S(2)}, u32[]{:S(2)}) collective-permute-start(bf16[3,320,320]{2,1,0:T(8,128)(2,1)S(1)} %temporal_grads.3), channel_id=1, source_target_pairs={{0,16},{16,0},{1,17},{17,1},{2,18},{18,2},{3,19},{19,3},{4,20},{20... | collective-permute-start | bytes 1843208 | tf_op jit(solution)/shard_map/ppermute | solution.py:407
  66.0 1.4 %temporal_conv.3 = (bf16[2,200,320]{2,1,0:T(8,128)(2,1)S(1)}, f32[2,200,320]{2,1,0:T(8,128)S(1)}) custom-call(bf16[400,320]{1,0:T(8,128)(2,1)S(1)} %add_parts.6.refs_4_.refs_0_, bf16[400,320]{1,0:T(8,128)(2,1)S(1)} %collective-permute-done.12.refs_5_.refs_1_, bf16[400,320]{1,0:T(8,128)(2,1)S(1)} %add_parts.8.refs_4_.refs_2_, ...), custom_call_target="tpu_custom_call" | custom-call | flops 11500000 | bytes 1 | tf_op jit(solution)/shard_map/temporal_conv/pallas_call | solution.py:279
  67.4 0.2 collective-permute-start.13
  67.7 1.2 %collective-permute-start.15 = (bf16[2,200,320]{2,1,0:T(8,128)(2,1)S(1)}, bf16[2,200,320]{2,1,0:T(8,128)(2,1)S(1)}, u32[]{:S(2)}, u32[]{:S(2)}) collective-permute-start(bf16[2,200,320]{2,1,0:T(8,128)(2,1)S(1)} %add_parts.9), channel_id=1, source_target_pairs={{0,8},{4,12},{8,0},{12,4},{1,9},{5,13},{9,1},{13,5},{2,10},{6,14},... | collective-permute-start | bytes 768008 | tf_op jit(solution)/shard_map/ppermute | solution.py:404
  69.1 8.2 %collective-permute-done.15 = bf16[2,200,320]{2,1,0:T(8,128)(2,1)S(1)} collective-permute-done((bf16[2,200,320]{2,1,0:T(8,128)(2,1)S(1)}, bf16[2,200,320]{2,1,0:T(8,128)(2,1)S(1)}, u32[]{:S(2)}, u32[]{:S(2)}) %collective-permute-start.15) | collective-permute-done | bytes 256032 | tf_op jit(solution)/shard_map/ppermute | solution.py:404
  77.3 0.8 add_convert_fusion
  78.1 5.2 %collective-permute-done.16 = bf16[3,320,320]{2,1,0:T(8,128)(2,1)S(1)} collective-permute-done((bf16[3,320,320]{2,1,0:T(8,128)(2,1)S(1)}, bf16[3,320,320]{2,1,0:T(8,128)(2,1)S(1)}, u32[]{:S(2)}, u32[]{:S(2)}) %collective-permute-start.16) | collective-permute-done | bytes 614432 | tf_op jit(solution)/shard_map/ppermute | solution.py:407
  83.4 1.3 %add_multiply_fusion = f32[3,320,320]{2,1,0:T(8,128)} fusion(bf16[3,320,320]{2,1,0:T(8,128)(2,1)S(1)} %collective-permute-done.16, bf16[3,320,320]{2,1,0:T(8,128)(2,1)S(1)} %temporal_grads.3), kind=kLoop, calls=%fused_computation | loop fusion | flops 1228800 | bytes 2457600 | tf_op jit(solution)/shard_map/div | solution.py:408
  (29 shorter events, 0.9 us)
Async XLA Ops:
  0.6 7.0 %copy-start.2 = (bf16[9,320,320]{2,1,0:T(8,128)(2,1)S(1)}, bf16[9,320,320]{2,1,0:T(8,128)(2,1)}, u32[]{:S(2)}) copy-start(bf16[9,320,320]{2,1,0:T(8,128)(2,1)} %param.9) | copy-start | bytes 5529604
  0.6 7.0 %copy-start.3 = (f32[320]{0:T(512)S(1)}, f32[320]{0:T(512)}, u32[]{:S(2)}) copy-start(f32[320]{0:T(512)} %gain_ref.1) | copy-start | bytes 3844
  0.7 7.0 %copy-start.4 = (f32[320]{0:T(512)S(1)}, f32[320]{0:T(512)}, u32[]{:S(2)}) copy-start(f32[320]{0:T(512)} %bias_ref.1) | copy-start | bytes 3844
  0.7 2.0 %collective-permute-start = (bf16[2,5,40,320]{3,2,1,0:T(8,128)(2,1)}, bf16[2,5,40,320]{3,2,1,0:T(8,128)(2,1)S(1)}, u32[]{:S(2)}, u32[]{:S(2)}) collective-permute-start(bf16[2,5,40,320]{3,2,1,0:T(8,128)(2,1)} %bitcast.own_ref), channel_id=1, source_target_pairs={{0,4},{4,0},{8,12},{12,8},{1,5},{5,1},{9,13},{13,9},{2,6},{6,2},{1... | collective-permute-start | bytes 768008 | tf_op jit(solution)/shard_map/ppermute | solution.py:365
  4.7 4.7 %collective-permute-start.1 = (f32[16,320]{1,0:T(8,128)S(1)}, f32[16,320]{1,0:T(8,128)S(1)}, u32[]{:S(2)}, u32[]{:S(2)}) collective-permute-start(f32[16,320]{1,0:T(8,128)S(1)} %get-tuple-element.27.s0_ref), channel_id=1, source_target_pairs={{0,8},{4,12},{8,0},{12,4},{1,9},{5,13},{9,1},{13,5},{2,10},{6,14},... | collective-permute-start | bytes 61448 | tf_op jit(solution)/shard_map/ppermute | solution.py:367
  7.9 9.3 %collective-permute-start.3 = (bf16[2,5,40,320]{3,2,1,0:T(8,128)(2,1)}, bf16[2,5,40,320]{3,2,1,0:T(8,128)(2,1)S(1)}, u32[]{:S(2)}, u32[]{:S(2)}) collective-permute-start(bf16[2,5,40,320]{3,2,1,0:T(8,128)(2,1)} %bitcast.own_ref), channel_id=1, source_target_pairs={{0,8},{4,12},{8,0},{12,4},{1,9},{5,13},{9,1},{13,5},{2,10},{6,14},... | collective-permute-start | bytes 768008 | tf_op jit(solution)/shard_map/ppermute | solution.py:369
  12.9 8.6 %collective-permute-start.2 = (bf16[400,320]{1,0:T(8,128)(2,1)S(1)}, bf16[400,320]{1,0:T(8,128)(2,1)S(1)}, u32[]{:S(2)}, u32[]{:S(2)}) collective-permute-start(bf16[400,320]{1,0:T(8,128)(2,1)S(1)} %get-tuple-element.31), channel_id=1, source_target_pairs={{0,1},{1,0},{2,3},{3,2},{4,5},{5,4},{6,7},{7,6},{8,9},{9,8},{10,11... | collective-permute-start | bytes 768008 | tf_op jit(solution)/shard_map/ppermute | solution.py:373
  17.2 8.2 %collective-permute-start.4 = (bf16[2,5,40,320]{3,2,1,0:T(8,128)(2,1)S(1)}, bf16[2,5,40,320]{3,2,1,0:T(8,128)(2,1)S(1)}, u32[]{:S(2)}, u32[]{:S(2)}) collective-permute-start(bf16[2,5,40,320]{3,2,1,0:T(8,128)(2,1)S(1)} %collective-permute-done.3.a_ref), channel_id=1, source_target_pairs={{0,4},{4,0},{8,12},{12,8},{1,5},{5,1},{9,13},{13,9},{2,6},{6,2},{1... | collective-permute-start | bytes 768008 | tf_op jit(solution)/shard_map/ppermute | solution.py:375
  21.6 11.9 %collective-permute-start.5 = (bf16[400,320]{1,0:T(8,128)(2,1)S(1)}, bf16[400,320]{1,0:T(8,128)(2,1)S(1)}, u32[]{:S(2)}, u32[]{:S(2)}) collective-permute-start(bf16[400,320]{1,0:T(8,128)(2,1)S(1)} %add_parts.5.a_ref), channel_id=1, source_target_pairs={{0,3},{1,2},{2,1},{3,0},{4,7},{5,6},{6,5},{7,4},{8,11},{9,10},{10,... | collective-permute-start | bytes 768008 | tf_op jit(solution)/shard_map/ppermute | solution.py:378
  29.2 12.1 %copy-start.1 = (bf16[1,2,5,40,320]{4,3,2,1,0:T(8,128)(2,1)S(1)}, bf16[1,2,5,40,320]{4,3,2,1,0:T(8,128)(2,1)}, u32[]{:S(2)}) copy-start(bf16[1,2,5,40,320]{4,3,2,1,0:T(8,128)(2,1)} %param.11) | copy-start | bytes 768004
  29.2 9.0 %collective-permute-start.8 = (bf16[400,320]{1,0:T(8,128)(2,1)S(1)}, bf16[400,320]{1,0:T(8,128)(2,1)S(1)}, u32[]{:S(2)}, u32[]{:S(2)}) collective-permute-start(bf16[400,320]{1,0:T(8,128)(2,1)S(1)} %get-tuple-element.39), channel_id=1, source_target_pairs={{0,1},{1,0},{2,3},{3,2},{4,5},{5,4},{6,7},{7,6},{8,9},{9,8},{10,11... | collective-permute-start | bytes 768008 | tf_op jit(solution)/shard_map/ppermute | solution.py:380
  38.2 12.1 %collective-permute-start.9 = (bf16[400,320]{1,0:T(8,128)(2,1)S(1)}, bf16[400,320]{1,0:T(8,128)(2,1)S(1)}, u32[]{:S(2)}, u32[]{:S(2)}) collective-permute-start(bf16[400,320]{1,0:T(8,128)(2,1)S(1)} %add_parts.7.a_ref), channel_id=1, source_target_pairs={{0,3},{1,2},{2,1},{3,0},{4,7},{5,6},{6,5},{7,4},{8,11},{9,10},{10,... | collective-permute-start | bytes 768008 | tf_op jit(solution)/shard_map/ppermute | solution.py:383
  41.3 12.4 %collective-permute-start.6 = (bf16[1,2,200,320]{3,2,1,0:T(8,128)(2,1)S(1)}, bf16[1,2,200,320]{3,2,1,0:T(8,128)(2,1)S(1)}, u32[]{:S(2)}, u32[]{:S(2)}) collective-permute-start(bf16[1,2,200,320]{3,2,1,0:T(8,128)(2,1)S(1)} %bitcast.4), channel_id=1, source_target_pairs={{0,4},{4,0},{8,12},{12,8},{1,5},{5,1},{9,13},{13,9},{2,6},{6,2},{1... | collective-permute-start | bytes 768008 | tf_op jit(solution)/shard_map/ppermute | solution.py:386
  41.3 9.7 %collective-permute-start.7 = (bf16[1,2,200,320]{3,2,1,0:T(8,128)(2,1)S(1)}, bf16[1,2,200,320]{3,2,1,0:T(8,128)(2,1)S(1)}, u32[]{:S(2)}, u32[]{:S(2)}) collective-permute-start(bf16[1,2,200,320]{3,2,1,0:T(8,128)(2,1)S(1)} %bitcast.5), channel_id=1, source_target_pairs={{0,8},{4,12},{8,0},{12,4},{1,9},{5,13},{9,1},{13,5},{2,10},{6,14},... | collective-permute-start | bytes 768008 | tf_op jit(solution)/shard_map/ppermute | solution.py:387
  42.5 12.4 %collective-permute-start.12 = (bf16[400,320]{1,0:T(8,128)(2,1)S(1)}, bf16[400,320]{1,0:T(8,128)(2,1)S(1)}, u32[]{:S(2)}, u32[]{:S(2)}) collective-permute-start(bf16[400,320]{1,0:T(8,128)(2,1)S(1)} %add_parts.6.refs_4_.refs_0_), channel_id=1, source_target_pairs={{0,1},{1,0},{2,3},{3,2},{4,5},{5,4},{6,7},{7,6},{8,9},{9,8},{10,11... | collective-permute-start | bytes 768008 | tf_op jit(solution)/shard_map/ppermute | solution.py:384
  51.0 3.9 %collective-permute-start.10 = (bf16[1,2,200,320]{3,2,1,0:T(8,128)(2,1)S(1)}, bf16[1,2,200,320]{3,2,1,0:T(8,128)(2,1)S(1)}, u32[]{:S(2)}, u32[]{:S(2)}) collective-permute-start(bf16[1,2,200,320]{3,2,1,0:T(8,128)(2,1)S(1)} %collective-permute-done.7.refs_2_), channel_id=1, source_target_pairs={{0,4},{4,0},{8,12},{12,8},{1,5},{5,1},{9,13},{13,9},{2,6},{6,2},{1... | collective-permute-start | bytes 768008 | tf_op jit(solution)/shard_map/ppermute | solution.py:390
  51.0 10.6 %collective-permute-start.11 = (bf16[400,320]{1,0:T(8,128)(2,1)S(1)}, bf16[400,320]{1,0:T(8,128)(2,1)S(1)}, u32[]{:S(2)}, u32[]{:S(2)}) collective-permute-start(bf16[400,320]{1,0:T(8,128)(2,1)S(1)} %add_parts.8.refs_4_.refs_2_), channel_id=1, source_target_pairs={{0,1},{1,0},{2,3},{3,2},{4,5},{5,4},{6,7},{7,6},{8,9},{9,8},{10,11... | collective-permute-start | bytes 768008 | tf_op jit(solution)/shard_map/ppermute | solution.py:389
  56.3 6.7 %copy-start = (bf16[3,320,320]{2,1,0:T(8,128)(2,1)S(1)}, bf16[3,320,320]{2,1,0:T(8,128)(2,1)}, u32[]{:S(2)}) copy-start(bf16[3,320,320]{2,1,0:T(8,128)(2,1)} %refs_4_.3) | copy-start | bytes 1843204
  64.4 3.3 %collective-permute-start.14 = (bf16[2,200,320]{2,1,0:T(8,128)(2,1)S(1)}, bf16[2,200,320]{2,1,0:T(8,128)(2,1)S(1)}, u32[]{:S(2)}, u32[]{:S(2)}) collective-permute-start(bf16[2,200,320]{2,1,0:T(8,128)(2,1)S(1)} %get-tuple-element.49), channel_id=1, source_target_pairs={{0,4},{4,0},{8,12},{12,8},{1,5},{5,1},{9,13},{13,9},{2,6},{6,2},{1... | collective-permute-start | bytes 768008 | tf_op jit(solution)/shard_map/ppermute | solution.py:399
  64.5 18.9 %collective-permute-start.16 = (bf16[3,320,320]{2,1,0:T(8,128)(2,1)S(1)}, bf16[3,320,320]{2,1,0:T(8,128)(2,1)S(1)}, u32[]{:S(2)}, u32[]{:S(2)}) collective-permute-start(bf16[3,320,320]{2,1,0:T(8,128)(2,1)S(1)} %temporal_grads.3), channel_id=1, source_target_pairs={{0,16},{16,0},{1,17},{17,1},{2,18},{18,2},{3,19},{19,3},{4,20},{20... | collective-permute-start | bytes 1843208 | tf_op jit(solution)/shard_map/ppermute | solution.py:407
  67.4 1.7 %collective-permute-start.13 = (bf16[2,200,320]{2,1,0:T(8,128)(2,1)S(1)}, bf16[2,200,320]{2,1,0:T(8,128)(2,1)S(1)}, u32[]{:S(2)}, u32[]{:S(2)}) collective-permute-start(bf16[2,200,320]{2,1,0:T(8,128)(2,1)S(1)} %get-tuple-element.47), channel_id=1, source_target_pairs={{0,4},{4,0},{8,12},{12,8},{1,5},{5,1},{9,13},{13,9},{2,6},{6,2},{1... | collective-permute-start | bytes 768008 | tf_op jit(solution)/shard_map/ppermute | solution.py:402
  67.7 9.6 %collective-permute-start.15 = (bf16[2,200,320]{2,1,0:T(8,128)(2,1)S(1)}, bf16[2,200,320]{2,1,0:T(8,128)(2,1)S(1)}, u32[]{:S(2)}, u32[]{:S(2)}) collective-permute-start(bf16[2,200,320]{2,1,0:T(8,128)(2,1)S(1)} %add_parts.9), channel_id=1, source_target_pairs={{0,8},{4,12},{8,0},{12,4},{1,9},{5,13},{9,1},{13,5},{2,10},{6,14},... | collective-permute-start | bytes 768008 | tf_op jit(solution)/shard_map/ppermute | solution.py:404

commit v4 on v3

--- a/solution.py
+++ b/solution.py
@@ -172,15 +172,17 @@
 CLAIM = {
     "merge": 50.0,
     "conv0": 50.0,
-    "collect": 0.01,
-    "part": 0.01,
+    "collect": 0.0,
+    "part": 0.0,
     "part0": 80.0,
     "conv1": 1.0,
     "mine": 50.0,
-    "t1": 0.01,
-    "g1": 0.01,
-    "t2": 0.01,
-    "g2": 50.0,
+    "t1": 50.0,
+    "g1": 0.0,
+    "t2": 0.0,
+    "g2": 0.0,
+    "g3": 0.0,
+    "g4": 50.0,
 }
 
 
@@ -207,52 +209,45 @@
             ref[lead + (at + 1 - odd, slice(0, count))] = other[j * count : (j + 1) * count]
 
 
-def grad_kernel(steps, held, *refs):
-    clips = refs[0].shape[0]
-    cots, refs = refs[:4], refs[4:]
-    *start, out_ref, s_ref, c_ref = refs[held * clips :]
-    pieces = refs[: held * clips]
+def grad_kernel(steps, held, extra, *refs):
+    cots, pieces, added = refs[:4], refs[4 : 4 + held], refs[4 + held : -3]
+    out_ref, s_ref, c_ref = refs[-3:]
     t = lax.axis_index("tm")
-    own = lax.axis_index("dp") if clips > 1 else 0
-    frames, rows, width = s_ref.shape[1:]
-    for clip in range(clips):
-        at = own if clip == 0 else 1 - own
-        zero_frames(s_ref, (at,), frames, rows, width)
-        zero_frames(c_ref, (at,), frames, rows, c_ref.shape[-1])
-        put_pairs(s_ref, (at,), steps, pieces[clip * held : (clip + 1) * held])
-        for block, cot in enumerate(cots):
-            first = 1 + 2 * jnp.bitwise_xor(t, block)
-            for f in range(2):
-                c_ref[at, first + f, 0 : rows - PAD] = cot[clip, f]
+    frames, rows, width = s_ref.shape
+    zero_frames(s_ref, (), frames, rows, width)
+    zero_frames(c_ref, (), frames, rows, c_ref.shape[-1])
+    put_pairs(s_ref, (), steps, pieces)
+    for block, cot in enumerate(cots):
+        first = 1 + 2 * jnp.bitwise_xor(t, block)
+        for f in range(2):
+            c_ref[first + f, 0 : rows - PAD] = cot[f]
     chip = t // 2 if steps[0] == 0 else 1 - t // 2
     first, length = 1 + 4 * chip, 4
-    turned = [
-        s_ref[clip, pl.ds(first, length)].reshape(length * rows, width).T for clip in range(clips)
-    ]
+    turned = s_ref[pl.ds(first, length)].reshape(length * rows, width).T
     for k in range(3):
-        total = start[0][k] if start else None
-        for clip in range(clips):
-            cot = c_ref[clip, pl.ds(first + 1 - k, length)].reshape(length * rows, -1)
-            term = jnp.dot(turned[clip], cot, preferred_element_type=f32)
-            total = term if total is None else total + term
-        out_ref[k] = total.astype(out_ref.dtype)
-
-
-def temporal_grads(steps, cots, pieces, start, dtype, weight):
-    clips, _, count, width_out = cots[0].shape
-    width = pieces[0][0].shape[-1]
-    held = len(pieces[0])
-    operands = (*cots, *(p for clip in pieces for p in clip), *start)
-    return pl.pallas_call(
-        functools.partial(grad_kernel, steps, held),
-        out_shape=jax.ShapeDtypeStruct((3, width, width_out), dtype),
+        cot = c_ref[pl.ds(first + 1 - k, length)].reshape(length * rows, -1)
+        total = jnp.dot(turned, cot, preferred_element_type=f32)
+        if added:
+            total = added[0][k] + total
+        if extra:
+            total = (total + added[1][k]) * 0.5
+        out_ref[k] = total
+
+
+def temporal_grads(steps, cots, pieces, added, weight):
+    count, width_out = cots[0].shape[-2:]
+    width = pieces[0].shape[-1]
+    operands = (*cots, *pieces, *added)
+    return pl.pallas_call(
+        functools.partial(grad_kernel, steps, len(pieces), len(added) == 2),
+        out_shape=jax.ShapeDtypeStruct((3, width, width_out), f32),
         in_specs=[vmem_spec()] * len(operands),
         out_specs=vmem_spec(),
         scratch_shapes=[
-            pltpu.VMEM((clips, 10, count + PAD, width), bf16),
-            pltpu.VMEM((clips, 10, count + PAD, width_out), bf16),
+            pltpu.VMEM((10, count + PAD, width), bf16),
+            pltpu.VMEM((10, count + PAD, width_out), bf16),
         ],
-        compiler_params=params(20),
+        compiler_params=params(14),
         cost_estimate=cost(weight),
         name="temporal_grads",
     )(*operands)
@@ -362,6 +357,11 @@
     near, across = xor(4, 1), xor(4, 3)
     count = rows * cols
     clips = lax.axis_size("dp")
+    pair_clips = clips == 2
+
+    def swap(x):
+        return lax.ppermute(x, "dp", [(0, 1), (1, 0)])
+
     sibling = lax.ppermute(own, "tm", core)
     st_own, pairs = chip_stats(own, sibling)
     st_chip = lax.ppermute(st_own, "tm", chip)
@@ -378,36 +378,48 @@
     came0 = lax.ppermute(part0, "mp", across)
     keep1, send1 = pair_conv(tie(far_pairs, part0), norm, taps, CLAIM["conv1"])
     got1 = lax.ppermute(send1, "mp", near)
-    mine0 = add16(tie(part0, keep1), came0, CLAIM["mine"])
+    cot = cotangent.reshape(frames, count, width)
+    theirs, far_cot = [], []
+    if pair_clips:
+        far_cot.append(tie(swap(tie(cot, keep0)), keep1))
+    mine0 = add16(tie(part0, keep1, *far_cot), came0, CLAIM["mine"])
     part1 = add16(tie(keep1, mine0), got1, CLAIM["part"])
     came1 = lax.ppermute(part1, "mp", across)
     other0 = lax.ppermute(mine0, "mp", near)
-    cot = cotangent.reshape(1, frames, count, width)
     cot_core = lax.ppermute(tie(cot, mine0), "tm", core)
     cot_chip = lax.ppermute(tie(cot, mine0), "tm", chip)
+    if pair_clips:
+        theirs.append(swap(mine0))
+        far_cot.append(lax.ppermute(tie(far_cot[0], mine0), "tm", core))
+        far_cot.append(lax.ppermute(tie(far_cot[0], mine0), "tm", chip))
     mine1 = add16(tie(part1, mine0), came1, CLAIM["mine"])
-    other1 = lax.ppermute(mine1, "mp", near)
-    cot_both = lax.ppermute(tie(cot_chip, mine1), "tm", core)
-    cots = (cot, cot_core, cot_chip, cot_both)
+    other1 = lax.ppermute(tie(mine1, *theirs), "mp", near)
+    cots = (cot, cot_core, cot_chip, lax.ppermute(tie(cot_chip, mine1), "tm", core))
+    if pair_clips:
+        theirs += [swap(tie(other0, mine1)), swap(mine1), swap(other1)]
+        far_cot.append(lax.ppermute(tie(far_cot[2], other1), "tm", core))
+    grad_own = temporal_grads((0, 1), cots, [tie(mine0, mine1), other0], (), CLAIM["g1"])
 
     steps = (0, 1, 2, 3)
-    held = [tie(mine0, mine1), other0]
-    grad = temporal_grads((0, 1), cots, [held], (), f32, CLAIM["g1"])
-    sent = temporal_grads((2, 3), cots, [[mine1, other1]], (grad,), bf16 if clips == 2 else f32, CLAIM["g2"])
-    pieces = [tie(mine0, sent), other0, mine1, other1]
+    pieces = [tie(mine0, grad_own), other0, mine1, other1]
     send, keep_chip = temporal_conv(steps, (3, 2), count, pieces, temporal_weight, CLAIM["t1"])
     far_part = lax.ppermute(send, "tm", core)
-    later = [tie(mine0, keep_chip)] + pieces[1:]
+    later = [tie(mine0, keep_chip, *theirs[2:3])] + pieces[1:]
     send, keep_own = temporal_conv(steps, (1, 0), count, later, temporal_weight, CLAIM["t2"])
     near_part = lax.ppermute(send, "tm", core)
     to_chip = add16(tie(keep_chip, keep_own), far_part, CLAIM["part"])
     from_chip = lax.ppermute(to_chip, "tm", chip)
+    last = [tie(mine1, to_chip), other1]
+    grad_own = temporal_grads((2, 3), cots, last, (grad_own,), CLAIM["g3"])
+    if pair_clips:
+        first = [tie(theirs[0], grad_own), theirs[1]]
+        grad_other = temporal_grads((0, 1), far_cot, first, (), CLAIM["g2"])
+        last = [tie(theirs[2], grad_other), theirs[3]]
+        temporal_grad = temporal_grads((2, 3), far_cot, last, (grad_other, grad_own), CLAIM["g4"])
+    else:
+        temporal_grad = lax.psum(grad_own, "dp") / clips
+    keep_own = tie(keep_own, temporal_grad)
     block = (keep_own + near_part.astype(f32) + from_chip.astype(f32)).astype(bf16)
-    if clips == 2:
-        theirs = lax.ppermute(sent, "dp", [(0, 1), (1, 0)])
-        temporal_grad = (sent.astype(f32) + theirs.astype(f32)) / clips
-    else:
-        temporal_grad = lax.psum(sent, "dp") / clips
     return block.reshape(activations.shape), temporal_grad
 
 

time: 84.8 us -> 83 us (0.979)
  waiting for transfers between devices: 46.5 us -> 34.3 us
  starting transfers between devices: 19.6 us -> 27.2 us
  Pallas kernels: 15.6 us -> 19.7 us
  other arithmetic: 2.13 us -> 0.84 us
    ppermute x1, waiting for transfers between devices: 8.24 us -> 0.01 us  [body(): from_chip = lax.ppermute(to_chip, 'tm', chip)]
    ppermute x3 -> x10, starting transfers between devices: 4.2 us -> 11.2 us  [the longest x5 6.58 us: swap(): return lax.ppermute(x, 'dp', [(0, 1), (1, 0)])]
    pallas_call x2 -> x4, Pallas kernels: 2.75 us -> 6.72 us  [temporal_grads(): pl.pallas_call(functools.partial(grad_kernel, steps, len(pieces), len(add...]
    ppermute x1, waiting for transfers between devices: 7.73 us -> 5.77 us  [body(): came1 = lax.ppermute(part1, 'mp', across)]
    ppermute x1, waiting for transfers between devices: 4.3 us -> 2.85 us  [body(): got0 = lax.ppermute(send0, 'mp', near)]
    ppermute x1, waiting for transfers between devices: 4.22 us -> 2.77 us  [body(): came0 = lax.ppermute(part0, 'mp', across)]
    div x1 -> x0, other arithmetic: 1.3 us -> none  [body(): temporal_grad = (sent.astype(f32) + theirs.astype(f32)) / clips]
    ppermute x1, waiting for transfers between devices: 1.22 us -> 0.01 us  [body(): other0 = lax.ppermute(mine0, 'mp', near)]
  transfers between devices with their start and end apart: 17 -> 24, of which waited for: 13 -> 11; matrix products, arithmetic and copies ran while one was open for 1% -> 0% of each run, Pallas kernels for 13% -> 21%
where the time goes in v4:
time: 83 us; the launch traced here: 82.9 us
  waiting for transfers between devices  34.3 us (41%)
  starting transfers between devices  27.2 us (33%)
  Pallas kernels  19.7 us (24%)
  other arithmetic  0.84 us (1%)
    ppermute x5, waiting for transfers between devices, swap(): return lax.ppermute(x, 'dp', [(0, 1), (1, 0)])  7.82 us
    pallas_call x2, Pallas kernels, pair_conv(): pl.pallas_call(conv_kernel, out_shape=(jax.ShapeDtypeStruct((count, width...  7.25 us
    pallas_call x4, Pallas kernels, temporal_grads(): pl.pallas_call(functools.partial(grad_kernel, steps, len(pieces), len(add...  6.72 us
    ppermute x5, starting transfers between devices, swap(): return lax.ppermute(x, 'dp', [(0, 1), (1, 0)])  6.58 us
    ppermute x1, waiting for transfers between devices, body(): came1 = lax.ppermute(part1, 'mp', across)  5.77 us
    ppermute x1, waiting for transfers between devices, body(): got1 = lax.ppermute(send1, 'mp', near)  5.52 us
    ppermute x1, starting transfers between devices, body(): came0 = lax.ppermute(part0, 'mp', across)  3.8 us
    ppermute x1, waiting for transfers between devices, body(): other1 = lax.ppermute(tie(mine1, *theirs), 'mp', near)  3.69 us
  transfers between devices with their start and end apart: 24, of which 11 were waited for; matrix products, arithmetic and copies ran while one was open for 0% of the time, Pallas kernels for 21%

profile of v4, /device:TPU:0, one launch (start us, length us, event | category | flops | bytes accessed | tf_op | source)
XLA Modules:
  0.0 82.9 jit_solution(14227063647171738672)
XLA Ops:
  1.2 1.4 %collective-permute-done.core_ref = bf16[2,5,40,320]{3,2,1,0:T(8,128)(2,1)S(1)} collective-permute-done((bf16[2,5,40,320]{3,2,1,0:T(8,128)(2,1)}, bf16[2,5,40,320]{3,2,1,0:T(8,128)(2,1)S(1)}, u32[]{:S(2)}, u32[]{:S(2)}) %collective-permute-start) | collective-permute-done | bytes 256032 | tf_op jit(solution)/shard_map/ppermute | solution.py:365
  2.6 2.1 %chip_stats.1 = (f32[16,320]{1,0:T(8,128)S(1)}, bf16[2,2,5,40,320]{4,3,2,1,0:T(8,128)(2,1)S(1)}) custom-call(bf16[2,5,40,320]{3,2,1,0:T(8,128)(2,1)} %bitcast.own_ref, bf16[2,5,40,320]{3,2,1,0:T(8,128)(2,1)S(1)} %collective-permute-done.core_ref), custom_call_target="tpu_custom_call" | custom-call | flops 1724999936 | bytes 1 | tf_op jit(solution)/shard_map/chip_stats/pallas_call | solution.py:57
  4.7 2.9 %collective-permute-start.1 = (f32[16,320]{1,0:T(8,128)S(1)}, f32[16,320]{1,0:T(8,128)S(1)}, u32[]{:S(2)}, u32[]{:S(2)}) collective-permute-start(f32[16,320]{1,0:T(8,128)S(1)} %get-tuple-element.37.s0_ref), channel_id=1, source_target_pairs={{0,8},{4,12},{8,0},{12,4},{1,9},{5,13},{9,1},{13,5},{2,10},{6,14},... | collective-permute-start | bytes 61448 | tf_op jit(solution)/shard_map/ppermute | solution.py:367
  8.0 1.4 %collective-permute-done.1.s1_ref = f32[16,320]{1,0:T(8,128)S(1)} collective-permute-done((f32[16,320]{1,0:T(8,128)S(1)}, f32[16,320]{1,0:T(8,128)S(1)}, u32[]{:S(2)}, u32[]{:S(2)}) %collective-permute-start.1) | collective-permute-done | bytes 20512 | tf_op jit(solution)/shard_map/ppermute | solution.py:367
  9.4 3.5 %pair_conv.2 = (f32[400,320]{1,0:T(8,128)S(1)}, bf16[400,320]{1,0:T(8,128)(2,1)S(1)}) custom-call(bf16[2,2,5,40,320]{4,3,2,1,0:T(8,128)(2,1)S(1)} %get-tuple-element.36.x_ref, f32[32,320]{1,0:T(8,128)S(1)} %merge_stats.1.norm_ref, bf16[3,960,320]{2,1,0:T(8,128)(2,1)S(1)} %get-tuple-element.39.w_ref), custom_call_target="tpu_custom_call" | custom-call | flops 57500000256 | bytes 1 | tf_op jit(solution)/shard_map/pair_conv/pallas_call | solution.py:155
  13.0 2.2 %collective-permute-start.2 = (bf16[400,320]{1,0:T(8,128)(2,1)S(1)}, bf16[400,320]{1,0:T(8,128)(2,1)S(1)}, u32[]{:S(2)}, u32[]{:S(2)}) collective-permute-start(bf16[400,320]{1,0:T(8,128)(2,1)S(1)} %get-tuple-element.41), channel_id=1, source_target_pairs={{0,1},{1,0},{2,3},{3,2},{4,5},{5,4},{6,7},{7,6},{8,9},{9,8},{10,11... | collective-permute-start | bytes 768008 | tf_op jit(solution)/shard_map/ppermute | solution.py:373
  15.2 2.1 %collective-permute-done.3.a_ref = bf16[2,5,40,320]{3,2,1,0:T(8,128)(2,1)S(1)} collective-permute-done((bf16[2,5,40,320]{3,2,1,0:T(8,128)(2,1)}, bf16[2,5,40,320]{3,2,1,0:T(8,128)(2,1)S(1)}, u32[]{:S(2)}, u32[]{:S(2)}) %collective-permute-start.3) | collective-permute-done | bytes 256032 | tf_op jit(solution)/shard_map/ppermute | solution.py:369
  17.2 1.5 %collective-permute-start.5 = (bf16[2,200,320]{2,1,0:T(8,128)(2,1)S(1)}, bf16[2,200,320]{2,1,0:T(8,128)(2,1)S(1)}, u32[]{:S(2)}, u32[]{:S(2)}) collective-permute-start(bf16[2,200,320]{2,1,0:T(8,128)(2,1)S(1)} %bitcast.4), channel_id=1, source_target_pairs={{0,16},{16,0},{1,17},{17,1},{2,18},{18,2},{3,19},{19,3},{4,20},{20... | collective-permute-start | bytes 768008 | tf_op jit(solution)/shard_map/ppermute | solution.py:363
  18.7 2.8 %collective-permute-done.2.b_ref = bf16[400,320]{1,0:T(8,128)(2,1)S(1)} collective-permute-done((bf16[400,320]{1,0:T(8,128)(2,1)S(1)}, bf16[400,320]{1,0:T(8,128)(2,1)S(1)}, u32[]{:S(2)}, u32[]{:S(2)}) %collective-permute-start.2) | collective-permute-done | bytes 256032 | tf_op jit(solution)/shard_map/ppermute | solution.py:373
  21.6 3.8 %collective-permute-start.6 = (bf16[400,320]{1,0:T(8,128)(2,1)S(1)}, bf16[400,320]{1,0:T(8,128)(2,1)S(1)}, u32[]{:S(2)}, u32[]{:S(2)}) collective-permute-start(bf16[400,320]{1,0:T(8,128)(2,1)S(1)} %add_parts.5.a_ref), channel_id=1, source_target_pairs={{0,3},{1,2},{2,1},{3,0},{4,7},{5,6},{6,5},{7,4},{8,11},{9,10},{10,... | collective-permute-start | bytes 768008 | tf_op jit(solution)/shard_map/ppermute | solution.py:378
  25.5 3.7 %pair_conv.3 = (f32[400,320]{1,0:T(8,128)S(1)}, bf16[400,320]{1,0:T(8,128)(2,1)S(1)}) custom-call(bf16[2,2,5,40,320]{4,3,2,1,0:T(8,128)(2,1)S(1)} %collect_pairs.1.x_ref, f32[32,320]{1,0:T(8,128)S(1)} %merge_stats.1.norm_ref, bf16[3,960,320]{2,1,0:T(8,128)(2,1)S(1)} %get-tuple-element.39.w_ref), custom_call_target="tpu_custom_call" | custom-call | flops 1150000000 | bytes 1 | tf_op jit(solution)/shard_map/pair_conv/pallas_call | solution.py:155
  29.3 2.8 %collective-permute-done.6.b_ref = bf16[400,320]{1,0:T(8,128)(2,1)S(1)} collective-permute-done((bf16[400,320]{1,0:T(8,128)(2,1)S(1)}, bf16[400,320]{1,0:T(8,128)(2,1)S(1)}, u32[]{:S(2)}, u32[]{:S(2)}) %collective-permute-start.6) | collective-permute-done | bytes 256032 | tf_op jit(solution)/shard_map/ppermute | solution.py:378
  32.2 5.5 %collective-permute-done.9.b_ref = bf16[400,320]{1,0:T(8,128)(2,1)S(1)} collective-permute-done((bf16[400,320]{1,0:T(8,128)(2,1)S(1)}, bf16[400,320]{1,0:T(8,128)(2,1)S(1)}, u32[]{:S(2)}, u32[]{:S(2)}) %collective-permute-start.9) | collective-permute-done | bytes 256032 | tf_op jit(solution)/shard_map/ppermute | solution.py:380
  37.8 3.6 %collective-permute-start.10 = (bf16[400,320]{1,0:T(8,128)(2,1)S(1)}, bf16[400,320]{1,0:T(8,128)(2,1)S(1)}, u32[]{:S(2)}, u32[]{:S(2)}) collective-permute-start(bf16[400,320]{1,0:T(8,128)(2,1)S(1)} %add_parts.7.a_ref), channel_id=1, source_target_pairs={{0,3},{1,2},{2,1},{3,0},{4,7},{5,6},{6,5},{7,4},{8,11},{9,10},{10,... | collective-permute-start | bytes 768008 | tf_op jit(solution)/shard_map/ppermute | solution.py:387
  41.3 1.5 %collective-permute-start.13 = (bf16[400,320]{1,0:T(8,128)(2,1)S(1)}, bf16[400,320]{1,0:T(8,128)(2,1)S(1)}, u32[]{:S(2)}, u32[]{:S(2)}) collective-permute-start(bf16[400,320]{1,0:T(8,128)(2,1)S(1)} %add_parts.6.refs_4_.refs_0_), channel_id=1, source_target_pairs={{0,16},{16,0},{1,17},{17,1},{2,18},{18,2},{3,19},{19,3},{4,20},{20... | collective-permute-start | bytes 768008 | tf_op jit(solution)/shard_map/ppermute | solution.py:363
  42.8 1.3 %collective-permute-start.8 = (bf16[2,200,320]{2,1,0:T(8,128)(2,1)S(1)}, bf16[2,200,320]{2,1,0:T(8,128)(2,1)S(1)}, u32[]{:S(2)}, u32[]{:S(2)}) collective-permute-start(bf16[2,200,320]{2,1,0:T(8,128)(2,1)S(1)} %bitcast.5), channel_id=1, source_target_pairs={{0,8},{4,12},{8,0},{12,4},{1,9},{5,13},{9,1},{13,5},{2,10},{6,14},... | collective-permute-start | bytes 768008 | tf_op jit(solution)/shard_map/ppermute | solution.py:390
  44.1 5.8 %collective-permute-done.10.b_ref = bf16[400,320]{1,0:T(8,128)(2,1)S(1)} collective-permute-done((bf16[400,320]{1,0:T(8,128)(2,1)S(1)}, bf16[400,320]{1,0:T(8,128)(2,1)S(1)}, u32[]{:S(2)}, u32[]{:S(2)}) %collective-permute-start.10) | collective-permute-done | bytes 256032 | tf_op jit(solution)/shard_map/ppermute | solution.py:387
  50.0 0.9 %collective-permute-done.8.refs_2_ = bf16[2,200,320]{2,1,0:T(8,128)(2,1)S(1)} collective-permute-done((bf16[2,200,320]{2,1,0:T(8,128)(2,1)S(1)}, bf16[2,200,320]{2,1,0:T(8,128)(2,1)S(1)}, u32[]{:S(2)}, u32[]{:S(2)}) %collective-permute-start.8) | collective-permute-done | bytes 256032 | tf_op jit(solution)/shard_map/ppermute | solution.py:390
  50.9 2.8 %collective-permute-start.14 = (bf16[400,320]{1,0:T(8,128)(2,1)S(1)}, bf16[400,320]{1,0:T(8,128)(2,1)S(1)}, u32[]{:S(2)}, u32[]{:S(2)}) collective-permute-start(bf16[400,320]{1,0:T(8,128)(2,1)S(1)} %add_parts.8.refs_2_.refs_4_), channel_id=1, source_target_pairs={{0,1},{1,0},{2,3},{3,2},{4,5},{5,4},{6,7},{7,6},{8,9},{9,8},{10,11... | collective-permute-start | bytes 768008 | tf_op jit(solution)/shard_map/ppermute | solution.py:396
  53.7 1.3 %collective-permute-start.17 = (bf16[2,200,320]{2,1,0:T(8,128)(2,1)S(1)}, bf16[2,200,320]{2,1,0:T(8,128)(2,1)S(1)}, u32[]{:S(2)}, u32[]{:S(2)}) collective-permute-start(bf16[2,200,320]{2,1,0:T(8,128)(2,1)S(1)} %collective-permute-done.5.refs_0_), channel_id=1, source_target_pairs={{0,8},{4,12},{8,0},{12,4},{1,9},{5,13},{9,1},{13,5},{2,10},{6,14},... | collective-permute-start | bytes 768008 | tf_op jit(solution)/shard_map/ppermute | solution.py:394
  55.0 1.5 %collective-permute-start.15 = (bf16[400,320]{1,0:T(8,128)(2,1)S(1)}, bf16[400,320]{1,0:T(8,128)(2,1)S(1)}, u32[]{:S(2)}, u32[]{:S(2)}) collective-permute-start(bf16[400,320]{1,0:T(8,128)(2,1)S(1)} %add_parts.8.refs_2_.refs_4_), channel_id=1, source_target_pairs={{0,16},{16,0},{1,17},{17,1},{2,18},{18,2},{3,19},{19,3},{4,20},{20... | collective-permute-start | bytes 768008 | tf_op jit(solution)/shard_map/ppermute | solution.py:363
  56.5 1.4 %temporal_grads.4.refs_6_ = f32[3,320,320]{2,1,0:T(8,128)S(1)} custom-call(bf16[2,200,320]{2,1,0:T(8,128)(2,1)S(1)} %bitcast.7, bf16[2,200,320]{2,1,0:T(8,128)(2,1)S(1)} %collective-permute-done.7.refs_1_, bf16[2,200,320]{2,1,0:T(8,128)(2,1)S(1)} %collective-permute-done.8.refs_2_, bf16[2,200,320]{2,1,0:T(8,128)(2,1)S(1)} %collective-permute-done.11.refs_3_, ...), custom_call_target="tpu_custom_call" | custom-call | bytes 1 | tf_op jit(solution)/shard_map/temporal_grads/pallas_call | solution.py:241
  57.9 3.7 %collective-permute-done.14.refs_3_.refs_5_ = bf16[400,320]{1,0:T(8,128)(2,1)S(1)} collective-permute-done((bf16[400,320]{1,0:T(8,128)(2,1)S(1)}, bf16[400,320]{1,0:T(8,128)(2,1)S(1)}, u32[]{:S(2)}, u32[]{:S(2)}) %collective-permute-start.14) | collective-permute-done | bytes 256032 | tf_op jit(solution)/shard_map/ppermute | solution.py:396
  61.6 1.5 %temporal_conv.2 = (bf16[2,200,320]{2,1,0:T(8,128)(2,1)S(1)}, f32[2,200,320]{2,1,0:T(8,128)S(1)}) custom-call(bf16[400,320]{1,0:T(8,128)(2,1)S(1)} %add_parts.6.refs_4_.refs_0_, bf16[400,320]{1,0:T(8,128)(2,1)S(1)} %collective-permute-done.12.refs_5_.refs_1_, bf16[400,320]{1,0:T(8,128)(2,1)S(1)} %add_parts.8.refs_2_.refs_4_, ...), custom_call_target="tpu_custom_call" | custom-call | flops 57500000256 | bytes 1 | tf_op jit(solution)/shard_map/temporal_conv/pallas_call | solution.py:274
  63.6 1.5 %collective-permute-start.20 = (bf16[400,320]{1,0:T(8,128)(2,1)S(1)}, bf16[400,320]{1,0:T(8,128)(2,1)S(1)}, u32[]{:S(2)}, u32[]{:S(2)}) collective-permute-start(bf16[400,320]{1,0:T(8,128)(2,1)S(1)} %collective-permute-done.12.refs_5_.refs_1_), channel_id=1, source_target_pairs={{0,16},{16,0},{1,17},{17,1},{2,18},{18,2},{3,19},{19,3},{4,20},{20... | collective-permute-start | bytes 768008 | tf_op jit(solution)/shard_map/ppermute | solution.py:363
  65.7 1.4 %temporal_conv.3 = (bf16[2,200,320]{2,1,0:T(8,128)(2,1)S(1)}, f32[2,200,320]{2,1,0:T(8,128)S(1)}) custom-call(bf16[400,320]{1,0:T(8,128)(2,1)S(1)} %add_parts.6.refs_4_.refs_0_, bf16[400,320]{1,0:T(8,128)(2,1)S(1)} %collective-permute-done.12.refs_5_.refs_1_, bf16[400,320]{1,0:T(8,128)(2,1)S(1)} %add_parts.8.refs_2_.refs_4_, ...), custom_call_target="tpu_custom_call" | custom-call | bytes 1 | tf_op jit(solution)/shard_map/temporal_conv/pallas_call | solution.py:274
  67.5 1.4 %temporal_grads.5.refs_7_ = f32[3,320,320]{2,1,0:T(8,128)S(1)} custom-call(bf16[2,200,320]{2,1,0:T(8,128)(2,1)S(1)} %bitcast.8, bf16[2,200,320]{2,1,0:T(8,128)(2,1)S(1)} %collective-permute-done.7.refs_1_, bf16[2,200,320]{2,1,0:T(8,128)(2,1)S(1)} %collective-permute-done.8.refs_2_, bf16[2,200,320]{2,1,0:T(8,128)(2,1)S(1)} %collective-permute-done.11.refs_3_, ...), custom_call_target="tpu_custom_call" | custom-call | bytes 1 | tf_op jit(solution)/shard_map/temporal_grads/pallas_call | solution.py:241
  68.9 1.3 %collective-permute-start.23 = (bf16[2,200,320]{2,1,0:T(8,128)(2,1)S(1)}, bf16[2,200,320]{2,1,0:T(8,128)(2,1)S(1)}, u32[]{:S(2)}, u32[]{:S(2)}) collective-permute-start(bf16[2,200,320]{2,1,0:T(8,128)(2,1)S(1)} %add_parts.9), channel_id=1, source_target_pairs={{0,8},{4,12},{8,0},{12,4},{1,9},{5,13},{9,1},{13,5},{2,10},{6,14},... | collective-permute-start | bytes 768008 | tf_op jit(solution)/shard_map/ppermute | solution.py:411
  70.3 3.5 %collective-permute-done.20.refs_5_ = bf16[400,320]{1,0:T(8,128)(2,1)S(1)} collective-permute-done((bf16[400,320]{1,0:T(8,128)(2,1)S(1)}, bf16[400,320]{1,0:T(8,128)(2,1)S(1)}, u32[]{:S(2)}, u32[]{:S(2)}) %collective-permute-start.20) | collective-permute-done | bytes 256032 | tf_op jit(solution)/shard_map/ppermute | solution.py:363
  73.8 1.4 %temporal_grads.6.refs_6_ = f32[3,320,320]{2,1,0:T(8,128)S(1)} custom-call(bf16[2,200,320]{2,1,0:T(8,128)(2,1)S(1)} %collective-permute-done.5.refs_0_, bf16[2,200,320]{2,1,0:T(8,128)(2,1)S(1)} %collective-permute-done.16.refs_1_, bf16[2,200,320]{2,1,0:T(8,128)(2,1)S(1)} %collective-permute-done.17.refs_2_, ...), custom_call_target="tpu_custom_call" | custom-call | bytes 1 | tf_op jit(solution)/shard_map/temporal_grads/pallas_call | solution.py:241
  75.1 4.3 %collective-permute-done.21.refs_5_ = bf16[400,320]{1,0:T(8,128)(2,1)S(1)} collective-permute-done((bf16[400,320]{1,0:T(8,128)(2,1)S(1)}, bf16[400,320]{1,0:T(8,128)(2,1)S(1)}, u32[]{:S(2)}, u32[]{:S(2)}) %collective-permute-start.21) | collective-permute-done | bytes 256032 | tf_op jit(solution)/shard_map/ppermute | solution.py:363
  79.5 2.6 %temporal_grads.7 = f32[3,320,320]{2,1,0:T(8,128)} custom-call(bf16[2,200,320]{2,1,0:T(8,128)(2,1)S(1)} %collective-permute-done.5.refs_0_, bf16[2,200,320]{2,1,0:T(8,128)(2,1)S(1)} %collective-permute-done.16.refs_1_, bf16[2,200,320]{2,1,0:T(8,128)(2,1)S(1)} %collective-permute-done.17.refs_2_, bf16[2,200,320]{2,1,0:T(8,128)(2,1)S(1)} %collective-permute-done.18.refs_3_, ...), custom_call_target="tpu_custom_call" | custom-call | flops 57500000256 | bytes 1 | tf_op jit(solution)/shard_map/temporal_grads/pallas_call | solution.py:241
  (46 shorter events, 3.8 us)
Async XLA Ops:
  0.6 7.0 %copy-start.3 = (bf16[9,320,320]{2,1,0:T(8,128)(2,1)S(1)}, bf16[9,320,320]{2,1,0:T(8,128)(2,1)}, u32[]{:S(2)}) copy-start(bf16[9,320,320]{2,1,0:T(8,128)(2,1)} %param.9) | copy-start | bytes 5529604
  0.6 7.0 %copy-start.4 = (f32[320]{0:T(512)S(1)}, f32[320]{0:T(512)}, u32[]{:S(2)}) copy-start(f32[320]{0:T(512)} %gain_ref.1) | copy-start | bytes 3844
  0.7 7.0 %copy-start.5 = (f32[320]{0:T(512)S(1)}, f32[320]{0:T(512)}, u32[]{:S(2)}) copy-start(f32[320]{0:T(512)} %bias_ref.1) | copy-start | bytes 3844
  0.7 2.0 %collective-permute-start = (bf16[2,5,40,320]{3,2,1,0:T(8,128)(2,1)}, bf16[2,5,40,320]{3,2,1,0:T(8,128)(2,1)S(1)}, u32[]{:S(2)}, u32[]{:S(2)}) collective-permute-start(bf16[2,5,40,320]{3,2,1,0:T(8,128)(2,1)} %bitcast.own_ref), channel_id=1, source_target_pairs={{0,4},{4,0},{8,12},{12,8},{1,5},{5,1},{9,13},{13,9},{2,6},{6,2},{1... | collective-permute-start | bytes 768008 | tf_op jit(solution)/shard_map/ppermute | solution.py:365
  4.7 4.7 %collective-permute-start.1 = (f32[16,320]{1,0:T(8,128)S(1)}, f32[16,320]{1,0:T(8,128)S(1)}, u32[]{:S(2)}, u32[]{:S(2)}) collective-permute-start(f32[16,320]{1,0:T(8,128)S(1)} %get-tuple-element.37.s0_ref), channel_id=1, source_target_pairs={{0,8},{4,12},{8,0},{12,4},{1,9},{5,13},{9,1},{13,5},{2,10},{6,14},... | collective-permute-start | bytes 61448 | tf_op jit(solution)/shard_map/ppermute | solution.py:367
  7.9 9.3 %collective-permute-start.3 = (bf16[2,5,40,320]{3,2,1,0:T(8,128)(2,1)}, bf16[2,5,40,320]{3,2,1,0:T(8,128)(2,1)S(1)}, u32[]{:S(2)}, u32[]{:S(2)}) collective-permute-start(bf16[2,5,40,320]{3,2,1,0:T(8,128)(2,1)} %bitcast.own_ref), channel_id=1, source_target_pairs={{0,8},{4,12},{8,0},{12,4},{1,9},{5,13},{9,1},{13,5},{2,10},{6,14},... | collective-permute-start | bytes 768008 | tf_op jit(solution)/shard_map/ppermute | solution.py:369
  9.4 7.8 %copy-start = (bf16[1,2,5,40,320]{4,3,2,1,0:T(8,128)(2,1)S(1)}, bf16[1,2,5,40,320]{4,3,2,1,0:T(8,128)(2,1)}, u32[]{:S(2)}) copy-start(bf16[1,2,5,40,320]{4,3,2,1,0:T(8,128)(2,1)} %param.11) | copy-start | bytes 768004
  13.0 8.6 %collective-permute-start.2 = (bf16[400,320]{1,0:T(8,128)(2,1)S(1)}, bf16[400,320]{1,0:T(8,128)(2,1)S(1)}, u32[]{:S(2)}, u32[]{:S(2)}) collective-permute-start(bf16[400,320]{1,0:T(8,128)(2,1)S(1)} %get-tuple-element.41), channel_id=1, source_target_pairs={{0,1},{1,0},{2,3},{3,2},{4,5},{5,4},{6,7},{7,6},{8,9},{9,8},{10,11... | collective-permute-start | bytes 768008 | tf_op jit(solution)/shard_map/ppermute | solution.py:373
  17.2 8.2 %collective-permute-start.4 = (bf16[2,5,40,320]{3,2,1,0:T(8,128)(2,1)S(1)}, bf16[2,5,40,320]{3,2,1,0:T(8,128)(2,1)S(1)}, u32[]{:S(2)}, u32[]{:S(2)}) collective-permute-start(bf16[2,5,40,320]{3,2,1,0:T(8,128)(2,1)S(1)} %collective-permute-done.3.a_ref), channel_id=1, source_target_pairs={{0,4},{4,0},{8,12},{12,8},{1,5},{5,1},{9,13},{13,9},{2,6},{6,2},{1... | collective-permute-start | bytes 768008 | tf_op jit(solution)/shard_map/ppermute | solution.py:375
  17.2 12.0 %collective-permute-start.5 = (bf16[2,200,320]{2,1,0:T(8,128)(2,1)S(1)}, bf16[2,200,320]{2,1,0:T(8,128)(2,1)S(1)}, u32[]{:S(2)}, u32[]{:S(2)}) collective-permute-start(bf16[2,200,320]{2,1,0:T(8,128)(2,1)S(1)} %bitcast.4), channel_id=1, source_target_pairs={{0,16},{16,0},{1,17},{17,1},{2,18},{18,2},{3,19},{19,3},{4,20},{20... | collective-permute-start | bytes 768008 | tf_op jit(solution)/shard_map/ppermute | solution.py:363
  21.6 10.5 %collective-permute-start.6 = (bf16[400,320]{1,0:T(8,128)(2,1)S(1)}, bf16[400,320]{1,0:T(8,128)(2,1)S(1)}, u32[]{:S(2)}, u32[]{:S(2)}) collective-permute-start(bf16[400,320]{1,0:T(8,128)(2,1)S(1)} %add_parts.5.a_ref), channel_id=1, source_target_pairs={{0,3},{1,2},{2,1},{3,0},{4,7},{5,6},{6,5},{7,4},{8,11},{9,10},{10,... | collective-permute-start | bytes 768008 | tf_op jit(solution)/shard_map/ppermute | solution.py:378
  29.2 13.6 %copy-start.1 = (bf16[1,2,5,40,320]{4,3,2,1,0:T(8,128)(2,1)S(1)}, bf16[1,2,5,40,320]{4,3,2,1,0:T(8,128)(2,1)}, u32[]{:S(2)}) copy-start(bf16[1,2,5,40,320]{4,3,2,1,0:T(8,128)(2,1)} %param.11) | copy-start | bytes 768004
  29.3 8.5 %collective-permute-start.9 = (bf16[400,320]{1,0:T(8,128)(2,1)S(1)}, bf16[400,320]{1,0:T(8,128)(2,1)S(1)}, u32[]{:S(2)}, u32[]{:S(2)}) collective-permute-start(bf16[400,320]{1,0:T(8,128)(2,1)S(1)} %get-tuple-element.51), channel_id=1, source_target_pairs={{0,1},{1,0},{2,3},{3,2},{4,5},{5,4},{6,7},{7,6},{8,9},{9,8},{10,11... | collective-permute-start | bytes 768008 | tf_op jit(solution)/shard_map/ppermute | solution.py:380
  37.8 12.1 %collective-permute-start.10 = (bf16[400,320]{1,0:T(8,128)(2,1)S(1)}, bf16[400,320]{1,0:T(8,128)(2,1)S(1)}, u32[]{:S(2)}, u32[]{:S(2)}) collective-permute-start(bf16[400,320]{1,0:T(8,128)(2,1)S(1)} %add_parts.7.a_ref), channel_id=1, source_target_pairs={{0,3},{1,2},{2,1},{3,0},{4,7},{5,6},{6,5},{7,4},{8,11},{9,10},{10,... | collective-permute-start | bytes 768008 | tf_op jit(solution)/shard_map/ppermute | solution.py:387
  41.3 13.7 %collective-permute-start.12 = (bf16[400,320]{1,0:T(8,128)(2,1)S(1)}, bf16[400,320]{1,0:T(8,128)(2,1)S(1)}, u32[]{:S(2)}, u32[]{:S(2)}) collective-permute-start(bf16[400,320]{1,0:T(8,128)(2,1)S(1)} %add_parts.6.refs_4_.refs_0_), channel_id=1, source_target_pairs={{0,1},{1,0},{2,3},{3,2},{4,5},{5,4},{6,7},{7,6},{8,9},{9,8},{10,11... | collective-permute-start | bytes 768008 | tf_op jit(solution)/shard_map/ppermute | solution.py:388
  41.3 9.6 %collective-permute-start.13 = (bf16[400,320]{1,0:T(8,128)(2,1)S(1)}, bf16[400,320]{1,0:T(8,128)(2,1)S(1)}, u32[]{:S(2)}, u32[]{:S(2)}) collective-permute-start(bf16[400,320]{1,0:T(8,128)(2,1)S(1)} %add_parts.6.refs_4_.refs_0_), channel_id=1, source_target_pairs={{0,16},{16,0},{1,17},{17,1},{2,18},{18,2},{3,19},{19,3},{4,20},{20... | collective-permute-start | bytes 768008 | tf_op jit(solution)/shard_map/ppermute | solution.py:363
  42.8 8.1 %collective-permute-start.8 = (bf16[2,200,320]{2,1,0:T(8,128)(2,1)S(1)}, bf16[2,200,320]{2,1,0:T(8,128)(2,1)S(1)}, u32[]{:S(2)}, u32[]{:S(2)}) collective-permute-start(bf16[2,200,320]{2,1,0:T(8,128)(2,1)S(1)} %bitcast.5), channel_id=1, source_target_pairs={{0,8},{4,12},{8,0},{12,4},{1,9},{5,13},{9,1},{13,5},{2,10},{6,14},... | collective-permute-start | bytes 768008 | tf_op jit(solution)/shard_map/ppermute | solution.py:390
  44.1 12.4 %collective-permute-start.7 = (bf16[2,200,320]{2,1,0:T(8,128)(2,1)S(1)}, bf16[2,200,320]{2,1,0:T(8,128)(2,1)S(1)}, u32[]{:S(2)}, u32[]{:S(2)}) collective-permute-start(bf16[2,200,320]{2,1,0:T(8,128)(2,1)S(1)} %bitcast.6), channel_id=1, source_target_pairs={{0,4},{4,0},{8,12},{12,8},{1,5},{5,1},{9,13},{13,9},{2,6},{6,2},{1... | collective-permute-start | bytes 768008 | tf_op jit(solution)/shard_map/ppermute | solution.py:389
  50.0 11.6 %copy-start.2 = (bf16[3,320,320]{2,1,0:T(8,128)(2,1)S(1)}, bf16[3,320,320]{2,1,0:T(8,128)(2,1)}, u32[]{:S(2)}) copy-start(bf16[3,320,320]{2,1,0:T(8,128)(2,1)} %refs_4_.3) | copy-start | bytes 1843204
  50.9 5.6 %collective-permute-start.11 = (bf16[2,200,320]{2,1,0:T(8,128)(2,1)S(1)}, bf16[2,200,320]{2,1,0:T(8,128)(2,1)S(1)}, u32[]{:S(2)}, u32[]{:S(2)}) collective-permute-start(bf16[2,200,320]{2,1,0:T(8,128)(2,1)S(1)} %collective-permute-done.8.refs_2_), channel_id=1, source_target_pairs={{0,4},{4,0},{8,12},{12,8},{1,5},{5,1},{9,13},{13,9},{2,6},{6,2},{1... | collective-permute-start | bytes 768008 | tf_op jit(solution)/shard_map/ppermute | solution.py:397
  50.9 10.7 %collective-permute-start.14 = (bf16[400,320]{1,0:T(8,128)(2,1)S(1)}, bf16[400,320]{1,0:T(8,128)(2,1)S(1)}, u32[]{:S(2)}, u32[]{:S(2)}) collective-permute-start(bf16[400,320]{1,0:T(8,128)(2,1)S(1)} %add_parts.8.refs_2_.refs_4_), channel_id=1, source_target_pairs={{0,1},{1,0},{2,3},{3,2},{4,5},{5,4},{6,7},{7,6},{8,9},{9,8},{10,11... | collective-permute-start | bytes 768008 | tf_op jit(solution)/shard_map/ppermute | solution.py:396
  53.7 11.4 %collective-permute-start.17 = (bf16[2,200,320]{2,1,0:T(8,128)(2,1)S(1)}, bf16[2,200,320]{2,1,0:T(8,128)(2,1)S(1)}, u32[]{:S(2)}, u32[]{:S(2)}) collective-permute-start(bf16[2,200,320]{2,1,0:T(8,128)(2,1)S(1)} %collective-permute-done.5.refs_0_), channel_id=1, source_target_pairs={{0,8},{4,12},{8,0},{12,4},{1,9},{5,13},{9,1},{13,5},{2,10},{6,14},... | collective-permute-start | bytes 768008 | tf_op jit(solution)/shard_map/ppermute | solution.py:394
  55.0 10.1 %collective-permute-start.15 = (bf16[400,320]{1,0:T(8,128)(2,1)S(1)}, bf16[400,320]{1,0:T(8,128)(2,1)S(1)}, u32[]{:S(2)}, u32[]{:S(2)}) collective-permute-start(bf16[400,320]{1,0:T(8,128)(2,1)S(1)} %add_parts.8.refs_2_.refs_4_), channel_id=1, source_target_pairs={{0,16},{16,0},{1,17},{17,1},{2,18},{18,2},{3,19},{19,3},{4,20},{20... | collective-permute-start | bytes 768008 | tf_op jit(solution)/shard_map/ppermute | solution.py:363
  63.1 4.1 %collective-permute-start.19 = (bf16[2,200,320]{2,1,0:T(8,128)(2,1)S(1)}, bf16[2,200,320]{2,1,0:T(8,128)(2,1)S(1)}, u32[]{:S(2)}, u32[]{:S(2)}) collective-permute-start(bf16[2,200,320]{2,1,0:T(8,128)(2,1)S(1)} %get-tuple-element.63), channel_id=1, source_target_pairs={{0,4},{4,0},{8,12},{12,8},{1,5},{5,1},{9,13},{13,9},{2,6},{6,2},{1... | collective-permute-start | bytes 768008 | tf_op jit(solution)/shard_map/ppermute | solution.py:406
  63.1 5.8 %collective-permute-start.16 = (bf16[2,200,320]{2,1,0:T(8,128)(2,1)S(1)}, bf16[2,200,320]{2,1,0:T(8,128)(2,1)S(1)}, u32[]{:S(2)}, u32[]{:S(2)}) collective-permute-start(bf16[2,200,320]{2,1,0:T(8,128)(2,1)S(1)} %collective-permute-done.5.refs_0_), channel_id=1, source_target_pairs={{0,4},{4,0},{8,12},{12,8},{1,5},{5,1},{9,13},{13,9},{2,6},{6,2},{1... | collective-permute-start | bytes 768008 | tf_op jit(solution)/shard_map/ppermute | solution.py:393
  63.6 10.1 %collective-permute-start.20 = (bf16[400,320]{1,0:T(8,128)(2,1)S(1)}, bf16[400,320]{1,0:T(8,128)(2,1)S(1)}, u32[]{:S(2)}, u32[]{:S(2)}) collective-permute-start(bf16[400,320]{1,0:T(8,128)(2,1)S(1)} %collective-permute-done.12.refs_5_.refs_1_), channel_id=1, source_target_pairs={{0,16},{16,0},{1,17},{17,1},{2,18},{18,2},{3,19},{19,3},{4,20},{20... | collective-permute-start | bytes 768008 | tf_op jit(solution)/shard_map/ppermute | solution.py:363
  65.1 8.6 %collective-permute-start.18 = (bf16[2,200,320]{2,1,0:T(8,128)(2,1)S(1)}, bf16[2,200,320]{2,1,0:T(8,128)(2,1)S(1)}, u32[]{:S(2)}, u32[]{:S(2)}) collective-permute-start(bf16[2,200,320]{2,1,0:T(8,128)(2,1)S(1)} %collective-permute-done.17.refs_2_), channel_id=1, source_target_pairs={{0,4},{4,0},{8,12},{12,8},{1,5},{5,1},{9,13},{13,9},{2,6},{6,2},{1... | collective-permute-start | bytes 768008 | tf_op jit(solution)/shard_map/ppermute | solution.py:400
  65.1 14.3 %collective-permute-start.21 = (bf16[400,320]{1,0:T(8,128)(2,1)S(1)}, bf16[400,320]{1,0:T(8,128)(2,1)S(1)}, u32[]{:S(2)}, u32[]{:S(2)}) collective-permute-start(bf16[400,320]{1,0:T(8,128)(2,1)S(1)} %collective-permute-done.14.refs_3_.refs_5_), channel_id=1, source_target_pairs={{0,16},{16,0},{1,17},{17,1},{2,18},{18,2},{3,19},{19,3},{4,20},{20... | collective-permute-start | bytes 768008 | tf_op jit(solution)/shard_map/ppermute | solution.py:363
  67.2 14.8 %collective-permute-start.22 = (bf16[2,200,320]{2,1,0:T(8,128)(2,1)S(1)}, bf16[2,200,320]{2,1,0:T(8,128)(2,1)S(1)}, u32[]{:S(2)}, u32[]{:S(2)}) collective-permute-start(bf16[2,200,320]{2,1,0:T(8,128)(2,1)S(1)} %get-tuple-element.69), channel_id=1, source_target_pairs={{0,4},{4,0},{8,12},{12,8},{1,5},{5,1},{9,13},{13,9},{2,6},{6,2},{1... | collective-permute-start | bytes 768008 | tf_op jit(solution)/shard_map/ppermute | solution.py:409
  68.9 13.1 %collective-permute-start.23 = (bf16[2,200,320]{2,1,0:T(8,128)(2,1)S(1)}, bf16[2,200,320]{2,1,0:T(8,128)(2,1)S(1)}, u32[]{:S(2)}, u32[]{:S(2)}) collective-permute-start(bf16[2,200,320]{2,1,0:T(8,128)(2,1)S(1)} %add_parts.9), channel_id=1, source_target_pairs={{0,8},{4,12},{8,0},{12,4},{1,9},{5,13},{9,1},{13,5},{2,10},{6,14},... | collective-permute-start | bytes 768008 | tf_op jit(solution)/shard_map/ppermute | solution.py:411

commit v5 on v4

--- a/solution.py
+++ b/solution.py
@@ -66,6 +66,25 @@
         cost_estimate=cost(1.5),
         name="chip_stats",
     )(own, sibling)
+
+
+def fetch_kernel(x_ref, out_ref, sem):
+    copy = pltpu.make_async_copy(x_ref, out_ref, sem)
+    copy.start()
+    copy.wait()
+
+
+def fetch(x, weight):
+    return pl.pallas_call(
+        fetch_kernel,
+        out_shape=jax.ShapeDtypeStruct(x.shape, x.dtype),
+        in_specs=[any_spec()],
+        out_specs=vmem_spec(),
+        scratch_shapes=[pltpu.SemaphoreType.DMA],
+        compiler_params=params(2),
+        cost_estimate=cost(weight),
+        name="fetch",
+    )(x)
 
 
 def hold_kernel(w_ref, gain_ref, bias_ref, taps_ref, affine_ref, sem):
@@ -107,61 +126,45 @@
     return (z + z // 2) % 2
 
 
-def conv_kernel(x_ref, norm_ref, w_ref, keep_ref, send_ref, cols_ref):
-    n, frames, rows, cols, width = x_ref.shape
-    band = frames * cols
-    odd = held_half()
+def conv_kernel(kept, x_ref, norm_ref, w_ref, out_ref, cols_ref):
+    pairs, frames, rows, cols, width = x_ref.shape
+    band = pairs * cols
+    frame = held_half() if kept else 1 - held_half()
     mean, scale = norm_ref[0:1, :], norm_ref[8:9, :]
     gain, bias = norm_ref[16:17, :], norm_ref[24:25, :]
     column = lax.broadcasted_iota(jnp.int32, (band, width), 0) % cols
-    size = keep_ref.shape[0] // n
-    for j in range(n):
-        cols_ref[j, 0:band, :] = jnp.zeros((band, 3 * width), bf16)
-        cols_ref[j, (rows + 1) * band :, :] = jnp.zeros((band, 3 * width), bf16)
-        for row in range(rows):
-            values = jnp.concatenate([x_ref[j, f, row].astype(f32) for f in range(frames)], axis=0)
-            normed = (values - mean) * scale * gain + bias
-            hidden = normed / (1.0 + jnp.exp(-normed))
-            left = jnp.where(column == 0, 0.0, pltpu.roll(hidden, 1, 0))
-            right = jnp.where(column == cols - 1, 0.0, pltpu.roll(hidden, band - 1, 0))
-            line = [left.astype(bf16), hidden.astype(bf16), right.astype(bf16)]
-            cols_ref[j, (row + 1) * band : (row + 2) * band, :] = jnp.concatenate(line, axis=1)
-        total = None
-        for tap in range(3):
-            window = cols_ref[j, tap * band : (tap + rows) * band, :]
-            term = jnp.dot(window, w_ref[tap], preferred_element_type=f32)
-            total = term if total is None else total + term
-        total = total.reshape(rows, frames, cols, total.shape[-1])
-        half = frames // 2
-        low = total[:, :half].reshape(size, -1)
-        high = total[:, half:].reshape(size, -1)
-        here = slice(j * size, (j + 1) * size)
-
-        @pl.when(odd == 0)
-        def _():
-            keep_ref[here] = low
-            send_ref[here] = high.astype(bf16)
-
-        @pl.when(odd == 1)
-        def _():
-            keep_ref[here] = high
-            send_ref[here] = low.astype(bf16)
-
-
-def pair_conv(pairs, norm, taps, weight):
+    cols_ref[0:band, :] = jnp.zeros((band, 3 * width), bf16)
+    cols_ref[(rows + 1) * band :, :] = jnp.zeros((band, 3 * width), bf16)
+    for row in range(rows):
+        values = jnp.concatenate([x_ref[j, frame, row].astype(f32) for j in range(pairs)], axis=0)
+        normed = (values - mean) * scale * gain + bias
+        hidden = normed / (1.0 + jnp.exp(-normed))
+        left = jnp.where(column == 0, 0.0, pltpu.roll(hidden, 1, 0))
+        right = jnp.where(column == cols - 1, 0.0, pltpu.roll(hidden, band - 1, 0))
+        line = [left.astype(bf16), hidden.astype(bf16), right.astype(bf16)]
+        cols_ref[(row + 1) * band : (row + 2) * band, :] = jnp.concatenate(line, axis=1)
+    total = None
+    for tap in range(3):
+        window = cols_ref[tap * band : (tap + rows) * band, :]
+        term = jnp.dot(window, w_ref[tap], preferred_element_type=f32)
+        total = term if total is None else total + term
+    total = total.reshape(rows, pairs, cols, total.shape[-1])
+    size = rows * cols
+    for j in range(pairs):
+        out_ref[j * size : (j + 1) * size] = total[:, j].reshape(size, -1).astype(out_ref.dtype)
+
+
+def pair_conv(pairs, norm, taps, kept, weight):
     n, frames, rows, cols, width = pairs.shape
     width_out = taps.shape[-1]
-    count = n * frames * rows * cols // 2
-    return pl.pallas_call(
-        conv_kernel,
-        out_shape=(
-            jax.ShapeDtypeStruct((count, width_out), f32),
-            jax.ShapeDtypeStruct((count, width_out), bf16),
-        ),
+    count = n * rows * cols
+    return pl.pallas_call(
+        functools.partial(conv_kernel, kept),
+        out_shape=jax.ShapeDtypeStruct((count, width_out), f32 if kept else bf16),
         in_specs=[vmem_spec()] * 3,
-        out_specs=(vmem_spec(),) * 2,
-        scratch_shapes=[pltpu.VMEM((n, (rows + 2) * frames * cols, 3 * width), bf16)],
-        compiler_params=params(20),
+        out_specs=vmem_spec(),
+        scratch_shapes=[pltpu.VMEM(((rows + 2) * n * cols, 3 * width), bf16)],
+        compiler_params=params(14),
         cost_estimate=cost(weight),
         name="pair_conv",
     )(pairs, norm, taps)
@@ -170,8 +173,10 @@
 PAD = 8
 
 CLAIM = {
+    "fetch": 50.0,
     "merge": 50.0,
     "conv0": 50.0,
+    "keep": 0.0,
     "collect": 0.0,
     "part": 0.0,
     "part0": 80.0,
@@ -363,26 +368,28 @@
         return lax.ppermute(x, "dp", [(0, 1), (1, 0)])
 
     sibling = lax.ppermute(own, "tm", core)
-    st_own, pairs = chip_stats(own, sibling)
+    st_own, pairs = chip_stats(fetch(own, CLAIM["fetch"]), sibling)
     st_chip = lax.ppermute(st_own, "tm", chip)
     taps, affine = hold(spatial_weight.reshape(3, 3 * width, width_out), norm_gain, norm_bias)
     raw_chip = lax.ppermute(tie(own, affine), "tm", chip)
     norm = merge_stats(st_own, st_chip, affine, 2 * frames * count * GROUP_WIDTH, CLAIM["merge"])
 
-    keep0, send0 = pair_conv(pairs, norm, taps, CLAIM["conv0"])
+    send0 = pair_conv(pairs, norm, taps, False, CLAIM["conv0"])
     got0 = lax.ppermute(send0, "mp", near)
-    raw_chip = tie(raw_chip, keep0)
+    keep0 = pair_conv(tie(pairs, send0), norm, taps, True, CLAIM["keep"])
+    raw_chip = tie(raw_chip, send0)
     raw_both = lax.ppermute(raw_chip, "tm", core)
     far_pairs = collect(raw_chip, raw_both, CLAIM["collect"])
     part0 = add16(keep0, got0, CLAIM["part0"])
     came0 = lax.ppermute(part0, "mp", across)
-    keep1, send1 = pair_conv(tie(far_pairs, part0), norm, taps, CLAIM["conv1"])
+    send1 = pair_conv(tie(far_pairs, part0), norm, taps, False, CLAIM["conv1"])
     got1 = lax.ppermute(send1, "mp", near)
+    keep1 = pair_conv(tie(far_pairs, send1), norm, taps, True, CLAIM["keep"])
     cot = cotangent.reshape(frames, count, width)
     theirs, far_cot = [], []
     if pair_clips:
-        far_cot.append(tie(swap(tie(cot, keep0)), keep1))
-    mine0 = add16(tie(part0, keep1, *far_cot), came0, CLAIM["mine"])
+        far_cot.append(tie(swap(tie(cot, send0)), send1))
+    mine0 = add16(tie(part0, send1, *far_cot), came0, CLAIM["mine"])
     part1 = add16(tie(keep1, mine0), got1, CLAIM["part"])
     came1 = lax.ppermute(part1, "mp", across)
     other0 = lax.ppermute(mine0, "mp", near)
@@ -409,16 +416,18 @@
     near_part = lax.ppermute(send, "tm", core)
     to_chip = add16(tie(keep_chip, keep_own), far_part, CLAIM["part"])
     from_chip = lax.ppermute(to_chip, "tm", chip)
-    last = [tie(mine1, to_chip), other1]
-    grad_own = temporal_grads((2, 3), cots, last, (grad_own,), CLAIM["g3"])
     if pair_clips:
-        first = [tie(theirs[0], grad_own), theirs[1]]
+        first = [tie(theirs[0], to_chip), theirs[1]]
         grad_other = temporal_grads((0, 1), far_cot, first, (), CLAIM["g2"])
-        last = [tie(theirs[2], grad_other), theirs[3]]
+        last = [tie(mine1, grad_other), other1]
+        grad_own = temporal_grads((2, 3), cots, last, (grad_own,), CLAIM["g3"])
+        last = [tie(theirs[2], grad_own), theirs[3]]
         temporal_grad = temporal_grads((2, 3), far_cot, last, (grad_other, grad_own), CLAIM["g4"])
+        keep_own = tie(keep_own, temporal_grad)
     else:
+        last = [tie(mine1, to_chip), other1]
+        grad_own = temporal_grads((2, 3), cots, last, (grad_own,), CLAIM["g3"])
         temporal_grad = lax.psum(grad_own, "dp") / clips
-    keep_own = tie(keep_own, temporal_grad)
     block = (keep_own + near_part.astype(f32) + from_chip.astype(f32)).astype(bf16)
     return block.reshape(activations.shape), temporal_grad
 

time: 83 us -> 82.2 us (level)
  starting transfers between devices: 27.2 us -> 24.3 us
  local copies, waits for them, and re-layouts: 0.03 us -> 1.64 us
    ppermute x1, waiting for transfers between devices: 2.85 us -> 0.63 us  [body(): got0 = lax.ppermute(send0, 'mp', near)]
    ppermute x5, starting transfers between devices: 6.58 us -> 4.67 us  [swap(): return lax.ppermute(x, 'dp', [(0, 1), (1, 0)])]
    pallas_call x4, Pallas kernels: 6.72 us -> 8.61 us  [temporal_grads(): pl.pallas_call(functools.partial(grad_kernel, steps, len(pieces), len(add...]
    unnamed x12, local copies, waits for them, and re-layouts: 0.03 us -> 1.64 us
    ppermute x1, waiting for transfers between devices: 2.77 us -> 4.35 us  [body(): came0 = lax.ppermute(part0, 'mp', across)]
    ppermute x1, waiting for transfers between devices: 1.44 us -> 0.35 us  [body(): sibling = lax.ppermute(own, 'tm', core)]
    ppermute x1, waiting for transfers between devices: 5.77 us -> 6.83 us  [body(): came1 = lax.ppermute(part1, 'mp', across)]
    pallas_call x1, Pallas kernels: 2.06 us -> 1.09 us  [chip_stats(): pl.pallas_call(stats_kernel, out_shape=(jax.ShapeDtypeStruct((16, width),...]
  transfers between devices with their start and end apart: 24 -> 24, of which waited for: 11 -> 13; matrix products, arithmetic and copies ran while one was open for 0% -> 0% of each run, Pallas kernels for 21% -> 23%
where the time goes in v5:
time: 82.2 us; the launch traced here: 82 us
  waiting for transfers between devices  34 us (41%)
  starting transfers between devices  24.3 us (30%)
  Pallas kernels  20.4 us (25%)
  local copies, waits for them, and re-layouts  1.64 us (2%)
  other arithmetic  0.86 us (1%)
  between operations  0.83 us (1%)
    pallas_call x4, Pallas kernels, temporal_grads(): pl.pallas_call(functools.partial(grad_kernel, steps, len(pieces), len(add...  8.61 us
    ppermute x5, waiting for transfers between devices, swap(): return lax.ppermute(x, 'dp', [(0, 1), (1, 0)])  7.9 us
    pallas_call x4, Pallas kernels, pair_conv(): pl.pallas_call(functools.partial(conv_kernel, kept), out_shape=jax.ShapeD...  6.93 us
    ppermute x1, waiting for transfers between devices, body(): came1 = lax.ppermute(part1, 'mp', across)  6.83 us
    ppermute x1, waiting for transfers between devices, body(): got1 = lax.ppermute(send1, 'mp', near)  5.25 us
    ppermute x5, starting transfers between devices, swap(): return lax.ppermute(x, 'dp', [(0, 1), (1, 0)])  4.67 us
    ppermute x1, waiting for transfers between devices, body(): came0 = lax.ppermute(part0, 'mp', across)  4.35 us
    ppermute x1, starting transfers between devices, body(): came0 = lax.ppermute(part0, 'mp', across)  3.83 us
  transfers between devices with their start and end apart: 24, of which 13 were waited for; matrix products, arithmetic and copies ran while one was open for 0% of the time, Pallas kernels for 23%

profile of v5, /device:TPU:0, one launch (start us, length us, event | category | flops | bytes accessed | tf_op | source)
XLA Modules:
  0.0 82.0 jit_solution(13399400744414950351)
XLA Ops:
  1.1 1.0 %copy-done.2 = bf16[1,2,5,40,320]{4,3,2,1,0:T(8,128)(2,1)S(1)} copy-done((bf16[1,2,5,40,320]{4,3,2,1,0:T(8,128)(2,1)S(1)}, bf16[1,2,5,40,320]{4,3,2,1,0:T(8,128)(2,1)}, u32[]{:S(2)}) %copy-start.2) | copy-done | bytes 256024
  2.6 1.1 %chip_stats.1 = (f32[16,320]{1,0:T(8,128)S(1)}, bf16[2,2,5,40,320]{4,3,2,1,0:T(8,128)(2,1)S(1)}) custom-call(bf16[2,5,40,320]{3,2,1,0:T(8,128)(2,1)S(1)} %fetch.1.own_ref, bf16[2,5,40,320]{3,2,1,0:T(8,128)(2,1)S(1)} %collective-permute-done.core_ref), custom_call_target="tpu_custom_call" | custom-call | flops 1724999936 | bytes 1 | tf_op jit(solution)/shard_map/chip_stats/pallas_call | solution.py:57
  3.7 2.9 %collective-permute-start.1 = (f32[16,320]{1,0:T(8,128)S(1)}, f32[16,320]{1,0:T(8,128)S(1)}, u32[]{:S(2)}, u32[]{:S(2)}) collective-permute-start(f32[16,320]{1,0:T(8,128)S(1)} %get-tuple-element.35.s0_ref), channel_id=1, source_target_pairs={{0,8},{4,12},{8,0},{12,4},{1,9},{5,13},{9,1},{13,5},{2,10},{6,14},... | collective-permute-start | bytes 61448 | tf_op jit(solution)/shard_map/ppermute | solution.py:372
  6.9 0.6 copy-done.3
  7.6 0.8 collective-permute-done.1.s1_ref
  8.4 1.7 %pair_conv.4 = bf16[400,320]{1,0:T(8,128)(2,1)S(1)} custom-call(bf16[2,2,5,40,320]{4,3,2,1,0:T(8,128)(2,1)S(1)} %get-tuple-element.38.x_ref, f32[32,320]{1,0:T(8,128)S(1)} %merge_stats.1.norm_ref, bf16[3,960,320]{2,1,0:T(8,128)(2,1)S(1)} %get-tuple-element.37.w_ref), custom_call_target="tpu_custom_call" | custom-call | flops 57500000256 | bytes 1 | tf_op jit(solution)/shard_map/pair_conv/pallas_call | solution.py:161
  10.2 2.1 %collective-permute-start.2 = (bf16[400,320]{1,0:T(8,128)(2,1)S(1)}, bf16[400,320]{1,0:T(8,128)(2,1)S(1)}, u32[]{:S(2)}, u32[]{:S(2)}) collective-permute-start(bf16[400,320]{1,0:T(8,128)(2,1)S(1)} %pair_conv.4), channel_id=1, source_target_pairs={{0,1},{1,0},{2,3},{3,2},{4,5},{5,4},{6,7},{7,6},{8,9},{9,8},{10,11... | collective-permute-start | bytes 768008 | tf_op jit(solution)/shard_map/ppermute | solution.py:378
  12.3 1.7 %pair_conv.5.a_ref = f32[400,320]{1,0:T(8,128)S(1)} custom-call(bf16[2,2,5,40,320]{4,3,2,1,0:T(8,128)(2,1)S(1)} %get-tuple-element.38.x_ref, f32[32,320]{1,0:T(8,128)S(1)} %merge_stats.1.norm_ref, bf16[3,960,320]{2,1,0:T(8,128)(2,1)S(1)} %get-tuple-element.37.w_ref), custom_call_target="tpu_custom_call" | custom-call | bytes 1 | tf_op jit(solution)/shard_map/pair_conv/pallas_call | solution.py:161
  14.0 2.6 %collective-permute-done.3.a_ref = bf16[2,5,40,320]{3,2,1,0:T(8,128)(2,1)S(1)} collective-permute-done((bf16[2,5,40,320]{3,2,1,0:T(8,128)(2,1)S(1)}, bf16[2,5,40,320]{3,2,1,0:T(8,128)(2,1)S(1)}, u32[]{:S(2)}, u32[]{:S(2)}) %collective-permute-start.3) | collective-permute-done | bytes 256032 | tf_op jit(solution)/shard_map/ppermute | solution.py:374
  16.6 1.5 %collective-permute-start.5 = (bf16[2,200,320]{2,1,0:T(8,128)(2,1)}, bf16[2,200,320]{2,1,0:T(8,128)(2,1)S(1)}, u32[]{:S(2)}, u32[]{:S(2)}) collective-permute-start(bf16[2,200,320]{2,1,0:T(8,128)(2,1)} %bitcast.2.refs_0_), channel_id=1, source_target_pairs={{0,16},{16,0},{1,17},{17,1},{2,18},{18,2},{3,19},{19,3},{4,20},{20... | collective-permute-start | bytes 768008 | tf_op jit(solution)/shard_map/ppermute | solution.py:368
  18.8 3.8 %collective-permute-start.6 = (bf16[400,320]{1,0:T(8,128)(2,1)S(1)}, bf16[400,320]{1,0:T(8,128)(2,1)S(1)}, u32[]{:S(2)}, u32[]{:S(2)}) collective-permute-start(bf16[400,320]{1,0:T(8,128)(2,1)S(1)} %add_parts.5.a_ref), channel_id=1, source_target_pairs={{0,3},{1,2},{2,1},{3,0},{4,7},{5,6},{6,5},{7,4},{8,11},{9,10},{10,... | collective-permute-start | bytes 768008 | tf_op jit(solution)/shard_map/ppermute | solution.py:384
  22.7 1.7 %pair_conv.6 = bf16[400,320]{1,0:T(8,128)(2,1)S(1)} custom-call(bf16[2,2,5,40,320]{4,3,2,1,0:T(8,128)(2,1)S(1)} %collect_pairs.1.x_ref, f32[32,320]{1,0:T(8,128)S(1)} %merge_stats.1.norm_ref, bf16[3,960,320]{2,1,0:T(8,128)(2,1)S(1)} %get-tuple-element.37.w_ref), custom_call_target="tpu_custom_call" | custom-call | flops 1150000000 | bytes 1 | tf_op jit(solution)/shard_map/pair_conv/pallas_call | solution.py:161
  24.5 1.7 %pair_conv.7.a_ref = f32[400,320]{1,0:T(8,128)S(1)} custom-call(bf16[2,2,5,40,320]{4,3,2,1,0:T(8,128)(2,1)S(1)} %collect_pairs.1.x_ref, f32[32,320]{1,0:T(8,128)S(1)} %merge_stats.1.norm_ref, bf16[3,960,320]{2,1,0:T(8,128)(2,1)S(1)} %get-tuple-element.37.w_ref), custom_call_target="tpu_custom_call" | custom-call | bytes 1 | tf_op jit(solution)/shard_map/pair_conv/pallas_call | solution.py:161
  26.5 4.4 %collective-permute-done.6.b_ref = bf16[400,320]{1,0:T(8,128)(2,1)S(1)} collective-permute-done((bf16[400,320]{1,0:T(8,128)(2,1)S(1)}, bf16[400,320]{1,0:T(8,128)(2,1)S(1)}, u32[]{:S(2)}, u32[]{:S(2)}) %collective-permute-start.6) | collective-permute-done | bytes 256032 | tf_op jit(solution)/shard_map/ppermute | solution.py:384
  30.9 5.3 %collective-permute-done.9.b_ref = bf16[400,320]{1,0:T(8,128)(2,1)S(1)} collective-permute-done((bf16[400,320]{1,0:T(8,128)(2,1)S(1)}, bf16[400,320]{1,0:T(8,128)(2,1)S(1)}, u32[]{:S(2)}, u32[]{:S(2)}) %collective-permute-start.9) | collective-permute-done | bytes 256032 | tf_op jit(solution)/shard_map/ppermute | solution.py:386
  36.3 3.6 %collective-permute-start.10 = (bf16[400,320]{1,0:T(8,128)(2,1)S(1)}, bf16[400,320]{1,0:T(8,128)(2,1)S(1)}, u32[]{:S(2)}, u32[]{:S(2)}) collective-permute-start(bf16[400,320]{1,0:T(8,128)(2,1)S(1)} %add_parts.7.a_ref), channel_id=1, source_target_pairs={{0,3},{1,2},{2,1},{3,0},{4,7},{5,6},{6,5},{7,4},{8,11},{9,10},{10,... | collective-permute-start | bytes 768008 | tf_op jit(solution)/shard_map/ppermute | solution.py:394
  40.4 1.1 %collective-permute-start.8 = (bf16[2,200,320]{2,1,0:T(8,128)(2,1)}, bf16[2,200,320]{2,1,0:T(8,128)(2,1)S(1)}, u32[]{:S(2)}, u32[]{:S(2)}) collective-permute-start(bf16[2,200,320]{2,1,0:T(8,128)(2,1)} %bitcast.2.refs_0_), channel_id=1, source_target_pairs={{0,8},{4,12},{8,0},{12,4},{1,9},{5,13},{9,1},{13,5},{2,10},{6,14},... | collective-permute-start | bytes 768008 | tf_op jit(solution)/shard_map/ppermute | solution.py:397
  41.5 6.8 %collective-permute-done.10.b_ref = bf16[400,320]{1,0:T(8,128)(2,1)S(1)} collective-permute-done((bf16[400,320]{1,0:T(8,128)(2,1)S(1)}, bf16[400,320]{1,0:T(8,128)(2,1)S(1)}, u32[]{:S(2)}, u32[]{:S(2)}) %collective-permute-start.10) | collective-permute-done | bytes 256032 | tf_op jit(solution)/shard_map/ppermute | solution.py:394
  48.4 0.8 collective-permute-done.8.refs_2_
  49.3 3.5 %collective-permute-start.14 = (bf16[400,320]{1,0:T(8,128)(2,1)S(1)}, bf16[400,320]{1,0:T(8,128)(2,1)S(1)}, u32[]{:S(2)}, u32[]{:S(2)}) collective-permute-start(bf16[400,320]{1,0:T(8,128)(2,1)S(1)} %add_parts.8.refs_2_.refs_4_), channel_id=1, source_target_pairs={{0,1},{1,0},{2,3},{3,2},{4,5},{5,4},{6,7},{7,6},{8,9},{9,8},{10,11... | collective-permute-start | bytes 768008 | tf_op jit(solution)/shard_map/ppermute | solution.py:403
  53.3 0.7 collective-permute-done.12.refs_5_.refs_1_
  54.6 2.3 %temporal_grads.4.refs_6_ = f32[3,320,320]{2,1,0:T(8,128)S(1)} custom-call(bf16[2,200,320]{2,1,0:T(8,128)(2,1)} %bitcast.2.refs_0_, bf16[2,200,320]{2,1,0:T(8,128)(2,1)S(1)} %collective-permute-done.7.refs_1_, bf16[2,200,320]{2,1,0:T(8,128)(2,1)S(1)} %collective-permute-done.8.refs_2_, bf16[2,200,320]{2,1,0:T(8,128)(2,1)S(1)} %collective-permute-done.11.refs_3_, ...), custom_call_target="tpu_custom_call" | custom-call | bytes 1 | tf_op jit(solution)/shard_map/temporal_grads/pallas_call | solution.py:246
  56.9 3.8 %collective-permute-done.14.refs_3_.refs_5_ = bf16[400,320]{1,0:T(8,128)(2,1)S(1)} collective-permute-done((bf16[400,320]{1,0:T(8,128)(2,1)S(1)}, bf16[400,320]{1,0:T(8,128)(2,1)S(1)}, u32[]{:S(2)}, u32[]{:S(2)}) %collective-permute-start.14) | collective-permute-done | bytes 256032 | tf_op jit(solution)/shard_map/ppermute | solution.py:403
  60.6 1.5 %temporal_conv.2 = (bf16[2,200,320]{2,1,0:T(8,128)(2,1)S(1)}, f32[2,200,320]{2,1,0:T(8,128)S(1)}) custom-call(bf16[400,320]{1,0:T(8,128)(2,1)S(1)} %add_parts.6.refs_4_.refs_0_, bf16[400,320]{1,0:T(8,128)(2,1)S(1)} %collective-permute-done.12.refs_5_.refs_1_, bf16[400,320]{1,0:T(8,128)(2,1)S(1)} %add_parts.8.refs_2_.refs_4_, ...), custom_call_target="tpu_custom_call" | custom-call | flops 57500000256 | bytes 1 | tf_op jit(solution)/shard_map/temporal_conv/pallas_call | solution.py:279
  63.3 1.5 %collective-permute-start.21 = (bf16[400,320]{1,0:T(8,128)(2,1)S(1)}, bf16[400,320]{1,0:T(8,128)(2,1)S(1)}, u32[]{:S(2)}, u32[]{:S(2)}) collective-permute-start(bf16[400,320]{1,0:T(8,128)(2,1)S(1)} %collective-permute-done.14.refs_3_.refs_5_), channel_id=1, source_target_pairs={{0,16},{16,0},{1,17},{17,1},{2,18},{18,2},{3,19},{19,3},{4,20},{20... | collective-permute-start | bytes 768008 | tf_op jit(solution)/shard_map/ppermute | solution.py:368
  64.8 1.5 %temporal_conv.3 = (bf16[2,200,320]{2,1,0:T(8,128)(2,1)S(1)}, f32[2,200,320]{2,1,0:T(8,128)S(1)}) custom-call(bf16[400,320]{1,0:T(8,128)(2,1)S(1)} %add_parts.6.refs_4_.refs_0_, bf16[400,320]{1,0:T(8,128)(2,1)S(1)} %collective-permute-done.12.refs_5_.refs_1_, bf16[400,320]{1,0:T(8,128)(2,1)S(1)} %add_parts.8.refs_2_.refs_4_, ...), custom_call_target="tpu_custom_call" | custom-call | bytes 1 | tf_op jit(solution)/shard_map/temporal_conv/pallas_call | solution.py:279
  67.1 5.7 %collective-permute-done.20.refs_5_ = bf16[400,320]{1,0:T(8,128)(2,1)S(1)} collective-permute-done((bf16[400,320]{1,0:T(8,128)(2,1)S(1)}, bf16[400,320]{1,0:T(8,128)(2,1)S(1)}, u32[]{:S(2)}, u32[]{:S(2)}) %collective-permute-start.20) | collective-permute-done | bytes 256032 | tf_op jit(solution)/shard_map/ppermute | solution.py:368
  72.8 1.4 %temporal_grads.5.refs_6_ = f32[3,320,320]{2,1,0:T(8,128)S(1)} custom-call(bf16[2,200,320]{2,1,0:T(8,128)(2,1)S(1)} %collective-permute-done.5.refs_0_, bf16[2,200,320]{2,1,0:T(8,128)(2,1)S(1)} %collective-permute-done.16.refs_1_, bf16[2,200,320]{2,1,0:T(8,128)(2,1)S(1)} %collective-permute-done.17.refs_2_, ...), custom_call_target="tpu_custom_call" | custom-call | bytes 1 | tf_op jit(solution)/shard_map/temporal_grads/pallas_call | solution.py:246
  74.2 2.4 %temporal_grads.6.refs_7_ = f32[3,320,320]{2,1,0:T(8,128)S(1)} custom-call(bf16[2,200,320]{2,1,0:T(8,128)(2,1)} %bitcast.2.refs_0_, bf16[2,200,320]{2,1,0:T(8,128)(2,1)S(1)} %collective-permute-done.7.refs_1_, bf16[2,200,320]{2,1,0:T(8,128)(2,1)S(1)} %collective-permute-done.8.refs_2_, bf16[2,200,320]{2,1,0:T(8,128)(2,1)S(1)} %collective-permute-done.11.refs_3_, ...), custom_call_target="tpu_custom_call" | custom-call | bytes 1 | tf_op jit(solution)/shard_map/temporal_grads/pallas_call | solution.py:246
  76.6 2.0 %collective-permute-done.21.refs_5_ = bf16[400,320]{1,0:T(8,128)(2,1)S(1)} collective-permute-done((bf16[400,320]{1,0:T(8,128)(2,1)S(1)}, bf16[400,320]{1,0:T(8,128)(2,1)S(1)}, u32[]{:S(2)}, u32[]{:S(2)}) %collective-permute-start.21) | collective-permute-done | bytes 256032 | tf_op jit(solution)/shard_map/ppermute | solution.py:368
  78.5 2.6 %temporal_grads.7 = f32[3,320,320]{2,1,0:T(8,128)} custom-call(bf16[2,200,320]{2,1,0:T(8,128)(2,1)S(1)} %collective-permute-done.5.refs_0_, bf16[2,200,320]{2,1,0:T(8,128)(2,1)S(1)} %collective-permute-done.16.refs_1_, bf16[2,200,320]{2,1,0:T(8,128)(2,1)S(1)} %collective-permute-done.17.refs_2_, bf16[2,200,320]{2,1,0:T(8,128)(2,1)S(1)} %collective-permute-done.18.refs_3_, ...), custom_call_target="tpu_custom_call" | custom-call | flops 57500000256 | bytes 1 | tf_op jit(solution)/shard_map/temporal_grads/pallas_call | solution.py:246
  81.1 0.9 %add_convert_fusion = bf16[2,200,320]{2,1,0:T(8,128)(2,1)} fusion(bf16[2,200,320]{2,1,0:T(8,128)(2,1)S(1)} %collective-permute-done.23, f32[2,200,320]{2,1,0:T(8,128)S(1)} %get-tuple-element.64, bf16[2,200,320]{2,1,0:T(8,128)(2,1)S(1)} %collective-permute-done.22), kind=kLoop, calls=%fused_computation | loop fusion | flops 640000 | bytes 1280000 | tf_op jit(solution)/shard_map/convert_element_type | solution.py:431
  (49 shorter events, 6.3 us)
Async XLA Ops:
  0.6 2.0 %collective-permute-start = (bf16[2,5,40,320]{3,2,1,0:T(8,128)(2,1)}, bf16[2,5,40,320]{3,2,1,0:T(8,128)(2,1)S(1)}, u32[]{:S(2)}, u32[]{:S(2)}) collective-permute-start(bf16[2,5,40,320]{3,2,1,0:T(8,128)(2,1)} %bitcast.5), channel_id=1, source_target_pairs={{0,4},{4,0},{8,12},{12,8},{1,5},{5,1},{9,13},{13,9},{2,6},{6,2},{1... | collective-permute-start | bytes 768008 | tf_op jit(solution)/shard_map/ppermute | solution.py:370
  1.1 1.0 %copy-start.2 = (bf16[1,2,5,40,320]{4,3,2,1,0:T(8,128)(2,1)S(1)}, bf16[1,2,5,40,320]{4,3,2,1,0:T(8,128)(2,1)}, u32[]{:S(2)}) copy-start(bf16[1,2,5,40,320]{4,3,2,1,0:T(8,128)(2,1)} %param.6) | copy-start | bytes 768004
  2.2 4.4 %copy-start.1 = (bf16[9,320,320]{2,1,0:T(8,128)(2,1)S(1)}, bf16[9,320,320]{2,1,0:T(8,128)(2,1)}, u32[]{:S(2)}) copy-start(bf16[9,320,320]{2,1,0:T(8,128)(2,1)} %param.9) | copy-start | bytes 5529604
  2.2 4.4 %copy-start.4 = (f32[320]{0:T(512)S(1)}, f32[320]{0:T(512)}, u32[]{:S(2)}) copy-start(f32[320]{0:T(512)} %gain_ref.1) | copy-start | bytes 3844
  2.2 4.4 %copy-start.5 = (f32[320]{0:T(512)S(1)}, f32[320]{0:T(512)}, u32[]{:S(2)}) copy-start(f32[320]{0:T(512)} %bias_ref.1) | copy-start | bytes 3844
  3.7 4.7 %collective-permute-start.1 = (f32[16,320]{1,0:T(8,128)S(1)}, f32[16,320]{1,0:T(8,128)S(1)}, u32[]{:S(2)}, u32[]{:S(2)}) collective-permute-start(f32[16,320]{1,0:T(8,128)S(1)} %get-tuple-element.35.s0_ref), channel_id=1, source_target_pairs={{0,8},{4,12},{8,0},{12,4},{1,9},{5,13},{9,1},{13,5},{2,10},{6,14},... | collective-permute-start | bytes 61448 | tf_op jit(solution)/shard_map/ppermute | solution.py:372
  6.6 1.0 %copy-start.3 = (bf16[1,2,5,40,320]{4,3,2,1,0:T(8,128)(2,1)S(1)}, bf16[1,2,5,40,320]{4,3,2,1,0:T(8,128)(2,1)}, u32[]{:S(2)}) copy-start(bf16[1,2,5,40,320]{4,3,2,1,0:T(8,128)(2,1)} %param.6) | copy-start | bytes 768004
  7.6 9.0 %collective-permute-start.3 = (bf16[2,5,40,320]{3,2,1,0:T(8,128)(2,1)S(1)}, bf16[2,5,40,320]{3,2,1,0:T(8,128)(2,1)S(1)}, u32[]{:S(2)}, u32[]{:S(2)}) collective-permute-start(bf16[2,5,40,320]{3,2,1,0:T(8,128)(2,1)S(1)} %bitcast.7), channel_id=1, source_target_pairs={{0,8},{4,12},{8,0},{12,4},{1,9},{5,13},{9,1},{13,5},{2,10},{6,14},... | collective-permute-start | bytes 768008 | tf_op jit(solution)/shard_map/ppermute | solution.py:374
  10.2 8.6 %collective-permute-start.2 = (bf16[400,320]{1,0:T(8,128)(2,1)S(1)}, bf16[400,320]{1,0:T(8,128)(2,1)S(1)}, u32[]{:S(2)}, u32[]{:S(2)}) collective-permute-start(bf16[400,320]{1,0:T(8,128)(2,1)S(1)} %pair_conv.4), channel_id=1, source_target_pairs={{0,1},{1,0},{2,3},{3,2},{4,5},{5,4},{6,7},{7,6},{8,9},{9,8},{10,11... | collective-permute-start | bytes 768008 | tf_op jit(solution)/shard_map/ppermute | solution.py:378
  16.6 6.0 %collective-permute-start.4 = (bf16[2,5,40,320]{3,2,1,0:T(8,128)(2,1)S(1)}, bf16[2,5,40,320]{3,2,1,0:T(8,128)(2,1)S(1)}, u32[]{:S(2)}, u32[]{:S(2)}) collective-permute-start(bf16[2,5,40,320]{3,2,1,0:T(8,128)(2,1)S(1)} %collective-permute-done.3.a_ref), channel_id=1, source_target_pairs={{0,4},{4,0},{8,12},{12,8},{1,5},{5,1},{9,13},{13,9},{2,6},{6,2},{1... | collective-permute-start | bytes 768008 | tf_op jit(solution)/shard_map/ppermute | solution.py:381
  16.6 9.9 %collective-permute-start.5 = (bf16[2,200,320]{2,1,0:T(8,128)(2,1)}, bf16[2,200,320]{2,1,0:T(8,128)(2,1)S(1)}, u32[]{:S(2)}, u32[]{:S(2)}) collective-permute-start(bf16[2,200,320]{2,1,0:T(8,128)(2,1)} %bitcast.2.refs_0_), channel_id=1, source_target_pairs={{0,16},{16,0},{1,17},{17,1},{2,18},{18,2},{3,19},{19,3},{4,20},{20... | collective-permute-start | bytes 768008 | tf_op jit(solution)/shard_map/ppermute | solution.py:368
  18.8 12.0 %collective-permute-start.6 = (bf16[400,320]{1,0:T(8,128)(2,1)S(1)}, bf16[400,320]{1,0:T(8,128)(2,1)S(1)}, u32[]{:S(2)}, u32[]{:S(2)}) collective-permute-start(bf16[400,320]{1,0:T(8,128)(2,1)S(1)} %add_parts.5.a_ref), channel_id=1, source_target_pairs={{0,3},{1,2},{2,1},{3,0},{4,7},{5,6},{6,5},{7,4},{8,11},{9,10},{10,... | collective-permute-start | bytes 768008 | tf_op jit(solution)/shard_map/ppermute | solution.py:384
  24.4 11.7 %collective-permute-start.9 = (bf16[400,320]{1,0:T(8,128)(2,1)S(1)}, bf16[400,320]{1,0:T(8,128)(2,1)S(1)}, u32[]{:S(2)}, u32[]{:S(2)}) collective-permute-start(bf16[400,320]{1,0:T(8,128)(2,1)S(1)} %pair_conv.6), channel_id=1, source_target_pairs={{0,1},{1,0},{2,3},{3,2},{4,5},{5,4},{6,7},{7,6},{8,9},{9,8},{10,11... | collective-permute-start | bytes 768008 | tf_op jit(solution)/shard_map/ppermute | solution.py:386
  36.3 12.1 %collective-permute-start.10 = (bf16[400,320]{1,0:T(8,128)(2,1)S(1)}, bf16[400,320]{1,0:T(8,128)(2,1)S(1)}, u32[]{:S(2)}, u32[]{:S(2)}) collective-permute-start(bf16[400,320]{1,0:T(8,128)(2,1)S(1)} %add_parts.7.a_ref), channel_id=1, source_target_pairs={{0,3},{1,2},{2,1},{3,0},{4,7},{5,6},{6,5},{7,4},{8,11},{9,10},{10,... | collective-permute-start | bytes 768008 | tf_op jit(solution)/shard_map/ppermute | solution.py:394
  39.9 14.1 %collective-permute-start.12 = (bf16[400,320]{1,0:T(8,128)(2,1)S(1)}, bf16[400,320]{1,0:T(8,128)(2,1)S(1)}, u32[]{:S(2)}, u32[]{:S(2)}) collective-permute-start(bf16[400,320]{1,0:T(8,128)(2,1)S(1)} %add_parts.6.refs_4_.refs_0_), channel_id=1, source_target_pairs={{0,1},{1,0},{2,3},{3,2},{4,5},{5,4},{6,7},{7,6},{8,9},{9,8},{10,11... | collective-permute-start | bytes 768008 | tf_op jit(solution)/shard_map/ppermute | solution.py:395
  39.9 9.4 %collective-permute-start.13 = (bf16[400,320]{1,0:T(8,128)(2,1)S(1)}, bf16[400,320]{1,0:T(8,128)(2,1)S(1)}, u32[]{:S(2)}, u32[]{:S(2)}) collective-permute-start(bf16[400,320]{1,0:T(8,128)(2,1)S(1)} %add_parts.6.refs_4_.refs_0_), channel_id=1, source_target_pairs={{0,16},{16,0},{1,17},{17,1},{2,18},{18,2},{3,19},{19,3},{4,20},{20... | collective-permute-start | bytes 768008 | tf_op jit(solution)/shard_map/ppermute | solution.py:368
  40.4 8.8 %collective-permute-start.8 = (bf16[2,200,320]{2,1,0:T(8,128)(2,1)}, bf16[2,200,320]{2,1,0:T(8,128)(2,1)S(1)}, u32[]{:S(2)}, u32[]{:S(2)}) collective-permute-start(bf16[2,200,320]{2,1,0:T(8,128)(2,1)} %bitcast.2.refs_0_), channel_id=1, source_target_pairs={{0,8},{4,12},{8,0},{12,4},{1,9},{5,13},{9,1},{13,5},{2,10},{6,14},... | collective-permute-start | bytes 768008 | tf_op jit(solution)/shard_map/ppermute | solution.py:397
  41.5 13.0 %collective-permute-start.7 = (bf16[2,200,320]{2,1,0:T(8,128)(2,1)}, bf16[2,200,320]{2,1,0:T(8,128)(2,1)S(1)}, u32[]{:S(2)}, u32[]{:S(2)}) collective-permute-start(bf16[2,200,320]{2,1,0:T(8,128)(2,1)} %bitcast.2.refs_0_), channel_id=1, source_target_pairs={{0,4},{4,0},{8,12},{12,8},{1,5},{5,1},{9,13},{13,9},{2,6},{6,2},{1... | collective-permute-start | bytes 768008 | tf_op jit(solution)/shard_map/ppermute | solution.py:396
  48.4 12.2 %copy-start = (bf16[3,320,320]{2,1,0:T(8,128)(2,1)S(1)}, bf16[3,320,320]{2,1,0:T(8,128)(2,1)}, u32[]{:S(2)}) copy-start(bf16[3,320,320]{2,1,0:T(8,128)(2,1)} %refs_4_.3) | copy-start | bytes 1843204
  49.3 5.3 %collective-permute-start.11 = (bf16[2,200,320]{2,1,0:T(8,128)(2,1)S(1)}, bf16[2,200,320]{2,1,0:T(8,128)(2,1)S(1)}, u32[]{:S(2)}, u32[]{:S(2)}) collective-permute-start(bf16[2,200,320]{2,1,0:T(8,128)(2,1)S(1)} %collective-permute-done.8.refs_2_), channel_id=1, source_target_pairs={{0,4},{4,0},{8,12},{12,8},{1,5},{5,1},{9,13},{13,9},{2,6},{6,2},{1... | collective-permute-start | bytes 768008 | tf_op jit(solution)/shard_map/ppermute | solution.py:404
  49.3 11.4 %collective-permute-start.14 = (bf16[400,320]{1,0:T(8,128)(2,1)S(1)}, bf16[400,320]{1,0:T(8,128)(2,1)S(1)}, u32[]{:S(2)}, u32[]{:S(2)}) collective-permute-start(bf16[400,320]{1,0:T(8,128)(2,1)S(1)} %add_parts.8.refs_2_.refs_4_), channel_id=1, source_target_pairs={{0,1},{1,0},{2,3},{3,2},{4,5},{5,4},{6,7},{7,6},{8,9},{9,8},{10,11... | collective-permute-start | bytes 768008 | tf_op jit(solution)/shard_map/ppermute | solution.py:403
  52.8 10.5 %collective-permute-start.17 = (bf16[2,200,320]{2,1,0:T(8,128)(2,1)S(1)}, bf16[2,200,320]{2,1,0:T(8,128)(2,1)S(1)}, u32[]{:S(2)}, u32[]{:S(2)}) collective-permute-start(bf16[2,200,320]{2,1,0:T(8,128)(2,1)S(1)} %collective-permute-done.5.refs_0_), channel_id=1, source_target_pairs={{0,8},{4,12},{8,0},{12,4},{1,9},{5,13},{9,1},{13,5},{2,10},{6,14},... | collective-permute-start | bytes 768008 | tf_op jit(solution)/shard_map/ppermute | solution.py:401
  54.0 9.3 %collective-permute-start.15 = (bf16[400,320]{1,0:T(8,128)(2,1)S(1)}, bf16[400,320]{1,0:T(8,128)(2,1)S(1)}, u32[]{:S(2)}, u32[]{:S(2)}) collective-permute-start(bf16[400,320]{1,0:T(8,128)(2,1)S(1)} %add_parts.8.refs_2_.refs_4_), channel_id=1, source_target_pairs={{0,16},{16,0},{1,17},{17,1},{2,18},{18,2},{3,19},{19,3},{4,20},{20... | collective-permute-start | bytes 768008 | tf_op jit(solution)/shard_map/ppermute | solution.py:368
  62.1 4.1 %collective-permute-start.19 = (bf16[2,200,320]{2,1,0:T(8,128)(2,1)S(1)}, bf16[2,200,320]{2,1,0:T(8,128)(2,1)S(1)}, u32[]{:S(2)}, u32[]{:S(2)}) collective-permute-start(bf16[2,200,320]{2,1,0:T(8,128)(2,1)S(1)} %get-tuple-element.59), channel_id=1, source_target_pairs={{0,4},{4,0},{8,12},{12,8},{1,5},{5,1},{9,13},{13,9},{2,6},{6,2},{1... | collective-permute-start | bytes 768008 | tf_op jit(solution)/shard_map/ppermute | solution.py:413
  62.2 4.4 %collective-permute-start.16 = (bf16[2,200,320]{2,1,0:T(8,128)(2,1)S(1)}, bf16[2,200,320]{2,1,0:T(8,128)(2,1)S(1)}, u32[]{:S(2)}, u32[]{:S(2)}) collective-permute-start(bf16[2,200,320]{2,1,0:T(8,128)(2,1)S(1)} %collective-permute-done.5.refs_0_), channel_id=1, source_target_pairs={{0,4},{4,0},{8,12},{12,8},{1,5},{5,1},{9,13},{13,9},{2,6},{6,2},{1... | collective-permute-start | bytes 768008 | tf_op jit(solution)/shard_map/ppermute | solution.py:400
  62.7 10.1 %collective-permute-start.20 = (bf16[400,320]{1,0:T(8,128)(2,1)S(1)}, bf16[400,320]{1,0:T(8,128)(2,1)S(1)}, u32[]{:S(2)}, u32[]{:S(2)}) collective-permute-start(bf16[400,320]{1,0:T(8,128)(2,1)S(1)} %collective-permute-done.12.refs_5_.refs_1_), channel_id=1, source_target_pairs={{0,16},{16,0},{1,17},{17,1},{2,18},{18,2},{3,19},{19,3},{4,20},{20... | collective-permute-start | bytes 768008 | tf_op jit(solution)/shard_map/ppermute | solution.py:368
  63.3 9.6 %collective-permute-start.18 = (bf16[2,200,320]{2,1,0:T(8,128)(2,1)S(1)}, bf16[2,200,320]{2,1,0:T(8,128)(2,1)S(1)}, u32[]{:S(2)}, u32[]{:S(2)}) collective-permute-start(bf16[2,200,320]{2,1,0:T(8,128)(2,1)S(1)} %collective-permute-done.17.refs_2_), channel_id=1, source_target_pairs={{0,4},{4,0},{8,12},{12,8},{1,5},{5,1},{9,13},{13,9},{2,6},{6,2},{1... | collective-permute-start | bytes 768008 | tf_op jit(solution)/shard_map/ppermute | solution.py:407
  63.3 15.3 %collective-permute-start.21 = (bf16[400,320]{1,0:T(8,128)(2,1)S(1)}, bf16[400,320]{1,0:T(8,128)(2,1)S(1)}, u32[]{:S(2)}, u32[]{:S(2)}) collective-permute-start(bf16[400,320]{1,0:T(8,128)(2,1)S(1)} %collective-permute-done.14.refs_3_.refs_5_), channel_id=1, source_target_pairs={{0,16},{16,0},{1,17},{17,1},{2,18},{18,2},{3,19},{19,3},{4,20},{20... | collective-permute-start | bytes 768008 | tf_op jit(solution)/shard_map/ppermute | solution.py:368
  66.3 14.8 %collective-permute-start.22 = (bf16[2,200,320]{2,1,0:T(8,128)(2,1)S(1)}, bf16[2,200,320]{2,1,0:T(8,128)(2,1)S(1)}, u32[]{:S(2)}, u32[]{:S(2)}) collective-permute-start(bf16[2,200,320]{2,1,0:T(8,128)(2,1)S(1)} %get-tuple-element.65), channel_id=1, source_target_pairs={{0,4},{4,0},{8,12},{12,8},{1,5},{5,1},{9,13},{13,9},{2,6},{6,2},{1... | collective-permute-start | bytes 768008 | tf_op jit(solution)/shard_map/ppermute | solution.py:416
  66.6 14.5 %collective-permute-start.23 = (bf16[2,200,320]{2,1,0:T(8,128)(2,1)S(1)}, bf16[2,200,320]{2,1,0:T(8,128)(2,1)S(1)}, u32[]{:S(2)}, u32[]{:S(2)}) collective-permute-start(bf16[2,200,320]{2,1,0:T(8,128)(2,1)S(1)} %add_parts.9), channel_id=1, source_target_pairs={{0,8},{4,12},{8,0},{12,4},{1,9},{5,13},{9,1},{13,5},{2,10},{6,14},... | collective-permute-start | bytes 768008 | tf_op jit(solution)/shard_map/ppermute | solution.py:418

commit v6 on v5

--- a/solution.py
+++ b/solution.py
@@ -84,6 +84,22 @@
         compiler_params=params(2),
         cost_estimate=cost(weight),
         name="fetch",
+    )(x)
+
+
+def copy_kernel(x_ref, out_ref):
+    out_ref[...] = x_ref[...]
+
+
+def copy(x, weight):
+    return pl.pallas_call(
+        copy_kernel,
+        out_shape=jax.ShapeDtypeStruct(x.shape, x.dtype),
+        in_specs=[vmem_spec()],
+        out_specs=vmem_spec(),
+        compiler_params=params(4),
+        cost_estimate=cost(weight),
+        name="copy_piece",
     )(x)
 
 
@@ -177,13 +193,14 @@
     "merge": 50.0,
     "conv0": 50.0,
     "keep": 0.0,
+    "copy": 1.0,
     "collect": 0.0,
     "part": 0.0,
     "part0": 80.0,
     "conv1": 1.0,
     "mine": 50.0,
     "t1": 50.0,
-    "g1": 0.0,
+    "g1": 1.0,
     "t2": 0.0,
     "g2": 0.0,
     "g3": 0.0,
@@ -215,6 +232,8 @@
 
 
 def grad_kernel(steps, held, extra, *refs):
+    if extra:
+        *refs, made_ref, sems = refs
     cots, pieces, added = refs[:4], refs[4 : 4 + held], refs[4 + held : -3]
     out_ref, s_ref, c_ref = refs[-3:]
     t = lax.axis_index("tm")
@@ -229,41 +248,53 @@
     chip = t // 2 if steps[0] == 0 else 1 - t // 2
     first, length = 1 + 4 * chip, 4
     turned = s_ref[pl.ds(first, length)].reshape(length * rows, width).T
+    stores = []
     for k in range(3):
         cot = c_ref[pl.ds(first + 1 - k, length)].reshape(length * rows, -1)
         total = jnp.dot(turned, cot, preferred_element_type=f32)
-        if added:
-            total = added[0][k] + total
         if extra:
-            total = (total + added[1][k]) * 0.5
-        out_ref[k] = total
+            made_ref[k] = ((added[0][k] + total) + added[1][k]) * 0.5
+            stores.append(pltpu.make_async_copy(made_ref.at[k], out_ref.at[k], sems.at[k]))
+            stores[k].start()
+        elif added:
+            out_ref[k] = added[0][k] + total
+        else:
+            out_ref[k] = total
+    for store in stores:
+        store.wait()
 
 
 def temporal_grads(steps, cots, pieces, added, weight):
     count, width_out = cots[0].shape[-2:]
     width = pieces[0].shape[-1]
+    extra = len(added) == 2
     operands = (*cots, *pieces, *added)
-    return pl.pallas_call(
-        functools.partial(grad_kernel, steps, len(pieces), len(added) == 2),
+    scratch = [
+        pltpu.VMEM((10, count + PAD, width), bf16),
+        pltpu.VMEM((10, count + PAD, width_out), bf16),
+    ]
+    in_specs = [vmem_spec()] * len(operands)
+    if extra:
+        scratch += [pltpu.VMEM((3, width, width_out), f32), pltpu.SemaphoreType.DMA((3,))]
+    return pl.pallas_call(
+        functools.partial(grad_kernel, steps, len(pieces), extra),
         out_shape=jax.ShapeDtypeStruct((3, width, width_out), f32),
-        in_specs=[vmem_spec()] * len(operands),
-        out_specs=vmem_spec(),
-        scratch_shapes=[
-            pltpu.VMEM((10, count + PAD, width), bf16),
-            pltpu.VMEM((10, count + PAD, width_out), bf16),
-        ],
-        compiler_params=params(14),
+        in_specs=in_specs,
+        out_specs=any_spec() if extra else vmem_spec(),
+        scratch_shapes=scratch,
+        compiler_params=params(20 if extra else 14),
         cost_estimate=cost(weight),
         name="temporal_grads",
     )(*operands)
 
 
 def temporal_kernel(steps, blocks, *refs):
-    *pieces, w_ref, send_ref, keep_ref, s_ref = refs
+    *refs, s_ref = refs
+    pieces, w_ref, outs = refs[: -1 - len(blocks)], refs[-1 - len(blocks)], refs[-len(blocks) :]
     frames, rows, width = s_ref.shape
     zero_frames(s_ref, (), frames, rows, width)
     put_pairs(s_ref, (), steps, pieces)
-    for i, out in zip(blocks, (send_ref, keep_ref), strict=True):
+    for i, out in zip(blocks, outs, strict=True):
         first = 2 * jnp.bitwise_xor(lax.axis_index("tm"), i)
         total = None
         for k in range(3):
@@ -274,16 +305,13 @@
         out[...] = total.astype(out.dtype)
 
 
-def temporal_conv(steps, blocks, count, pieces, taps, weight):
+def temporal_conv(steps, blocks, types, count, pieces, taps, weight):
     width, width_out = taps.shape[1:]
     return pl.pallas_call(
         functools.partial(temporal_kernel, steps, blocks),
-        out_shape=(
-            jax.ShapeDtypeStruct((2, count, width_out), bf16),
-            jax.ShapeDtypeStruct((2, count, width_out), f32),
-        ),
+        out_shape=tuple(jax.ShapeDtypeStruct((2, count, width_out), t) for t in types),
         in_specs=[vmem_spec()] * (len(pieces) + 1),
-        out_specs=(vmem_spec(), vmem_spec()),
+        out_specs=(vmem_spec(),) * len(blocks),
         scratch_shapes=[pltpu.VMEM((10, count + PAD, width), bf16)],
         compiler_params=params(16),
         cost_estimate=cost(weight),
@@ -389,7 +417,7 @@
     theirs, far_cot = [], []
     if pair_clips:
         far_cot.append(tie(swap(tie(cot, send0)), send1))
-    mine0 = add16(tie(part0, send1, *far_cot), came0, CLAIM["mine"])
+    mine0 = add16(tie(part0, keep1, *far_cot), came0, CLAIM["mine"])
     part1 = add16(tie(keep1, mine0), got1, CLAIM["part"])
     came1 = lax.ppermute(part1, "mp", across)
     other0 = lax.ppermute(mine0, "mp", near)
@@ -399,22 +427,25 @@
         theirs.append(swap(mine0))
         far_cot.append(lax.ppermute(tie(far_cot[0], mine0), "tm", core))
         far_cot.append(lax.ppermute(tie(far_cot[0], mine0), "tm", chip))
-    mine1 = add16(tie(part1, mine0), came1, CLAIM["mine"])
+    other0 = copy(other0, CLAIM["copy"])
+    mine1 = add16(tie(part1, other0), came1, CLAIM["mine"])
     other1 = lax.ppermute(tie(mine1, *theirs), "mp", near)
-    cots = (cot, cot_core, cot_chip, lax.ppermute(tie(cot_chip, mine1), "tm", core))
+    cots = (cot, cot_core, cot_chip, lax.ppermute(tie(cot_chip, other0), "tm", core))
     if pair_clips:
-        theirs += [swap(tie(other0, mine1)), swap(mine1), swap(other1)]
+        theirs += [swap(other0), swap(mine1), swap(other1)]
         far_cot.append(lax.ppermute(tie(far_cot[2], other1), "tm", core))
-    grad_own = temporal_grads((0, 1), cots, [tie(mine0, mine1), other0], (), CLAIM["g1"])
+    grad_own = temporal_grads((0, 1), cots, [tie(mine0, mine1, *theirs[1:2]), other0], (), CLAIM["g1"])
 
     steps = (0, 1, 2, 3)
     pieces = [tie(mine0, grad_own), other0, mine1, other1]
-    send, keep_chip = temporal_conv(steps, (3, 2), count, pieces, temporal_weight, CLAIM["t1"])
+    (send,) = temporal_conv(steps, (3,), (bf16,), count, pieces, temporal_weight, CLAIM["t1"])
     far_part = lax.ppermute(send, "tm", core)
-    later = [tie(mine0, keep_chip, *theirs[2:3])] + pieces[1:]
-    send, keep_own = temporal_conv(steps, (1, 0), count, later, temporal_weight, CLAIM["t2"])
+    later = [tie(mine0, send)] + pieces[1:]
+    keep_chip, send, keep_own = temporal_conv(
+        steps, (2, 1, 0), (f32, bf16, f32), count, later, temporal_weight, CLAIM["t2"]
+    )
     near_part = lax.ppermute(send, "tm", core)
-    to_chip = add16(tie(keep_chip, keep_own), far_part, CLAIM["part"])
+    to_chip = add16(tie(keep_chip, *theirs[2:3]), far_part, CLAIM["part"])
     from_chip = lax.ppermute(to_chip, "tm", chip)
     if pair_clips:
         first = [tie(theirs[0], to_chip), theirs[1]]

time: 82.2 us -> 74.4 us (0.905)
  waiting for transfers between devices: 34 us -> 26.3 us
  Pallas kernels: 20.4 us -> 18.2 us
  starting transfers between devices: 24.3 us -> 26.4 us
    ppermute x1, waiting for transfers between devices: 5.25 us -> 0.01 us  [body(): got1 = lax.ppermute(send1, 'mp', near)]
    ppermute x1, starting transfers between devices: 0.01 us -> 5 us  [body(): other0 = lax.ppermute(mine0, 'mp', near)]
    ppermute x1, waiting for transfers between devices: 3.76 us -> 0.98 us  [body(): other1 = lax.ppermute(tie(mine1, *theirs), 'mp', near)]
    ppermute x1, waiting for transfers between devices: 0.71 us -> 3.48 us  [body(): other0 = lax.ppermute(mine0, 'mp', near)]
    pallas_call x4 -> x5, Pallas kernels: 8.61 us -> 6.39 us  [the longest x4 6.36 us: temporal_grads(): pl.pallas_call(functools.partial(grad_kernel, steps, len(pieces), extra),...]
    ppermute x1, starting transfers between devices: 3.53 us -> 1.83 us  [body(): other1 = lax.ppermute(tie(mine1, *theirs), 'mp', near)]
    ppermute x1, waiting for transfers between devices: 6.83 us -> 5.31 us  [body(): came1 = lax.ppermute(part1, 'mp', across)]
    ppermute x1, waiting for transfers between devices: 4.35 us -> 2.84 us  [body(): came0 = lax.ppermute(part0, 'mp', across)]
where the time goes in v6:
time: 74.4 us; the launch traced here: 74.2 us
  starting transfers between devices  26.4 us (35%)
  waiting for transfers between devices  26.3 us (35%)
  Pallas kernels  18.2 us (24%)
  local copies, waits for them, and re-layouts  1.65 us (2%)
  between operations  0.86 us (1%)
  other arithmetic  0.84 us (1%)
    ppermute x5, waiting for transfers between devices, swap(): return lax.ppermute(x, 'dp', [(0, 1), (1, 0)])  7.97 us
    pallas_call x4, Pallas kernels, pair_conv(): pl.pallas_call(functools.partial(conv_kernel, kept), out_shape=jax.ShapeD...  6.91 us
    pallas_call x4, Pallas kernels, temporal_grads(): pl.pallas_call(functools.partial(grad_kernel, steps, len(pieces), extra),...  6.36 us
    ppermute x1, waiting for transfers between devices, body(): came1 = lax.ppermute(part1, 'mp', across)  5.31 us
    ppermute x1, starting transfers between devices, body(): other0 = lax.ppermute(mine0, 'mp', near)  5 us
    ppermute x5, starting transfers between devices, swap(): return lax.ppermute(x, 'dp', [(0, 1), (1, 0)])  4.52 us
    ppermute x1, starting transfers between devices, body(): came0 = lax.ppermute(part0, 'mp', across)  3.83 us
    ppermute x1, waiting for transfers between devices, body(): other0 = lax.ppermute(mine0, 'mp', near)  3.48 us
  transfers between devices with their start and end apart: 24, of which 13 were waited for; matrix products, arithmetic and copies ran while one was open for 0% of the time, Pallas kernels for 23%

profile of v6, /device:TPU:0, one launch (start us, length us, event | category | flops | bytes accessed | tf_op | source)
XLA Modules:
  0.0 74.2 jit_solution(69910876543600969)
XLA Ops:
  1.1 1.0 %copy-done.4 = bf16[1,2,5,40,320]{4,3,2,1,0:T(8,128)(2,1)S(1)} copy-done((bf16[1,2,5,40,320]{4,3,2,1,0:T(8,128)(2,1)S(1)}, bf16[1,2,5,40,320]{4,3,2,1,0:T(8,128)(2,1)}, u32[]{:S(2)}) %copy-start.4) | copy-done | bytes 256024
  2.6 1.1 %chip_stats.1 = (f32[16,320]{1,0:T(8,128)S(1)}, bf16[2,2,5,40,320]{4,3,2,1,0:T(8,128)(2,1)S(1)}) custom-call(bf16[2,5,40,320]{3,2,1,0:T(8,128)(2,1)S(1)} %fetch.1.own_ref, bf16[2,5,40,320]{3,2,1,0:T(8,128)(2,1)S(1)} %collective-permute-done.core_ref), custom_call_target="tpu_custom_call" | custom-call | flops 1724999936 | bytes 1 | tf_op jit(solution)/shard_map/chip_stats/pallas_call | solution.py:57
  3.7 2.9 %collective-permute-start.1 = (f32[16,320]{1,0:T(8,128)S(1)}, f32[16,320]{1,0:T(8,128)S(1)}, u32[]{:S(2)}, u32[]{:S(2)}) collective-permute-start(f32[16,320]{1,0:T(8,128)S(1)} %get-tuple-element.33.s0_ref), channel_id=1, source_target_pairs={{0,8},{4,12},{8,0},{12,4},{1,9},{5,13},{9,1},{13,5},{2,10},{6,14},... | collective-permute-start | bytes 61448 | tf_op jit(solution)/shard_map/ppermute | solution.py:400
  7.6 0.8 %collective-permute-done.1.s1_ref = f32[16,320]{1,0:T(8,128)S(1)} collective-permute-done((f32[16,320]{1,0:T(8,128)S(1)}, f32[16,320]{1,0:T(8,128)S(1)}, u32[]{:S(2)}, u32[]{:S(2)}) %collective-permute-start.1) | collective-permute-done | bytes 20512 | tf_op jit(solution)/shard_map/ppermute | solution.py:400
  8.4 1.7 %pair_conv.4 = bf16[400,320]{1,0:T(8,128)(2,1)S(1)} custom-call(bf16[2,2,5,40,320]{4,3,2,1,0:T(8,128)(2,1)S(1)} %get-tuple-element.36.x_ref, f32[32,320]{1,0:T(8,128)S(1)} %merge_stats.1.norm_ref, bf16[3,960,320]{2,1,0:T(8,128)(2,1)S(1)} %get-tuple-element.35.w_ref), custom_call_target="tpu_custom_call" | custom-call | flops 57500000256 | bytes 1 | tf_op jit(solution)/shard_map/pair_conv/pallas_call | solution.py:177
  10.2 2.1 %collective-permute-start.2 = (bf16[400,320]{1,0:T(8,128)(2,1)S(1)}, bf16[400,320]{1,0:T(8,128)(2,1)S(1)}, u32[]{:S(2)}, u32[]{:S(2)}) collective-permute-start(bf16[400,320]{1,0:T(8,128)(2,1)S(1)} %pair_conv.4), channel_id=1, source_target_pairs={{0,1},{1,0},{2,3},{3,2},{4,5},{5,4},{6,7},{7,6},{8,9},{9,8},{10,11... | collective-permute-start | bytes 768008 | tf_op jit(solution)/shard_map/ppermute | solution.py:406
  12.3 1.7 %pair_conv.5.a_ref = f32[400,320]{1,0:T(8,128)S(1)} custom-call(bf16[2,2,5,40,320]{4,3,2,1,0:T(8,128)(2,1)S(1)} %get-tuple-element.36.x_ref, f32[32,320]{1,0:T(8,128)S(1)} %merge_stats.1.norm_ref, bf16[3,960,320]{2,1,0:T(8,128)(2,1)S(1)} %get-tuple-element.35.w_ref), custom_call_target="tpu_custom_call" | custom-call | bytes 1 | tf_op jit(solution)/shard_map/pair_conv/pallas_call | solution.py:177
  14.0 2.5 %collective-permute-done.3.a_ref = bf16[2,5,40,320]{3,2,1,0:T(8,128)(2,1)S(1)} collective-permute-done((bf16[2,5,40,320]{3,2,1,0:T(8,128)(2,1)S(1)}, bf16[2,5,40,320]{3,2,1,0:T(8,128)(2,1)S(1)}, u32[]{:S(2)}, u32[]{:S(2)}) %collective-permute-start.3) | collective-permute-done | bytes 256032 | tf_op jit(solution)/shard_map/ppermute | solution.py:402
  16.6 1.5 %collective-permute-start.5 = (bf16[2,200,320]{2,1,0:T(8,128)(2,1)S(1)}, bf16[2,200,320]{2,1,0:T(8,128)(2,1)S(1)}, u32[]{:S(2)}, u32[]{:S(2)}) collective-permute-start(bf16[2,200,320]{2,1,0:T(8,128)(2,1)S(1)} %bitcast.4), channel_id=1, source_target_pairs={{0,16},{16,0},{1,17},{17,1},{2,18},{18,2},{3,19},{19,3},{4,20},{20... | collective-permute-start | bytes 768008 | tf_op jit(solution)/shard_map/ppermute | solution.py:396
  18.8 3.8 %collective-permute-start.6 = (bf16[400,320]{1,0:T(8,128)(2,1)S(1)}, bf16[400,320]{1,0:T(8,128)(2,1)S(1)}, u32[]{:S(2)}, u32[]{:S(2)}) collective-permute-start(bf16[400,320]{1,0:T(8,128)(2,1)S(1)} %add_parts.5.a_ref), channel_id=1, source_target_pairs={{0,3},{1,2},{2,1},{3,0},{4,7},{5,6},{6,5},{7,4},{8,11},{9,10},{10,... | collective-permute-start | bytes 768008 | tf_op jit(solution)/shard_map/ppermute | solution.py:412
  22.7 1.7 %pair_conv.6 = bf16[400,320]{1,0:T(8,128)(2,1)S(1)} custom-call(bf16[2,2,5,40,320]{4,3,2,1,0:T(8,128)(2,1)S(1)} %collect_pairs.1.x_ref, f32[32,320]{1,0:T(8,128)S(1)} %merge_stats.1.norm_ref, bf16[3,960,320]{2,1,0:T(8,128)(2,1)S(1)} %get-tuple-element.35.w_ref), custom_call_target="tpu_custom_call" | custom-call | flops 1150000000 | bytes 1 | tf_op jit(solution)/shard_map/pair_conv/pallas_call | solution.py:177
  24.5 1.8 %collective-permute-done.5.refs_0_ = bf16[2,200,320]{2,1,0:T(8,128)(2,1)S(1)} collective-permute-done((bf16[2,200,320]{2,1,0:T(8,128)(2,1)S(1)}, bf16[2,200,320]{2,1,0:T(8,128)(2,1)S(1)}, u32[]{:S(2)}, u32[]{:S(2)}) %collective-permute-start.5) | collective-permute-done | bytes 256032 | tf_op jit(solution)/shard_map/ppermute | solution.py:396
  26.3 1.7 %pair_conv.7.a_ref = f32[400,320]{1,0:T(8,128)S(1)} custom-call(bf16[2,2,5,40,320]{4,3,2,1,0:T(8,128)(2,1)S(1)} %collect_pairs.1.x_ref, f32[32,320]{1,0:T(8,128)S(1)} %merge_stats.1.norm_ref, bf16[3,960,320]{2,1,0:T(8,128)(2,1)S(1)} %get-tuple-element.35.w_ref), custom_call_target="tpu_custom_call" | custom-call | bytes 1 | tf_op jit(solution)/shard_map/pair_conv/pallas_call | solution.py:177
  28.0 2.8 %collective-permute-done.6.b_ref = bf16[400,320]{1,0:T(8,128)(2,1)S(1)} collective-permute-done((bf16[400,320]{1,0:T(8,128)(2,1)S(1)}, bf16[400,320]{1,0:T(8,128)(2,1)S(1)}, u32[]{:S(2)}, u32[]{:S(2)}) %collective-permute-start.6) | collective-permute-done | bytes 256032 | tf_op jit(solution)/shard_map/ppermute | solution.py:412
  30.9 5.0 %collective-permute-start.9 = (bf16[400,320]{1,0:T(8,128)(2,1)S(1)}, bf16[400,320]{1,0:T(8,128)(2,1)S(1)}, u32[]{:S(2)}, u32[]{:S(2)}) collective-permute-start(bf16[400,320]{1,0:T(8,128)(2,1)S(1)} %add_parts.6.refs_4_.refs_0_), channel_id=1, source_target_pairs={{0,1},{1,0},{2,3},{3,2},{4,5},{5,4},{6,7},{7,6},{8,9},{9,8},{10,11... | collective-permute-start | bytes 768008 | tf_op jit(solution)/shard_map/ppermute | solution.py:423
  36.5 3.4 %collective-permute-start.12 = (bf16[400,320]{1,0:T(8,128)(2,1)S(1)}, bf16[400,320]{1,0:T(8,128)(2,1)S(1)}, u32[]{:S(2)}, u32[]{:S(2)}) collective-permute-start(bf16[400,320]{1,0:T(8,128)(2,1)S(1)} %add_parts.7.a_ref), channel_id=1, source_target_pairs={{0,3},{1,2},{2,1},{3,0},{4,7},{5,6},{6,5},{7,4},{8,11},{9,10},{10,... | collective-permute-start | bytes 768008 | tf_op jit(solution)/shard_map/ppermute | solution.py:422
  40.5 3.5 %collective-permute-done.9.x_ref = bf16[400,320]{1,0:T(8,128)(2,1)S(1)} collective-permute-done((bf16[400,320]{1,0:T(8,128)(2,1)S(1)}, bf16[400,320]{1,0:T(8,128)(2,1)S(1)}, u32[]{:S(2)}, u32[]{:S(2)}) %collective-permute-start.9) | collective-permute-done | bytes 256032 | tf_op jit(solution)/shard_map/ppermute | solution.py:423
  44.0 1.4 %collective-permute-start.13 = (bf16[400,320]{1,0:T(8,128)(2,1)S(1)}, bf16[400,320]{1,0:T(8,128)(2,1)S(1)}, u32[]{:S(2)}, u32[]{:S(2)}) collective-permute-start(bf16[400,320]{1,0:T(8,128)(2,1)S(1)} %copy_piece.1.refs_5_.refs_1_), channel_id=1, source_target_pairs={{0,16},{16,0},{1,17},{17,1},{2,18},{18,2},{3,19},{19,3},{4,20},{20... | collective-permute-start | bytes 768008 | tf_op jit(solution)/shard_map/ppermute | solution.py:396
  45.5 5.3 %collective-permute-done.12.b_ref = bf16[400,320]{1,0:T(8,128)(2,1)S(1)} collective-permute-done((bf16[400,320]{1,0:T(8,128)(2,1)S(1)}, bf16[400,320]{1,0:T(8,128)(2,1)S(1)}, u32[]{:S(2)}, u32[]{:S(2)}) %collective-permute-start.12) | collective-permute-done | bytes 256032 | tf_op jit(solution)/shard_map/ppermute | solution.py:422
  50.9 1.8 %collective-permute-start.15 = (bf16[400,320]{1,0:T(8,128)(2,1)S(1)}, bf16[400,320]{1,0:T(8,128)(2,1)S(1)}, u32[]{:S(2)}, u32[]{:S(2)}) collective-permute-start(bf16[400,320]{1,0:T(8,128)(2,1)S(1)} %add_parts.8.refs_2_.refs_4_), channel_id=1, source_target_pairs={{0,1},{1,0},{2,3},{3,2},{4,5},{5,4},{6,7},{7,6},{8,9},{9,8},{10,11... | collective-permute-start | bytes 768008 | tf_op jit(solution)/shard_map/ppermute | solution.py:432
  53.2 2.1 %collective-permute-done.13.refs_5_ = bf16[400,320]{1,0:T(8,128)(2,1)S(1)} collective-permute-done((bf16[400,320]{1,0:T(8,128)(2,1)S(1)}, bf16[400,320]{1,0:T(8,128)(2,1)S(1)}, u32[]{:S(2)}, u32[]{:S(2)}) %collective-permute-start.13) | collective-permute-done | bytes 256032 | tf_op jit(solution)/shard_map/ppermute | solution.py:396
  55.9 1.4 %temporal_grads.4.refs_6_ = f32[3,320,320]{2,1,0:T(8,128)S(1)} custom-call(bf16[2,200,320]{2,1,0:T(8,128)(2,1)S(1)} %bitcast.7, bf16[2,200,320]{2,1,0:T(8,128)(2,1)S(1)} %collective-permute-done.7.refs_1_, bf16[2,200,320]{2,1,0:T(8,128)(2,1)S(1)} %collective-permute-done.8.refs_2_, bf16[2,200,320]{2,1,0:T(8,128)(2,1)S(1)} %collective-permute-done.10.refs_3_, ...), custom_call_target="tpu_custom_call" | custom-call | flops 1150000000 | bytes 1 | tf_op jit(solution)/shard_map/temporal_grads/pallas_call | solution.py:279
  57.3 1.0 %collective-permute-done.15.refs_3_.refs_5_ = bf16[400,320]{1,0:T(8,128)(2,1)S(1)} collective-permute-done((bf16[400,320]{1,0:T(8,128)(2,1)S(1)}, bf16[400,320]{1,0:T(8,128)(2,1)S(1)}, u32[]{:S(2)}, u32[]{:S(2)}) %collective-permute-start.15) | collective-permute-done | bytes 256032 | tf_op jit(solution)/shard_map/ppermute | solution.py:432
  58.3 0.9 %temporal_conv.2 = bf16[2,200,320]{2,1,0:T(8,128)(2,1)S(1)} custom-call(bf16[400,320]{1,0:T(8,128)(2,1)S(1)} %add_parts.6.refs_4_.refs_0_, bf16[400,320]{1,0:T(8,128)(2,1)S(1)} %copy_piece.1.refs_5_.refs_1_, bf16[400,320]{1,0:T(8,128)(2,1)S(1)} %add_parts.8.refs_2_.refs_4_, bf16[400,320]{1,0:T(8,128)(2,1)S(1)} %collective-permute-done.15.refs_3_.refs_5_, ...), custom_call_target="tpu_custom_call" | custom-call | flops 57500000256 | bytes 1 | tf_op jit(solution)/shard_map/temporal_conv/pallas_call | solution.py:310
  60.3 2.1 %temporal_conv.3 = (f32[2,200,320]{2,1,0:T(8,128)S(1)}, bf16[2,200,320]{2,1,0:T(8,128)(2,1)S(1)}, f32[2,200,320]{2,1,0:T(8,128)S(1)}) custom-call(bf16[400,320]{1,0:T(8,128)(2,1)S(1)} %add_parts.6.refs_4_.refs_0_, bf16[400,320]{1,0:T(8,128)(2,1)S(1)} %copy_piece.1.refs_5_.refs_1_, bf16[400,320]{1,0:T(8,128)(2,1)S(1)} %add_parts.8.refs_2_.refs_4_, ...), custom_call_target="tpu_custom_call" | custom-call | bytes 1 | tf_op jit(solution)/shard_map/temporal_conv/pallas_call | solution.py:310
  62.4 1.1 %collective-permute-done.19.refs_4_ = bf16[400,320]{1,0:T(8,128)(2,1)S(1)} collective-permute-done((bf16[400,320]{1,0:T(8,128)(2,1)S(1)}, bf16[400,320]{1,0:T(8,128)(2,1)S(1)}, u32[]{:S(2)}, u32[]{:S(2)}) %collective-permute-start.19) | collective-permute-done | bytes 256032 | tf_op jit(solution)/shard_map/ppermute | solution.py:396
  64.1 1.4 %temporal_grads.5.refs_6_ = f32[3,320,320]{2,1,0:T(8,128)S(1)} custom-call(bf16[2,200,320]{2,1,0:T(8,128)(2,1)S(1)} %collective-permute-done.5.refs_0_, bf16[2,200,320]{2,1,0:T(8,128)(2,1)S(1)} %collective-permute-done.16.refs_1_, bf16[2,200,320]{2,1,0:T(8,128)(2,1)S(1)} %collective-permute-done.17.refs_2_, ...), custom_call_target="tpu_custom_call" | custom-call | bytes 1 | tf_op jit(solution)/shard_map/temporal_grads/pallas_call | solution.py:279
  65.5 1.4 %temporal_grads.6.refs_7_ = f32[3,320,320]{2,1,0:T(8,128)S(1)} custom-call(bf16[2,200,320]{2,1,0:T(8,128)(2,1)S(1)} %bitcast.8, bf16[2,200,320]{2,1,0:T(8,128)(2,1)S(1)} %collective-permute-done.7.refs_1_, bf16[2,200,320]{2,1,0:T(8,128)(2,1)S(1)} %collective-permute-done.8.refs_2_, bf16[2,200,320]{2,1,0:T(8,128)(2,1)S(1)} %collective-permute-done.10.refs_3_, ...), custom_call_target="tpu_custom_call" | custom-call | bytes 1 | tf_op jit(solution)/shard_map/temporal_grads/pallas_call | solution.py:279
  66.9 2.9 %collective-permute-done.21.refs_5_ = bf16[400,320]{1,0:T(8,128)(2,1)S(1)} collective-permute-done((bf16[400,320]{1,0:T(8,128)(2,1)S(1)}, bf16[400,320]{1,0:T(8,128)(2,1)S(1)}, u32[]{:S(2)}, u32[]{:S(2)}) %collective-permute-start.21) | collective-permute-done | bytes 256032 | tf_op jit(solution)/shard_map/ppermute | solution.py:396
  69.8 2.2 %temporal_grads.7 = f32[3,320,320]{2,1,0:T(8,128)} custom-call(bf16[2,200,320]{2,1,0:T(8,128)(2,1)S(1)} %collective-permute-done.5.refs_0_, bf16[2,200,320]{2,1,0:T(8,128)(2,1)S(1)} %collective-permute-done.16.refs_1_, bf16[2,200,320]{2,1,0:T(8,128)(2,1)S(1)} %collective-permute-done.17.refs_2_, bf16[2,200,320]{2,1,0:T(8,128)(2,1)S(1)} %collective-permute-done.18.refs_3_, ...), custom_call_target="tpu_custom_call" | custom-call | flops 57500000256 | bytes 1 | tf_op jit(solution)/shard_map/temporal_grads/pallas_call | solution.py:279
  72.0 1.3 %collective-permute-done.23 = bf16[2,200,320]{2,1,0:T(8,128)(2,1)S(1)} collective-permute-done((bf16[2,200,320]{2,1,0:T(8,128)(2,1)S(1)}, bf16[2,200,320]{2,1,0:T(8,128)(2,1)S(1)}, u32[]{:S(2)}, u32[]{:S(2)}) %collective-permute-start.23) | collective-permute-done | bytes 256032 | tf_op jit(solution)/shard_map/ppermute | solution.py:449
  73.4 0.8 %add_convert_fusion = bf16[2,200,320]{2,1,0:T(8,128)(2,1)} fusion(bf16[2,200,320]{2,1,0:T(8,128)(2,1)S(1)} %collective-permute-done.23, f32[2,200,320]{2,1,0:T(8,128)S(1)} %get-tuple-element.60, bf16[2,200,320]{2,1,0:T(8,128)(2,1)S(1)} %collective-permute-done.22), kind=kLoop, calls=%fused_computation | loop fusion | flops 640000 | bytes 1280000 | tf_op jit(solution)/shard_map/convert_element_type | solution.py:462
  (54 shorter events, 6.9 us)
Async XLA Ops:
  0.6 2.0 %collective-permute-start = (bf16[2,5,40,320]{3,2,1,0:T(8,128)(2,1)}, bf16[2,5,40,320]{3,2,1,0:T(8,128)(2,1)S(1)}, u32[]{:S(2)}, u32[]{:S(2)}) collective-permute-start(bf16[2,5,40,320]{3,2,1,0:T(8,128)(2,1)} %bitcast.10), channel_id=1, source_target_pairs={{0,4},{4,0},{8,12},{12,8},{1,5},{5,1},{9,13},{13,9},{2,6},{6,2},{1... | collective-permute-start | bytes 768008 | tf_op jit(solution)/shard_map/ppermute | solution.py:398
  1.1 1.0 %copy-start.4 = (bf16[1,2,5,40,320]{4,3,2,1,0:T(8,128)(2,1)S(1)}, bf16[1,2,5,40,320]{4,3,2,1,0:T(8,128)(2,1)}, u32[]{:S(2)}) copy-start(bf16[1,2,5,40,320]{4,3,2,1,0:T(8,128)(2,1)} %param.6) | copy-start | bytes 768004
  2.2 4.4 %copy-start.3 = (bf16[9,320,320]{2,1,0:T(8,128)(2,1)S(1)}, bf16[9,320,320]{2,1,0:T(8,128)(2,1)}, u32[]{:S(2)}) copy-start(bf16[9,320,320]{2,1,0:T(8,128)(2,1)} %param.9) | copy-start | bytes 5529604
  2.2 4.4 %copy-start.6 = (f32[320]{0:T(512)S(1)}, f32[320]{0:T(512)}, u32[]{:S(2)}) copy-start(f32[320]{0:T(512)} %gain_ref.1) | copy-start | bytes 3844
  2.2 4.4 %copy-start.7 = (f32[320]{0:T(512)S(1)}, f32[320]{0:T(512)}, u32[]{:S(2)}) copy-start(f32[320]{0:T(512)} %bias_ref.1) | copy-start | bytes 3844
  3.7 4.7 %collective-permute-start.1 = (f32[16,320]{1,0:T(8,128)S(1)}, f32[16,320]{1,0:T(8,128)S(1)}, u32[]{:S(2)}, u32[]{:S(2)}) collective-permute-start(f32[16,320]{1,0:T(8,128)S(1)} %get-tuple-element.33.s0_ref), channel_id=1, source_target_pairs={{0,8},{4,12},{8,0},{12,4},{1,9},{5,13},{9,1},{13,5},{2,10},{6,14},... | collective-permute-start | bytes 61448 | tf_op jit(solution)/shard_map/ppermute | solution.py:400
  6.6 1.0 %copy-start.5 = (bf16[1,2,5,40,320]{4,3,2,1,0:T(8,128)(2,1)S(1)}, bf16[1,2,5,40,320]{4,3,2,1,0:T(8,128)(2,1)}, u32[]{:S(2)}) copy-start(bf16[1,2,5,40,320]{4,3,2,1,0:T(8,128)(2,1)} %param.6) | copy-start | bytes 768004
  7.6 9.0 %collective-permute-start.3 = (bf16[2,5,40,320]{3,2,1,0:T(8,128)(2,1)S(1)}, bf16[2,5,40,320]{3,2,1,0:T(8,128)(2,1)S(1)}, u32[]{:S(2)}, u32[]{:S(2)}) collective-permute-start(bf16[2,5,40,320]{3,2,1,0:T(8,128)(2,1)S(1)} %bitcast.12), channel_id=1, source_target_pairs={{0,8},{4,12},{8,0},{12,4},{1,9},{5,13},{9,1},{13,5},{2,10},{6,14},... | collective-permute-start | bytes 768008 | tf_op jit(solution)/shard_map/ppermute | solution.py:402
  10.2 6.4 %copy-start.1 = (bf16[1,2,5,40,320]{4,3,2,1,0:T(8,128)(2,1)S(1)}, bf16[1,2,5,40,320]{4,3,2,1,0:T(8,128)(2,1)}, u32[]{:S(2)}) copy-start(bf16[1,2,5,40,320]{4,3,2,1,0:T(8,128)(2,1)} %param.11) | copy-start | bytes 768004
  10.2 8.6 %collective-permute-start.2 = (bf16[400,320]{1,0:T(8,128)(2,1)S(1)}, bf16[400,320]{1,0:T(8,128)(2,1)S(1)}, u32[]{:S(2)}, u32[]{:S(2)}) collective-permute-start(bf16[400,320]{1,0:T(8,128)(2,1)S(1)} %pair_conv.4), channel_id=1, source_target_pairs={{0,1},{1,0},{2,3},{3,2},{4,5},{5,4},{6,7},{7,6},{8,9},{9,8},{10,11... | collective-permute-start | bytes 768008 | tf_op jit(solution)/shard_map/ppermute | solution.py:406
  16.6 6.0 %collective-permute-start.4 = (bf16[2,5,40,320]{3,2,1,0:T(8,128)(2,1)S(1)}, bf16[2,5,40,320]{3,2,1,0:T(8,128)(2,1)S(1)}, u32[]{:S(2)}, u32[]{:S(2)}) collective-permute-start(bf16[2,5,40,320]{3,2,1,0:T(8,128)(2,1)S(1)} %collective-permute-done.3.a_ref), channel_id=1, source_target_pairs={{0,4},{4,0},{8,12},{12,8},{1,5},{5,1},{9,13},{13,9},{2,6},{6,2},{1... | collective-permute-start | bytes 768008 | tf_op jit(solution)/shard_map/ppermute | solution.py:409
  16.6 9.7 %collective-permute-start.5 = (bf16[2,200,320]{2,1,0:T(8,128)(2,1)S(1)}, bf16[2,200,320]{2,1,0:T(8,128)(2,1)S(1)}, u32[]{:S(2)}, u32[]{:S(2)}) collective-permute-start(bf16[2,200,320]{2,1,0:T(8,128)(2,1)S(1)} %bitcast.4), channel_id=1, source_target_pairs={{0,16},{16,0},{1,17},{17,1},{2,18},{18,2},{3,19},{19,3},{4,20},{20... | collective-permute-start | bytes 768008 | tf_op jit(solution)/shard_map/ppermute | solution.py:396
  18.8 12.1 %collective-permute-start.6 = (bf16[400,320]{1,0:T(8,128)(2,1)S(1)}, bf16[400,320]{1,0:T(8,128)(2,1)S(1)}, u32[]{:S(2)}, u32[]{:S(2)}) collective-permute-start(bf16[400,320]{1,0:T(8,128)(2,1)S(1)} %add_parts.5.a_ref), channel_id=1, source_target_pairs={{0,3},{1,2},{2,1},{3,0},{4,7},{5,6},{6,5},{7,4},{8,11},{9,10},{10,... | collective-permute-start | bytes 768008 | tf_op jit(solution)/shard_map/ppermute | solution.py:412
  24.4 12.0 %collective-permute-start.11 = (bf16[400,320]{1,0:T(8,128)(2,1)S(1)}, bf16[400,320]{1,0:T(8,128)(2,1)S(1)}, u32[]{:S(2)}, u32[]{:S(2)}) collective-permute-start(bf16[400,320]{1,0:T(8,128)(2,1)S(1)} %pair_conv.6), channel_id=1, source_target_pairs={{0,1},{1,0},{2,3},{3,2},{4,5},{5,4},{6,7},{7,6},{8,9},{9,8},{10,11... | collective-permute-start | bytes 768008 | tf_op jit(solution)/shard_map/ppermute | solution.py:414
  28.0 7.9 %copy-start.2 = (bf16[1,2,5,40,320]{4,3,2,1,0:T(8,128)(2,1)S(1)}, bf16[1,2,5,40,320]{4,3,2,1,0:T(8,128)(2,1)}, u32[]{:S(2)}) copy-start(bf16[1,2,5,40,320]{4,3,2,1,0:T(8,128)(2,1)} %param.11) | copy-start | bytes 768004
  30.9 13.0 %collective-permute-start.9 = (bf16[400,320]{1,0:T(8,128)(2,1)S(1)}, bf16[400,320]{1,0:T(8,128)(2,1)S(1)}, u32[]{:S(2)}, u32[]{:S(2)}) collective-permute-start(bf16[400,320]{1,0:T(8,128)(2,1)S(1)} %add_parts.6.refs_4_.refs_0_), channel_id=1, source_target_pairs={{0,1},{1,0},{2,3},{3,2},{4,5},{5,4},{6,7},{7,6},{8,9},{9,8},{10,11... | collective-permute-start | bytes 768008 | tf_op jit(solution)/shard_map/ppermute | solution.py:423
  35.9 9.5 %collective-permute-start.8 = (bf16[2,200,320]{2,1,0:T(8,128)(2,1)S(1)}, bf16[2,200,320]{2,1,0:T(8,128)(2,1)S(1)}, u32[]{:S(2)}, u32[]{:S(2)}) collective-permute-start(bf16[2,200,320]{2,1,0:T(8,128)(2,1)S(1)} %bitcast.5), channel_id=1, source_target_pairs={{0,8},{4,12},{8,0},{12,4},{1,9},{5,13},{9,1},{13,5},{2,10},{6,14},... | collective-permute-start | bytes 768008 | tf_op jit(solution)/shard_map/ppermute | solution.py:425
  36.5 14.2 %collective-permute-start.12 = (bf16[400,320]{1,0:T(8,128)(2,1)S(1)}, bf16[400,320]{1,0:T(8,128)(2,1)S(1)}, u32[]{:S(2)}, u32[]{:S(2)}) collective-permute-start(bf16[400,320]{1,0:T(8,128)(2,1)S(1)} %add_parts.7.a_ref), channel_id=1, source_target_pairs={{0,3},{1,2},{2,1},{3,0},{4,7},{5,6},{6,5},{7,4},{8,11},{9,10},{10,... | collective-permute-start | bytes 768008 | tf_op jit(solution)/shard_map/ppermute | solution.py:422
  40.0 10.9 %collective-permute-start.14 = (bf16[400,320]{1,0:T(8,128)(2,1)S(1)}, bf16[400,320]{1,0:T(8,128)(2,1)S(1)}, u32[]{:S(2)}, u32[]{:S(2)}) collective-permute-start(bf16[400,320]{1,0:T(8,128)(2,1)S(1)} %add_parts.6.refs_4_.refs_0_), channel_id=1, source_target_pairs={{0,16},{16,0},{1,17},{17,1},{2,18},{18,2},{3,19},{19,3},{4,20},{20... | collective-permute-start | bytes 768008 | tf_op jit(solution)/shard_map/ppermute | solution.py:396
  40.5 15.4 %collective-permute-start.7 = (bf16[2,200,320]{2,1,0:T(8,128)(2,1)S(1)}, bf16[2,200,320]{2,1,0:T(8,128)(2,1)S(1)}, u32[]{:S(2)}, u32[]{:S(2)}) collective-permute-start(bf16[2,200,320]{2,1,0:T(8,128)(2,1)S(1)} %bitcast.6), channel_id=1, source_target_pairs={{0,4},{4,0},{8,12},{12,8},{1,5},{5,1},{9,13},{13,9},{2,6},{6,2},{1... | collective-permute-start | bytes 768008 | tf_op jit(solution)/shard_map/ppermute | solution.py:424
  44.0 11.3 %collective-permute-start.13 = (bf16[400,320]{1,0:T(8,128)(2,1)S(1)}, bf16[400,320]{1,0:T(8,128)(2,1)S(1)}, u32[]{:S(2)}, u32[]{:S(2)}) collective-permute-start(bf16[400,320]{1,0:T(8,128)(2,1)S(1)} %copy_piece.1.refs_5_.refs_1_), channel_id=1, source_target_pairs={{0,16},{16,0},{1,17},{17,1},{2,18},{18,2},{3,19},{19,3},{4,20},{20... | collective-permute-start | bytes 768008 | tf_op jit(solution)/shard_map/ppermute | solution.py:396
  45.4 10.5 %collective-permute-start.10 = (bf16[2,200,320]{2,1,0:T(8,128)(2,1)S(1)}, bf16[2,200,320]{2,1,0:T(8,128)(2,1)S(1)}, u32[]{:S(2)}, u32[]{:S(2)}) collective-permute-start(bf16[2,200,320]{2,1,0:T(8,128)(2,1)S(1)} %collective-permute-done.8.refs_2_), channel_id=1, source_target_pairs={{0,4},{4,0},{8,12},{12,8},{1,5},{5,1},{9,13},{13,9},{2,6},{6,2},{1... | collective-permute-start | bytes 768008 | tf_op jit(solution)/shard_map/ppermute | solution.py:433
  50.8 7.4 %copy-start = (bf16[3,320,320]{2,1,0:T(8,128)(2,1)S(1)}, bf16[3,320,320]{2,1,0:T(8,128)(2,1)}, u32[]{:S(2)}) copy-start(bf16[3,320,320]{2,1,0:T(8,128)(2,1)} %refs_4_.3) | copy-start | bytes 1843204
  50.9 7.4 %collective-permute-start.15 = (bf16[400,320]{1,0:T(8,128)(2,1)S(1)}, bf16[400,320]{1,0:T(8,128)(2,1)S(1)}, u32[]{:S(2)}, u32[]{:S(2)}) collective-permute-start(bf16[400,320]{1,0:T(8,128)(2,1)S(1)} %add_parts.8.refs_2_.refs_4_), channel_id=1, source_target_pairs={{0,1},{1,0},{2,3},{3,2},{4,5},{5,4},{6,7},{7,6},{8,9},{9,8},{10,11... | collective-permute-start | bytes 768008 | tf_op jit(solution)/shard_map/ppermute | solution.py:432
  52.7 7.0 %collective-permute-start.17 = (bf16[2,200,320]{2,1,0:T(8,128)(2,1)S(1)}, bf16[2,200,320]{2,1,0:T(8,128)(2,1)S(1)}, u32[]{:S(2)}, u32[]{:S(2)}) collective-permute-start(bf16[2,200,320]{2,1,0:T(8,128)(2,1)S(1)} %collective-permute-done.5.refs_0_), channel_id=1, source_target_pairs={{0,8},{4,12},{8,0},{12,4},{1,9},{5,13},{9,1},{13,5},{2,10},{6,14},... | collective-permute-start | bytes 768008 | tf_op jit(solution)/shard_map/ppermute | solution.py:429
  55.3 8.2 %collective-permute-start.19 = (bf16[400,320]{1,0:T(8,128)(2,1)S(1)}, bf16[400,320]{1,0:T(8,128)(2,1)S(1)}, u32[]{:S(2)}, u32[]{:S(2)}) collective-permute-start(bf16[400,320]{1,0:T(8,128)(2,1)S(1)} %add_parts.8.refs_2_.refs_4_), channel_id=1, source_target_pairs={{0,16},{16,0},{1,17},{17,1},{2,18},{18,2},{3,19},{19,3},{4,20},{20... | collective-permute-start | bytes 768008 | tf_op jit(solution)/shard_map/ppermute | solution.py:396
  59.2 4.4 %collective-permute-start.20 = (bf16[2,200,320]{2,1,0:T(8,128)(2,1)S(1)}, bf16[2,200,320]{2,1,0:T(8,128)(2,1)S(1)}, u32[]{:S(2)}, u32[]{:S(2)}) collective-permute-start(bf16[2,200,320]{2,1,0:T(8,128)(2,1)S(1)} %temporal_conv.2), channel_id=1, source_target_pairs={{0,4},{4,0},{8,12},{12,8},{1,5},{5,1},{9,13},{13,9},{2,6},{6,2},{1... | collective-permute-start | bytes 768008 | tf_op jit(solution)/shard_map/ppermute | solution.py:442
  59.2 4.9 %collective-permute-start.16 = (bf16[2,200,320]{2,1,0:T(8,128)(2,1)S(1)}, bf16[2,200,320]{2,1,0:T(8,128)(2,1)S(1)}, u32[]{:S(2)}, u32[]{:S(2)}) collective-permute-start(bf16[2,200,320]{2,1,0:T(8,128)(2,1)S(1)} %collective-permute-done.5.refs_0_), channel_id=1, source_target_pairs={{0,4},{4,0},{8,12},{12,8},{1,5},{5,1},{9,13},{13,9},{2,6},{6,2},{1... | collective-permute-start | bytes 768008 | tf_op jit(solution)/shard_map/ppermute | solution.py:428
  59.7 4.4 %collective-permute-start.18 = (bf16[2,200,320]{2,1,0:T(8,128)(2,1)S(1)}, bf16[2,200,320]{2,1,0:T(8,128)(2,1)S(1)}, u32[]{:S(2)}, u32[]{:S(2)}) collective-permute-start(bf16[2,200,320]{2,1,0:T(8,128)(2,1)S(1)} %collective-permute-done.17.refs_2_), channel_id=1, source_target_pairs={{0,4},{4,0},{8,12},{12,8},{1,5},{5,1},{9,13},{13,9},{2,6},{6,2},{1... | collective-permute-start | bytes 768008 | tf_op jit(solution)/shard_map/ppermute | solution.py:436
  59.8 10.0 %collective-permute-start.21 = (bf16[400,320]{1,0:T(8,128)(2,1)S(1)}, bf16[400,320]{1,0:T(8,128)(2,1)S(1)}, u32[]{:S(2)}, u32[]{:S(2)}) collective-permute-start(bf16[400,320]{1,0:T(8,128)(2,1)S(1)} %collective-permute-done.15.refs_3_.refs_5_), channel_id=1, source_target_pairs={{0,16},{16,0},{1,17},{17,1},{2,18},{18,2},{3,19},{19,3},{4,20},{20... | collective-permute-start | bytes 768008 | tf_op jit(solution)/shard_map/ppermute | solution.py:396
  63.5 8.5 %collective-permute-start.22 = (bf16[2,200,320]{2,1,0:T(8,128)(2,1)S(1)}, bf16[2,200,320]{2,1,0:T(8,128)(2,1)S(1)}, u32[]{:S(2)}, u32[]{:S(2)}) collective-permute-start(bf16[2,200,320]{2,1,0:T(8,128)(2,1)S(1)} %get-tuple-element.61), channel_id=1, source_target_pairs={{0,4},{4,0},{8,12},{12,8},{1,5},{5,1},{9,13},{13,9},{2,6},{6,2},{1... | collective-permute-start | bytes 768008 | tf_op jit(solution)/shard_map/ppermute | solution.py:447
  63.6 9.7 %collective-permute-start.23 = (bf16[2,200,320]{2,1,0:T(8,128)(2,1)S(1)}, bf16[2,200,320]{2,1,0:T(8,128)(2,1)S(1)}, u32[]{:S(2)}, u32[]{:S(2)}) collective-permute-start(bf16[2,200,320]{2,1,0:T(8,128)(2,1)S(1)} %add_parts.9), channel_id=1, source_target_pairs={{0,8},{4,12},{8,0},{12,4},{1,9},{5,13},{9,1},{13,5},{2,10},{6,14},... | collective-permute-start | bytes 768008 | tf_op jit(solution)/shard_map/ppermute | solution.py:449

commit v7 on v6

--- a/solution.py
+++ b/solution.py
@@ -427,9 +427,9 @@
         theirs.append(swap(mine0))
         far_cot.append(lax.ppermute(tie(far_cot[0], mine0), "tm", core))
         far_cot.append(lax.ppermute(tie(far_cot[0], mine0), "tm", chip))
-    other0 = copy(other0, CLAIM["copy"])
+    other0 = copy(tie(other0, *theirs), CLAIM["copy"])
     mine1 = add16(tie(part1, other0), came1, CLAIM["mine"])
-    other1 = lax.ppermute(tie(mine1, *theirs), "mp", near)
+    other1 = lax.ppermute(mine1, "mp", near)
     cots = (cot, cot_core, cot_chip, lax.ppermute(tie(cot_chip, other0), "tm", core))
     if pair_clips:
         theirs += [swap(other0), swap(mine1), swap(other1)]
@@ -441,11 +441,11 @@
     (send,) = temporal_conv(steps, (3,), (bf16,), count, pieces, temporal_weight, CLAIM["t1"])
     far_part = lax.ppermute(send, "tm", core)
     later = [tie(mine0, send)] + pieces[1:]
-    keep_chip, send, keep_own = temporal_conv(
-        steps, (2, 1, 0), (f32, bf16, f32), count, later, temporal_weight, CLAIM["t2"]
-    )
+    (keep_chip,) = temporal_conv(steps, (2,), (f32,), count, later, temporal_weight, CLAIM["t2"])
+    to_chip = add16(tie(keep_chip, *theirs[2:3]), far_part, CLAIM["part"])
+    later = [tie(mine0, to_chip)] + pieces[1:]
+    send, keep_own = temporal_conv(steps, (1, 0), (bf16, f32), count, later, temporal_weight, CLAIM["t2"])
     near_part = lax.ppermute(send, "tm", core)
-    to_chip = add16(tie(keep_chip, *theirs[2:3]), far_part, CLAIM["part"])
     from_chip = lax.ppermute(to_chip, "tm", chip)
     if pair_clips:
         first = [tie(theirs[0], to_chip), theirs[1]]

time: 74.4 us -> 72.5 us (0.974)
  waiting for transfers between devices: 26.3 us -> 22.4 us
  starting transfers between devices: 26.4 us -> 27.9 us
    ppermute x5, waiting for transfers between devices: 7.97 us -> 3.96 us  [swap(): return lax.ppermute(x, 'dp', [(0, 1), (1, 0)])]
    ppermute x5, starting transfers between devices: 4.52 us -> 7.65 us  [swap(): return lax.ppermute(x, 'dp', [(0, 1), (1, 0)])]
    ppermute x1, waiting for transfers between devices: 1.32 us -> 0.01 us  [body(): from_chip = lax.ppermute(to_chip, 'tm', chip)]
    ppermute x1, starting transfers between devices: 5 us -> 3.8 us  [body(): other0 = lax.ppermute(mine0, 'mp', near)]
    ppermute x1, waiting for transfers between devices: 0.98 us -> 1.9 us  [body(): other1 = lax.ppermute(mine1, 'mp', near)]
    ppermute x1, starting transfers between devices: 3.43 us -> 2.54 us  [body(): came1 = lax.ppermute(part1, 'mp', across)]
    pallas_call x2 -> x3, Pallas kernels: 2.93 us -> 3.39 us  [temporal_conv(): pl.pallas_call(functools.partial(temporal_kernel, steps, blocks), out_sha...]
  transfers between devices with their start and end apart: 24 -> 24, of which waited for: 13 -> 11; matrix products, arithmetic and copies ran while one was open for 0% -> 0% of each run, Pallas kernels for 23% -> 24%
where the time goes in v7:
time: 72.5 us; the launch traced here: 72.3 us
  starting transfers between devices  27.9 us (38%)
  waiting for transfers between devices  22.4 us (31%)
  Pallas kernels  18.6 us (26%)
  local copies, waits for them, and re-layouts  1.65 us (2%)
  between operations  0.9 us (1%)
  other arithmetic  0.84 us (1%)
    ppermute x5, starting transfers between devices, swap(): return lax.ppermute(x, 'dp', [(0, 1), (1, 0)])  7.65 us
    pallas_call x4, Pallas kernels, pair_conv(): pl.pallas_call(functools.partial(conv_kernel, kept), out_shape=jax.ShapeD...  6.92 us
    pallas_call x4, Pallas kernels, temporal_grads(): pl.pallas_call(functools.partial(grad_kernel, steps, len(pieces), extra),...  6.39 us
    ppermute x1, waiting for transfers between devices, body(): came1 = lax.ppermute(part1, 'mp', across)  5.06 us
    ppermute x1, waiting for transfers between devices, body(): other0 = lax.ppermute(mine0, 'mp', near)  4.15 us
    ppermute x5, waiting for transfers between devices, swap(): return lax.ppermute(x, 'dp', [(0, 1), (1, 0)])  3.96 us
    ppermute x1, starting transfers between devices, body(): came0 = lax.ppermute(part0, 'mp', across)  3.83 us
    ppermute x1, starting transfers between devices, body(): other0 = lax.ppermute(mine0, 'mp', near)  3.8 us
  transfers between devices with their start and end apart: 24, of which 11 were waited for; matrix products, arithmetic and copies ran while one was open for 0% of the time, Pallas kernels for 24%

profile of v7, /device:TPU:0, one launch (start us, length us, event | category | flops | bytes accessed | tf_op | source)
XLA Modules:
  0.0 72.3 jit_solution(14087175506367551011)
XLA Ops:
  1.1 1.0 %copy-done.4 = bf16[1,2,5,40,320]{4,3,2,1,0:T(8,128)(2,1)S(1)} copy-done((bf16[1,2,5,40,320]{4,3,2,1,0:T(8,128)(2,1)S(1)}, bf16[1,2,5,40,320]{4,3,2,1,0:T(8,128)(2,1)}, u32[]{:S(2)}) %copy-start.4) | copy-done | bytes 256024
  2.6 1.1 %chip_stats.1 = (f32[16,320]{1,0:T(8,128)S(1)}, bf16[2,2,5,40,320]{4,3,2,1,0:T(8,128)(2,1)S(1)}) custom-call(bf16[2,5,40,320]{3,2,1,0:T(8,128)(2,1)S(1)} %fetch.1.own_ref, bf16[2,5,40,320]{3,2,1,0:T(8,128)(2,1)S(1)} %collective-permute-done.core_ref), custom_call_target="tpu_custom_call" | custom-call | flops 1724999936 | bytes 1 | tf_op jit(solution)/shard_map/chip_stats/pallas_call | solution.py:57
  3.7 2.9 %collective-permute-start.1 = (f32[16,320]{1,0:T(8,128)S(1)}, f32[16,320]{1,0:T(8,128)S(1)}, u32[]{:S(2)}, u32[]{:S(2)}) collective-permute-start(f32[16,320]{1,0:T(8,128)S(1)} %get-tuple-element.33.s0_ref), channel_id=1, source_target_pairs={{0,8},{4,12},{8,0},{12,4},{1,9},{5,13},{9,1},{13,5},{2,10},{6,14},... | collective-permute-start | bytes 61448 | tf_op jit(solution)/shard_map/ppermute | solution.py:400
  8.4 1.7 %pair_conv.4 = bf16[400,320]{1,0:T(8,128)(2,1)S(1)} custom-call(bf16[2,2,5,40,320]{4,3,2,1,0:T(8,128)(2,1)S(1)} %get-tuple-element.36.x_ref, f32[32,320]{1,0:T(8,128)S(1)} %merge_stats.1.norm_ref, bf16[3,960,320]{2,1,0:T(8,128)(2,1)S(1)} %get-tuple-element.35.w_ref), custom_call_target="tpu_custom_call" | custom-call | flops 57500000256 | bytes 1 | tf_op jit(solution)/shard_map/pair_conv/pallas_call | solution.py:177
  10.2 2.1 %collective-permute-start.2 = (bf16[400,320]{1,0:T(8,128)(2,1)S(1)}, bf16[400,320]{1,0:T(8,128)(2,1)S(1)}, u32[]{:S(2)}, u32[]{:S(2)}) collective-permute-start(bf16[400,320]{1,0:T(8,128)(2,1)S(1)} %pair_conv.4), channel_id=1, source_target_pairs={{0,1},{1,0},{2,3},{3,2},{4,5},{5,4},{6,7},{7,6},{8,9},{9,8},{10,11... | collective-permute-start | bytes 768008 | tf_op jit(solution)/shard_map/ppermute | solution.py:406
  12.3 1.7 %pair_conv.5.a_ref = f32[400,320]{1,0:T(8,128)S(1)} custom-call(bf16[2,2,5,40,320]{4,3,2,1,0:T(8,128)(2,1)S(1)} %get-tuple-element.36.x_ref, f32[32,320]{1,0:T(8,128)S(1)} %merge_stats.1.norm_ref, bf16[3,960,320]{2,1,0:T(8,128)(2,1)S(1)} %get-tuple-element.35.w_ref), custom_call_target="tpu_custom_call" | custom-call | bytes 1 | tf_op jit(solution)/shard_map/pair_conv/pallas_call | solution.py:177
  14.0 2.6 %collective-permute-done.3.a_ref = bf16[2,5,40,320]{3,2,1,0:T(8,128)(2,1)S(1)} collective-permute-done((bf16[2,5,40,320]{3,2,1,0:T(8,128)(2,1)S(1)}, bf16[2,5,40,320]{3,2,1,0:T(8,128)(2,1)S(1)}, u32[]{:S(2)}, u32[]{:S(2)}) %collective-permute-start.3) | collective-permute-done | bytes 256032 | tf_op jit(solution)/shard_map/ppermute | solution.py:402
  16.6 1.5 %collective-permute-start.5 = (bf16[2,200,320]{2,1,0:T(8,128)(2,1)S(1)}, bf16[2,200,320]{2,1,0:T(8,128)(2,1)S(1)}, u32[]{:S(2)}, u32[]{:S(2)}) collective-permute-start(bf16[2,200,320]{2,1,0:T(8,128)(2,1)S(1)} %bitcast.4), channel_id=1, source_target_pairs={{0,16},{16,0},{1,17},{17,1},{2,18},{18,2},{3,19},{19,3},{4,20},{20... | collective-permute-start | bytes 768008 | tf_op jit(solution)/shard_map/ppermute | solution.py:396
  18.8 3.8 %collective-permute-start.6 = (bf16[400,320]{1,0:T(8,128)(2,1)S(1)}, bf16[400,320]{1,0:T(8,128)(2,1)S(1)}, u32[]{:S(2)}, u32[]{:S(2)}) collective-permute-start(bf16[400,320]{1,0:T(8,128)(2,1)S(1)} %add_parts.5.a_ref), channel_id=1, source_target_pairs={{0,3},{1,2},{2,1},{3,0},{4,7},{5,6},{6,5},{7,4},{8,11},{9,10},{10,... | collective-permute-start | bytes 768008 | tf_op jit(solution)/shard_map/ppermute | solution.py:412
  22.7 1.7 %pair_conv.6 = bf16[400,320]{1,0:T(8,128)(2,1)S(1)} custom-call(bf16[2,2,5,40,320]{4,3,2,1,0:T(8,128)(2,1)S(1)} %collect_pairs.1.x_ref, f32[32,320]{1,0:T(8,128)S(1)} %merge_stats.1.norm_ref, bf16[3,960,320]{2,1,0:T(8,128)(2,1)S(1)} %get-tuple-element.35.w_ref), custom_call_target="tpu_custom_call" | custom-call | flops 1150000000 | bytes 1 | tf_op jit(solution)/shard_map/pair_conv/pallas_call | solution.py:177
  24.5 1.8 %collective-permute-done.5.refs_0_ = bf16[2,200,320]{2,1,0:T(8,128)(2,1)S(1)} collective-permute-done((bf16[2,200,320]{2,1,0:T(8,128)(2,1)S(1)}, bf16[2,200,320]{2,1,0:T(8,128)(2,1)S(1)}, u32[]{:S(2)}, u32[]{:S(2)}) %collective-permute-start.5) | collective-permute-done | bytes 256032 | tf_op jit(solution)/shard_map/ppermute | solution.py:396
  26.3 1.7 %pair_conv.7.a_ref = f32[400,320]{1,0:T(8,128)S(1)} custom-call(bf16[2,2,5,40,320]{4,3,2,1,0:T(8,128)(2,1)S(1)} %collect_pairs.1.x_ref, f32[32,320]{1,0:T(8,128)S(1)} %merge_stats.1.norm_ref, bf16[3,960,320]{2,1,0:T(8,128)(2,1)S(1)} %get-tuple-element.35.w_ref), custom_call_target="tpu_custom_call" | custom-call | bytes 1 | tf_op jit(solution)/shard_map/pair_conv/pallas_call | solution.py:177
  28.0 2.8 %collective-permute-done.6.b_ref = bf16[400,320]{1,0:T(8,128)(2,1)S(1)} collective-permute-done((bf16[400,320]{1,0:T(8,128)(2,1)S(1)}, bf16[400,320]{1,0:T(8,128)(2,1)S(1)}, u32[]{:S(2)}, u32[]{:S(2)}) %collective-permute-start.6) | collective-permute-done | bytes 256032 | tf_op jit(solution)/shard_map/ppermute | solution.py:412
  30.9 1.7 %collective-permute-start.10 = (bf16[400,320]{1,0:T(8,128)(2,1)S(1)}, bf16[400,320]{1,0:T(8,128)(2,1)S(1)}, u32[]{:S(2)}, u32[]{:S(2)}) collective-permute-start(bf16[400,320]{1,0:T(8,128)(2,1)S(1)} %add_parts.6.refs_4_.refs_0_), channel_id=1, source_target_pairs={{0,16},{16,0},{1,17},{17,1},{2,18},{18,2},{3,19},{19,3},{4,20},{20... | collective-permute-start | bytes 768008 | tf_op jit(solution)/shard_map/ppermute | solution.py:396
  32.7 3.8 %collective-permute-start.9 = (bf16[400,320]{1,0:T(8,128)(2,1)S(1)}, bf16[400,320]{1,0:T(8,128)(2,1)S(1)}, u32[]{:S(2)}, u32[]{:S(2)}) collective-permute-start(bf16[400,320]{1,0:T(8,128)(2,1)S(1)} %add_parts.6.refs_4_.refs_0_), channel_id=1, source_target_pairs={{0,1},{1,0},{2,3},{3,2},{4,5},{5,4},{6,7},{7,6},{8,9},{9,8},{10,11... | collective-permute-start | bytes 768008 | tf_op jit(solution)/shard_map/ppermute | solution.py:423
  36.5 1.1 %collective-permute-start.8 = (bf16[2,200,320]{2,1,0:T(8,128)(2,1)S(1)}, bf16[2,200,320]{2,1,0:T(8,128)(2,1)S(1)}, u32[]{:S(2)}, u32[]{:S(2)}) collective-permute-start(bf16[2,200,320]{2,1,0:T(8,128)(2,1)S(1)} %bitcast.5), channel_id=1, source_target_pairs={{0,8},{4,12},{8,0},{12,4},{1,9},{5,13},{9,1},{13,5},{2,10},{6,14},... | collective-permute-start | bytes 768008 | tf_op jit(solution)/shard_map/ppermute | solution.py:425
  37.7 2.5 %collective-permute-start.13 = (bf16[400,320]{1,0:T(8,128)(2,1)S(1)}, bf16[400,320]{1,0:T(8,128)(2,1)S(1)}, u32[]{:S(2)}, u32[]{:S(2)}) collective-permute-start(bf16[400,320]{1,0:T(8,128)(2,1)S(1)} %add_parts.7.a_ref), channel_id=1, source_target_pairs={{0,3},{1,2},{2,1},{3,0},{4,7},{5,6},{6,5},{7,4},{8,11},{9,10},{10,... | collective-permute-start | bytes 768008 | tf_op jit(solution)/shard_map/ppermute | solution.py:422
  40.2 4.1 %collective-permute-done.9.x_ref = bf16[400,320]{1,0:T(8,128)(2,1)S(1)} collective-permute-done((bf16[400,320]{1,0:T(8,128)(2,1)S(1)}, bf16[400,320]{1,0:T(8,128)(2,1)S(1)}, u32[]{:S(2)}, u32[]{:S(2)}) %collective-permute-start.9) | collective-permute-done | bytes 256032 | tf_op jit(solution)/shard_map/ppermute | solution.py:423
  44.4 1.4 %collective-permute-start.14 = (bf16[400,320]{1,0:T(8,128)(2,1)S(1)}, bf16[400,320]{1,0:T(8,128)(2,1)S(1)}, u32[]{:S(2)}, u32[]{:S(2)}) collective-permute-start(bf16[400,320]{1,0:T(8,128)(2,1)S(1)} %copy_piece.1.refs_5_.refs_1_), channel_id=1, source_target_pairs={{0,16},{16,0},{1,17},{17,1},{2,18},{18,2},{3,19},{19,3},{4,20},{20... | collective-permute-start | bytes 768008 | tf_op jit(solution)/shard_map/ppermute | solution.py:396
  45.8 5.1 %collective-permute-done.13.b_ref = bf16[400,320]{1,0:T(8,128)(2,1)S(1)} collective-permute-done((bf16[400,320]{1,0:T(8,128)(2,1)S(1)}, bf16[400,320]{1,0:T(8,128)(2,1)S(1)}, u32[]{:S(2)}, u32[]{:S(2)}) %collective-permute-start.13) | collective-permute-done | bytes 256032 | tf_op jit(solution)/shard_map/ppermute | solution.py:422
  51.0 1.7 %collective-permute-start.15 = (bf16[400,320]{1,0:T(8,128)(2,1)S(1)}, bf16[400,320]{1,0:T(8,128)(2,1)S(1)}, u32[]{:S(2)}, u32[]{:S(2)}) collective-permute-start(bf16[400,320]{1,0:T(8,128)(2,1)S(1)} %add_parts.8.refs_2_.refs_4_), channel_id=1, source_target_pairs={{0,1},{1,0},{2,3},{3,2},{4,5},{5,4},{6,7},{7,6},{8,9},{9,8},{10,11... | collective-permute-start | bytes 768008 | tf_op jit(solution)/shard_map/ppermute | solution.py:432
  53.2 1.4 %collective-permute-start.16 = (bf16[400,320]{1,0:T(8,128)(2,1)S(1)}, bf16[400,320]{1,0:T(8,128)(2,1)S(1)}, u32[]{:S(2)}, u32[]{:S(2)}) collective-permute-start(bf16[400,320]{1,0:T(8,128)(2,1)S(1)} %add_parts.8.refs_2_.refs_4_), channel_id=1, source_target_pairs={{0,16},{16,0},{1,17},{17,1},{2,18},{18,2},{3,19},{19,3},{4,20},{20... | collective-permute-start | bytes 768008 | tf_op jit(solution)/shard_map/ppermute | solution.py:396
  54.6 1.4 %temporal_grads.4.refs_6_ = f32[3,320,320]{2,1,0:T(8,128)S(1)} custom-call(bf16[2,200,320]{2,1,0:T(8,128)(2,1)S(1)} %bitcast.7, bf16[2,200,320]{2,1,0:T(8,128)(2,1)S(1)} %collective-permute-done.7.refs_1_, bf16[2,200,320]{2,1,0:T(8,128)(2,1)S(1)} %collective-permute-done.8.refs_2_, bf16[2,200,320]{2,1,0:T(8,128)(2,1)S(1)} %collective-permute-done.11.refs_3_, ...), custom_call_target="tpu_custom_call" | custom-call | flops 1150000000 | bytes 1 | tf_op jit(solution)/shard_map/temporal_grads/pallas_call | solution.py:279
  56.0 1.9 %collective-permute-done.15.refs_3_.refs_5_ = bf16[400,320]{1,0:T(8,128)(2,1)S(1)} collective-permute-done((bf16[400,320]{1,0:T(8,128)(2,1)S(1)}, bf16[400,320]{1,0:T(8,128)(2,1)S(1)}, u32[]{:S(2)}, u32[]{:S(2)}) %collective-permute-start.15) | collective-permute-done | bytes 256032 | tf_op jit(solution)/shard_map/ppermute | solution.py:432
  57.9 0.9 %temporal_conv.3 = bf16[2,200,320]{2,1,0:T(8,128)(2,1)S(1)} custom-call(bf16[400,320]{1,0:T(8,128)(2,1)S(1)} %add_parts.6.refs_4_.refs_0_, bf16[400,320]{1,0:T(8,128)(2,1)S(1)} %copy_piece.1.refs_5_.refs_1_, bf16[400,320]{1,0:T(8,128)(2,1)S(1)} %add_parts.8.refs_2_.refs_4_, bf16[400,320]{1,0:T(8,128)(2,1)S(1)} %collective-permute-done.15.refs_3_.refs_5_, ...), custom_call_target="tpu_custom_call" | custom-call | flops 57500000256 | bytes 1 | tf_op jit(solution)/shard_map/temporal_conv/pallas_call | solution.py:310
  59.5 1.6 %collective-permute-start.21 = (bf16[400,320]{1,0:T(8,128)(2,1)S(1)}, bf16[400,320]{1,0:T(8,128)(2,1)S(1)}, u32[]{:S(2)}, u32[]{:S(2)}) collective-permute-start(bf16[400,320]{1,0:T(8,128)(2,1)S(1)} %collective-permute-done.15.refs_3_.refs_5_), channel_id=1, source_target_pairs={{0,16},{16,0},{1,17},{17,1},{2,18},{18,2},{3,19},{19,3},{4,20},{20... | collective-permute-start | bytes 768008 | tf_op jit(solution)/shard_map/ppermute | solution.py:396
  61.1 0.9 %temporal_conv.4.a_ref = f32[2,200,320]{2,1,0:T(8,128)S(1)} custom-call(bf16[400,320]{1,0:T(8,128)(2,1)S(1)} %add_parts.6.refs_4_.refs_0_, bf16[400,320]{1,0:T(8,128)(2,1)S(1)} %copy_piece.1.refs_5_.refs_1_, bf16[400,320]{1,0:T(8,128)(2,1)S(1)} %add_parts.8.refs_2_.refs_4_, bf16[400,320]{1,0:T(8,128)(2,1)S(1)} %collective-permute-done.15.refs_3_.refs_5_, ...), custom_call_target="tpu_custom_call" | custom-call | bytes 1 | tf_op jit(solution)/shard_map/temporal_conv/pallas_call | solution.py:310
  62.5 1.4 %temporal_grads.5.refs_6_ = f32[3,320,320]{2,1,0:T(8,128)S(1)} custom-call(bf16[2,200,320]{2,1,0:T(8,128)(2,1)S(1)} %collective-permute-done.5.refs_0_, bf16[2,200,320]{2,1,0:T(8,128)(2,1)S(1)} %collective-permute-done.18.refs_1_, bf16[2,200,320]{2,1,0:T(8,128)(2,1)S(1)} %collective-permute-done.19.refs_2_, ...), custom_call_target="tpu_custom_call" | custom-call | bytes 1 | tf_op jit(solution)/shard_map/temporal_grads/pallas_call | solution.py:279
  63.9 1.4 %temporal_grads.6.refs_7_ = f32[3,320,320]{2,1,0:T(8,128)S(1)} custom-call(bf16[2,200,320]{2,1,0:T(8,128)(2,1)S(1)} %bitcast.8, bf16[2,200,320]{2,1,0:T(8,128)(2,1)S(1)} %collective-permute-done.7.refs_1_, bf16[2,200,320]{2,1,0:T(8,128)(2,1)S(1)} %collective-permute-done.8.refs_2_, bf16[2,200,320]{2,1,0:T(8,128)(2,1)S(1)} %collective-permute-done.11.refs_3_, ...), custom_call_target="tpu_custom_call" | custom-call | bytes 1 | tf_op jit(solution)/shard_map/temporal_grads/pallas_call | solution.py:279
  65.3 1.6 %temporal_conv.5 = (bf16[2,200,320]{2,1,0:T(8,128)(2,1)S(1)}, f32[2,200,320]{2,1,0:T(8,128)S(1)}) custom-call(bf16[400,320]{1,0:T(8,128)(2,1)S(1)} %add_parts.6.refs_4_.refs_0_, bf16[400,320]{1,0:T(8,128)(2,1)S(1)} %copy_piece.1.refs_5_.refs_1_, bf16[400,320]{1,0:T(8,128)(2,1)S(1)} %add_parts.8.refs_2_.refs_4_, ...), custom_call_target="tpu_custom_call" | custom-call | bytes 1 | tf_op jit(solution)/shard_map/temporal_conv/pallas_call | solution.py:310
  67.0 2.2 %collective-permute-done.21.refs_5_ = bf16[400,320]{1,0:T(8,128)(2,1)S(1)} collective-permute-done((bf16[400,320]{1,0:T(8,128)(2,1)S(1)}, bf16[400,320]{1,0:T(8,128)(2,1)S(1)}, u32[]{:S(2)}, u32[]{:S(2)}) %collective-permute-start.21) | collective-permute-done | bytes 256032 | tf_op jit(solution)/shard_map/ppermute | solution.py:396
  69.2 2.3 %temporal_grads.7 = f32[3,320,320]{2,1,0:T(8,128)} custom-call(bf16[2,200,320]{2,1,0:T(8,128)(2,1)S(1)} %collective-permute-done.5.refs_0_, bf16[2,200,320]{2,1,0:T(8,128)(2,1)S(1)} %collective-permute-done.18.refs_1_, bf16[2,200,320]{2,1,0:T(8,128)(2,1)S(1)} %collective-permute-done.19.refs_2_, bf16[2,200,320]{2,1,0:T(8,128)(2,1)S(1)} %collective-permute-done.20.refs_3_, ...), custom_call_target="tpu_custom_call" | custom-call | flops 57500000256 | bytes 1 | tf_op jit(solution)/shard_map/temporal_grads/pallas_call | solution.py:279
  (55 shorter events, 6.6 us)
Async XLA Ops:
  0.6 2.0 %collective-permute-start = (bf16[2,5,40,320]{3,2,1,0:T(8,128)(2,1)}, bf16[2,5,40,320]{3,2,1,0:T(8,128)(2,1)S(1)}, u32[]{:S(2)}, u32[]{:S(2)}) collective-permute-start(bf16[2,5,40,320]{3,2,1,0:T(8,128)(2,1)} %bitcast.10), channel_id=1, source_target_pairs={{0,4},{4,0},{8,12},{12,8},{1,5},{5,1},{9,13},{13,9},{2,6},{6,2},{1... | collective-permute-start | bytes 768008 | tf_op jit(solution)/shard_map/ppermute | solution.py:398
  1.1 1.0 %copy-start.4 = (bf16[1,2,5,40,320]{4,3,2,1,0:T(8,128)(2,1)S(1)}, bf16[1,2,5,40,320]{4,3,2,1,0:T(8,128)(2,1)}, u32[]{:S(2)}) copy-start(bf16[1,2,5,40,320]{4,3,2,1,0:T(8,128)(2,1)} %param.6) | copy-start | bytes 768004
  2.2 4.4 %copy-start.3 = (bf16[9,320,320]{2,1,0:T(8,128)(2,1)S(1)}, bf16[9,320,320]{2,1,0:T(8,128)(2,1)}, u32[]{:S(2)}) copy-start(bf16[9,320,320]{2,1,0:T(8,128)(2,1)} %param.9) | copy-start | bytes 5529604
  2.2 4.4 %copy-start.6 = (f32[320]{0:T(512)S(1)}, f32[320]{0:T(512)}, u32[]{:S(2)}) copy-start(f32[320]{0:T(512)} %gain_ref.1) | copy-start | bytes 3844
  2.2 4.4 %copy-start.7 = (f32[320]{0:T(512)S(1)}, f32[320]{0:T(512)}, u32[]{:S(2)}) copy-start(f32[320]{0:T(512)} %bias_ref.1) | copy-start | bytes 3844
  3.7 4.7 %collective-permute-start.1 = (f32[16,320]{1,0:T(8,128)S(1)}, f32[16,320]{1,0:T(8,128)S(1)}, u32[]{:S(2)}, u32[]{:S(2)}) collective-permute-start(f32[16,320]{1,0:T(8,128)S(1)} %get-tuple-element.33.s0_ref), channel_id=1, source_target_pairs={{0,8},{4,12},{8,0},{12,4},{1,9},{5,13},{9,1},{13,5},{2,10},{6,14},... | collective-permute-start | bytes 61448 | tf_op jit(solution)/shard_map/ppermute | solution.py:400
  6.6 1.0 %copy-start.5 = (bf16[1,2,5,40,320]{4,3,2,1,0:T(8,128)(2,1)S(1)}, bf16[1,2,5,40,320]{4,3,2,1,0:T(8,128)(2,1)}, u32[]{:S(2)}) copy-start(bf16[1,2,5,40,320]{4,3,2,1,0:T(8,128)(2,1)} %param.6) | copy-start | bytes 768004
  7.6 9.0 %collective-permute-start.3 = (bf16[2,5,40,320]{3,2,1,0:T(8,128)(2,1)S(1)}, bf16[2,5,40,320]{3,2,1,0:T(8,128)(2,1)S(1)}, u32[]{:S(2)}, u32[]{:S(2)}) collective-permute-start(bf16[2,5,40,320]{3,2,1,0:T(8,128)(2,1)S(1)} %bitcast.12), channel_id=1, source_target_pairs={{0,8},{4,12},{8,0},{12,4},{1,9},{5,13},{9,1},{13,5},{2,10},{6,14},... | collective-permute-start | bytes 768008 | tf_op jit(solution)/shard_map/ppermute | solution.py:402
  10.2 6.4 %copy-start.1 = (bf16[1,2,5,40,320]{4,3,2,1,0:T(8,128)(2,1)S(1)}, bf16[1,2,5,40,320]{4,3,2,1,0:T(8,128)(2,1)}, u32[]{:S(2)}) copy-start(bf16[1,2,5,40,320]{4,3,2,1,0:T(8,128)(2,1)} %param.11) | copy-start | bytes 768004
  10.2 8.6 %collective-permute-start.2 = (bf16[400,320]{1,0:T(8,128)(2,1)S(1)}, bf16[400,320]{1,0:T(8,128)(2,1)S(1)}, u32[]{:S(2)}, u32[]{:S(2)}) collective-permute-start(bf16[400,320]{1,0:T(8,128)(2,1)S(1)} %pair_conv.4), channel_id=1, source_target_pairs={{0,1},{1,0},{2,3},{3,2},{4,5},{5,4},{6,7},{7,6},{8,9},{9,8},{10,11... | collective-permute-start | bytes 768008 | tf_op jit(solution)/shard_map/ppermute | solution.py:406
  16.6 6.0 %collective-permute-start.4 = (bf16[2,5,40,320]{3,2,1,0:T(8,128)(2,1)S(1)}, bf16[2,5,40,320]{3,2,1,0:T(8,128)(2,1)S(1)}, u32[]{:S(2)}, u32[]{:S(2)}) collective-permute-start(bf16[2,5,40,320]{3,2,1,0:T(8,128)(2,1)S(1)} %collective-permute-done.3.a_ref), channel_id=1, source_target_pairs={{0,4},{4,0},{8,12},{12,8},{1,5},{5,1},{9,13},{13,9},{2,6},{6,2},{1... | collective-permute-start | bytes 768008 | tf_op jit(solution)/shard_map/ppermute | solution.py:409
  16.6 9.7 %collective-permute-start.5 = (bf16[2,200,320]{2,1,0:T(8,128)(2,1)S(1)}, bf16[2,200,320]{2,1,0:T(8,128)(2,1)S(1)}, u32[]{:S(2)}, u32[]{:S(2)}) collective-permute-start(bf16[2,200,320]{2,1,0:T(8,128)(2,1)S(1)} %bitcast.4), channel_id=1, source_target_pairs={{0,16},{16,0},{1,17},{17,1},{2,18},{18,2},{3,19},{19,3},{4,20},{20... | collective-permute-start | bytes 768008 | tf_op jit(solution)/shard_map/ppermute | solution.py:396
  18.8 12.1 %collective-permute-start.6 = (bf16[400,320]{1,0:T(8,128)(2,1)S(1)}, bf16[400,320]{1,0:T(8,128)(2,1)S(1)}, u32[]{:S(2)}, u32[]{:S(2)}) collective-permute-start(bf16[400,320]{1,0:T(8,128)(2,1)S(1)} %add_parts.5.a_ref), channel_id=1, source_target_pairs={{0,3},{1,2},{2,1},{3,0},{4,7},{5,6},{6,5},{7,4},{8,11},{9,10},{10,... | collective-permute-start | bytes 768008 | tf_op jit(solution)/shard_map/ppermute | solution.py:412
  24.4 13.2 %collective-permute-start.12 = (bf16[400,320]{1,0:T(8,128)(2,1)S(1)}, bf16[400,320]{1,0:T(8,128)(2,1)S(1)}, u32[]{:S(2)}, u32[]{:S(2)}) collective-permute-start(bf16[400,320]{1,0:T(8,128)(2,1)S(1)} %pair_conv.6), channel_id=1, source_target_pairs={{0,1},{1,0},{2,3},{3,2},{4,5},{5,4},{6,7},{7,6},{8,9},{9,8},{10,11... | collective-permute-start | bytes 768008 | tf_op jit(solution)/shard_map/ppermute | solution.py:414
  28.0 8.5 %copy-start.2 = (bf16[1,2,5,40,320]{4,3,2,1,0:T(8,128)(2,1)S(1)}, bf16[1,2,5,40,320]{4,3,2,1,0:T(8,128)(2,1)}, u32[]{:S(2)}) copy-start(bf16[1,2,5,40,320]{4,3,2,1,0:T(8,128)(2,1)} %param.11) | copy-start | bytes 768004
  30.9 9.3 %collective-permute-start.10 = (bf16[400,320]{1,0:T(8,128)(2,1)S(1)}, bf16[400,320]{1,0:T(8,128)(2,1)S(1)}, u32[]{:S(2)}, u32[]{:S(2)}) collective-permute-start(bf16[400,320]{1,0:T(8,128)(2,1)S(1)} %add_parts.6.refs_4_.refs_0_), channel_id=1, source_target_pairs={{0,16},{16,0},{1,17},{17,1},{2,18},{18,2},{3,19},{19,3},{4,20},{20... | collective-permute-start | bytes 768008 | tf_op jit(solution)/shard_map/ppermute | solution.py:396
  32.7 11.7 %collective-permute-start.9 = (bf16[400,320]{1,0:T(8,128)(2,1)S(1)}, bf16[400,320]{1,0:T(8,128)(2,1)S(1)}, u32[]{:S(2)}, u32[]{:S(2)}) collective-permute-start(bf16[400,320]{1,0:T(8,128)(2,1)S(1)} %add_parts.6.refs_4_.refs_0_), channel_id=1, source_target_pairs={{0,1},{1,0},{2,3},{3,2},{4,5},{5,4},{6,7},{7,6},{8,9},{9,8},{10,11... | collective-permute-start | bytes 768008 | tf_op jit(solution)/shard_map/ppermute | solution.py:423
  36.5 9.3 %collective-permute-start.8 = (bf16[2,200,320]{2,1,0:T(8,128)(2,1)S(1)}, bf16[2,200,320]{2,1,0:T(8,128)(2,1)S(1)}, u32[]{:S(2)}, u32[]{:S(2)}) collective-permute-start(bf16[2,200,320]{2,1,0:T(8,128)(2,1)S(1)} %bitcast.5), channel_id=1, source_target_pairs={{0,8},{4,12},{8,0},{12,4},{1,9},{5,13},{9,1},{13,5},{2,10},{6,14},... | collective-permute-start | bytes 768008 | tf_op jit(solution)/shard_map/ppermute | solution.py:425
  37.7 13.2 %collective-permute-start.13 = (bf16[400,320]{1,0:T(8,128)(2,1)S(1)}, bf16[400,320]{1,0:T(8,128)(2,1)S(1)}, u32[]{:S(2)}, u32[]{:S(2)}) collective-permute-start(bf16[400,320]{1,0:T(8,128)(2,1)S(1)} %add_parts.7.a_ref), channel_id=1, source_target_pairs={{0,3},{1,2},{2,1},{3,0},{4,7},{5,6},{6,5},{7,4},{8,11},{9,10},{10,... | collective-permute-start | bytes 768008 | tf_op jit(solution)/shard_map/ppermute | solution.py:422
  40.2 14.4 %collective-permute-start.7 = (bf16[2,200,320]{2,1,0:T(8,128)(2,1)S(1)}, bf16[2,200,320]{2,1,0:T(8,128)(2,1)S(1)}, u32[]{:S(2)}, u32[]{:S(2)}) collective-permute-start(bf16[2,200,320]{2,1,0:T(8,128)(2,1)S(1)} %bitcast.6), channel_id=1, source_target_pairs={{0,4},{4,0},{8,12},{12,8},{1,5},{5,1},{9,13},{13,9},{2,6},{6,2},{1... | collective-permute-start | bytes 768008 | tf_op jit(solution)/shard_map/ppermute | solution.py:424
  44.4 8.8 %collective-permute-start.14 = (bf16[400,320]{1,0:T(8,128)(2,1)S(1)}, bf16[400,320]{1,0:T(8,128)(2,1)S(1)}, u32[]{:S(2)}, u32[]{:S(2)}) collective-permute-start(bf16[400,320]{1,0:T(8,128)(2,1)S(1)} %copy_piece.1.refs_5_.refs_1_), channel_id=1, source_target_pairs={{0,16},{16,0},{1,17},{17,1},{2,18},{18,2},{3,19},{19,3},{4,20},{20... | collective-permute-start | bytes 768008 | tf_op jit(solution)/shard_map/ppermute | solution.py:396
  45.8 8.8 %collective-permute-start.11 = (bf16[2,200,320]{2,1,0:T(8,128)(2,1)S(1)}, bf16[2,200,320]{2,1,0:T(8,128)(2,1)S(1)}, u32[]{:S(2)}, u32[]{:S(2)}) collective-permute-start(bf16[2,200,320]{2,1,0:T(8,128)(2,1)S(1)} %collective-permute-done.8.refs_2_), channel_id=1, source_target_pairs={{0,4},{4,0},{8,12},{12,8},{1,5},{5,1},{9,13},{13,9},{2,6},{6,2},{1... | collective-permute-start | bytes 768008 | tf_op jit(solution)/shard_map/ppermute | solution.py:433
  51.0 6.9 %copy-start = (bf16[3,320,320]{2,1,0:T(8,128)(2,1)S(1)}, bf16[3,320,320]{2,1,0:T(8,128)(2,1)}, u32[]{:S(2)}) copy-start(bf16[3,320,320]{2,1,0:T(8,128)(2,1)} %refs_4_.5) | copy-start | bytes 1843204
  51.0 6.9 %collective-permute-start.15 = (bf16[400,320]{1,0:T(8,128)(2,1)S(1)}, bf16[400,320]{1,0:T(8,128)(2,1)S(1)}, u32[]{:S(2)}, u32[]{:S(2)}) collective-permute-start(bf16[400,320]{1,0:T(8,128)(2,1)S(1)} %add_parts.8.refs_2_.refs_4_), channel_id=1, source_target_pairs={{0,1},{1,0},{2,3},{3,2},{4,5},{5,4},{6,7},{7,6},{8,9},{9,8},{10,11... | collective-permute-start | bytes 768008 | tf_op jit(solution)/shard_map/ppermute | solution.py:432
  52.7 6.9 %collective-permute-start.19 = (bf16[2,200,320]{2,1,0:T(8,128)(2,1)S(1)}, bf16[2,200,320]{2,1,0:T(8,128)(2,1)S(1)}, u32[]{:S(2)}, u32[]{:S(2)}) collective-permute-start(bf16[2,200,320]{2,1,0:T(8,128)(2,1)S(1)} %collective-permute-done.5.refs_0_), channel_id=1, source_target_pairs={{0,8},{4,12},{8,0},{12,4},{1,9},{5,13},{9,1},{13,5},{2,10},{6,14},... | collective-permute-start | bytes 768008 | tf_op jit(solution)/shard_map/ppermute | solution.py:429
  53.2 8.8 %collective-permute-start.16 = (bf16[400,320]{1,0:T(8,128)(2,1)S(1)}, bf16[400,320]{1,0:T(8,128)(2,1)S(1)}, u32[]{:S(2)}, u32[]{:S(2)}) collective-permute-start(bf16[400,320]{1,0:T(8,128)(2,1)S(1)} %add_parts.8.refs_2_.refs_4_), channel_id=1, source_target_pairs={{0,16},{16,0},{1,17},{17,1},{2,18},{18,2},{3,19},{19,3},{4,20},{20... | collective-permute-start | bytes 768008 | tf_op jit(solution)/shard_map/ppermute | solution.py:396
  58.8 3.2 %collective-permute-start.17 = (bf16[2,200,320]{2,1,0:T(8,128)(2,1)S(1)}, bf16[2,200,320]{2,1,0:T(8,128)(2,1)S(1)}, u32[]{:S(2)}, u32[]{:S(2)}) collective-permute-start(bf16[2,200,320]{2,1,0:T(8,128)(2,1)S(1)} %temporal_conv.3), channel_id=1, source_target_pairs={{0,4},{4,0},{8,12},{12,8},{1,5},{5,1},{9,13},{13,9},{2,6},{6,2},{1... | collective-permute-start | bytes 768008 | tf_op jit(solution)/shard_map/ppermute | solution.py:442
  58.9 3.6 %collective-permute-start.18 = (bf16[2,200,320]{2,1,0:T(8,128)(2,1)S(1)}, bf16[2,200,320]{2,1,0:T(8,128)(2,1)S(1)}, u32[]{:S(2)}, u32[]{:S(2)}) collective-permute-start(bf16[2,200,320]{2,1,0:T(8,128)(2,1)S(1)} %collective-permute-done.5.refs_0_), channel_id=1, source_target_pairs={{0,4},{4,0},{8,12},{12,8},{1,5},{5,1},{9,13},{13,9},{2,6},{6,2},{1... | collective-permute-start | bytes 768008 | tf_op jit(solution)/shard_map/ppermute | solution.py:428
  59.5 3.0 %collective-permute-start.20 = (bf16[2,200,320]{2,1,0:T(8,128)(2,1)S(1)}, bf16[2,200,320]{2,1,0:T(8,128)(2,1)S(1)}, u32[]{:S(2)}, u32[]{:S(2)}) collective-permute-start(bf16[2,200,320]{2,1,0:T(8,128)(2,1)S(1)} %collective-permute-done.19.refs_2_), channel_id=1, source_target_pairs={{0,4},{4,0},{8,12},{12,8},{1,5},{5,1},{9,13},{13,9},{2,6},{6,2},{1... | collective-permute-start | bytes 768008 | tf_op jit(solution)/shard_map/ppermute | solution.py:436
  59.5 9.7 %collective-permute-start.21 = (bf16[400,320]{1,0:T(8,128)(2,1)S(1)}, bf16[400,320]{1,0:T(8,128)(2,1)S(1)}, u32[]{:S(2)}, u32[]{:S(2)}) collective-permute-start(bf16[400,320]{1,0:T(8,128)(2,1)S(1)} %collective-permute-done.15.refs_3_.refs_5_), channel_id=1, source_target_pairs={{0,16},{16,0},{1,17},{17,1},{2,18},{18,2},{3,19},{19,3},{4,20},{20... | collective-permute-start | bytes 768008 | tf_op jit(solution)/shard_map/ppermute | solution.py:396
  62.1 9.4 %collective-permute-start.23 = (bf16[2,200,320]{2,1,0:T(8,128)(2,1)S(1)}, bf16[2,200,320]{2,1,0:T(8,128)(2,1)S(1)}, u32[]{:S(2)}, u32[]{:S(2)}) collective-permute-start(bf16[2,200,320]{2,1,0:T(8,128)(2,1)S(1)} %add_parts.9), channel_id=1, source_target_pairs={{0,8},{4,12},{8,0},{12,4},{1,9},{5,13},{9,1},{13,5},{2,10},{6,14},... | collective-permute-start | bytes 768008 | tf_op jit(solution)/shard_map/ppermute | solution.py:449
  66.9 4.5 %collective-permute-start.22 = (bf16[2,200,320]{2,1,0:T(8,128)(2,1)S(1)}, bf16[2,200,320]{2,1,0:T(8,128)(2,1)S(1)}, u32[]{:S(2)}, u32[]{:S(2)}) collective-permute-start(bf16[2,200,320]{2,1,0:T(8,128)(2,1)S(1)} %get-tuple-element.61), channel_id=1, source_target_pairs={{0,4},{4,0},{8,12},{12,8},{1,5},{5,1},{9,13},{13,9},{2,6},{6,2},{1... | collective-permute-start | bytes 768008 | tf_op jit(solution)/shard_map/ppermute | solution.py:448

commit v8 on v7

--- a/solution.py
+++ b/solution.py
@@ -238,7 +238,8 @@
     out_ref, s_ref, c_ref = refs[-3:]
     t = lax.axis_index("tm")
     frames, rows, width = s_ref.shape
-    zero_frames(s_ref, (), frames, rows, width)
+    for f in range(1, frames - 1):
+        s_ref[f, rows - PAD :] = jnp.zeros((PAD, width), bf16)
     zero_frames(c_ref, (), frames, rows, c_ref.shape[-1])
     put_pairs(s_ref, (), steps, pieces)
     for block, cot in enumerate(cots):
@@ -292,7 +293,8 @@
     *refs, s_ref = refs
     pieces, w_ref, outs = refs[: -1 - len(blocks)], refs[-1 - len(blocks)], refs[-len(blocks) :]
     frames, rows, width = s_ref.shape
-    zero_frames(s_ref, (), frames, rows, width)
+    s_ref[0] = jnp.zeros((rows, width), bf16)
+    s_ref[frames - 1] = jnp.zeros((rows, width), bf16)
     put_pairs(s_ref, (), steps, pieces)
     for i, out in zip(blocks, outs, strict=True):
         first = 2 * jnp.bitwise_xor(lax.axis_index("tm"), i)

time: 72.5 us -> 72.5 us (level)
  no operation moved by 1% of the time
where the time goes in v8:
time: 72.5 us; the launch traced here: 72.3 us
  starting transfers between devices  27.9 us (38%)
  waiting for transfers between devices  22.7 us (31%)
  Pallas kernels  18.3 us (25%)
  local copies, waits for them, and re-layouts  1.65 us (2%)
  between operations  0.89 us (1%)
  other arithmetic  0.84 us (1%)
    ppermute x5, starting transfers between devices, swap(): return lax.ppermute(x, 'dp', [(0, 1), (1, 0)])  7.62 us
    pallas_call x4, Pallas kernels, pair_conv(): pl.pallas_call(functools.partial(conv_kernel, kept), out_shape=jax.ShapeD...  6.91 us
    pallas_call x4, Pallas kernels, temporal_grads(): pl.pallas_call(functools.partial(grad_kernel, steps, len(pieces), extra),...  6.28 us
    ppermute x1, waiting for transfers between devices, body(): came1 = lax.ppermute(part1, 'mp', across)  5.06 us
    ppermute x5, waiting for transfers between devices, swap(): return lax.ppermute(x, 'dp', [(0, 1), (1, 0)])  4.2 us
    ppermute x1, waiting for transfers between devices, body(): other0 = lax.ppermute(mine0, 'mp', near)  4.15 us
    ppermute x1, starting transfers between devices, body(): came0 = lax.ppermute(part0, 'mp', across)  3.83 us
    ppermute x1, starting transfers between devices, body(): other0 = lax.ppermute(mine0, 'mp', near)  3.8 us
  transfers between devices with their start and end apart: 24, of which 11 were waited for; matrix products, arithmetic and copies ran while one was open for 0% of the time, Pallas kernels for 24%

profile of v8, /device:TPU:0, one launch (start us, length us, event | category | flops | bytes accessed | tf_op | source)
XLA Modules:
  0.0 72.3 jit_solution(10265195868726380793)
XLA Ops:
  1.1 1.0 %copy-done.4 = bf16[1,2,5,40,320]{4,3,2,1,0:T(8,128)(2,1)S(1)} copy-done((bf16[1,2,5,40,320]{4,3,2,1,0:T(8,128)(2,1)S(1)}, bf16[1,2,5,40,320]{4,3,2,1,0:T(8,128)(2,1)}, u32[]{:S(2)}) %copy-start.4) | copy-done | bytes 256024
  2.6 1.1 %chip_stats.1 = (f32[16,320]{1,0:T(8,128)S(1)}, bf16[2,2,5,40,320]{4,3,2,1,0:T(8,128)(2,1)S(1)}) custom-call(bf16[2,5,40,320]{3,2,1,0:T(8,128)(2,1)S(1)} %fetch.1.own_ref, bf16[2,5,40,320]{3,2,1,0:T(8,128)(2,1)S(1)} %collective-permute-done.core_ref), custom_call_target="tpu_custom_call" | custom-call | flops 1724999936 | bytes 1 | tf_op jit(solution)/shard_map/chip_stats/pallas_call | solution.py:57
  3.7 2.9 %collective-permute-start.1 = (f32[16,320]{1,0:T(8,128)S(1)}, f32[16,320]{1,0:T(8,128)S(1)}, u32[]{:S(2)}, u32[]{:S(2)}) collective-permute-start(f32[16,320]{1,0:T(8,128)S(1)} %get-tuple-element.33.s0_ref), channel_id=1, source_target_pairs={{0,8},{4,12},{8,0},{12,4},{1,9},{5,13},{9,1},{13,5},{2,10},{6,14},... | collective-permute-start | bytes 61448 | tf_op jit(solution)/shard_map/ppermute | solution.py:402
  8.4 1.7 %pair_conv.4 = bf16[400,320]{1,0:T(8,128)(2,1)S(1)} custom-call(bf16[2,2,5,40,320]{4,3,2,1,0:T(8,128)(2,1)S(1)} %get-tuple-element.36.x_ref, f32[32,320]{1,0:T(8,128)S(1)} %merge_stats.1.norm_ref, bf16[3,960,320]{2,1,0:T(8,128)(2,1)S(1)} %get-tuple-element.35.w_ref), custom_call_target="tpu_custom_call" | custom-call | flops 57500000256 | bytes 1 | tf_op jit(solution)/shard_map/pair_conv/pallas_call | solution.py:177
  10.2 2.1 %collective-permute-start.2 = (bf16[400,320]{1,0:T(8,128)(2,1)S(1)}, bf16[400,320]{1,0:T(8,128)(2,1)S(1)}, u32[]{:S(2)}, u32[]{:S(2)}) collective-permute-start(bf16[400,320]{1,0:T(8,128)(2,1)S(1)} %pair_conv.4), channel_id=1, source_target_pairs={{0,1},{1,0},{2,3},{3,2},{4,5},{5,4},{6,7},{7,6},{8,9},{9,8},{10,11... | collective-permute-start | bytes 768008 | tf_op jit(solution)/shard_map/ppermute | solution.py:408
  12.3 1.7 %pair_conv.5.a_ref = f32[400,320]{1,0:T(8,128)S(1)} custom-call(bf16[2,2,5,40,320]{4,3,2,1,0:T(8,128)(2,1)S(1)} %get-tuple-element.36.x_ref, f32[32,320]{1,0:T(8,128)S(1)} %merge_stats.1.norm_ref, bf16[3,960,320]{2,1,0:T(8,128)(2,1)S(1)} %get-tuple-element.35.w_ref), custom_call_target="tpu_custom_call" | custom-call | bytes 1 | tf_op jit(solution)/shard_map/pair_conv/pallas_call | solution.py:177
  14.0 2.5 %collective-permute-done.3.a_ref = bf16[2,5,40,320]{3,2,1,0:T(8,128)(2,1)S(1)} collective-permute-done((bf16[2,5,40,320]{3,2,1,0:T(8,128)(2,1)S(1)}, bf16[2,5,40,320]{3,2,1,0:T(8,128)(2,1)S(1)}, u32[]{:S(2)}, u32[]{:S(2)}) %collective-permute-start.3) | collective-permute-done | bytes 256032 | tf_op jit(solution)/shard_map/ppermute | solution.py:404
  16.6 1.5 %collective-permute-start.5 = (bf16[2,200,320]{2,1,0:T(8,128)(2,1)S(1)}, bf16[2,200,320]{2,1,0:T(8,128)(2,1)S(1)}, u32[]{:S(2)}, u32[]{:S(2)}) collective-permute-start(bf16[2,200,320]{2,1,0:T(8,128)(2,1)S(1)} %bitcast.4), channel_id=1, source_target_pairs={{0,16},{16,0},{1,17},{17,1},{2,18},{18,2},{3,19},{19,3},{4,20},{20... | collective-permute-start | bytes 768008 | tf_op jit(solution)/shard_map/ppermute | solution.py:398
  18.8 3.8 %collective-permute-start.6 = (bf16[400,320]{1,0:T(8,128)(2,1)S(1)}, bf16[400,320]{1,0:T(8,128)(2,1)S(1)}, u32[]{:S(2)}, u32[]{:S(2)}) collective-permute-start(bf16[400,320]{1,0:T(8,128)(2,1)S(1)} %add_parts.5.a_ref), channel_id=1, source_target_pairs={{0,3},{1,2},{2,1},{3,0},{4,7},{5,6},{6,5},{7,4},{8,11},{9,10},{10,... | collective-permute-start | bytes 768008 | tf_op jit(solution)/shard_map/ppermute | solution.py:414
  22.7 1.7 %pair_conv.6 = bf16[400,320]{1,0:T(8,128)(2,1)S(1)} custom-call(bf16[2,2,5,40,320]{4,3,2,1,0:T(8,128)(2,1)S(1)} %collect_pairs.1.x_ref, f32[32,320]{1,0:T(8,128)S(1)} %merge_stats.1.norm_ref, bf16[3,960,320]{2,1,0:T(8,128)(2,1)S(1)} %get-tuple-element.35.w_ref), custom_call_target="tpu_custom_call" | custom-call | flops 1150000000 | bytes 1 | tf_op jit(solution)/shard_map/pair_conv/pallas_call | solution.py:177
  24.5 1.8 %collective-permute-done.5.refs_0_ = bf16[2,200,320]{2,1,0:T(8,128)(2,1)S(1)} collective-permute-done((bf16[2,200,320]{2,1,0:T(8,128)(2,1)S(1)}, bf16[2,200,320]{2,1,0:T(8,128)(2,1)S(1)}, u32[]{:S(2)}, u32[]{:S(2)}) %collective-permute-start.5) | collective-permute-done | bytes 256032 | tf_op jit(solution)/shard_map/ppermute | solution.py:398
  26.3 1.7 %pair_conv.7.a_ref = f32[400,320]{1,0:T(8,128)S(1)} custom-call(bf16[2,2,5,40,320]{4,3,2,1,0:T(8,128)(2,1)S(1)} %collect_pairs.1.x_ref, f32[32,320]{1,0:T(8,128)S(1)} %merge_stats.1.norm_ref, bf16[3,960,320]{2,1,0:T(8,128)(2,1)S(1)} %get-tuple-element.35.w_ref), custom_call_target="tpu_custom_call" | custom-call | bytes 1 | tf_op jit(solution)/shard_map/pair_conv/pallas_call | solution.py:177
  28.0 2.8 %collective-permute-done.6.b_ref = bf16[400,320]{1,0:T(8,128)(2,1)S(1)} collective-permute-done((bf16[400,320]{1,0:T(8,128)(2,1)S(1)}, bf16[400,320]{1,0:T(8,128)(2,1)S(1)}, u32[]{:S(2)}, u32[]{:S(2)}) %collective-permute-start.6) | collective-permute-done | bytes 256032 | tf_op jit(solution)/shard_map/ppermute | solution.py:414
  30.9 1.7 %collective-permute-start.10 = (bf16[400,320]{1,0:T(8,128)(2,1)S(1)}, bf16[400,320]{1,0:T(8,128)(2,1)S(1)}, u32[]{:S(2)}, u32[]{:S(2)}) collective-permute-start(bf16[400,320]{1,0:T(8,128)(2,1)S(1)} %add_parts.6.refs_4_.refs_0_), channel_id=1, source_target_pairs={{0,16},{16,0},{1,17},{17,1},{2,18},{18,2},{3,19},{19,3},{4,20},{20... | collective-permute-start | bytes 768008 | tf_op jit(solution)/shard_map/ppermute | solution.py:398
  32.7 3.8 %collective-permute-start.9 = (bf16[400,320]{1,0:T(8,128)(2,1)S(1)}, bf16[400,320]{1,0:T(8,128)(2,1)S(1)}, u32[]{:S(2)}, u32[]{:S(2)}) collective-permute-start(bf16[400,320]{1,0:T(8,128)(2,1)S(1)} %add_parts.6.refs_4_.refs_0_), channel_id=1, source_target_pairs={{0,1},{1,0},{2,3},{3,2},{4,5},{5,4},{6,7},{7,6},{8,9},{9,8},{10,11... | collective-permute-start | bytes 768008 | tf_op jit(solution)/shard_map/ppermute | solution.py:425
  36.5 1.1 %collective-permute-start.8 = (bf16[2,200,320]{2,1,0:T(8,128)(2,1)S(1)}, bf16[2,200,320]{2,1,0:T(8,128)(2,1)S(1)}, u32[]{:S(2)}, u32[]{:S(2)}) collective-permute-start(bf16[2,200,320]{2,1,0:T(8,128)(2,1)S(1)} %bitcast.5), channel_id=1, source_target_pairs={{0,8},{4,12},{8,0},{12,4},{1,9},{5,13},{9,1},{13,5},{2,10},{6,14},... | collective-permute-start | bytes 768008 | tf_op jit(solution)/shard_map/ppermute | solution.py:427
  37.7 2.5 %collective-permute-start.13 = (bf16[400,320]{1,0:T(8,128)(2,1)S(1)}, bf16[400,320]{1,0:T(8,128)(2,1)S(1)}, u32[]{:S(2)}, u32[]{:S(2)}) collective-permute-start(bf16[400,320]{1,0:T(8,128)(2,1)S(1)} %add_parts.7.a_ref), channel_id=1, source_target_pairs={{0,3},{1,2},{2,1},{3,0},{4,7},{5,6},{6,5},{7,4},{8,11},{9,10},{10,... | collective-permute-start | bytes 768008 | tf_op jit(solution)/shard_map/ppermute | solution.py:424
  40.2 4.1 %collective-permute-done.9.x_ref = bf16[400,320]{1,0:T(8,128)(2,1)S(1)} collective-permute-done((bf16[400,320]{1,0:T(8,128)(2,1)S(1)}, bf16[400,320]{1,0:T(8,128)(2,1)S(1)}, u32[]{:S(2)}, u32[]{:S(2)}) %collective-permute-start.9) | collective-permute-done | bytes 256032 | tf_op jit(solution)/shard_map/ppermute | solution.py:425
  44.4 1.4 %collective-permute-start.14 = (bf16[400,320]{1,0:T(8,128)(2,1)S(1)}, bf16[400,320]{1,0:T(8,128)(2,1)S(1)}, u32[]{:S(2)}, u32[]{:S(2)}) collective-permute-start(bf16[400,320]{1,0:T(8,128)(2,1)S(1)} %copy_piece.1.refs_5_.refs_1_), channel_id=1, source_target_pairs={{0,16},{16,0},{1,17},{17,1},{2,18},{18,2},{3,19},{19,3},{4,20},{20... | collective-permute-start | bytes 768008 | tf_op jit(solution)/shard_map/ppermute | solution.py:398
  45.8 5.1 %collective-permute-done.13.b_ref = bf16[400,320]{1,0:T(8,128)(2,1)S(1)} collective-permute-done((bf16[400,320]{1,0:T(8,128)(2,1)S(1)}, bf16[400,320]{1,0:T(8,128)(2,1)S(1)}, u32[]{:S(2)}, u32[]{:S(2)}) %collective-permute-start.13) | collective-permute-done | bytes 256032 | tf_op jit(solution)/shard_map/ppermute | solution.py:424
  51.0 1.7 %collective-permute-start.15 = (bf16[400,320]{1,0:T(8,128)(2,1)S(1)}, bf16[400,320]{1,0:T(8,128)(2,1)S(1)}, u32[]{:S(2)}, u32[]{:S(2)}) collective-permute-start(bf16[400,320]{1,0:T(8,128)(2,1)S(1)} %add_parts.8.refs_2_.refs_4_), channel_id=1, source_target_pairs={{0,1},{1,0},{2,3},{3,2},{4,5},{5,4},{6,7},{7,6},{8,9},{9,8},{10,11... | collective-permute-start | bytes 768008 | tf_op jit(solution)/shard_map/ppermute | solution.py:434
  53.2 1.4 %collective-permute-start.16 = (bf16[400,320]{1,0:T(8,128)(2,1)S(1)}, bf16[400,320]{1,0:T(8,128)(2,1)S(1)}, u32[]{:S(2)}, u32[]{:S(2)}) collective-permute-start(bf16[400,320]{1,0:T(8,128)(2,1)S(1)} %add_parts.8.refs_2_.refs_4_), channel_id=1, source_target_pairs={{0,16},{16,0},{1,17},{17,1},{2,18},{18,2},{3,19},{19,3},{4,20},{20... | collective-permute-start | bytes 768008 | tf_op jit(solution)/shard_map/ppermute | solution.py:398
  54.6 1.3 %temporal_grads.4.refs_6_ = f32[3,320,320]{2,1,0:T(8,128)S(1)} custom-call(bf16[2,200,320]{2,1,0:T(8,128)(2,1)S(1)} %bitcast.7, bf16[2,200,320]{2,1,0:T(8,128)(2,1)S(1)} %collective-permute-done.7.refs_1_, bf16[2,200,320]{2,1,0:T(8,128)(2,1)S(1)} %collective-permute-done.8.refs_2_, bf16[2,200,320]{2,1,0:T(8,128)(2,1)S(1)} %collective-permute-done.11.refs_3_, ...), custom_call_target="tpu_custom_call" | custom-call | flops 1150000000 | bytes 1 | tf_op jit(solution)/shard_map/temporal_grads/pallas_call | solution.py:280
  56.0 1.9 %collective-permute-done.15.refs_3_.refs_5_ = bf16[400,320]{1,0:T(8,128)(2,1)S(1)} collective-permute-done((bf16[400,320]{1,0:T(8,128)(2,1)S(1)}, bf16[400,320]{1,0:T(8,128)(2,1)S(1)}, u32[]{:S(2)}, u32[]{:S(2)}) %collective-permute-start.15) | collective-permute-done | bytes 256032 | tf_op jit(solution)/shard_map/ppermute | solution.py:434
  57.9 0.9 %temporal_conv.3 = bf16[2,200,320]{2,1,0:T(8,128)(2,1)S(1)} custom-call(bf16[400,320]{1,0:T(8,128)(2,1)S(1)} %add_parts.6.refs_4_.refs_0_, bf16[400,320]{1,0:T(8,128)(2,1)S(1)} %copy_piece.1.refs_5_.refs_1_, bf16[400,320]{1,0:T(8,128)(2,1)S(1)} %add_parts.8.refs_2_.refs_4_, bf16[400,320]{1,0:T(8,128)(2,1)S(1)} %collective-permute-done.15.refs_3_.refs_5_, ...), custom_call_target="tpu_custom_call" | custom-call | flops 57500000256 | bytes 1 | tf_op jit(solution)/shard_map/temporal_conv/pallas_call | solution.py:312
  59.5 1.6 %collective-permute-start.21 = (bf16[400,320]{1,0:T(8,128)(2,1)S(1)}, bf16[400,320]{1,0:T(8,128)(2,1)S(1)}, u32[]{:S(2)}, u32[]{:S(2)}) collective-permute-start(bf16[400,320]{1,0:T(8,128)(2,1)S(1)} %collective-permute-done.15.refs_3_.refs_5_), channel_id=1, source_target_pairs={{0,16},{16,0},{1,17},{17,1},{2,18},{18,2},{3,19},{19,3},{4,20},{20... | collective-permute-start | bytes 768008 | tf_op jit(solution)/shard_map/ppermute | solution.py:398
  61.1 0.9 %temporal_conv.4.a_ref = f32[2,200,320]{2,1,0:T(8,128)S(1)} custom-call(bf16[400,320]{1,0:T(8,128)(2,1)S(1)} %add_parts.6.refs_4_.refs_0_, bf16[400,320]{1,0:T(8,128)(2,1)S(1)} %copy_piece.1.refs_5_.refs_1_, bf16[400,320]{1,0:T(8,128)(2,1)S(1)} %add_parts.8.refs_2_.refs_4_, bf16[400,320]{1,0:T(8,128)(2,1)S(1)} %collective-permute-done.15.refs_3_.refs_5_, ...), custom_call_target="tpu_custom_call" | custom-call | bytes 1 | tf_op jit(solution)/shard_map/temporal_conv/pallas_call | solution.py:312
  62.5 1.3 %temporal_grads.5.refs_6_ = f32[3,320,320]{2,1,0:T(8,128)S(1)} custom-call(bf16[2,200,320]{2,1,0:T(8,128)(2,1)S(1)} %collective-permute-done.5.refs_0_, bf16[2,200,320]{2,1,0:T(8,128)(2,1)S(1)} %collective-permute-done.18.refs_1_, bf16[2,200,320]{2,1,0:T(8,128)(2,1)S(1)} %collective-permute-done.19.refs_2_, ...), custom_call_target="tpu_custom_call" | custom-call | bytes 1 | tf_op jit(solution)/shard_map/temporal_grads/pallas_call | solution.py:280
  63.9 1.4 %temporal_grads.6.refs_7_ = f32[3,320,320]{2,1,0:T(8,128)S(1)} custom-call(bf16[2,200,320]{2,1,0:T(8,128)(2,1)S(1)} %bitcast.8, bf16[2,200,320]{2,1,0:T(8,128)(2,1)S(1)} %collective-permute-done.7.refs_1_, bf16[2,200,320]{2,1,0:T(8,128)(2,1)S(1)} %collective-permute-done.8.refs_2_, bf16[2,200,320]{2,1,0:T(8,128)(2,1)S(1)} %collective-permute-done.11.refs_3_, ...), custom_call_target="tpu_custom_call" | custom-call | bytes 1 | tf_op jit(solution)/shard_map/temporal_grads/pallas_call | solution.py:280
  65.2 1.5 %temporal_conv.5 = (bf16[2,200,320]{2,1,0:T(8,128)(2,1)S(1)}, f32[2,200,320]{2,1,0:T(8,128)S(1)}) custom-call(bf16[400,320]{1,0:T(8,128)(2,1)S(1)} %add_parts.6.refs_4_.refs_0_, bf16[400,320]{1,0:T(8,128)(2,1)S(1)} %copy_piece.1.refs_5_.refs_1_, bf16[400,320]{1,0:T(8,128)(2,1)S(1)} %add_parts.8.refs_2_.refs_4_, ...), custom_call_target="tpu_custom_call" | custom-call | bytes 1 | tf_op jit(solution)/shard_map/temporal_conv/pallas_call | solution.py:312
  66.8 2.4 %collective-permute-done.21.refs_5_ = bf16[400,320]{1,0:T(8,128)(2,1)S(1)} collective-permute-done((bf16[400,320]{1,0:T(8,128)(2,1)S(1)}, bf16[400,320]{1,0:T(8,128)(2,1)S(1)}, u32[]{:S(2)}, u32[]{:S(2)}) %collective-permute-start.21) | collective-permute-done | bytes 256032 | tf_op jit(solution)/shard_map/ppermute | solution.py:398
  69.2 2.2 %temporal_grads.7 = f32[3,320,320]{2,1,0:T(8,128)} custom-call(bf16[2,200,320]{2,1,0:T(8,128)(2,1)S(1)} %collective-permute-done.5.refs_0_, bf16[2,200,320]{2,1,0:T(8,128)(2,1)S(1)} %collective-permute-done.18.refs_1_, bf16[2,200,320]{2,1,0:T(8,128)(2,1)S(1)} %collective-permute-done.19.refs_2_, bf16[2,200,320]{2,1,0:T(8,128)(2,1)S(1)} %collective-permute-done.20.refs_3_, ...), custom_call_target="tpu_custom_call" | custom-call | flops 57500000256 | bytes 1 | tf_op jit(solution)/shard_map/temporal_grads/pallas_call | solution.py:280
  (55 shorter events, 6.6 us)
Async XLA Ops:
  0.6 2.0 %collective-permute-start = (bf16[2,5,40,320]{3,2,1,0:T(8,128)(2,1)}, bf16[2,5,40,320]{3,2,1,0:T(8,128)(2,1)S(1)}, u32[]{:S(2)}, u32[]{:S(2)}) collective-permute-start(bf16[2,5,40,320]{3,2,1,0:T(8,128)(2,1)} %bitcast.10), channel_id=1, source_target_pairs={{0,4},{4,0},{8,12},{12,8},{1,5},{5,1},{9,13},{13,9},{2,6},{6,2},{1... | collective-permute-start | bytes 768008 | tf_op jit(solution)/shard_map/ppermute | solution.py:400
  1.1 1.0 %copy-start.4 = (bf16[1,2,5,40,320]{4,3,2,1,0:T(8,128)(2,1)S(1)}, bf16[1,2,5,40,320]{4,3,2,1,0:T(8,128)(2,1)}, u32[]{:S(2)}) copy-start(bf16[1,2,5,40,320]{4,3,2,1,0:T(8,128)(2,1)} %param.6) | copy-start | bytes 768004
  2.2 4.4 %copy-start.3 = (bf16[9,320,320]{2,1,0:T(8,128)(2,1)S(1)}, bf16[9,320,320]{2,1,0:T(8,128)(2,1)}, u32[]{:S(2)}) copy-start(bf16[9,320,320]{2,1,0:T(8,128)(2,1)} %param.9) | copy-start | bytes 5529604
  2.2 4.4 %copy-start.6 = (f32[320]{0:T(512)S(1)}, f32[320]{0:T(512)}, u32[]{:S(2)}) copy-start(f32[320]{0:T(512)} %gain_ref.1) | copy-start | bytes 3844
  2.2 4.4 %copy-start.7 = (f32[320]{0:T(512)S(1)}, f32[320]{0:T(512)}, u32[]{:S(2)}) copy-start(f32[320]{0:T(512)} %bias_ref.1) | copy-start | bytes 3844
  3.7 4.7 %collective-permute-start.1 = (f32[16,320]{1,0:T(8,128)S(1)}, f32[16,320]{1,0:T(8,128)S(1)}, u32[]{:S(2)}, u32[]{:S(2)}) collective-permute-start(f32[16,320]{1,0:T(8,128)S(1)} %get-tuple-element.33.s0_ref), channel_id=1, source_target_pairs={{0,8},{4,12},{8,0},{12,4},{1,9},{5,13},{9,1},{13,5},{2,10},{6,14},... | collective-permute-start | bytes 61448 | tf_op jit(solution)/shard_map/ppermute | solution.py:402
  6.6 1.0 %copy-start.5 = (bf16[1,2,5,40,320]{4,3,2,1,0:T(8,128)(2,1)S(1)}, bf16[1,2,5,40,320]{4,3,2,1,0:T(8,128)(2,1)}, u32[]{:S(2)}) copy-start(bf16[1,2,5,40,320]{4,3,2,1,0:T(8,128)(2,1)} %param.6) | copy-start | bytes 768004
  7.6 9.0 %collective-permute-start.3 = (bf16[2,5,40,320]{3,2,1,0:T(8,128)(2,1)S(1)}, bf16[2,5,40,320]{3,2,1,0:T(8,128)(2,1)S(1)}, u32[]{:S(2)}, u32[]{:S(2)}) collective-permute-start(bf16[2,5,40,320]{3,2,1,0:T(8,128)(2,1)S(1)} %bitcast.12), channel_id=1, source_target_pairs={{0,8},{4,12},{8,0},{12,4},{1,9},{5,13},{9,1},{13,5},{2,10},{6,14},... | collective-permute-start | bytes 768008 | tf_op jit(solution)/shard_map/ppermute | solution.py:404
  10.2 6.4 %copy-start.1 = (bf16[1,2,5,40,320]{4,3,2,1,0:T(8,128)(2,1)S(1)}, bf16[1,2,5,40,320]{4,3,2,1,0:T(8,128)(2,1)}, u32[]{:S(2)}) copy-start(bf16[1,2,5,40,320]{4,3,2,1,0:T(8,128)(2,1)} %param.11) | copy-start | bytes 768004
  10.2 8.6 %collective-permute-start.2 = (bf16[400,320]{1,0:T(8,128)(2,1)S(1)}, bf16[400,320]{1,0:T(8,128)(2,1)S(1)}, u32[]{:S(2)}, u32[]{:S(2)}) collective-permute-start(bf16[400,320]{1,0:T(8,128)(2,1)S(1)} %pair_conv.4), channel_id=1, source_target_pairs={{0,1},{1,0},{2,3},{3,2},{4,5},{5,4},{6,7},{7,6},{8,9},{9,8},{10,11... | collective-permute-start | bytes 768008 | tf_op jit(solution)/shard_map/ppermute | solution.py:408
  16.6 6.0 %collective-permute-start.4 = (bf16[2,5,40,320]{3,2,1,0:T(8,128)(2,1)S(1)}, bf16[2,5,40,320]{3,2,1,0:T(8,128)(2,1)S(1)}, u32[]{:S(2)}, u32[]{:S(2)}) collective-permute-start(bf16[2,5,40,320]{3,2,1,0:T(8,128)(2,1)S(1)} %collective-permute-done.3.a_ref), channel_id=1, source_target_pairs={{0,4},{4,0},{8,12},{12,8},{1,5},{5,1},{9,13},{13,9},{2,6},{6,2},{1... | collective-permute-start | bytes 768008 | tf_op jit(solution)/shard_map/ppermute | solution.py:411
  16.6 9.7 %collective-permute-start.5 = (bf16[2,200,320]{2,1,0:T(8,128)(2,1)S(1)}, bf16[2,200,320]{2,1,0:T(8,128)(2,1)S(1)}, u32[]{:S(2)}, u32[]{:S(2)}) collective-permute-start(bf16[2,200,320]{2,1,0:T(8,128)(2,1)S(1)} %bitcast.4), channel_id=1, source_target_pairs={{0,16},{16,0},{1,17},{17,1},{2,18},{18,2},{3,19},{19,3},{4,20},{20... | collective-permute-start | bytes 768008 | tf_op jit(solution)/shard_map/ppermute | solution.py:398
  18.8 12.1 %collective-permute-start.6 = (bf16[400,320]{1,0:T(8,128)(2,1)S(1)}, bf16[400,320]{1,0:T(8,128)(2,1)S(1)}, u32[]{:S(2)}, u32[]{:S(2)}) collective-permute-start(bf16[400,320]{1,0:T(8,128)(2,1)S(1)} %add_parts.5.a_ref), channel_id=1, source_target_pairs={{0,3},{1,2},{2,1},{3,0},{4,7},{5,6},{6,5},{7,4},{8,11},{9,10},{10,... | collective-permute-start | bytes 768008 | tf_op jit(solution)/shard_map/ppermute | solution.py:414
  24.4 13.2 %collective-permute-start.12 = (bf16[400,320]{1,0:T(8,128)(2,1)S(1)}, bf16[400,320]{1,0:T(8,128)(2,1)S(1)}, u32[]{:S(2)}, u32[]{:S(2)}) collective-permute-start(bf16[400,320]{1,0:T(8,128)(2,1)S(1)} %pair_conv.6), channel_id=1, source_target_pairs={{0,1},{1,0},{2,3},{3,2},{4,5},{5,4},{6,7},{7,6},{8,9},{9,8},{10,11... | collective-permute-start | bytes 768008 | tf_op jit(solution)/shard_map/ppermute | solution.py:416
  28.0 8.5 %copy-start.2 = (bf16[1,2,5,40,320]{4,3,2,1,0:T(8,128)(2,1)S(1)}, bf16[1,2,5,40,320]{4,3,2,1,0:T(8,128)(2,1)}, u32[]{:S(2)}) copy-start(bf16[1,2,5,40,320]{4,3,2,1,0:T(8,128)(2,1)} %param.11) | copy-start | bytes 768004
  30.9 9.3 %collective-permute-start.10 = (bf16[400,320]{1,0:T(8,128)(2,1)S(1)}, bf16[400,320]{1,0:T(8,128)(2,1)S(1)}, u32[]{:S(2)}, u32[]{:S(2)}) collective-permute-start(bf16[400,320]{1,0:T(8,128)(2,1)S(1)} %add_parts.6.refs_4_.refs_0_), channel_id=1, source_target_pairs={{0,16},{16,0},{1,17},{17,1},{2,18},{18,2},{3,19},{19,3},{4,20},{20... | collective-permute-start | bytes 768008 | tf_op jit(solution)/shard_map/ppermute | solution.py:398
  32.7 11.7 %collective-permute-start.9 = (bf16[400,320]{1,0:T(8,128)(2,1)S(1)}, bf16[400,320]{1,0:T(8,128)(2,1)S(1)}, u32[]{:S(2)}, u32[]{:S(2)}) collective-permute-start(bf16[400,320]{1,0:T(8,128)(2,1)S(1)} %add_parts.6.refs_4_.refs_0_), channel_id=1, source_target_pairs={{0,1},{1,0},{2,3},{3,2},{4,5},{5,4},{6,7},{7,6},{8,9},{9,8},{10,11... | collective-permute-start | bytes 768008 | tf_op jit(solution)/shard_map/ppermute | solution.py:425
  36.5 9.3 %collective-permute-start.8 = (bf16[2,200,320]{2,1,0:T(8,128)(2,1)S(1)}, bf16[2,200,320]{2,1,0:T(8,128)(2,1)S(1)}, u32[]{:S(2)}, u32[]{:S(2)}) collective-permute-start(bf16[2,200,320]{2,1,0:T(8,128)(2,1)S(1)} %bitcast.5), channel_id=1, source_target_pairs={{0,8},{4,12},{8,0},{12,4},{1,9},{5,13},{9,1},{13,5},{2,10},{6,14},... | collective-permute-start | bytes 768008 | tf_op jit(solution)/shard_map/ppermute | solution.py:427
  37.7 13.2 %collective-permute-start.13 = (bf16[400,320]{1,0:T(8,128)(2,1)S(1)}, bf16[400,320]{1,0:T(8,128)(2,1)S(1)}, u32[]{:S(2)}, u32[]{:S(2)}) collective-permute-start(bf16[400,320]{1,0:T(8,128)(2,1)S(1)} %add_parts.7.a_ref), channel_id=1, source_target_pairs={{0,3},{1,2},{2,1},{3,0},{4,7},{5,6},{6,5},{7,4},{8,11},{9,10},{10,... | collective-permute-start | bytes 768008 | tf_op jit(solution)/shard_map/ppermute | solution.py:424
  40.2 14.4 %collective-permute-start.7 = (bf16[2,200,320]{2,1,0:T(8,128)(2,1)S(1)}, bf16[2,200,320]{2,1,0:T(8,128)(2,1)S(1)}, u32[]{:S(2)}, u32[]{:S(2)}) collective-permute-start(bf16[2,200,320]{2,1,0:T(8,128)(2,1)S(1)} %bitcast.6), channel_id=1, source_target_pairs={{0,4},{4,0},{8,12},{12,8},{1,5},{5,1},{9,13},{13,9},{2,6},{6,2},{1... | collective-permute-start | bytes 768008 | tf_op jit(solution)/shard_map/ppermute | solution.py:426
  44.4 8.8 %collective-permute-start.14 = (bf16[400,320]{1,0:T(8,128)(2,1)S(1)}, bf16[400,320]{1,0:T(8,128)(2,1)S(1)}, u32[]{:S(2)}, u32[]{:S(2)}) collective-permute-start(bf16[400,320]{1,0:T(8,128)(2,1)S(1)} %copy_piece.1.refs_5_.refs_1_), channel_id=1, source_target_pairs={{0,16},{16,0},{1,17},{17,1},{2,18},{18,2},{3,19},{19,3},{4,20},{20... | collective-permute-start | bytes 768008 | tf_op jit(solution)/shard_map/ppermute | solution.py:398
  45.8 8.8 %collective-permute-start.11 = (bf16[2,200,320]{2,1,0:T(8,128)(2,1)S(1)}, bf16[2,200,320]{2,1,0:T(8,128)(2,1)S(1)}, u32[]{:S(2)}, u32[]{:S(2)}) collective-permute-start(bf16[2,200,320]{2,1,0:T(8,128)(2,1)S(1)} %collective-permute-done.8.refs_2_), channel_id=1, source_target_pairs={{0,4},{4,0},{8,12},{12,8},{1,5},{5,1},{9,13},{13,9},{2,6},{6,2},{1... | collective-permute-start | bytes 768008 | tf_op jit(solution)/shard_map/ppermute | solution.py:435
  51.0 6.9 %copy-start = (bf16[3,320,320]{2,1,0:T(8,128)(2,1)S(1)}, bf16[3,320,320]{2,1,0:T(8,128)(2,1)}, u32[]{:S(2)}) copy-start(bf16[3,320,320]{2,1,0:T(8,128)(2,1)} %refs_4_.5) | copy-start | bytes 1843204
  51.0 6.9 %collective-permute-start.15 = (bf16[400,320]{1,0:T(8,128)(2,1)S(1)}, bf16[400,320]{1,0:T(8,128)(2,1)S(1)}, u32[]{:S(2)}, u32[]{:S(2)}) collective-permute-start(bf16[400,320]{1,0:T(8,128)(2,1)S(1)} %add_parts.8.refs_2_.refs_4_), channel_id=1, source_target_pairs={{0,1},{1,0},{2,3},{3,2},{4,5},{5,4},{6,7},{7,6},{8,9},{9,8},{10,11... | collective-permute-start | bytes 768008 | tf_op jit(solution)/shard_map/ppermute | solution.py:434
  52.7 6.9 %collective-permute-start.19 = (bf16[2,200,320]{2,1,0:T(8,128)(2,1)S(1)}, bf16[2,200,320]{2,1,0:T(8,128)(2,1)S(1)}, u32[]{:S(2)}, u32[]{:S(2)}) collective-permute-start(bf16[2,200,320]{2,1,0:T(8,128)(2,1)S(1)} %collective-permute-done.5.refs_0_), channel_id=1, source_target_pairs={{0,8},{4,12},{8,0},{12,4},{1,9},{5,13},{9,1},{13,5},{2,10},{6,14},... | collective-permute-start | bytes 768008 | tf_op jit(solution)/shard_map/ppermute | solution.py:431
  53.2 8.8 %collective-permute-start.16 = (bf16[400,320]{1,0:T(8,128)(2,1)S(1)}, bf16[400,320]{1,0:T(8,128)(2,1)S(1)}, u32[]{:S(2)}, u32[]{:S(2)}) collective-permute-start(bf16[400,320]{1,0:T(8,128)(2,1)S(1)} %add_parts.8.refs_2_.refs_4_), channel_id=1, source_target_pairs={{0,16},{16,0},{1,17},{17,1},{2,18},{18,2},{3,19},{19,3},{4,20},{20... | collective-permute-start | bytes 768008 | tf_op jit(solution)/shard_map/ppermute | solution.py:398
  58.8 3.2 %collective-permute-start.17 = (bf16[2,200,320]{2,1,0:T(8,128)(2,1)S(1)}, bf16[2,200,320]{2,1,0:T(8,128)(2,1)S(1)}, u32[]{:S(2)}, u32[]{:S(2)}) collective-permute-start(bf16[2,200,320]{2,1,0:T(8,128)(2,1)S(1)} %temporal_conv.3), channel_id=1, source_target_pairs={{0,4},{4,0},{8,12},{12,8},{1,5},{5,1},{9,13},{13,9},{2,6},{6,2},{1... | collective-permute-start | bytes 768008 | tf_op jit(solution)/shard_map/ppermute | solution.py:444
  58.9 3.6 %collective-permute-start.18 = (bf16[2,200,320]{2,1,0:T(8,128)(2,1)S(1)}, bf16[2,200,320]{2,1,0:T(8,128)(2,1)S(1)}, u32[]{:S(2)}, u32[]{:S(2)}) collective-permute-start(bf16[2,200,320]{2,1,0:T(8,128)(2,1)S(1)} %collective-permute-done.5.refs_0_), channel_id=1, source_target_pairs={{0,4},{4,0},{8,12},{12,8},{1,5},{5,1},{9,13},{13,9},{2,6},{6,2},{1... | collective-permute-start | bytes 768008 | tf_op jit(solution)/shard_map/ppermute | solution.py:430
  59.5 3.0 %collective-permute-start.20 = (bf16[2,200,320]{2,1,0:T(8,128)(2,1)S(1)}, bf16[2,200,320]{2,1,0:T(8,128)(2,1)S(1)}, u32[]{:S(2)}, u32[]{:S(2)}) collective-permute-start(bf16[2,200,320]{2,1,0:T(8,128)(2,1)S(1)} %collective-permute-done.19.refs_2_), channel_id=1, source_target_pairs={{0,4},{4,0},{8,12},{12,8},{1,5},{5,1},{9,13},{13,9},{2,6},{6,2},{1... | collective-permute-start | bytes 768008 | tf_op jit(solution)/shard_map/ppermute | solution.py:438
  59.5 9.7 %collective-permute-start.21 = (bf16[400,320]{1,0:T(8,128)(2,1)S(1)}, bf16[400,320]{1,0:T(8,128)(2,1)S(1)}, u32[]{:S(2)}, u32[]{:S(2)}) collective-permute-start(bf16[400,320]{1,0:T(8,128)(2,1)S(1)} %collective-permute-done.15.refs_3_.refs_5_), channel_id=1, source_target_pairs={{0,16},{16,0},{1,17},{17,1},{2,18},{18,2},{3,19},{19,3},{4,20},{20... | collective-permute-start | bytes 768008 | tf_op jit(solution)/shard_map/ppermute | solution.py:398
  62.0 9.4 %collective-permute-start.23 = (bf16[2,200,320]{2,1,0:T(8,128)(2,1)S(1)}, bf16[2,200,320]{2,1,0:T(8,128)(2,1)S(1)}, u32[]{:S(2)}, u32[]{:S(2)}) collective-permute-start(bf16[2,200,320]{2,1,0:T(8,128)(2,1)S(1)} %add_parts.9), channel_id=1, source_target_pairs={{0,8},{4,12},{8,0},{12,4},{1,9},{5,13},{9,1},{13,5},{2,10},{6,14},... | collective-permute-start | bytes 768008 | tf_op jit(solution)/shard_map/ppermute | solution.py:451
  66.7 4.7 %collective-permute-start.22 = (bf16[2,200,320]{2,1,0:T(8,128)(2,1)S(1)}, bf16[2,200,320]{2,1,0:T(8,128)(2,1)S(1)}, u32[]{:S(2)}, u32[]{:S(2)}) collective-permute-start(bf16[2,200,320]{2,1,0:T(8,128)(2,1)S(1)} %get-tuple-element.61), channel_id=1, source_target_pairs={{0,4},{4,0},{8,12},{12,8},{1,5},{5,1},{9,13},{13,9},{2,6},{6,2},{1... | collective-permute-start | bytes 768008 | tf_op jit(solution)/shard_map/ppermute | solution.py:450
